TPU v7x, 32 devices: a whole 2x2x4 slice. The times are simulated.
32 devices in a mesh: band: 2 (over y), rows: 16 (over z, x, core).
Axes of the slice: x: 2, y: 2, z: 4, core: 2. Of those that a mesh axis runs over, the one named last changes fastest.
Arguments:
- start_iterate: float32 [1024, 16, 128], P(('band', 'rows')), may hold values from 0 to 2
- right_side: float32 [1024, 16, 128], P(('band', 'rows')), as said below
- diag_table: float32 [8, 128, 128], replicated, as said below
- inverse_table: float32 [8, 128, 128], replicated, as said below
- coupling_tiles: float32 [8, 128, 128], replicated, may hold values from 0 to 0.009375
- diag_index: int32 [1024], P(('band', 'rows')), may hold values from 0 to 7
- tile_index: int32 [1024, 4], P(('band', 'rows')), may hold values from 0 to 7
- source_owner: int32 [1024, 2], P(('band', 'rows')), may hold values from 0 to 15, all different within a row; in each aligned block of 32 rows (0 to 31, 32 to 63, ...) at most 8 rows name the same one
- source_local: int32 [1024, 2], P(('band', 'rows')), may hold values from 0 to 31
- aggregate_map: int32 [1024, 1], P(('band', 'rows')), may hold values from 0 to 255
Outputs:
- swept_iterate: float32 [1024, 16, 128], P(('band', 'rows'))
Inputs may be any that keep to these rules, and one draw needn't show every extreme that they name: `source_owner`: within each aligned block of 32 rows (the rows of one device) no owner is named by more than 8 entries, a bound that some block reaches; the 2 owners of one row differ. `aggregate_map`: every aggregate is named by at least one block row. `diag_table`: diagonal entries lie from 6 to 10; off-diagonal entries are nonpositive with magnitude at most 5 / 128. `inverse_table`: entries are nonnegative; each block is a first-order approximation of the inverse of the diagonal block of the same index, not its exact inverse. `right_side`: entries are nonnegative.
All inputs are finite; a program needn't handle non-finite values.
Results may differ from a plain program's by a relative error of at most 0.0001.
Values sent between devices are 32-bit elements; how exact they have to be, the bound alone decides.
No kernel may reach another device: no remote copies, remote signals or barrier semaphores. Data moves between devices by JAX's collectives and lax.ppermute only.
A program may use at most 64 MiB of HBM per device.

v0:
```python
import jax
import jax.numpy as jnp
from jax import lax
from jax.sharding import PartitionSpec as P

AGG_DEV = 8


HIGH = lax.Precision.HIGHEST


def shifted(value, axis, steps):
    count = lax.axis_size(axis)
    initial, last = (max(0, -steps), min(count, count - steps))
    return lax.ppermute(value, axis, [(source, source + steps) for source in range(initial, last)])


def apply_table(table, index, iterate):
    chosen = jnp.take(table, index, axis=0)
    return jnp.einsum("rst,rvt->rvs", chosen, iterate, precision=HIGH)


def coupling(iterate, wanted, slot_place, tile_mats, n_rows, capacity):
    inner = iterate.shape[1:]
    fetched = jnp.take(iterate, wanted, axis=0).reshape((n_rows, capacity) + inner)
    arrived = lax.all_to_all(fetched, "rows", split_axis=0, concat_axis=0, tiled=True)
    arrived = arrived.reshape((n_rows * capacity,) + inner)
    remote = jnp.take(arrived, slot_place, axis=0).reshape((iterate.shape[0], -1) + inner)
    from_lower = shifted(iterate, "band", 1)
    from_upper = shifted(iterate, "band", -1)
    sources = jnp.concatenate([remote, from_lower[:, None], from_upper[:, None]], axis=1)
    return jnp.einsum("rkst,rkvt->rvs", tile_mats, sources, precision=HIGH)


def on_device(
    start_iterate,
    right_side,
    diag_table,
    inverse_table,
    coupling_tiles,
    diag_index,
    tile_index,
    source_owner,
    source_local,
    aggregate_map,
):
    block_rows = start_iterate.shape[0]
    width_k = source_owner.shape[1]
    n_rows = lax.axis_size("rows")
    capacity = max(2, 2 * width_k * block_rows // n_rows)
    owners_flat = source_owner.reshape(-1)
    locals_flat = source_local.reshape(-1)
    matches = (owners_flat[:, None] == jnp.arange(n_rows, dtype=jnp.int32)[None, :]).astype(
        jnp.int32
    )
    before = jnp.cumsum(matches, axis=0) - matches
    slot_rank = jnp.sum(before * matches, axis=1)
    slot_place = owners_flat * capacity + slot_rank
    requests = jnp.zeros((n_rows * capacity,), jnp.int32).at[slot_place].set(locals_flat)
    wanted = lax.all_to_all(
        requests.reshape(n_rows, capacity), "rows", split_axis=0, concat_axis=0, tiled=True
    ).reshape(-1)
    tile_mats = jnp.take(coupling_tiles, tile_index, axis=0)
    iterate = start_iterate
    for sweep_pass in range(2):
        coupled = coupling(iterate, wanted, slot_place, tile_mats, n_rows, capacity)
        iterate = apply_table(inverse_table, diag_index, right_side + coupled)
    coupled = coupling(iterate, wanted, slot_place, tile_mats, n_rows, capacity)
    residual = right_side + coupled - apply_table(diag_table, diag_index, iterate)
    groups = aggregate_map[:, 0]
    total_groups = AGG_DEV * lax.axis_size("band") * lax.axis_size("rows")
    residual_sums = jnp.sum(residual, axis=2)
    table_sums = jnp.sum(diag_table, axis=(1, 2))
    block_sums = jnp.take(table_sums, diag_index)
    partial_residual = jax.ops.segment_sum(residual_sums, groups, num_segments=total_groups)
    partial_diag = jax.ops.segment_sum(block_sums, groups, num_segments=total_groups)
    whole_residual, whole_diag = lax.psum((partial_residual, partial_diag), ("band", "rows"))
    correction = whole_residual / whole_diag[:, None]
    return iterate + jnp.take(correction, groups, axis=0)[:, :, None]


def solution(mesh):
    in_specs = (
        P(("band", "rows"), None, None),
        P(("band", "rows"), None, None),
        P(),
        P(),
        P(),
        P(("band", "rows")),
        P(("band", "rows"), None),
        P(("band", "rows"), None),
        P(("band", "rows"), None),
        P(("band", "rows"), None),
    )
    out_specs = P(("band", "rows"), None, None)
    return jax.shard_map(
        on_device, mesh=mesh, in_specs=in_specs, out_specs=out_specs, check_vma=False
    )
```

profile of v0, /device:TPU:0, one launch (start us, length us, event | category | flops | bytes accessed | tf_op | source)
XLA Modules:
  0.0 212.5 jit_solution(2915737976742640406)
XLA Ops:
  3.9 13.6 %all_to_all.24 = s32[16,1,8]{2,1,0:T(1,128)S(1)} all-to-all(s32[16,1,8]{2,1,0:T(1,128)S(1)} %bitcast.61), channel_id=1, replica_groups=mesh['band'=2,'rows'=16] {'rows'}, dimensions={0} | all-to-all | bytes 1024 | tf_op jit(solution)/shard_map/all_to_all | solution.py:60
  21.6 4.3 %all-to-all-start.1 = ((f32[16,8,16,128]{3,2,1,0:T(8,128)}), f32[16,8,16,128]{3,2,1,0:T(8,128)}, u32[]{:S(2)}, u32[]{:S(2)}) async-start(f32[16,8,16,128]{3,2,1,0:T(8,128)} %bitcast.3), calls=%async_computation.1 | async-start | bytes 2097152 | tf_op jit(solution)/shard_map/all_to_all | solution.py:26
  26.0 4.1 %collective-permute-start = (f32[32,16,128]{2,1,0:T(8,128)S(1)}, f32[32,16,128]{2,1,0:T(8,128)}, u32[]{:S(2)}, u32[]{:S(2)}) collective-permute-start(f32[32,16,128]{2,1,0:T(8,128)S(1)} %copy-done.2), channel_id=1, source_target_pairs={{0,16},{1,17},{2,18},{3,19},{4,20},{5,21},{6,22},{7,23},{8,24},{9,... | collective-permute-start | bytes 786440 | tf_op jit(solution)/shard_map/ppermute | solution.py:15
  32.7 1.7 gather_fusion.5
  34.4 4.3 %gather_fusion = f32[128,128,128]{2,1,0:T(8,128)} fusion(f32[8,128,128]{2,1,0:T(8,128)S(1)} %copy-done, s32[1024]{0:T(1024)S(1)} %pad_clamp_fusion.2), kind=kCustom, calls=%fused_computation.8 | custom fusion | bytes 16777728 | tf_op jit(solution)/shard_map/jit(_take)/gather | solution.py:63
  38.7 10.2 %all-to-all-done.1 = f32[16,8,16,128]{3,2,1,0:T(8,128)} async-done(((f32[16,8,16,128]{3,2,1,0:T(8,128)}), f32[16,8,16,128]{3,2,1,0:T(8,128)}, u32[]{:S(2)}, u32[]{:S(2)}) %all-to-all-start.1) | async-done | bytes 1048608 | tf_op jit(solution)/shard_map/all_to_all | solution.py:26
  48.9 2.6 %gather_fusion.4 = f32[64,16,128]{2,1,0:T(8,128)} fusion(f32[128,16,128]{2,1,0:T(8,128)} %bitcast.4, s32[1024]{0:T(1024)S(1)} %pad_clamp_fusion.3), kind=kCustom, calls=%fused_computation.1.clone | custom fusion | bytes 1048832 | tf_op jit(solution)/shard_map/jit(_take)/gather | solution.py:28
  52.7 9.5 %fusion.36 = f32[32,16,128]{2,1,0:T(8,128)S(1)} fusion(f32[32,16,128]{2,1,0:T(8,128)} %param.17, f32[32,4,128,128]{3,2,1,0:T(8,128)} %bitcast.54, pred[32,4]{1,0:T(8,128)(4,1)S(1)} %copy.37, f32[32,1,16,128]{3,2,1,0:T(8,128)} %bitcast.7, f32[32,1,16,128]{3,2,1,0:T(8,128)} %bitcast.6, f32[32,2,16,128]{3,2,1,0:T(8,128)S(1)} %bitcast.60), kind=kOutput, calls=%fused_computation.38 | convolution fusion | flops 405340160 | bytes 9961600 | tf_op jit(solution)/shard_map/rkst,rkvt->rvs/dot_general | solution.py:32
  62.2 3.4 %fusion.16 = f32[32,16,128]{2,1,0:T(8,128)S(1)} fusion(f32[32,16,128]{2,1,0:T(8,128)S(1)} %fusion.36, f32[32,128,128]{2,1,0:T(8,128)S(1)} %gather_fusion.5, pred[32]{0:T(512)(128)(4,1)S(1)} %get-tuple-element.11), kind=kOutput, calls=%fused_computation.30 | convolution fusion | flops 101187584 | bytes 2621472 | tf_op jit(solution)/shard_map/rst,rvt->rvs/dot_general | solution.py:20
  65.6 1.7 gather_fusion.6
  67.4 2.4 %broadcast_select_fusion.1 = f32[128,16,128]{2,1,0:T(8,128)} fusion(f32[128,16,128]{2,1,0:T(8,128)} %gather_fusion.6, pred[128]{0:T(512)(128)(4,1)S(1)} %compare_and_fusion.1), kind=kLoop, calls=%fused_computation.62 | loop fusion | flops 262144 | bytes 2097280 | tf_op jit(solution)/shard_map/jit(_take)/select_n | solution.py:25
  69.8 6.9 %all-to-all-start.2 = ((f32[16,8,16,128]{3,2,1,0:T(8,128)}), f32[16,8,16,128]{3,2,1,0:T(8,128)}, u32[]{:S(2)}, u32[]{:S(2)}) async-start(f32[16,8,16,128]{3,2,1,0:T(8,128)} %bitcast.57), calls=%async_computation.2 | async-start | bytes 2097152 | tf_op jit(solution)/shard_map/all_to_all | solution.py:26
  76.7 4.1 %collective-permute-start.2 = (f32[32,16,128]{2,1,0:T(8,128)S(1)}, f32[32,16,128]{2,1,0:T(8,128)}, u32[]{:S(2)}, u32[]{:S(2)}) collective-permute-start(f32[32,16,128]{2,1,0:T(8,128)S(1)} %fusion.16), channel_id=1, source_target_pairs={{0,16},{1,17},{2,18},{3,19},{4,20},{5,21},{6,22},{7,23},{8,24},{9,... | collective-permute-start | bytes 786440 | tf_op jit(solution)/shard_map/ppermute | solution.py:15
  82.3 17.4 %all-to-all-done.2 = f32[16,8,16,128]{3,2,1,0:T(8,128)} async-done(((f32[16,8,16,128]{3,2,1,0:T(8,128)}), f32[16,8,16,128]{3,2,1,0:T(8,128)}, u32[]{:S(2)}, u32[]{:S(2)}) %all-to-all-start.2) | async-done | bytes 1048608 | tf_op jit(solution)/shard_map/all_to_all | solution.py:26
  99.7 2.6 %gather_fusion.7 = f32[64,16,128]{2,1,0:T(8,128)} fusion(f32[128,16,128]{2,1,0:T(8,128)} %bitcast.12, s32[1024]{0:T(1024)S(1)} %pad_clamp_fusion.3), kind=kCustom, calls=%fused_computation.5.clone | custom fusion | bytes 1048832 | tf_op jit(solution)/shard_map/jit(_take)/gather | solution.py:28
  103.5 9.5 %fusion.33 = f32[32,16,128]{2,1,0:T(8,128)S(1)} fusion(f32[32,16,128]{2,1,0:T(8,128)} %param.17, f32[32,4,128,128]{3,2,1,0:T(8,128)} %bitcast.55, pred[32,4]{1,0:T(8,128)(4,1)S(1)} %copy.37, f32[32,1,16,128]{3,2,1,0:T(8,128)} %bitcast.17, f32[32,1,16,128]{3,2,1,0:T(8,128)} %bitcast.15, f32[32,2,16,128]{3,2,1,0:T(8,128)S(1)} %bitcast.59), kind=kOutput, calls=%fused_computation.37 | convolution fusion | flops 405340160 | bytes 9961600 | tf_op jit(solution)/shard_map/rkst,rkvt->rvs/dot_general | solution.py:32
  113.0 3.4 %fusion.14 = f32[32,16,128]{2,1,0:T(8,128)S(1)} fusion(f32[32,16,128]{2,1,0:T(8,128)S(1)} %fusion.33, f32[32,128,128]{2,1,0:T(8,128)S(1)} %gather_fusion.5, pred[32]{0:T(512)(128)(4,1)S(1)} %get-tuple-element.11), kind=kOutput, calls=%fused_computation.28 | convolution fusion | flops 101187584 | bytes 2621472 | tf_op jit(solution)/shard_map/rst,rvt->rvs/dot_general | solution.py:20
  118.3 6.9 %all-to-all-start.3 = ((f32[16,8,16,128]{3,2,1,0:T(8,128)}), f32[16,8,16,128]{3,2,1,0:T(8,128)}, u32[]{:S(2)}, u32[]{:S(2)}) async-start(f32[16,8,16,128]{3,2,1,0:T(8,128)} %bitcast.22), calls=%async_computation.3 | async-start | bytes 2097152 | tf_op jit(solution)/shard_map/all_to_all | solution.py:26
  125.3 4.1 %collective-permute-start.4 = (f32[32,16,128]{2,1,0:T(8,128)S(1)}, f32[32,16,128]{2,1,0:T(8,128)}, u32[]{:S(2)}, u32[]{:S(2)}) collective-permute-start(f32[32,16,128]{2,1,0:T(8,128)S(1)} %fusion.14), channel_id=1, source_target_pairs={{0,16},{1,17},{2,18},{3,19},{4,20},{5,21},{6,22},{7,23},{8,24},{9,... | collective-permute-start | bytes 786440 | tf_op jit(solution)/shard_map/ppermute | solution.py:15
  132.4 15.8 %all-to-all-done.3 = f32[16,8,16,128]{3,2,1,0:T(8,128)} async-done(((f32[16,8,16,128]{3,2,1,0:T(8,128)}), f32[16,8,16,128]{3,2,1,0:T(8,128)}, u32[]{:S(2)}, u32[]{:S(2)}) %all-to-all-start.3) | async-done | bytes 1048608 | tf_op jit(solution)/shard_map/all_to_all | solution.py:26
  148.3 2.6 %gather_fusion.9 = f32[64,16,128]{2,1,0:T(8,128)} fusion(f32[128,16,128]{2,1,0:T(8,128)} %bitcast.23, s32[1024]{0:T(1024)S(1)} %pad_clamp_fusion.3), kind=kCustom, calls=%fused_computation.6.clone | custom fusion | bytes 1048832 | tf_op jit(solution)/shard_map/jit(_take)/gather | solution.py:28
  152.1 9.3 %fusion.30 = f32[32,16,128]{2,1,0:T(8,128)S(1)} fusion(f32[32,16,128]{2,1,0:T(8,128)S(1)} %copy-done.3, f32[32,4,128,128]{3,2,1,0:T(8,128)} %bitcast.56, pred[32,4]{1,0:T(8,128)(4,1)S(1)} %copy.37, f32[32,1,16,128]{3,2,1,0:T(8,128)} %bitcast.28, f32[32,1,16,128]{3,2,1,0:T(8,128)} %bitcast.26, f32[32,2,16,128]{3,2,1,0:T(8,128)S(1)} %bitcast.58), kind=kOutput, calls=%fused_computation.36 | convolution fusion | flops 405340160 | bytes 9961600 | tf_op jit(solution)/shard_map/rkst,rkvt->rvs/dot_general | solution.py:32
  161.4 3.5 %fusion.39 = f32[32,16]{1,0:T(8,128)S(1)} fusion(f32[32,16,128]{2,1,0:T(8,128)S(1)} %fusion.30, f32[32,16,128]{2,1,0:T(8,128)S(1)} %fusion.14, f32[32,128,128]{2,1,0:T(8,128)S(1)} %gather_fusion.10, pred[32]{0:T(512)(128)(4,1)S(1)} %get-tuple-element.11), kind=kOutput, calls=%fused_computation.39 | convolution fusion | flops 101318144 | bytes 2623520 | tf_op jit(solution)/shard_map/rst,rvt->rvs/dot_general | solution.py:20
  165.6 45.2 %all-reduce = (f32[256,16]{1,0:T(8,128)S(1)}, f32[256]{0:T(256)S(1)}) all-reduce(f32[256,16]{1,0:T(8,128)S(1)} %scatter_custom_fusion.1, f32[256]{0:T(256)S(1)} %scatter_custom_fusion.2), channel_id=1, replica_groups=mesh['band'=2,'rows'=16] {'band','rows'}, use_global_device_ids=true, to_apply=%region_5.9 | all-reduce | flops 4352 | bytes 34816 | tf_op jit(solution)/shard_map/psum | solution.py:77
  (72 shorter events, 22.7 us)
Async XLA Ops:
  0.0 34.4 %copy-start = (f32[8,128,128]{2,1,0:T(8,128)S(1)}, f32[8,128,128]{2,1,0:T(8,128)}, u32[]{:S(2)}) copy-start(f32[8,128,128]{2,1,0:T(8,128)} %param.20) | copy-start | bytes 1572868
  20.4 5.6 %copy-start.2 = (f32[32,16,128]{2,1,0:T(8,128)S(1)}, f32[32,16,128]{2,1,0:T(8,128)}, u32[]{:S(2)}) copy-start(f32[32,16,128]{2,1,0:T(8,128)} %param.16) | copy-start | bytes 786436
  20.4 11.0 %copy-start.4 = (s32[32,4]{0,1:T(4,128)S(1)}, s32[32,4]{0,1:T(4,128)}, u32[]{:S(2)}) copy-start(s32[32,4]{0,1:T(4,128)} %param.22) | copy-start | bytes 1540
  20.4 11.2 %copy-start.1 = (f32[8,128,128]{2,1,0:T(8,128)S(1)}, f32[8,128,128]{2,1,0:T(8,128)}, u32[]{:S(2)}) copy-start(f32[8,128,128]{2,1,0:T(8,128)} %param.18) | copy-start | bytes 1572868
  20.4 11.4 %copy-start.5 = (s32[32]{0:T(128)S(1)}, s32[32]{0:T(128)}, u32[]{:S(2)}) copy-start(s32[32]{0:T(128)} %param.21) | copy-start | bytes 388
  21.6 27.3 %all-to-all-start.1 = ((f32[16,8,16,128]{3,2,1,0:T(8,128)}), f32[16,8,16,128]{3,2,1,0:T(8,128)}, u32[]{:S(2)}, u32[]{:S(2)}) async-start(f32[16,8,16,128]{3,2,1,0:T(8,128)} %bitcast.3), calls=%async_computation.1 | async-start | bytes 2097152 | tf_op jit(solution)/shard_map/all_to_all | solution.py:26
  26.0 26.7 %collective-permute-start = (f32[32,16,128]{2,1,0:T(8,128)S(1)}, f32[32,16,128]{2,1,0:T(8,128)}, u32[]{:S(2)}, u32[]{:S(2)}) collective-permute-start(f32[32,16,128]{2,1,0:T(8,128)S(1)} %copy-done.2), channel_id=1, source_target_pairs={{0,16},{1,17},{2,18},{3,19},{4,20},{5,21},{6,22},{7,23},{8,24},{9,... | collective-permute-start | bytes 786440 | tf_op jit(solution)/shard_map/ppermute | solution.py:15
  30.1 22.6 %collective-permute-start.1 = (f32[32,16,128]{2,1,0:T(8,128)S(1)}, f32[32,16,128]{2,1,0:T(8,128)}, u32[]{:S(2)}, u32[]{:S(2)}) collective-permute-start(f32[32,16,128]{2,1,0:T(8,128)S(1)} %copy-done.2), channel_id=1, source_target_pairs={{16,0},{17,1},{18,2},{19,3},{20,4},{21,5},{22,6},{23,7},{24,8},{25... | collective-permute-start | bytes 786440 | tf_op jit(solution)/shard_map/ppermute | solution.py:15
  69.8 29.9 %all-to-all-start.2 = ((f32[16,8,16,128]{3,2,1,0:T(8,128)}), f32[16,8,16,128]{3,2,1,0:T(8,128)}, u32[]{:S(2)}, u32[]{:S(2)}) async-start(f32[16,8,16,128]{3,2,1,0:T(8,128)} %bitcast.57), calls=%async_computation.2 | async-start | bytes 2097152 | tf_op jit(solution)/shard_map/all_to_all | solution.py:26
  76.7 26.8 %collective-permute-start.2 = (f32[32,16,128]{2,1,0:T(8,128)S(1)}, f32[32,16,128]{2,1,0:T(8,128)}, u32[]{:S(2)}, u32[]{:S(2)}) collective-permute-start(f32[32,16,128]{2,1,0:T(8,128)S(1)} %fusion.16), channel_id=1, source_target_pairs={{0,16},{1,17},{2,18},{3,19},{4,20},{5,21},{6,22},{7,23},{8,24},{9,... | collective-permute-start | bytes 786440 | tf_op jit(solution)/shard_map/ppermute | solution.py:15
  80.8 22.7 %collective-permute-start.3 = (f32[32,16,128]{2,1,0:T(8,128)S(1)}, f32[32,16,128]{2,1,0:T(8,128)}, u32[]{:S(2)}, u32[]{:S(2)}) collective-permute-start(f32[32,16,128]{2,1,0:T(8,128)S(1)} %fusion.16), channel_id=1, source_target_pairs={{16,0},{17,1},{18,2},{19,3},{20,4},{21,5},{22,6},{23,7},{24,8},{25... | collective-permute-start | bytes 786440 | tf_op jit(solution)/shard_map/ppermute | solution.py:15
  117.2 8.1 %copy-start.6 = (s32[32,1]{0,1:T(1,128)S(1)}, s32[32,1]{0,1:T(1,128)}, u32[]{:S(2)}) copy-start(s32[32,1]{0,1:T(1,128)} %param.25) | copy-start | bytes 388
  118.3 29.9 %all-to-all-start.3 = ((f32[16,8,16,128]{3,2,1,0:T(8,128)}), f32[16,8,16,128]{3,2,1,0:T(8,128)}, u32[]{:S(2)}, u32[]{:S(2)}) async-start(f32[16,8,16,128]{3,2,1,0:T(8,128)} %bitcast.22), calls=%async_computation.3 | async-start | bytes 2097152 | tf_op jit(solution)/shard_map/all_to_all | solution.py:26
  125.3 26.8 %collective-permute-start.4 = (f32[32,16,128]{2,1,0:T(8,128)S(1)}, f32[32,16,128]{2,1,0:T(8,128)}, u32[]{:S(2)}, u32[]{:S(2)}) collective-permute-start(f32[32,16,128]{2,1,0:T(8,128)S(1)} %fusion.14), channel_id=1, source_target_pairs={{0,16},{1,17},{2,18},{3,19},{4,20},{5,21},{6,22},{7,23},{8,24},{9,... | collective-permute-start | bytes 786440 | tf_op jit(solution)/shard_map/ppermute | solution.py:15
  129.5 22.6 %collective-permute-start.5 = (f32[32,16,128]{2,1,0:T(8,128)S(1)}, f32[32,16,128]{2,1,0:T(8,128)}, u32[]{:S(2)}, u32[]{:S(2)}) collective-permute-start(f32[32,16,128]{2,1,0:T(8,128)S(1)} %fusion.14), channel_id=1, source_target_pairs={{16,0},{17,1},{18,2},{19,3},{20,4},{21,5},{22,6},{23,7},{24,8},{25... | collective-permute-start | bytes 786440 | tf_op jit(solution)/shard_map/ppermute | solution.py:15
  131.4 20.6 %copy-start.3 = (f32[32,16,128]{2,1,0:T(8,128)S(1)}, f32[32,16,128]{2,1,0:T(8,128)}, u32[]{:S(2)}) copy-start(f32[32,16,128]{2,1,0:T(8,128)} %param.17) | copy-start | bytes 786436
where the time goes:
time: 213 us; the launch traced here: 212 us
  blocking collectives  58.8 us (28%)
  waiting for transfers between devices  43.4 us (20%)
  matrix products  38.6 us (18%)
  starting transfers between devices  34.6 us (16%)
  local copies, waits for them, and re-layouts  23.7 us (11%)
  other arithmetic  13 us (6%)
    psum x1, blocking collectives, on_device(): lax.psum((partial_residual, partial_diag), ('band', 'rows'))  45.2 us
    all_to_all x3, waiting for transfers between devices, coupling(): lax.all_to_all(fetched, 'rows', split_axis=0, concat_axis=0, tiled=True)  43.4 us
    dot_general x3, matrix products, coupling(): return jnp.einsum('rkst,rkvt->rvs', tile_mats, sources, precision=HIGH)  28.3 us
    all_to_all x3, starting transfers between devices, coupling(): lax.all_to_all(fetched, 'rows', split_axis=0, concat_axis=0, tiled=True)  18.1 us
    ppermute x6, starting transfers between devices, shifted(): lax.ppermute(value, axis, [(source, source + steps) for source in range(i...  16.5 us
    all_to_all x1, blocking collectives, on_device(): lax.all_to_all(requests.reshape(n_rows, capacity), 'rows', split_axis=0,...  13.6 us
    dot_general x3, matrix products, apply_table(): return jnp.einsum('rst,rvt->rvs', chosen, iterate, precision=HIGH)  10.3 us
    gather x3, local copies, waits for them, and re-layouts, coupling(): jnp.take(arrived, slot_place, axis=0)  7.83 us
  transfers between devices with their start and end apart: 9, of which 3 were waited for; matrix products, arithmetic and copies ran while one was open for 10% of the time, Pallas kernels for 0%

commit v1 on v0

v1 whole, which is shorter than its diff:
```python
import functools

import jax
import jax.numpy as jnp
from jax import lax
from jax.experimental import pallas as pl
from jax.experimental.pallas import tpu as pltpu
from jax.sharding import PartitionSpec as P

AGG_DEV = 8
LANES = 128
DENSE_LIMIT = 1 << 19

VMEM = pl.BlockSpec(memory_space=pltpu.VMEM)
SMEM = pl.BlockSpec(memory_space=pltpu.SMEM)
HIGH = lax.Precision.HIGHEST


def params():
    return pltpu.CompilerParams(vmem_limit_bytes=48 * 1024 * 1024)


def call(kernel, out_shape, in_specs, scratch=(), flops=0, moved=0):
    single = not isinstance(out_shape, (tuple, list))
    count = 1 if single else len(out_shape)
    return pl.pallas_call(
        kernel,
        out_shape=out_shape,
        in_specs=in_specs,
        out_specs=VMEM if single else [VMEM] * count,
        scratch_shapes=list(scratch),
        compiler_params=params(),
        cost_estimate=pl.CostEstimate(flops=flops, bytes_accessed=moved, transcendentals=0),
    )


def halves(value):
    high = value.astype(jnp.bfloat16)
    low = (value - high.astype(jnp.float32)).astype(jnp.bfloat16)
    return high, low


def left_operand(value):
    high, low = halves(value)
    return jnp.concatenate([high, low, high], axis=1)


def right_operand(value):
    high, low = halves(value)
    return jnp.concatenate([high, high, low], axis=1)


def dot_nt(left, right):
    return lax.dot_general(
        left, right, (((1,), (1,)), ((), ())), preferred_element_type=jnp.float32
    )


def table_products(value, table_ref, out_ref):
    left = left_operand(value)
    count, width = table_ref.shape[0], table_ref.shape[1]
    for first in range(0, count, 2):
        last = min(first + 2, count)
        right = right_operand(table_ref[first:last].reshape((last - first) * width, -1))
        product = dot_nt(left, right)
        for t in range(first, last):
            out_ref[t] = product[:, (t - first) * width : (t - first + 1) * width]


def dot_exact(left, value):
    high, low = halves(value)
    return jnp.dot(left, high, preferred_element_type=jnp.float32) + jnp.dot(
        left, low, preferred_element_type=jnp.float32
    )


def request_kernel(
    sizes, owner_ref, local_ref, tile_ref, diag_ref, group_ref, payload_ref, slot_ref
):
    rows, width_k, n_rows, cap, n_tiles = sizes
    entries = rows * width_k

    def column(ref, k):
        return ref[:, k : k + 1]

    def stacked(ref):
        return jnp.concatenate([column(ref, k) for k in range(width_k)], axis=0)

    owner, local, tile = stacked(owner_ref), stacked(local_ref), stacked(tile_ref)
    group = jnp.concatenate([group_ref[:, 0:1]] * width_k, axis=0)
    code = local + rows * (tile + n_tiles * group) + 1
    row_of = lax.broadcasted_iota(jnp.int32, (entries, entries), 0)
    col_of = lax.broadcasted_iota(jnp.int32, (entries, entries), 1)

    def as_row(col):
        return jnp.sum(jnp.where(row_of == col_of, col, 0), axis=0, keepdims=True)

    owner_row = as_row(owner)
    earlier = jnp.where((owner == owner_row) & (col_of < row_of), 1, 0)
    rank = jnp.sum(earlier, axis=1, keepdims=True)
    slot_ref[...] = as_row(owner * cap + rank)
    lane = lax.broadcasted_iota(jnp.int32, (entries, LANES), 1)
    by_rank = jnp.where(lane == rank, code, 0).astype(jnp.float32)
    owners = lax.broadcasted_iota(jnp.int32, (n_rows, entries), 0)
    mine = jnp.where(owners == owner_row, 1.0, 0.0)
    lists = jnp.dot(mine, by_rank, precision=HIGH, preferred_element_type=jnp.float32)
    lists = (lists + 0.5).astype(jnp.int32)
    wide = payload_ref.shape[2] - LANES
    row_of = lax.broadcasted_iota(jnp.int32, (rows, wide), 0)
    col_of = lax.broadcasted_iota(jnp.int32, (rows, wide), 1)
    common = jnp.zeros((rows, wide), jnp.int32)
    parts = (
        group_ref[:, 0:1],
        diag_ref[...],
        column(tile_ref, width_k),
        column(tile_ref, width_k + 1),
    )
    for q, part in enumerate(parts):
        common = jnp.where(col_of == row_of + q * rows, part, common)
    common = jnp.sum(common, axis=0, keepdims=True)
    whole = jnp.concatenate([lists, jnp.broadcast_to(common, (n_rows, wide))], axis=1)
    for band in range(payload_ref.shape[0]):
        payload_ref[band] = whole


def pack(sizes, product_ref, request_ref, tiles_ref, send_ref, band_refs):
    rows, n_rows, cap, n_tiles, n_rhs = sizes
    for owner in range(n_rows):
        for rank in range(cap):
            code = jnp.maximum(request_ref[owner, rank] - 1, 0)
            tile = lax.rem(lax.div(code, rows), n_tiles)
            start = pl.multiple_of(lax.rem(code, rows) * n_rhs, n_rhs)
            send_ref[owner, rank] = product_ref[tile, pl.ds(start, n_rhs), :]
    for way, band_ref in enumerate(band_refs):
        for row in range(rows):
            tile = tiles_ref[way, row]
            band_ref[row] = product_ref[tile, pl.ds(row * n_rhs, n_rhs), :]


def first_kernel(sizes, start_ref, tile_ref, request_ref, tiles_ref, send_ref, *rest):
    product_ref, band_refs = rest[-1], rest[:-1]
    table_products(start_ref[...].reshape(product_ref.shape[1:]), tile_ref, product_ref)
    pack(sizes, product_ref, request_ref, tiles_ref, send_ref, band_refs)


def gather_solve(
    sizes, slot_ref, diag_ref, arrived_ref, band_refs, right_ref, inverse_ref, sum_ref, product_ref
):
    rows, n_rows, cap, n_tiles, n_rhs = sizes
    for row in range(rows):
        total = right_ref[row]
        for entry in range(row, slot_ref.shape[1], rows):
            slot = slot_ref[0, entry]
            total = total + arrived_ref[lax.div(slot, cap), lax.rem(slot, cap)]
        for band_ref in band_refs:
            total = total + band_ref[row]
        sum_ref[pl.ds(row * n_rhs, n_rhs), :] = total
    table_products(sum_ref[...], inverse_ref, product_ref)
    for row in range(rows):
        place = pl.ds(row * n_rhs, n_rhs)
        sum_ref[place, :] = product_ref[diag_ref[0, row], place, :]


def middle_kernel(sizes, n_band, *refs):
    slot_ref, diag_ref, request_ref, tiles_ref, arrived_ref = refs[:5]
    band_in = refs[5 : 5 + n_band]
    right_ref, inverse_ref, tile_ref, send_ref = refs[5 + n_band : 9 + n_band]
    band_out = refs[9 + n_band : 9 + 2 * n_band]
    sum_ref, product_ref = refs[9 + 2 * n_band :]
    gather_solve(
        sizes, slot_ref, diag_ref, arrived_ref, band_in, right_ref, inverse_ref, sum_ref, product_ref
    )
    table_products(sum_ref[...], tile_ref, product_ref)
    pack(sizes, product_ref, request_ref, tiles_ref, send_ref, band_out)


def last_kernel(sizes, n_band, dense, *refs):
    slot_ref, diag_ref, arrived_ref = refs[:3]
    band_in = refs[3 : 3 + n_band]
    refs = refs[3 + n_band :]
    right_ref, inverse_ref = refs[:2]
    if dense:
        tile_ref, table_ref, count_ref, place_ref, second_ref, part_ref = refs[2:8]
    else:
        second_ref = refs[2]
    sum_ref, product_ref = refs[-2:]
    rows, n_rhs = sizes[0], sizes[4]
    gather_solve(
        sizes, slot_ref, diag_ref, arrived_ref, band_in, right_ref, inverse_ref, sum_ref, product_ref
    )
    second = sum_ref[...]
    second_ref[...] = second.reshape(second_ref.shape)
    if not dense:
        return
    functionals = jnp.concatenate(
        [jnp.sum(tile_ref[...], axis=1), -jnp.sum(table_ref[...], axis=1)], axis=0
    )
    weights = dot_nt(right_operand(functionals), left_operand(second))
    ones = jnp.ones((8, right_ref.shape[2]), jnp.bfloat16)
    high, low = halves(right_ref[...].reshape(second.shape))
    rights = dot_nt(ones, high) + dot_nt(ones, low)
    per_tile = LANES // n_rhs
    n_func = functionals.shape[0]
    lane = lax.broadcasted_iota(jnp.int32, (n_func + 8, LANES), 1)
    weights = jnp.concatenate([weights, rights], axis=0)
    pieces = []
    for row in range(rows):
        tile, spot = row // per_tile, row % per_tile
        piece = weights[:, tile * LANES : (tile + 1) * LANES]
        pieces.append(jnp.where(lax.div(lane, n_rhs) == spot, piece, 0.0))
    spread = jnp.concatenate(pieces, axis=0)
    partial = dot_exact(count_ref[...], spread)
    source = lax.broadcasted_iota(jnp.int32, (LANES, LANES), 0)
    target = lax.broadcasted_iota(jnp.int32, (LANES, LANES), 1)
    same = jnp.where(lax.rem(source, n_rhs) == lax.rem(target, n_rhs), 1.0, 0.0)
    same = same.astype(jnp.bfloat16)
    high, low = halves(partial)
    partial = jnp.dot(high, same, preferred_element_type=jnp.float32) + jnp.dot(
        low, same, preferred_element_type=jnp.float32
    )
    high, low = halves(partial)
    both = jnp.concatenate([high, low], axis=1)
    depth = part_ref.shape[0]
    lane = lax.broadcasted_iota(jnp.int32, (depth, LANES), 1)
    result = jnp.zeros((depth, LANES), jnp.float32)
    for spot in range(per_tile):
        chosen = jnp.dot(
            place_ref[spot * depth : (spot + 1) * depth, :],
            both,
            preferred_element_type=jnp.float32,
        )
        chosen = chosen[:, :LANES] + chosen[:, LANES:]
        result = jnp.where(lax.div(lane, n_rhs) == spot, chosen, result)
    part_ref[...] = result


def final_kernel(sizes, part_ref, scale_ref, second_ref, out_ref):
    rows, n_rhs = sizes[0], sizes[4]
    depth = scale_ref.shape[0]
    total = part_ref[0]
    for source in range(1, part_ref.shape[0]):
        total = total + part_ref[source]
    correction = total / scale_ref[...]
    padded = jnp.concatenate([correction, jnp.zeros((8 - depth, LANES), jnp.float32)], axis=0)
    turned = padded.T
    for row in range(rows):
        spot, place = row // depth, row % depth
        column = turned[spot * n_rhs : (spot + 1) * n_rhs, place : place + 1]
        out_ref[row] = second_ref[row] + column


def shifted(value, axis, steps):
    count = lax.axis_size(axis)
    initial, last = (max(0, -steps), min(count, count - steps))
    return lax.ppermute(value, axis, [(source, source + steps) for source in range(initial, last)])


def to_bands(sends):
    if len(sends) == 1:
        return (lax.ppermute(sends[0], "band", [(0, 1), (1, 0)]),)
    return shifted(sends[0], "band", 1), shifted(sends[1], "band", -1)


def on_device(
    start_iterate,
    right_side,
    diag_table,
    inverse_table,
    coupling_tiles,
    diag_index,
    tile_index,
    source_owner,
    source_local,
    aggregate_map,
):
    rows, n_rhs, states = start_iterate.shape
    width_k = source_owner.shape[1]
    n_tiles, n_diag = coupling_tiles.shape[0], inverse_table.shape[0]
    n_rows, n_bands = lax.axis_size("rows"), lax.axis_size("band")
    n_dev = n_rows * n_bands
    cap = max(2, 2 * width_k * rows // n_rows)
    slots = n_rows * cap
    total_groups = AGG_DEV * n_dev
    dense = n_dev * rows * total_groups <= DENSE_LIMIT and LANES % n_rhs == 0
    sizes = (rows, n_rows, cap, n_tiles, n_rhs)
    f32, i32 = jnp.float32, jnp.int32
    my_band = lax.axis_index("band")
    my_row = lax.axis_index("rows")

    wide = -(-4 * rows // LANES) * LANES
    payload, slot_place = call(
        functools.partial(request_kernel, (rows, width_k, n_rows, cap, n_tiles)),
        (
            jax.ShapeDtypeStruct((n_bands, n_rows, LANES + wide), i32),
            jax.ShapeDtypeStruct((1, width_k * rows), i32),
        ),
        [VMEM] * 5,
    )(source_owner, source_local, tile_index, diag_index[:, None], aggregate_map)
    arrived = lax.all_to_all(
        payload.reshape(n_dev, LANES + wide), ("band", "rows"), split_axis=0, concat_axis=0, tiled=True
    ).reshape(n_bands, n_rows, LANES + wide)
    requests = lax.dynamic_index_in_dim(arrived[:, :, :LANES], my_band, 0, keepdims=False)
    common = arrived[:, :, LANES:]
    groups_all = common[:, :, :rows]
    diags_all = common[:, :, rows : 2 * rows]

    def neighbour(steps):
        other = lax.rem(my_band + steps + n_bands, n_bands)
        part = lax.dynamic_index_in_dim(common, other, 0, keepdims=False)
        return lax.dynamic_index_in_dim(part, my_row, 0, keepdims=False)

    above, below = neighbour(1), neighbour(-1)
    has_above, has_below = my_band + 1 < n_bands, my_band > 0
    tiles_above, tiles_below = above[2 * rows : 3 * rows], below[3 * rows : 4 * rows]
    if n_bands == 2:
        band_tiles = jnp.where(has_above, tiles_above, tiles_below)[None]
        band_groups = jnp.where(has_above, above[:rows], below[:rows])[None]
        band_valid = jnp.ones((1, rows), bool)
    else:
        band_tiles = jnp.stack([tiles_above, tiles_below])
        band_groups = jnp.stack([above[:rows], below[:rows]])
        band_valid = jnp.stack(
            [jnp.broadcast_to(has_above, (rows,)), jnp.broadcast_to(has_below, (rows,))]
        )
    n_ways = band_tiles.shape[0]

    block = (rows, n_rhs, states)
    send_shapes = (
        jax.ShapeDtypeStruct((n_rows, cap, n_rhs, states), f32),
        *[jax.ShapeDtypeStruct(block, f32)] * n_ways,
    )
    flat = rows * n_rhs
    sums = pltpu.VMEM((flat, states), f32)
    products = pltpu.VMEM((max(n_tiles, n_diag), flat, states), f32)
    work = 6 * flat * states * states
    sends = call(
        functools.partial(first_kernel, sizes),
        send_shapes,
        [VMEM, VMEM, SMEM, SMEM],
        [products],
        work * n_tiles,
        4 << 20,
    )(start_iterate, coupling_tiles, requests, band_tiles)

    def exchange(sends):
        arrived = lax.all_to_all(sends[0], "rows", split_axis=0, concat_axis=0, tiled=True)
        return arrived, to_bands(sends[1:])

    diag_row = diag_index[None]
    arrived_blocks, arrived_bands = exchange(sends)
    sends = call(
        functools.partial(middle_kernel, sizes, n_ways),
        send_shapes,
        [SMEM] * 4 + [VMEM] * (4 + n_ways),
        [sums, products],
        work * (n_tiles + n_diag),
        4 << 20,
    )(
        slot_place,
        diag_row,
        requests,
        band_tiles,
        arrived_blocks,
        *arrived_bands,
        right_side,
        inverse_table,
        coupling_tiles,
    )
    arrived_blocks, arrived_bands = exchange(sends)

    n_func = n_tiles + n_diag + 8
    codes = requests[:, :cap].reshape(-1)
    code = jnp.maximum(codes - 1, 0)
    own = jnp.arange(rows, dtype=i32)
    groups = aggregate_map[:, 0]
    entry_group = jnp.concatenate(
        [code // (rows * n_tiles), band_groups.reshape(-1), groups, groups]
    )
    entry_func = jnp.concatenate(
        [
            (code % rows) * n_func + (code // rows) % n_tiles,
            (own[None] * n_func + band_tiles).reshape(-1),
            own * n_func + n_tiles + diag_index,
            own * n_func + n_tiles + n_diag,
        ]
    )
    entry_valid = jnp.concatenate(
        [codes > 0, band_valid.reshape(-1), jnp.ones((2 * rows,), bool)]
    )
    table_sums = jnp.sum(diag_table, axis=(1, 2))
    diag_onehot = diags_all.reshape(-1, 1) == jnp.arange(n_diag, dtype=i32)[None]
    block_sums = jnp.sum(jnp.where(diag_onehot, table_sums[None], 0.0), axis=1)
    all_groups = groups_all.reshape(-1)
    whole_diag = jnp.sum(
        jnp.where(groups[:, None] == all_groups[None], block_sums[None], 0.0), axis=1
    )
    if dense:
        per_tile = LANES // n_rhs
        depth = rows // per_tile
        group_ids = jnp.arange(total_groups, dtype=i32)
        left = (group_ids[:, None] == entry_group[None]).astype(jnp.bfloat16)
        right = (
            (entry_func[:, None] == jnp.arange(rows * n_func, dtype=i32)[None]) & entry_valid[:, None]
        ).astype(jnp.bfloat16)
        counts = jnp.dot(left, right, preferred_element_type=f32).astype(jnp.bfloat16)
        order = all_groups.reshape(n_dev, per_tile, depth).transpose(1, 0, 2).reshape(-1)
        placing = (order[:, None] == group_ids[None]).astype(jnp.bfloat16)
        scale = jnp.repeat(whole_diag.reshape(per_tile, depth).T, n_rhs, axis=1)
        second, parts = call(
            functools.partial(last_kernel, sizes, n_ways, True),
            (
                jax.ShapeDtypeStruct(block, f32),
                jax.ShapeDtypeStruct((n_dev * depth, LANES), f32),
            ),
            [SMEM] * 2 + [VMEM] * (7 + n_ways),
            [sums, products],
            2 * work * n_diag,
            4 << 20,
        )(
            slot_place,
            diag_row,
            arrived_blocks,
            *arrived_bands,
            right_side,
            inverse_table,
            coupling_tiles,
            diag_table,
            counts,
            placing,
        )
        parts = lax.all_to_all(
            parts.reshape(n_dev, depth, LANES), ("band", "rows"), split_axis=0, concat_axis=0, tiled=True
        )
        return call(
            functools.partial(final_kernel, sizes), jax.ShapeDtypeStruct(block, f32), [VMEM] * 3
        )(parts, scale, second)

    second = call(
        functools.partial(last_kernel, sizes, n_ways, False),
        jax.ShapeDtypeStruct(block, f32),
        [SMEM] * 2 + [VMEM] * (3 + n_ways),
        [sums, products],
        work * n_diag,
        4 << 20,
    )(slot_place, diag_row, arrived_blocks, *arrived_bands, right_side, inverse_table)
    functionals = jnp.concatenate(
        [jnp.sum(coupling_tiles, axis=1), -jnp.sum(diag_table, axis=1)], axis=0
    )
    weights = jnp.einsum("fp,rcp->rfc", functionals, second, precision=HIGH)
    rights = jnp.sum(right_side, axis=2)[:, None]
    weights = jnp.concatenate([weights, jnp.broadcast_to(rights, (rows, 8, n_rhs))], axis=1)
    chosen = jnp.take(weights.reshape(rows * n_func, n_rhs), entry_func, axis=0)
    chosen = jnp.where(entry_valid[:, None], chosen, 0.0)
    partial = jax.ops.segment_sum(chosen, entry_group, num_segments=total_groups)
    whole = lax.psum(partial, ("band", "rows"))
    correction = jnp.take(whole, groups, axis=0) / whole_diag[:, None]
    return second + correction[:, :, None]


def solution(mesh):
    in_specs = (
        P(("band", "rows"), None, None),
        P(("band", "rows"), None, None),
        P(),
        P(),
        P(),
        P(("band", "rows")),
        P(("band", "rows"), None),
        P(("band", "rows"), None),
        P(("band", "rows"), None),
        P(("band", "rows"), None),
    )
    out_specs = P(("band", "rows"), None, None)
    return jax.shard_map(
        on_device, mesh=mesh, in_specs=in_specs, out_specs=out_specs, check_vma=False
    )
```

time: 213 us -> 105 us (0.49)
  blocking collectives: 58.8 us -> 0 us
  matrix products: 38.6 us -> 0.45 us
  local copies, waits for them, and re-layouts: 23.7 us -> 11.9 us
  other arithmetic: 13 us -> 1.41 us
  Pallas kernels: 0 us -> 10.7 us
  waiting for transfers between devices: 43.4 us -> 53.9 us
  starting transfers between devices: 34.6 us -> 25.3 us
    psum x1 -> x0, blocking collectives: 45.2 us -> none  [on_device(): lax.psum((partial_residual, partial_diag), ('band', 'rows'))]
    dot_general x6 -> x1, matrix products: 38.6 us -> 0.45 us  [on_device(): jnp.dot(left, right, preferred_element_type=f32).astype(jnp.bfloat16)]
    gather x11 -> x0, local copies, waits for them, and re-layouts: 19.9 us -> none  [the longest x3 7.83 us: coupling(): jnp.take(arrived, slot_place, axis=0)]
    ppermute x6 -> x2, starting transfers between devices: 16.5 us -> 1.37 us  [to_bands(): return (lax.ppermute(sends[0], 'band', [(0, 1), (1, 0)]),)]
    ppermute x6 -> x2, waiting for transfers between devices: 0.02 us -> 14.8 us  [to_bands(): return (lax.ppermute(sends[0], 'band', [(0, 1), (1, 0)]),)]
    all_to_all x1 -> x0, blocking collectives: 13.6 us -> none  [on_device(): lax.all_to_all(requests.reshape(n_rows, capacity), 'rows', split_axis=0,...]
    pallas_call x0 -> x5, Pallas kernels: none -> 10.7 us  [the longest x1 3.62 us: on_device(): call(functools.partial(middle_kernel, sizes, n_ways), send_shapes, [SMEM]...]
    select_n x13 -> x2, other arithmetic: 8.39 us -> 0.02 us  [the longest x1 0.01 us: on_device(): code // (rows * n_tiles)]
  transfers between devices with their start and end apart: 9 -> 6, of which waited for: 3 -> 6; matrix products, arithmetic and copies ran while one was open for 10% -> 3% of each run, Pallas kernels for 0% -> 0%
where the time goes in v1:
time: 105 us; the launch traced here: 104 us
  waiting for transfers between devices  53.9 us (51%)
  starting transfers between devices  25.3 us (24%)
  local copies, waits for them, and re-layouts  11.9 us (11%)
  Pallas kernels  10.7 us (10%)
  other arithmetic  1.41 us (1%)
    all_to_all x2, waiting for transfers between devices, exchange(): lax.all_to_all(sends[0], 'rows', split_axis=0, concat_axis=0, tiled=True)  25.7 us
    ppermute x2, waiting for transfers between devices, to_bands(): return (lax.ppermute(sends[0], 'band', [(0, 1), (1, 0)]),)  14.8 us
    all_to_all x2, starting transfers between devices, exchange(): lax.all_to_all(sends[0], 'rows', split_axis=0, concat_axis=0, tiled=True)  10.7 us
    unnamed x37, local copies, waits for them, and re-layouts  9 us
    all_to_all x1, starting transfers between devices, on_device(): lax.all_to_all(payload.reshape(n_dev, LANES + wide), ('band', 'rows'), sp...  7.3 us
    all_to_all x1, waiting for transfers between devices, on_device(): lax.all_to_all(payload.reshape(n_dev, LANES + wide), ('band', 'rows'), sp...  7.22 us
    all_to_all x1, waiting for transfers between devices, on_device(): lax.all_to_all(parts.reshape(n_dev, depth, LANES), ('band', 'rows'), spli...  6.14 us
    all_to_all x1, starting transfers between devices, on_device(): lax.all_to_all(parts.reshape(n_dev, depth, LANES), ('band', 'rows'), spli...  5.91 us
  transfers between devices with their start and end apart: 6, of which 6 were waited for; matrix products, arithmetic and copies ran while one was open for 3% of the time, Pallas kernels for 0%

profile of v1, /device:TPU:0, one launch (start us, length us, event | category | flops | bytes accessed | tf_op | source)
XLA Modules:
  0.0 104.0 jit_solution(12746732901444904616)
XLA Ops:
  0.0 0.8 copy.43.owner_ref
  0.9 0.8 copy.45.tile_ref
  1.7 0.7 copy.46.diag_ref
  2.4 0.7 copy.47.group_ref
  4.2 7.3 %all-to-all-start = ((s32[32,1,256]{2,1,0:T(1,128)}), s32[32,1,256]{2,1,0:T(1,128)S(1)}, u32[]{:S(2)}, u32[]{:S(2)}) async-start(s32[32,1,256]{2,1,0:T(1,128)} %copy.48), calls=%async_computation | async-start | bytes 65536 | tf_op jit(solution)/shard_map/all_to_all | solution.py:299
  11.5 7.2 %all-to-all-done = s32[32,1,256]{2,1,0:T(1,128)S(1)} async-done(((s32[32,1,256]{2,1,0:T(1,128)}), s32[32,1,256]{2,1,0:T(1,128)S(1)}, u32[]{:S(2)}, u32[]{:S(2)}) %all-to-all-start) | async-done | bytes 32800 | tf_op jit(solution)/shard_map/all_to_all | solution.py:299
  18.9 1.0 copy-done.9
  19.8 2.8 %shard_map.101 = (f32[16,8,16,128]{3,2,1,0:T(8,128)}, f32[32,16,128]{2,1,0:T(8,128)S(1)}) custom-call(f32[32,16,128]{2,1,0:T(8,128)S(1)} %copy-done.9, f32[8,128,128]{2,1,0:T(8,128)S(1)} %copy-done.1, s32[16,128]{1,0:T(8,128)S(1)} %dynamic-slice_bitcast_fusion.request_ref.refs_2_, s32[1,32]{1,0:T(1,128)S(1)} %bitcast.22), custom_call_target="tpu_custom_call" | custom-call | flops 402653184 | bytes 4194304 | tf_op jit(solution)/shard_map/pallas_call | solution.py:336
  22.6 3.8 %all-to-all-start.1 = ((f32[16,8,16,128]{3,2,1,0:T(8,128)}), f32[16,8,16,128]{3,2,1,0:T(8,128)S(1)}, u32[]{:S(2)}, u32[]{:S(2)}) async-start(f32[16,8,16,128]{3,2,1,0:T(8,128)} %get-tuple-element.15), calls=%async_computation.1 | async-start | bytes 2097152 | tf_op jit(solution)/shard_map/all_to_all | solution.py:346
  26.4 0.7 collective-permute-start
  27.1 7.8 %collective-permute-done.refs_5_ = f32[32,16,128]{2,1,0:T(8,128)S(1)} collective-permute-done((f32[32,16,128]{2,1,0:T(8,128)S(1)}, f32[32,16,128]{2,1,0:T(8,128)S(1)}, u32[]{:S(2)}, u32[]{:S(2)}) %collective-permute-start) | collective-permute-done | bytes 262176 | tf_op jit(solution)/shard_map/ppermute | solution.py:260
  34.9 14.4 %all-to-all-done.1.refs_4_ = f32[16,8,16,128]{3,2,1,0:T(8,128)S(1)} async-done(((f32[16,8,16,128]{3,2,1,0:T(8,128)}), f32[16,8,16,128]{3,2,1,0:T(8,128)S(1)}, u32[]{:S(2)}, u32[]{:S(2)}) %all-to-all-start.1) | async-done | bytes 1048608 | tf_op jit(solution)/shard_map/all_to_all | solution.py:346
  50.0 3.6 %shard_map.102 = (f32[16,8,16,128]{3,2,1,0:T(8,128)}, f32[32,16,128]{2,1,0:T(8,128)}) custom-call(s32[1,64]{1,0:T(1,128)S(1)} %get-tuple-element.13.refs_0_, s32[1,32]{1,0:T(1,128)S(1)} %bitcast.20, s32[16,128]{1,0:T(8,128)S(1)} %dynamic-slice_bitcast_fusion.request_ref.refs_2_, s32[1,32]{1,0:T(1,128)S(1)} %bitcast.23, ...), custom_call_target="tpu_custom_call" | custom-call | flops 805306368 | bytes 4194304 | tf_op jit(solution)/shard_map/pallas_call | solution.py:351
  53.6 6.9 %all-to-all-start.2 = ((f32[16,8,16,128]{3,2,1,0:T(8,128)}), f32[16,8,16,128]{3,2,1,0:T(8,128)S(1)}, u32[]{:S(2)}, u32[]{:S(2)}) async-start(f32[16,8,16,128]{3,2,1,0:T(8,128)} %get-tuple-element.17), calls=%async_computation.2 | async-start | bytes 2097152 | tf_op jit(solution)/shard_map/all_to_all | solution.py:346
  63.2 0.7 collective-permute-start.1
  65.2 7.0 %collective-permute-done.1.refs_3_ = f32[32,16,128]{2,1,0:T(8,128)} collective-permute-done((f32[32,16,128]{2,1,0:T(8,128)}, f32[32,16,128]{2,1,0:T(8,128)}, u32[]{:S(2)}, u32[]{:S(2)}) %collective-permute-start.1) | collective-permute-done | bytes 262176 | tf_op jit(solution)/shard_map/ppermute | solution.py:260
  72.2 11.3 %all-to-all-done.2.refs_2_ = f32[16,8,16,128]{3,2,1,0:T(8,128)S(1)} async-done(((f32[16,8,16,128]{3,2,1,0:T(8,128)}), f32[16,8,16,128]{3,2,1,0:T(8,128)S(1)}, u32[]{:S(2)}, u32[]{:S(2)}) %all-to-all-start.2) | async-done | bytes 1048608 | tf_op jit(solution)/shard_map/all_to_all | solution.py:346
  83.5 0.9 copy-done.4
  84.5 2.9 %shard_map.103 = (f32[32,16,128]{2,1,0:T(8,128)S(1)}, f32[128,128]{1,0:T(8,128)S(1)}) custom-call(s32[1,64]{1,0:T(1,128)S(1)} %get-tuple-element.13.refs_0_, s32[1,32]{1,0:T(1,128)S(1)} %bitcast.21, f32[16,8,16,128]{3,2,1,0:T(8,128)S(1)} %all-to-all-done.2.refs_2_, f32[32,16,128]{2,1,0:T(8,128)} %collective-permute-done.1.refs_3_, ...), custom_call_target="tpu_custom_call" | custom-call | flops 805306368 | bytes 4194304 | tf_op jit(solution)/shard_map/pallas_call | solution.py:409
  87.4 0.7 copy-done.5
  88.7 5.9 %all-to-all-start.3 = ((f32[32,4,128]{2,1,0:T(4,128)}), f32[32,4,128]{2,1,0:T(4,128)S(1)}, u32[]{:S(2)}, u32[]{:S(2)}) async-start(f32[32,4,128]{2,1,0:T(4,128)} %bitcast.17), calls=%async_computation.3 | async-start | bytes 131072 | tf_op jit(solution)/shard_map/all_to_all | solution.py:431
  95.9 6.1 %all-to-all-done.3.part_ref = f32[32,4,128]{2,1,0:T(4,128)S(1)} async-done(((f32[32,4,128]{2,1,0:T(4,128)}), f32[32,4,128]{2,1,0:T(4,128)S(1)}, u32[]{:S(2)}, u32[]{:S(2)}) %all-to-all-start.3) | async-done | bytes 65568 | tf_op jit(solution)/shard_map/all_to_all | solution.py:431
  102.0 0.9 copy-done.6
  103.0 1.0 shard_map.104
  (68 shorter events, 7.6 us)
Async XLA Ops:
  0.0 0.8 copy-start.15
  0.0 18.9 %copy-start.1 = (f32[8,128,128]{2,1,0:T(8,128)S(1)}, f32[8,128,128]{2,1,0:T(8,128)}, u32[]{:S(2)}) copy-start(f32[8,128,128]{2,1,0:T(8,128)} %refs_6_.3) | copy-start | bytes 1572868
  4.2 14.6 %all-to-all-start = ((s32[32,1,256]{2,1,0:T(1,128)}), s32[32,1,256]{2,1,0:T(1,128)S(1)}, u32[]{:S(2)}, u32[]{:S(2)}) async-start(s32[32,1,256]{2,1,0:T(1,128)} %copy.48), calls=%async_computation | async-start | bytes 65536 | tf_op jit(solution)/shard_map/all_to_all | solution.py:299
  18.9 1.0 copy-start.9
  22.6 26.7 %copy-start.2 = (f32[8,128,128]{2,1,0:T(8,128)S(1)}, f32[8,128,128]{2,1,0:T(8,128)}, u32[]{:S(2)}) copy-start(f32[8,128,128]{2,1,0:T(8,128)} %refs_5_.1) | copy-start | bytes 1572868
  22.6 26.7 %copy-start.3 = (f32[32,16,128]{2,1,0:T(8,128)S(1)}, f32[32,16,128]{2,1,0:T(8,128)}, u32[]{:S(2)}) copy-start(f32[32,16,128]{2,1,0:T(8,128)} %refs_4_.1) | copy-start | bytes 786436
  22.6 26.7 %all-to-all-start.1 = ((f32[16,8,16,128]{3,2,1,0:T(8,128)}), f32[16,8,16,128]{3,2,1,0:T(8,128)S(1)}, u32[]{:S(2)}, u32[]{:S(2)}) async-start(f32[16,8,16,128]{3,2,1,0:T(8,128)} %get-tuple-element.15), calls=%async_computation.1 | async-start | bytes 2097152 | tf_op jit(solution)/shard_map/all_to_all | solution.py:346
  26.4 8.5 %collective-permute-start = (f32[32,16,128]{2,1,0:T(8,128)S(1)}, f32[32,16,128]{2,1,0:T(8,128)S(1)}, u32[]{:S(2)}, u32[]{:S(2)}) collective-permute-start(f32[32,16,128]{2,1,0:T(8,128)S(1)} %get-tuple-element.16), channel_id=1, source_target_pairs={{0,16},{16,0},{1,17},{17,1},{2,18},{18,2},{3,19},{19,3},{4,20},{20... | collective-permute-start | bytes 786440 | tf_op jit(solution)/shard_map/ppermute | solution.py:260
  49.3 0.7 copy-start.8
  53.6 7.0 %copy-start = (f32[8,128,128]{2,1,0:T(8,128)S(1)}, f32[8,128,128]{2,1,0:T(8,128)}, u32[]{:S(2)}) copy-start(f32[8,128,128]{2,1,0:T(8,128)} %refs_7_.3) | copy-start | bytes 1572868
  53.6 29.9 %all-to-all-start.2 = ((f32[16,8,16,128]{3,2,1,0:T(8,128)}), f32[16,8,16,128]{3,2,1,0:T(8,128)S(1)}, u32[]{:S(2)}, u32[]{:S(2)}) async-start(f32[16,8,16,128]{3,2,1,0:T(8,128)} %get-tuple-element.17), calls=%async_computation.2 | async-start | bytes 2097152 | tf_op jit(solution)/shard_map/all_to_all | solution.py:346
  62.0 0.7 copy-start.12
  63.2 9.0 %collective-permute-start.1 = (f32[32,16,128]{2,1,0:T(8,128)}, f32[32,16,128]{2,1,0:T(8,128)}, u32[]{:S(2)}, u32[]{:S(2)}) collective-permute-start(f32[32,16,128]{2,1,0:T(8,128)} %get-tuple-element.18), channel_id=1, source_target_pairs={{0,16},{16,0},{1,17},{17,1},{2,18},{18,2},{3,19},{19,3},{4,20},{20... | collective-permute-start | bytes 786440 | tf_op jit(solution)/shard_map/ppermute | solution.py:260
  63.9 0.6 copy-start.10
  83.5 1.0 copy-start.4
  87.4 0.7 copy-start.5
  88.1 0.6 copy-start.7
  88.7 5.9 %copy-start.14 = (f32[8]{0:T(128)S(1)}, f32[8]{0:T(128)}, u32[]{:S(2)}) copy-start(f32[8]{0:T(128)} %reduce_sum.27) | copy-start | bytes 100
  88.7 6.0 %copy-start.11 = (s32[2,16,32]{2,1,0:T(8,128)S(1)}, s32[2,16,32]{2,1,0:T(8,128)}, u32[]{:S(2)}) copy-start(s32[2,16,32]{2,1,0:T(8,128)} %copy-done.10) | copy-start | bytes 12292
  88.7 13.3 %all-to-all-start.3 = ((f32[32,4,128]{2,1,0:T(4,128)}), f32[32,4,128]{2,1,0:T(4,128)S(1)}, u32[]{:S(2)}, u32[]{:S(2)}) async-start(f32[32,4,128]{2,1,0:T(4,128)} %bitcast.17), calls=%async_computation.3 | async-start | bytes 131072 | tf_op jit(solution)/shard_map/all_to_all | solution.py:431
  94.7 0.7 copy-start.13
  102.0 1.0 copy-start.6

commit v2 on v1

--- a/solution.py
+++ b/solution.py
@@ -17,7 +17,7 @@
 
 
 def params():
-    return pltpu.CompilerParams(vmem_limit_bytes=48 * 1024 * 1024)
+    return pltpu.CompilerParams(vmem_limit_bytes=16 * 1024 * 1024)
 
 
 def call(kernel, out_shape, in_specs, scratch=(), flops=0, moved=0):
@@ -77,70 +77,85 @@
 def request_kernel(
     sizes, owner_ref, local_ref, tile_ref, diag_ref, group_ref, payload_ref, slot_ref
 ):
-    rows, width_k, n_rows, cap, n_tiles = sizes
-    entries = rows * width_k
-
-    def column(ref, k):
-        return ref[:, k : k + 1]
-
-    def stacked(ref):
-        return jnp.concatenate([column(ref, k) for k in range(width_k)], axis=0)
-
-    owner, local, tile = stacked(owner_ref), stacked(local_ref), stacked(tile_ref)
-    group = jnp.concatenate([group_ref[:, 0:1]] * width_k, axis=0)
-    code = local + rows * (tile + n_tiles * group) + 1
-    row_of = lax.broadcasted_iota(jnp.int32, (entries, entries), 0)
-    col_of = lax.broadcasted_iota(jnp.int32, (entries, entries), 1)
-
-    def as_row(col):
-        return jnp.sum(jnp.where(row_of == col_of, col, 0), axis=0, keepdims=True)
-
-    owner_row = as_row(owner)
-    earlier = jnp.where((owner == owner_row) & (col_of < row_of), 1, 0)
-    rank = jnp.sum(earlier, axis=1, keepdims=True)
-    slot_ref[...] = as_row(owner * cap + rank)
-    lane = lax.broadcasted_iota(jnp.int32, (entries, LANES), 1)
-    by_rank = jnp.where(lane == rank, code, 0).astype(jnp.float32)
-    owners = lax.broadcasted_iota(jnp.int32, (n_rows, entries), 0)
-    mine = jnp.where(owners == owner_row, 1.0, 0.0)
-    lists = jnp.dot(mine, by_rank, precision=HIGH, preferred_element_type=jnp.float32)
+    rows, n_rows, cap, n_tiles = sizes
+    width_k = owner_ref.shape[0]
+    half = n_rows // 2
+    row_of = lax.broadcasted_iota(jnp.int32, (rows, rows), 0)
+    col_of = lax.broadcasted_iota(jnp.int32, (rows, rows), 1)
+    lane = lax.broadcasted_iota(jnp.int32, (rows, LANES), 1)
+    owners = lax.broadcasted_iota(jnp.int32, (n_rows, rows), 0)
+
+    def column(row):
+        return jnp.sum(jnp.where(row_of == col_of, row, 0), axis=1, keepdims=True)
+
+    def owner_row(k):
+        return owner_ref[k : k + 1, :]
+
+    owner_columns = [column(owner_row(k)) for k in range(width_k)]
+    lists = jnp.zeros((n_rows, LANES), jnp.float32)
+    for k in range(width_k):
+        rank = jnp.zeros((1, rows), jnp.int32)
+        for other in range(k + 1):
+            match = owner_columns[other] == owner_row(k)
+            if other == k:
+                match = match & (row_of < col_of)
+            rank = rank + jnp.sum(jnp.where(match, 1, 0), axis=0, keepdims=True)
+        slot_ref[k : k + 1, :] = owner_row(k) * cap + rank
+        code = local_ref[k : k + 1, :] + rows * (
+            tile_ref[k : k + 1, :] + n_tiles * group_ref[...]
+        )
+        code, rank = column(code + 1), column(rank)
+        mirror = jnp.where(owner_row(k) >= half, owner_row(k) - half, owner_row(k) + half)
+        for owner, base in ((owner_row(k), 0), (mirror, LANES // 2)):
+            by_rank = jnp.where(lane == rank + base, code, 0).astype(jnp.float32)
+            mine = jnp.where(owners == owner, 1.0, 0.0)
+            lists = lists + jnp.dot(
+                mine, by_rank, precision=HIGH, preferred_element_type=jnp.float32
+            )
     lists = (lists + 0.5).astype(jnp.int32)
-    wide = payload_ref.shape[2] - LANES
-    row_of = lax.broadcasted_iota(jnp.int32, (rows, wide), 0)
-    col_of = lax.broadcasted_iota(jnp.int32, (rows, wide), 1)
-    common = jnp.zeros((rows, wide), jnp.int32)
-    parts = (
-        group_ref[:, 0:1],
-        diag_ref[...],
-        column(tile_ref, width_k),
-        column(tile_ref, width_k + 1),
-    )
-    for q, part in enumerate(parts):
-        common = jnp.where(col_of == row_of + q * rows, part, common)
-    common = jnp.sum(common, axis=0, keepdims=True)
-    whole = jnp.concatenate([lists, jnp.broadcast_to(common, (n_rows, wide))], axis=1)
-    for band in range(payload_ref.shape[0]):
-        payload_ref[band] = whole
-
-
-def pack(sizes, product_ref, request_ref, tiles_ref, send_ref, band_refs):
+    common = [group_ref[...], diag_ref[...], tile_ref[width_k : width_k + 1, :]]
+    common.append(tile_ref[width_k + 1 : width_k + 2, :])
+    spare = payload_ref.shape[2] - LANES - len(common) * rows
+    if spare:
+        common.append(jnp.zeros((1, spare), jnp.int32))
+    common = jnp.concatenate(common, axis=1)
+    for device in range(n_rows):
+        line = jnp.concatenate([lists[device : device + 1, :], common], axis=1)
+        for band in range(payload_ref.shape[0] // n_rows):
+            payload_ref[band * n_rows + device] = line
+
+
+def chosen_product(sizes, product_ref, code, base):
     rows, n_rows, cap, n_tiles, n_rhs = sizes
-    for owner in range(n_rows):
-        for rank in range(cap):
-            code = jnp.maximum(request_ref[owner, rank] - 1, 0)
-            tile = lax.rem(lax.div(code, rows), n_tiles)
-            start = pl.multiple_of(lax.rem(code, rows) * n_rhs, n_rhs)
-            send_ref[owner, rank] = product_ref[tile, pl.ds(start, n_rhs), :]
+    code = jnp.maximum(code - 1, 0)
+    tile = lax.rem(lax.div(code, rows), n_tiles)
+    start = pl.multiple_of((lax.rem(code, rows) + base) * n_rhs, n_rhs)
+    return product_ref[tile, pl.ds(start, n_rhs), :]
+
+
+def pack_bands(sizes, product_ref, tiles_ref, band_refs):
+    rows, n_rhs = sizes[0], sizes[4]
     for way, band_ref in enumerate(band_refs):
         for row in range(rows):
-            tile = tiles_ref[way, row]
-            band_ref[row] = product_ref[tile, pl.ds(row * n_rhs, n_rhs), :]
-
-
-def first_kernel(sizes, start_ref, tile_ref, request_ref, tiles_ref, send_ref, *rest):
+            band_ref[row] = product_ref[tiles_ref[way, row], pl.ds(row * n_rhs, n_rhs), :]
+
+
+def first_kernel(
+    sizes, start_ref, mirror_ref, tile_ref, request_ref, tiles_ref, send_ref, *rest
+):
+    rows, n_rows, cap, n_tiles, n_rhs = sizes
     product_ref, band_refs = rest[-1], rest[:-1]
-    table_products(start_ref[...].reshape(product_ref.shape[1:]), tile_ref, product_ref)
-    pack(sizes, product_ref, request_ref, tiles_ref, send_ref, band_refs)
+    flat = rows * n_rhs
+    values = [ref[...].reshape(flat, -1) for ref in (start_ref, mirror_ref)]
+    table_products(jnp.concatenate(values, axis=0), tile_ref, product_ref)
+    half = n_rows // 2
+    base = lax.div(lax.axis_index("rows"), half) * half
+    for device in range(half):
+        for slot in range(2 * cap):
+            side, rank = slot // cap, slot % cap
+            code = request_ref[base + device, side * (LANES // 2) + rank]
+            send_ref[device, slot] = chosen_product(sizes, product_ref, code, side * rows)
+    pack_bands(sizes, product_ref, tiles_ref, band_refs)
 
 
 def gather_solve(
@@ -149,9 +164,8 @@
     rows, n_rows, cap, n_tiles, n_rhs = sizes
     for row in range(rows):
         total = right_ref[row]
-        for entry in range(row, slot_ref.shape[1], rows):
-            slot = slot_ref[0, entry]
-            total = total + arrived_ref[lax.div(slot, cap), lax.rem(slot, cap)]
+        for k in range(slot_ref.shape[0]):
+            total = total + arrived_ref[slot_ref[k, row]]
         for band_ref in band_refs:
             total = total + band_ref[row]
         sum_ref[pl.ds(row * n_rhs, n_rhs), :] = total
@@ -171,7 +185,11 @@
         sizes, slot_ref, diag_ref, arrived_ref, band_in, right_ref, inverse_ref, sum_ref, product_ref
     )
     table_products(sum_ref[...], tile_ref, product_ref)
-    pack(sizes, product_ref, request_ref, tiles_ref, send_ref, band_out)
+    rows, n_rows, cap, n_tiles, n_rhs = sizes
+    for owner in range(n_rows):
+        for rank in range(cap):
+            send_ref[owner, rank] = chosen_product(sizes, product_ref, request_ref[owner, rank], 0)
+    pack_bands(sizes, product_ref, tiles_ref, band_out)
 
 
 def last_kernel(sizes, n_band, dense, *refs):
@@ -287,18 +305,23 @@
     my_band = lax.axis_index("band")
     my_row = lax.axis_index("rows")
 
+    half = n_rows // 2
+    mirror = lax.ppermute(start_iterate, "rows", [(i, (i + half) % n_rows) for i in range(n_rows)])
     wide = -(-4 * rows // LANES) * LANES
     payload, slot_place = call(
-        functools.partial(request_kernel, (rows, width_k, n_rows, cap, n_tiles)),
+        functools.partial(request_kernel, (rows, n_rows, cap, n_tiles)),
         (
-            jax.ShapeDtypeStruct((n_bands, n_rows, LANES + wide), i32),
-            jax.ShapeDtypeStruct((1, width_k * rows), i32),
+            jax.ShapeDtypeStruct((n_dev, 1, LANES + wide), i32),
+            jax.ShapeDtypeStruct((width_k, rows), i32),
         ),
         [VMEM] * 5,
-    )(source_owner, source_local, tile_index, diag_index[:, None], aggregate_map)
+    )(source_owner.T, source_local.T, tile_index.T, diag_index[None], aggregate_map.T)
     arrived = lax.all_to_all(
-        payload.reshape(n_dev, LANES + wide), ("band", "rows"), split_axis=0, concat_axis=0, tiled=True
+        payload, ("band", "rows"), split_axis=0, concat_axis=0, tiled=True
     ).reshape(n_bands, n_rows, LANES + wide)
+    owner = slot_place // cap
+    half_place = (owner % half) * 2 * cap + slot_place % cap
+    half_place = half_place + jnp.where(owner // half == my_row // half, 0, cap)
     requests = lax.dynamic_index_in_dim(arrived[:, :, :LANES], my_band, 0, keepdims=False)
     common = arrived[:, :, LANES:]
     groups_all = common[:, :, :rows]
@@ -325,38 +348,38 @@
     n_ways = band_tiles.shape[0]
 
     block = (rows, n_rhs, states)
-    send_shapes = (
-        jax.ShapeDtypeStruct((n_rows, cap, n_rhs, states), f32),
-        *[jax.ShapeDtypeStruct(block, f32)] * n_ways,
-    )
+    band_shapes = [jax.ShapeDtypeStruct(block, f32)] * n_ways
     flat = rows * n_rhs
     sums = pltpu.VMEM((flat, states), f32)
     products = pltpu.VMEM((max(n_tiles, n_diag), flat, states), f32)
     work = 6 * flat * states * states
     sends = call(
         functools.partial(first_kernel, sizes),
-        send_shapes,
-        [VMEM, VMEM, SMEM, SMEM],
-        [products],
-        work * n_tiles,
+        (jax.ShapeDtypeStruct((half, 2 * cap, n_rhs, states), f32), *band_shapes),
+        [VMEM, VMEM, VMEM, SMEM, SMEM],
+        [pltpu.VMEM((n_tiles, 2 * flat, states), f32)],
+        2 * work * n_tiles,
         4 << 20,
-    )(start_iterate, coupling_tiles, requests, band_tiles)
-
-    def exchange(sends):
-        arrived = lax.all_to_all(sends[0], "rows", split_axis=0, concat_axis=0, tiled=True)
-        return arrived, to_bands(sends[1:])
+    )(start_iterate, mirror, coupling_tiles, requests, band_tiles)
+    halves_of_rows = [list(range(half)), list(range(half, n_rows))]
+
+    def exchange(sends, groups=None):
+        arrived = lax.all_to_all(
+            sends[0], "rows", split_axis=0, concat_axis=0, tiled=True, axis_index_groups=groups
+        )
+        return arrived.reshape(slots, n_rhs, states), to_bands(sends[1:])
 
     diag_row = diag_index[None]
-    arrived_blocks, arrived_bands = exchange(sends)
+    arrived_blocks, arrived_bands = exchange(sends, halves_of_rows)
     sends = call(
         functools.partial(middle_kernel, sizes, n_ways),
-        send_shapes,
+        (jax.ShapeDtypeStruct((n_rows, cap, n_rhs, states), f32), *band_shapes),
         [SMEM] * 4 + [VMEM] * (4 + n_ways),
         [sums, products],
         work * (n_tiles + n_diag),
         4 << 20,
     )(
-        slot_place,
+        half_place,
         diag_row,
         requests,
         band_tiles,

time: 105 us -> 100 us (0.952)
  local copies, waits for them, and re-layouts: 11.9 us -> 7.65 us
  waiting for transfers between devices: 53.9 us -> 49.7 us
  starting transfers between devices: 25.3 us -> 28.4 us
  Pallas kernels: 10.7 us -> 11.8 us
    all_to_all x3, waiting for transfers between devices: 32.9 us -> 22.3 us  [the longest x2 17.7 us: exchange(): lax.all_to_all(sends[0], 'rows', split_axis=0, concat_axis=0, tiled=True,...]
    ppermute x0 -> x1, waiting for transfers between devices: none -> 8.26 us  [on_device(): lax.ppermute(start_iterate, 'rows', [(i, (i + half) % n_rows) for i in ra...]
    unnamed x37 -> x39, local copies, waits for them, and re-layouts: 9 us -> 5.51 us
    ppermute x0 -> x1, starting transfers between devices: none -> 2.74 us  [on_device(): lax.ppermute(start_iterate, 'rows', [(i, (i + half) % n_rows) for i in ra...]
    all_to_all x3, starting transfers between devices: 18 us -> 15.6 us  [the longest x2 8.3 us: exchange(): lax.all_to_all(sends[0], 'rows', split_axis=0, concat_axis=0, tiled=True,...]
    ppermute x2, waiting for transfers between devices: 14.8 us -> 12.4 us  [to_bands(): return (lax.ppermute(sends[0], 'band', [(0, 1), (1, 0)]),)]
    ppermute x2, starting transfers between devices: 1.37 us -> 3.29 us  [to_bands(): return (lax.ppermute(sends[0], 'band', [(0, 1), (1, 0)]),)]
    pallas_call x3, Pallas kernels: 6.82 us -> 7.96 us  [the longest x1 3.58 us: on_device(): call(functools.partial(middle_kernel, sizes, n_ways), (jax.ShapeDtypeStru...]
  transfers between devices with their start and end apart: 6 -> 7, of which waited for: 6 -> 7; matrix products, arithmetic and copies ran while one was open for 3% -> 4% of each run, Pallas kernels for 0% -> 0%
where the time goes in v2:
time: 100 us; the launch traced here: 99.8 us
  waiting for transfers between devices  49.7 us (50%)
  starting transfers between devices  28.4 us (28%)
  Pallas kernels  11.8 us (12%)
  local copies, waits for them, and re-layouts  7.65 us (8%)
  other arithmetic  1.51 us (2%)
    all_to_all x2, waiting for transfers between devices, exchange(): lax.all_to_all(sends[0], 'rows', split_axis=0, concat_axis=0, tiled=True,...  17.7 us
    ppermute x2, waiting for transfers between devices, to_bands(): return (lax.ppermute(sends[0], 'band', [(0, 1), (1, 0)]),)  12.4 us
    all_to_all x2, starting transfers between devices, exchange(): lax.all_to_all(sends[0], 'rows', split_axis=0, concat_axis=0, tiled=True,...  8.3 us
    ppermute x1, waiting for transfers between devices, on_device(): lax.ppermute(start_iterate, 'rows', [(i, (i + half) % n_rows) for i in ra...  8.26 us
    all_to_all x1, starting transfers between devices, on_device(): lax.all_to_all(payload, ('band', 'rows'), split_axis=0, concat_axis=0, ti...  7.3 us
    all_to_all x1, starting transfers between devices, on_device(): lax.all_to_all(parts.reshape(n_dev, depth, LANES), ('band', 'rows'), spli...  6.77 us
    all_to_all x1, waiting for transfers between devices, on_device(): lax.all_to_all(parts.reshape(n_dev, depth, LANES), ('band', 'rows'), spli...  6.71 us
    unnamed x39, local copies, waits for them, and re-layouts  5.51 us
  transfers between devices with their start and end apart: 7, of which 7 were waited for; matrix products, arithmetic and copies ran while one was open for 4% of the time, Pallas kernels for 0%

profile of v2, /device:TPU:0, one launch (start us, length us, event | category | flops | bytes accessed | tf_op | source)
XLA Modules:
  0.0 99.8 jit_solution(12660113184054108963)
XLA Ops:
  0.7 1.0 %shard_map.100 = (s32[32,1,256]{2,1,0:T(1,128)}, s32[2,32]{1,0:T(2,128)S(1)}) custom-call(s32[2,32]{1,0:T(2,128)S(1)} %bitcast.31, s32[2,32]{1,0:T(2,128)S(1)} %bitcast.32, s32[4,32]{1,0:T(4,128)S(1)} %bitcast.30, s32[1,32]{1,0:T(1,128)S(1)} %bitcast.27, s32[1,32]{1,0:T(1,128)S(1)} %bitcast.24), custom_call_target="tpu_custom_call" | custom-call | tf_op jit(solution)/shard_map/pallas_call | solution.py:311
  1.7 7.3 %all-to-all-start = ((s32[32,1,256]{2,1,0:T(1,128)}), s32[32,1,256]{2,1,0:T(1,128)S(1)}, u32[]{:S(2)}, u32[]{:S(2)}) async-start(s32[32,1,256]{2,1,0:T(1,128)} %get-tuple-element.14), calls=%async_computation | async-start | bytes 65536 | tf_op jit(solution)/shard_map/all_to_all | solution.py:319
  9.0 2.7 %collective-permute-start = (f32[32,16,128]{2,1,0:T(8,128)}, f32[32,16,128]{2,1,0:T(8,128)S(1)}, u32[]{:S(2)}, u32[]{:S(2)}) collective-permute-start(f32[32,16,128]{2,1,0:T(8,128)} %start_ref.1), channel_id=1, source_target_pairs={{0,8},{1,9},{2,10},{3,11},{4,12},{5,13},{6,14},{7,15},{8,0},{9,1},... | collective-permute-start | bytes 786440 | tf_op jit(solution)/shard_map/ppermute | solution.py:309
  11.8 4.7 %all-to-all-done = s32[32,1,256]{2,1,0:T(1,128)S(1)} async-done(((s32[32,1,256]{2,1,0:T(1,128)}), s32[32,1,256]{2,1,0:T(1,128)S(1)}, u32[]{:S(2)}, u32[]{:S(2)}) %all-to-all-start) | async-done | bytes 32800 | tf_op jit(solution)/shard_map/all_to_all | solution.py:319
  16.6 8.3 %collective-permute-done.mirror_ref = f32[32,16,128]{2,1,0:T(8,128)S(1)} collective-permute-done((f32[32,16,128]{2,1,0:T(8,128)}, f32[32,16,128]{2,1,0:T(8,128)S(1)}, u32[]{:S(2)}, u32[]{:S(2)}) %collective-permute-start) | collective-permute-done | bytes 262176 | tf_op jit(solution)/shard_map/ppermute | solution.py:309
  24.8 1.0 %copy-done.1 = f32[8,128,128]{2,1,0:T(8,128)S(1)} copy-done((f32[8,128,128]{2,1,0:T(8,128)S(1)}, f32[8,128,128]{2,1,0:T(8,128)}, u32[]{:S(2)}) %copy-start.1) | copy-done | bytes 524312
  25.9 3.4 %shard_map.101 = (f32[8,16,16,128]{3,2,1,0:T(8,128)}, f32[32,16,128]{2,1,0:T(8,128)S(1)}) custom-call(f32[32,16,128]{2,1,0:T(8,128)S(1)} %copy-done.14, f32[32,16,128]{2,1,0:T(8,128)S(1)} %collective-permute-done.mirror_ref, f32[8,128,128]{2,1,0:T(8,128)S(1)} %copy-done.1, s32[16,128]{1,0:T(8,128)S(1)} %dynamic-slice_bitcast_fusion.request_ref.refs_2_, ...), custom_call_target="tpu_custom_call" | custom-call | flops 805306368 | bytes 4194304 | tf_op jit(solution)/shard_map/pallas_call | solution.py:356
  29.2 3.7 %all-to-all-start.1 = ((f32[8,16,16,128]{3,2,1,0:T(8,128)}), f32[8,16,16,128]{3,2,1,0:T(8,128)S(1)}, u32[]{:S(2)}, u32[]{:S(2)}) async-start(f32[8,16,16,128]{3,2,1,0:T(8,128)} %get-tuple-element.15), calls=%async_computation.1 | async-start | bytes 2097152 | tf_op jit(solution)/shard_map/all_to_all | solution.py:367
  32.9 1.7 %collective-permute-start.1 = (f32[32,16,128]{2,1,0:T(8,128)S(1)}, f32[32,16,128]{2,1,0:T(8,128)S(1)}, u32[]{:S(2)}, u32[]{:S(2)}) collective-permute-start(f32[32,16,128]{2,1,0:T(8,128)S(1)} %get-tuple-element.16), channel_id=1, source_target_pairs={{0,16},{16,0},{1,17},{17,1},{2,18},{18,2},{3,19},{19,3},{4,20},{20... | collective-permute-start | bytes 786440 | tf_op jit(solution)/shard_map/ppermute | solution.py:278
  34.7 6.9 %collective-permute-done.1.refs_5_ = f32[32,16,128]{2,1,0:T(8,128)S(1)} collective-permute-done((f32[32,16,128]{2,1,0:T(8,128)S(1)}, f32[32,16,128]{2,1,0:T(8,128)S(1)}, u32[]{:S(2)}, u32[]{:S(2)}) %collective-permute-start.1) | collective-permute-done | bytes 262176 | tf_op jit(solution)/shard_map/ppermute | solution.py:278
  41.6 5.8 %all-to-all-done.1 = f32[8,16,16,128]{3,2,1,0:T(8,128)S(1)} async-done(((f32[8,16,16,128]{3,2,1,0:T(8,128)}), f32[8,16,16,128]{3,2,1,0:T(8,128)S(1)}, u32[]{:S(2)}, u32[]{:S(2)}) %all-to-all-start.1) | async-done | bytes 1048608 | tf_op jit(solution)/shard_map/all_to_all | solution.py:367
  47.3 3.6 %shard_map.102 = (f32[16,8,16,128]{3,2,1,0:T(8,128)}, f32[32,16,128]{2,1,0:T(8,128)}) custom-call(s32[2,32]{1,0:T(2,128)S(1)} %fusion.8.refs_0_, s32[1,32]{1,0:T(1,128)S(1)} %bitcast.28, s32[16,128]{1,0:T(8,128)S(1)} %dynamic-slice_bitcast_fusion.request_ref.refs_2_, s32[1,32]{1,0:T(1,128)S(1)} %bitcast.34, f32[128,16,128]{2,1,0:T(8,128)S(1)} %bitcast.22, ...), custom_call_target="tpu_custom_call" | custom-call | flops 805306368 | bytes 4194304 | tf_op jit(solution)/shard_map/pallas_call | solution.py:374
  50.9 4.6 %all-to-all-start.2 = ((f32[16,8,16,128]{3,2,1,0:T(8,128)}), f32[16,8,16,128]{3,2,1,0:T(8,128)S(1)}, u32[]{:S(2)}, u32[]{:S(2)}) async-start(f32[16,8,16,128]{3,2,1,0:T(8,128)} %get-tuple-element.17), calls=%async_computation.2 | async-start | bytes 2097152 | tf_op jit(solution)/shard_map/all_to_all | solution.py:367
  55.6 0.7 reduce_sum.27
  57.5 1.6 %collective-permute-start.2 = (f32[32,16,128]{2,1,0:T(8,128)}, f32[32,16,128]{2,1,0:T(8,128)}, u32[]{:S(2)}, u32[]{:S(2)}) collective-permute-start(f32[32,16,128]{2,1,0:T(8,128)} %get-tuple-element.18), channel_id=1, source_target_pairs={{0,16},{16,0},{1,17},{17,1},{2,18},{18,2},{3,19},{19,3},{4,20},{20... | collective-permute-start | bytes 786440 | tf_op jit(solution)/shard_map/ppermute | solution.py:278
  61.0 5.6 %collective-permute-done.2.refs_3_ = f32[32,16,128]{2,1,0:T(8,128)} collective-permute-done((f32[32,16,128]{2,1,0:T(8,128)}, f32[32,16,128]{2,1,0:T(8,128)}, u32[]{:S(2)}, u32[]{:S(2)}) %collective-permute-start.2) | collective-permute-done | bytes 262176 | tf_op jit(solution)/shard_map/ppermute | solution.py:278
  66.6 11.9 %all-to-all-done.2 = f32[16,8,16,128]{3,2,1,0:T(8,128)S(1)} async-done(((f32[16,8,16,128]{3,2,1,0:T(8,128)}), f32[16,8,16,128]{3,2,1,0:T(8,128)S(1)}, u32[]{:S(2)}, u32[]{:S(2)}) %all-to-all-start.2) | async-done | bytes 1048608 | tf_op jit(solution)/shard_map/all_to_all | solution.py:367
  78.5 0.9 copy-done.5
  79.4 2.9 %shard_map.103 = (f32[32,16,128]{2,1,0:T(8,128)S(1)}, f32[128,128]{1,0:T(8,128)S(1)}) custom-call(s32[2,32]{1,0:T(2,128)S(1)} %get-tuple-element.13.refs_0_, s32[1,32]{1,0:T(1,128)S(1)} %bitcast.29, f32[128,16,128]{2,1,0:T(8,128)S(1)} %bitcast.21, f32[32,16,128]{2,1,0:T(8,128)} %collective-permute-done.2.refs_3_, f32[32,16,128]{2,1,0:T(8,128)S(1)} %copy-done.5, ...), custom_call_target="tpu_custom_call" | custom-call | flops 805306368 | bytes 4194304 | tf_op jit(solution)/shard_map/pallas_call | solution.py:432
  82.3 0.7 copy-done.6
  83.6 6.8 %all-to-all-start.3 = ((f32[32,4,128]{2,1,0:T(4,128)}), f32[32,4,128]{2,1,0:T(4,128)S(1)}, u32[]{:S(2)}, u32[]{:S(2)}) async-start(f32[32,4,128]{2,1,0:T(4,128)} %bitcast.23), calls=%async_computation.3 | async-start | bytes 131072 | tf_op jit(solution)/shard_map/all_to_all | solution.py:454
  91.1 6.7 %all-to-all-done.3.part_ref = f32[32,4,128]{2,1,0:T(4,128)S(1)} async-done(((f32[32,4,128]{2,1,0:T(4,128)}), f32[32,4,128]{2,1,0:T(4,128)S(1)}, u32[]{:S(2)}, u32[]{:S(2)}) %all-to-all-start.3) | async-done | bytes 65568 | tf_op jit(solution)/shard_map/all_to_all | solution.py:454
  97.8 0.9 copy-done.7
  98.8 1.0 %shard_map.104 = f32[32,16,128]{2,1,0:T(8,128)} custom-call(f32[32,4,128]{2,1,0:T(4,128)S(1)} %all-to-all-done.3.part_ref, f32[4,128]{1,0:T(4,128)S(1)} %reshape.96.scale_ref, f32[32,16,128]{2,1,0:T(8,128)S(1)} %copy-done.7), custom_call_target="tpu_custom_call" | custom-call | tf_op jit(solution)/shard_map/pallas_call | solution.py:457
  (71 shorter events, 5.2 us)
Async XLA Ops:
  0.0 0.7 copy-start.12
  0.0 0.7 copy-start.13
  0.0 0.7 copy-start.11
  0.0 0.7 copy-start.9
  0.0 0.7 copy-start.10
  0.0 24.8 %copy-start.14 = (f32[32,16,128]{2,1,0:T(8,128)S(1)}, f32[32,16,128]{2,1,0:T(8,128)}, u32[]{:S(2)}) copy-start(f32[32,16,128]{2,1,0:T(8,128)} %start_ref.1) | copy-start | bytes 786436
  1.7 14.7 %all-to-all-start = ((s32[32,1,256]{2,1,0:T(1,128)}), s32[32,1,256]{2,1,0:T(1,128)S(1)}, u32[]{:S(2)}, u32[]{:S(2)}) async-start(s32[32,1,256]{2,1,0:T(1,128)} %get-tuple-element.14), calls=%async_computation | async-start | bytes 65536 | tf_op jit(solution)/shard_map/all_to_all | solution.py:319
  9.0 15.8 %collective-permute-start = (f32[32,16,128]{2,1,0:T(8,128)}, f32[32,16,128]{2,1,0:T(8,128)S(1)}, u32[]{:S(2)}, u32[]{:S(2)}) collective-permute-start(f32[32,16,128]{2,1,0:T(8,128)} %start_ref.1), channel_id=1, source_target_pairs={{0,8},{1,9},{2,10},{3,11},{4,12},{5,13},{6,14},{7,15},{8,0},{9,1},... | collective-permute-start | bytes 786440 | tf_op jit(solution)/shard_map/ppermute | solution.py:309
  24.8 1.0 %copy-start.1 = (f32[8,128,128]{2,1,0:T(8,128)S(1)}, f32[8,128,128]{2,1,0:T(8,128)}, u32[]{:S(2)}) copy-start(f32[8,128,128]{2,1,0:T(8,128)} %refs_6_.3) | copy-start | bytes 1572868
  29.2 18.1 %copy-start.2 = (f32[8,128,128]{2,1,0:T(8,128)S(1)}, f32[8,128,128]{2,1,0:T(8,128)}, u32[]{:S(2)}) copy-start(f32[8,128,128]{2,1,0:T(8,128)} %refs_6_.3) | copy-start | bytes 1572868
  29.2 18.1 %copy-start.3 = (f32[8,128,128]{2,1,0:T(8,128)S(1)}, f32[8,128,128]{2,1,0:T(8,128)}, u32[]{:S(2)}) copy-start(f32[8,128,128]{2,1,0:T(8,128)} %refs_5_.1) | copy-start | bytes 1572868
  29.2 18.1 %copy-start.4 = (f32[32,16,128]{2,1,0:T(8,128)S(1)}, f32[32,16,128]{2,1,0:T(8,128)}, u32[]{:S(2)}) copy-start(f32[32,16,128]{2,1,0:T(8,128)} %refs_4_.1) | copy-start | bytes 786436
  29.2 18.1 %all-to-all-start.1 = ((f32[8,16,16,128]{3,2,1,0:T(8,128)}), f32[8,16,16,128]{3,2,1,0:T(8,128)S(1)}, u32[]{:S(2)}, u32[]{:S(2)}) async-start(f32[8,16,16,128]{3,2,1,0:T(8,128)} %get-tuple-element.15), calls=%async_computation.1 | async-start | bytes 2097152 | tf_op jit(solution)/shard_map/all_to_all | solution.py:367
  32.9 8.6 %collective-permute-start.1 = (f32[32,16,128]{2,1,0:T(8,128)S(1)}, f32[32,16,128]{2,1,0:T(8,128)S(1)}, u32[]{:S(2)}, u32[]{:S(2)}) collective-permute-start(f32[32,16,128]{2,1,0:T(8,128)S(1)} %get-tuple-element.16), channel_id=1, source_target_pairs={{0,16},{16,0},{1,17},{17,1},{2,18},{18,2},{3,19},{19,3},{4,20},{20... | collective-permute-start | bytes 786440 | tf_op jit(solution)/shard_map/ppermute | solution.py:278
  50.9 4.6 %copy-start = (f32[8,128,128]{2,1,0:T(8,128)S(1)}, f32[8,128,128]{2,1,0:T(8,128)}, u32[]{:S(2)}) copy-start(f32[8,128,128]{2,1,0:T(8,128)} %refs_7_.3) | copy-start | bytes 1572868
  50.9 27.6 %all-to-all-start.2 = ((f32[16,8,16,128]{3,2,1,0:T(8,128)}), f32[16,8,16,128]{3,2,1,0:T(8,128)S(1)}, u32[]{:S(2)}, u32[]{:S(2)}) async-start(f32[16,8,16,128]{3,2,1,0:T(8,128)} %get-tuple-element.17), calls=%async_computation.2 | async-start | bytes 2097152 | tf_op jit(solution)/shard_map/all_to_all | solution.py:367
  57.5 9.0 %collective-permute-start.2 = (f32[32,16,128]{2,1,0:T(8,128)}, f32[32,16,128]{2,1,0:T(8,128)}, u32[]{:S(2)}, u32[]{:S(2)}) collective-permute-start(f32[32,16,128]{2,1,0:T(8,128)} %get-tuple-element.18), channel_id=1, source_target_pairs={{0,16},{16,0},{1,17},{17,1},{2,18},{18,2},{3,19},{19,3},{4,20},{20... | collective-permute-start | bytes 786440 | tf_op jit(solution)/shard_map/ppermute | solution.py:278
  78.5 1.0 copy-start.5
  82.3 0.7 copy-start.6
  83.6 6.8 %copy-start.17 = (s32[1024]{0:T(1024)S(1)}, s32[1024]{0:T(1024)}, u32[]{:S(2)}) copy-start(s32[1024]{0:T(1024)} %eq.99) | copy-start | bytes 12292
  83.6 6.8 %copy-start.18 = (f32[8]{0:T(128)S(1)}, f32[8]{0:T(128)}, u32[]{:S(2)}) copy-start(f32[8]{0:T(128)} %reduce_sum.27) | copy-start | bytes 100
  83.6 6.9 %copy-start.16 = (s32[2,16,32]{2,1,0:T(8,128)S(1)}, s32[2,16,32]{2,1,0:T(8,128)}, u32[]{:S(2)}) copy-start(s32[2,16,32]{2,1,0:T(8,128)} %copy-done.15) | copy-start | bytes 12292
  83.6 14.2 %all-to-all-start.3 = ((f32[32,4,128]{2,1,0:T(4,128)}), f32[32,4,128]{2,1,0:T(4,128)S(1)}, u32[]{:S(2)}, u32[]{:S(2)}) async-start(f32[32,4,128]{2,1,0:T(4,128)} %bitcast.23), calls=%async_computation.3 | async-start | bytes 131072 | tf_op jit(solution)/shard_map/all_to_all | solution.py:454
  97.8 1.0 copy-start.7
  (2 other events, 1.2 us)

commit v3 on v2

v3 whole, which is shorter than its diff:
```python
import functools

import jax
import jax.numpy as jnp
from jax import lax
from jax.experimental import pallas as pl
from jax.experimental.pallas import tpu as pltpu
from jax.sharding import PartitionSpec as P

AGG_DEV = 8
LANES = 128
DENSE_LIMIT = 1 << 19

VMEM = pl.BlockSpec(memory_space=pltpu.VMEM)
SMEM = pl.BlockSpec(memory_space=pltpu.SMEM)
HIGH = lax.Precision.HIGHEST


def params():
    return pltpu.CompilerParams(vmem_limit_bytes=16 * 1024 * 1024)


def call(kernel, out_shape, in_specs, scratch=(), flops=0, moved=0):
    single = not isinstance(out_shape, (tuple, list))
    count = 1 if single else len(out_shape)
    return pl.pallas_call(
        kernel,
        out_shape=out_shape,
        in_specs=in_specs,
        out_specs=VMEM if single else [VMEM] * count,
        scratch_shapes=list(scratch),
        compiler_params=params(),
        cost_estimate=pl.CostEstimate(flops=flops, bytes_accessed=moved, transcendentals=0),
    )


def halves(value):
    high = value.astype(jnp.bfloat16)
    low = (value - high.astype(jnp.float32)).astype(jnp.bfloat16)
    return high, low


def left_operand(value):
    high, low = halves(value)
    return jnp.concatenate([high, low, high], axis=1)


def right_operand(value):
    high, low = halves(value)
    return jnp.concatenate([high, high, low], axis=1)


def dot_nt(left, right):
    return lax.dot_general(
        left, right, (((1,), (1,)), ((), ())), preferred_element_type=jnp.float32
    )


def table_products(value, table_ref, out_ref):
    left = left_operand(value)
    count, width = table_ref.shape[0], table_ref.shape[1]
    for first in range(0, count, 2):
        last = min(first + 2, count)
        right = right_operand(table_ref[first:last].reshape((last - first) * width, -1))
        product = dot_nt(left, right)
        for t in range(first, last):
            out_ref[t] = product[:, (t - first) * width : (t - first + 1) * width]


def dot_exact(left, value):
    high, low = halves(value)
    return jnp.dot(left, high, preferred_element_type=jnp.float32) + jnp.dot(
        left, low, preferred_element_type=jnp.float32
    )


def request_kernel(
    sizes, owner_ref, local_ref, tile_ref, diag_ref, group_ref, payload_ref, slot_ref
):
    rows, n_rows, cap, n_tiles = sizes
    width_k = owner_ref.shape[0]
    half = n_rows // 2
    row_of = lax.broadcasted_iota(jnp.int32, (rows, rows), 0)
    col_of = lax.broadcasted_iota(jnp.int32, (rows, rows), 1)
    lane = lax.broadcasted_iota(jnp.int32, (rows, LANES), 1)
    owners = lax.broadcasted_iota(jnp.int32, (n_rows, rows), 0)

    def column(row):
        return jnp.sum(jnp.where(row_of == col_of, row, 0), axis=1, keepdims=True)

    def owner_row(k):
        return owner_ref[k : k + 1, :]

    row_ids = lax.broadcasted_iota(jnp.int32, (1, rows), 1)
    owner_columns = [column(owner_row(k)) for k in range(width_k)]
    lists = jnp.zeros((n_rows, LANES), jnp.float32)
    for k in range(width_k):
        rank = jnp.zeros((1, rows), jnp.int32)
        for other in range(k + 1):
            match = owner_columns[other] == owner_row(k)
            if other == k:
                match = match & (row_of < col_of)
            rank = rank + jnp.sum(jnp.where(match, 1, 0), axis=0, keepdims=True)
        slot_ref[k : k + 1, :] = owner_row(k) * cap + rank
        code = local_ref[k : k + 1, :] + rows * (
            tile_ref[k : k + 1, :] + n_tiles * row_ids
        )
        code, rank = column(code + 1), column(rank)
        mirror = jnp.where(owner_row(k) >= half, owner_row(k) - half, owner_row(k) + half)
        for owner, base in ((owner_row(k), 0), (mirror, LANES // 2)):
            by_rank = jnp.where(lane == rank + base, code, 0).astype(jnp.float32)
            mine = jnp.where(owners == owner, 1.0, 0.0)
            lists = lists + jnp.dot(
                mine, by_rank, precision=HIGH, preferred_element_type=jnp.float32
            )
    lists = (lists + 0.5).astype(jnp.int32)
    common = [group_ref[...], diag_ref[...]]
    common += [tile_ref[k : k + 1, :] for k in range(width_k + 2)]
    common += [owner_row(k) * rows + local_ref[k : k + 1, :] for k in range(width_k)]
    spare = payload_ref.shape[2] - LANES - len(common) * rows
    if spare:
        common.append(jnp.zeros((1, spare), jnp.int32))
    common = jnp.concatenate(common, axis=1)
    for device in range(n_rows):
        line = jnp.concatenate([lists[device : device + 1, :], common], axis=1)
        for band in range(payload_ref.shape[0] // n_rows):
            payload_ref[band * n_rows + device] = line


def chosen_product(sizes, product_ref, code, base):
    rows, n_rows, cap, n_tiles, n_rhs = sizes
    code = jnp.maximum(code - 1, 0)
    tile = lax.rem(lax.div(code, rows), n_tiles)
    start = pl.multiple_of((lax.rem(code, rows) + base) * n_rhs, n_rhs)
    return product_ref[tile, pl.ds(start, n_rhs), :]


def pack_bands(sizes, product_ref, tiles_ref, band_refs):
    rows, n_rhs = sizes[0], sizes[4]
    for way, band_ref in enumerate(band_refs):
        for row in range(rows):
            band_ref[row] = product_ref[tiles_ref[way, row], pl.ds(row * n_rhs, n_rhs), :]


def product_kernel(start_ref, mirror_ref, tile_ref, product_ref):
    flat = product_ref.shape[1] // 2
    values = [ref[...].reshape(flat, -1) for ref in (start_ref, mirror_ref)]
    table_products(jnp.concatenate(values, axis=0), tile_ref, product_ref)


def first_kernel(sizes, product_ref, request_ref, tiles_ref, send_ref, *band_refs):
    rows, n_rows, cap, n_tiles, n_rhs = sizes
    half = n_rows // 2
    base = lax.div(lax.axis_index("rows"), half) * half
    for device in range(half):
        for slot in range(2 * cap):
            side, rank = slot // cap, slot % cap
            code = request_ref[base + device, side * (LANES // 2) + rank]
            block = chosen_product(sizes, product_ref, code, side * rows)
            send_ref[device, slot * n_rhs : (slot + 1) * n_rhs, :] = block
    pack_bands(sizes, product_ref, tiles_ref, band_refs)


def count_kernel(n_func, *refs):
    *sides, group_ref, own_ref, tile_ref, table_ref, inverse_ref, count_ref, functional_ref = refs
    n_tiles, n_groups = tile_ref.shape[0], count_ref.shape[1]
    pieces = []
    for code_ref, source_ref, target_ref in (sides[:3], sides[3:]):
        hits = jnp.where(target_ref[...] == source_ref[...], 1.0, 0.0).astype(jnp.bfloat16)
        pieces.append((code_ref, hits))
    for t in range(n_tiles):
        found = []
        for code_ref, hits in pieces:
            ids = lax.broadcasted_iota(jnp.int32, (n_groups, code_ref.shape[1]), 0) + t * n_groups
            takes = jnp.where(ids == code_ref[...], 1.0, 0.0).astype(jnp.bfloat16)
            found.append(dot_nt(takes, hits))
        count_ref[t] = jnp.concatenate(found, axis=1).astype(jnp.bfloat16)
    ids = lax.broadcasted_iota(jnp.int32, count_ref.shape[1:], 0)
    count_ref[n_tiles] = jnp.where(ids == group_ref[...], 1.0, 0.0).astype(jnp.bfloat16)
    count_ref[n_tiles + 1] = jnp.where(ids == own_ref[...], 1.0, 0.0).astype(jnp.bfloat16)
    sums = jnp.sum(tile_ref[...], axis=1)
    line = lax.broadcasted_iota(jnp.int32, (n_func, sums.shape[1]), 0)
    sums = jnp.concatenate([sums, jnp.zeros((n_func - n_tiles, sums.shape[1]), jnp.float32)], axis=0)
    for d in range(inverse_ref.shape[0]):
        minus = -jnp.sum(table_ref[d], axis=0, keepdims=True)
        wanted = jnp.where(line == n_tiles, minus, sums)
        high, low = halves(inverse_ref[d])
        right = jnp.concatenate([high, high, low], axis=0)
        solved = jnp.dot(left_operand(wanted), right, preferred_element_type=jnp.float32)
        solved = jnp.where(line == n_tiles + 1, 1.0, solved)
        functional_ref[d * n_func : (d + 1) * n_func, :] = left_operand(solved)


def gather_solve(
    sizes, slot_ref, diag_ref, arrived_ref, band_refs, right_ref, inverse_ref, sum_ref, product_ref
):
    rows, n_rows, cap, n_tiles, n_rhs = sizes
    per = n_rows * cap // arrived_ref.shape[0]
    for row in range(rows):
        total = right_ref[row]
        for k in range(slot_ref.shape[0]):
            slot = slot_ref[k, row]
            start = pl.multiple_of(lax.rem(slot, per) * n_rhs, n_rhs)
            total = total + arrived_ref[lax.div(slot, per), pl.ds(start, n_rhs), :]
        for band_ref in band_refs:
            total = total + band_ref[row]
        sum_ref[pl.ds(row * n_rhs, n_rhs), :] = total
    table_products(sum_ref[...], inverse_ref, product_ref)
    for row in range(rows):
        place = pl.ds(row * n_rhs, n_rhs)
        sum_ref[place, :] = product_ref[diag_ref[0, row], place, :]


def middle_kernel(sizes, n_band, dense, *refs):
    slot_ref, diag_ref, request_ref, tiles_ref, arrived_ref = refs[:5]
    band_in = refs[5 : 5 + n_band]
    right_ref, inverse_ref, tile_ref = refs[5 + n_band : 8 + n_band]
    refs = refs[8 + n_band :]
    extra, refs = (refs[:4], refs[4:]) if dense else ((), refs)
    send_ref, band_out = refs[0], refs[1 : 1 + n_band]
    sum_ref, product_ref = refs[1 + n_band : 3 + n_band]
    gather_solve(
        sizes, slot_ref, diag_ref, arrived_ref, band_in, right_ref, inverse_ref, sum_ref, product_ref
    )
    table_products(sum_ref[...], tile_ref, product_ref)
    rows, n_rows, cap, n_tiles, n_rhs = sizes
    for owner in range(n_rows):
        for rank in range(cap):
            block = chosen_product(sizes, product_ref, request_ref[owner, rank], 0)
            send_ref[owner, rank * n_rhs : (rank + 1) * n_rhs, :] = block
    pack_bands(sizes, product_ref, tiles_ref, band_out)
    if dense:
        value_ref, spread_ref = refs[3 + n_band :]
        coarse_parts(sizes, extra, right_ref, send_ref, band_out, value_ref, spread_ref)


def coarse_parts(sizes, extra, right_ref, send_ref, band_out, value_ref, spread_ref):
    kind_ref, functional_ref, count_ref, place_ref = extra
    rows, n_rows, cap, n_tiles, n_rhs = sizes
    body = cap * n_rhs
    n_func = spread_ref.shape[0] // count_ref.shape[2]
    per_tile = LANES // n_rhs
    functional = functional_ref[...]
    done = 0
    for owner in range(0, n_rows, 2):
        values = [send_ref[owner + more, :body, :] for more in range(2)]
        values = jnp.concatenate(values, axis=0)
        value_ref[:, done : done + 2 * body] = dot_nt(functional, right_operand(values))
        done += 2 * body
    for ref in (right_ref, *band_out):
        values = ref[...].reshape(rows * n_rhs, -1)
        value_ref[:, done : done + rows * n_rhs] = dot_nt(functional, right_operand(values))
        done += rows * n_rhs
    lane = lax.broadcasted_iota(jnp.int32, (n_func, LANES), 1)
    for block in range(done // n_rhs):
        tile, spot = block // per_tile, block % per_tile
        start = pl.multiple_of(kind_ref[0, block] * n_func, n_func)
        piece = value_ref[pl.ds(start, n_func), tile * LANES : (tile + 1) * LANES]
        piece = jnp.where((lane >= spot * n_rhs) & (lane < (spot + 1) * n_rhs), piece, 0.0)
        spread_ref[block * n_func : (block + 1) * n_func, :] = piece
    partial = jnp.zeros((count_ref.shape[1], 2 * LANES), jnp.float32)
    for t in range(count_ref.shape[0]):
        values = spread_ref[pl.ds(t, done // n_rhs, stride=n_func), :]
        partial = partial + jnp.dot(
            count_ref[t],
            jnp.concatenate(halves(values), axis=1),
            preferred_element_type=jnp.float32,
        )
    partial = partial[:, :LANES] + partial[:, LANES:]
    source = lax.broadcasted_iota(jnp.int32, (LANES, LANES), 0)
    target = lax.broadcasted_iota(jnp.int32, (LANES, LANES), 1)
    same = jnp.where(lax.rem(source, n_rhs) == lax.rem(target, n_rhs), 1.0, 0.0)
    same = same.astype(jnp.bfloat16)
    same = jnp.concatenate([same, same], axis=0)
    partial = jnp.dot(
        jnp.concatenate(halves(partial), axis=1), same, preferred_element_type=jnp.float32
    )
    both = jnp.concatenate(halves(partial), axis=1)
    length = place_ref.shape[0] // per_tile
    lane = lax.broadcasted_iota(jnp.int32, (length, LANES), 1)
    result = jnp.zeros((length, LANES), jnp.float32)
    for spot in range(per_tile):
        chosen = jnp.dot(
            place_ref[spot * length : (spot + 1) * length, :],
            both,
            preferred_element_type=jnp.float32,
        )
        chosen = chosen[:, :LANES] + chosen[:, LANES:]
        result = jnp.where((lane >= spot * n_rhs) & (lane < (spot + 1) * n_rhs), chosen, result)
    depth = length // n_rows
    for owner in range(n_rows):
        send_ref[owner, body:, :] = result[owner * depth : (owner + 1) * depth, :]


def part_kernel(arrived_ref, mine_ref, other_ref):
    depth = mine_ref.shape[0]
    body = arrived_ref.shape[1] - 2 * depth
    total = arrived_ref[0, body:, :]
    for source in range(1, arrived_ref.shape[0]):
        total = total + arrived_ref[source, body:, :]
    upper = lax.axis_index("band") == 0
    mine_ref[...] = jnp.where(upper, total[:depth], total[depth:])
    other_ref[...] = jnp.where(upper, total[depth:], total[:depth])


def last_kernel(sizes, n_band, *refs):
    slot_ref, diag_ref, arrived_ref = refs[:3]
    band_in = refs[3 : 3 + n_band]
    right_ref, inverse_ref, second_ref, sum_ref, product_ref = refs[3 + n_band :]
    gather_solve(
        sizes, slot_ref, diag_ref, arrived_ref, band_in, right_ref, inverse_ref, sum_ref, product_ref
    )
    second_ref[...] = sum_ref[...].reshape(second_ref.shape)


def final_kernel(sizes, mine_ref, other_ref, scale_ref, second_ref, out_ref):
    rows, n_rhs = sizes[0], sizes[4]
    depth = scale_ref.shape[0]
    correction = (mine_ref[...] + other_ref[...]) / scale_ref[...]
    padded = jnp.concatenate([correction, jnp.zeros((8 - depth, LANES), jnp.float32)], axis=0)
    turned = padded.T
    for row in range(rows):
        spot, place = row // depth, row % depth
        column = turned[spot * n_rhs : (spot + 1) * n_rhs, place : place + 1]
        out_ref[row] = second_ref[row] + column


def shifted(value, axis, steps):
    count = lax.axis_size(axis)
    initial, last = (max(0, -steps), min(count, count - steps))
    return lax.ppermute(value, axis, [(source, source + steps) for source in range(initial, last)])


def to_bands(sends):
    if len(sends) == 1:
        return (lax.ppermute(sends[0], "band", [(0, 1), (1, 0)]),)
    return shifted(sends[0], "band", 1), shifted(sends[1], "band", -1)


def on_device(
    start_iterate,
    right_side,
    diag_table,
    inverse_table,
    coupling_tiles,
    diag_index,
    tile_index,
    source_owner,
    source_local,
    aggregate_map,
):
    rows, n_rhs, states = start_iterate.shape
    width_k = source_owner.shape[1]
    n_tiles, n_diag = coupling_tiles.shape[0], inverse_table.shape[0]
    n_rows, n_bands = lax.axis_size("rows"), lax.axis_size("band")
    n_dev = n_rows * n_bands
    cap = max(2, 2 * width_k * rows // n_rows)
    slots = n_rows * cap
    total_groups = AGG_DEV * n_dev
    per_tile = LANES // n_rhs
    depth = rows // per_tile
    n_func = 16
    dense = (
        n_bands == 2
        and n_dev * rows * total_groups <= DENSE_LIMIT
        and depth == 4
        and n_diag * n_func == LANES
        and n_tiles + 2 <= n_func
    )
    sizes = (rows, n_rows, cap, n_tiles, n_rhs)
    f32, i32 = jnp.float32, jnp.int32
    my_band = lax.axis_index("band")
    my_row = lax.axis_index("rows")

    half = n_rows // 2
    mirror = lax.ppermute(start_iterate, "rows", [(i, (i + half) % n_rows) for i in range(n_rows)])
    wide = -(-(4 + 2 * width_k) * rows // LANES) * LANES
    payload, slot_place = call(
        functools.partial(request_kernel, (rows, n_rows, cap, n_tiles)),
        (
            jax.ShapeDtypeStruct((n_dev, 1, LANES + wide), i32),
            jax.ShapeDtypeStruct((width_k, rows), i32),
        ),
        [VMEM] * 5,
    )(source_owner.T, source_local.T, tile_index.T, diag_index[None], aggregate_map.T)
    arrived = lax.all_to_all(
        payload, ("band", "rows"), split_axis=0, concat_axis=0, tiled=True
    ).reshape(n_bands, n_rows, LANES + wide)
    owner = slot_place // cap
    half_place = (owner % half) * 2 * cap + slot_place % cap
    half_place = half_place + jnp.where(owner // half == my_row // half, 0, cap)
    requests = lax.dynamic_index_in_dim(arrived[:, :, :LANES], my_band, 0, keepdims=False)
    common = arrived[:, :, LANES:]
    groups_all = common[:, :, :rows]
    diags_all = common[:, :, rows : 2 * rows]

    def neighbour(steps):
        other = lax.rem(my_band + steps + n_bands, n_bands)
        part = lax.dynamic_index_in_dim(common, other, 0, keepdims=False)
        return lax.dynamic_index_in_dim(part, my_row, 0, keepdims=False)

    above, below = neighbour(1), neighbour(-1)
    has_above, has_below = my_band + 1 < n_bands, my_band > 0
    field = (2 + width_k) * rows
    tiles_above = above[field : field + rows]
    tiles_below = below[field + rows : field + 2 * rows]
    if n_bands == 2:
        band_tiles = jnp.where(has_above, tiles_above, tiles_below)[None]
        band_groups = jnp.where(has_above, above[:rows], below[:rows])[None]
        band_valid = jnp.ones((1, rows), bool)
    else:
        band_tiles = jnp.stack([tiles_above, tiles_below])
        band_groups = jnp.stack([above[:rows], below[:rows]])
        band_valid = jnp.stack(
            [jnp.broadcast_to(has_above, (rows,)), jnp.broadcast_to(has_below, (rows,))]
        )
    n_ways = band_tiles.shape[0]

    block = (rows, n_rhs, states)
    band_shapes = [jax.ShapeDtypeStruct(block, f32)] * n_ways
    flat = rows * n_rhs
    sums = pltpu.VMEM((flat, states), f32)
    products = pltpu.VMEM((max(n_tiles, n_diag), flat, states), f32)
    work = 6 * flat * states * states
    made = call(
        product_kernel,
        jax.ShapeDtypeStruct((n_tiles, 2 * flat, states), f32),
        [VMEM] * 3,
        (),
        2 * work * n_tiles,
        4 << 20,
    )(start_iterate, mirror, coupling_tiles)
    sends = call(
        functools.partial(first_kernel, sizes),
        (jax.ShapeDtypeStruct((half, 2 * cap * n_rhs, states), f32), *band_shapes),
        [VMEM, SMEM, SMEM],
        (),
        0,
        4 << 20,
    )(made, requests, band_tiles)
    halves_of_rows = [list(range(half)), list(range(half, n_rows))]

    def exchange(sends, groups=None):
        arrived = lax.all_to_all(
            sends[0], "rows", split_axis=0, concat_axis=0, tiled=True, axis_index_groups=groups
        )
        return arrived, to_bands(sends[1:])

    diag_row = diag_index[None]
    arrived_blocks, arrived_bands = exchange(sends, halves_of_rows)

    groups = aggregate_map[:, 0]
    own = jnp.arange(rows, dtype=i32)
    codes = requests[:, :cap]
    asked = lax.broadcasted_iota(i32, codes.shape, 0) * rows + (codes - 1) // (rows * n_tiles)
    asked = jnp.where(codes > 0, asked, -1).reshape(-1)
    own_rows = my_row * rows + own
    table_sums = jnp.sum(diag_table, axis=(1, 2))
    diag_onehot = diags_all.reshape(-1, 1) == jnp.arange(n_diag, dtype=i32)[None]
    block_sums = jnp.sum(jnp.where(diag_onehot, table_sums[None], 0.0), axis=1)
    all_groups = groups_all.reshape(-1)
    whole_diag = jnp.sum(
        jnp.where(groups[:, None] == all_groups[None], block_sums[None], 0.0), axis=1
    )
    extra, extra_specs, extra_scratch, tail = (), [], [], 0
    if dense:
        fields = common.reshape(n_bands, n_rows, -1, rows).transpose(2, 0, 1, 3)
        fields = fields.reshape(-1, n_bands, n_rows * rows)
        by_group, by_diag = fields[0], fields[1]
        tiles_of, sources_of = fields[2 : 4 + width_k], fields[4 + width_k : 4 + 2 * width_k]
        across = jnp.stack([tiles_of[width_k, 1], tiles_of[width_k + 1, 0]])
        taken = [tiles_of[k] * total_groups + by_group for k in range(width_k)]
        taken = jnp.concatenate([*taken, across * total_groups + by_group[::-1]], axis=1)
        band_row_ids = jnp.broadcast_to(jnp.arange(n_rows * rows, dtype=i32)[None], by_group.shape)
        origin = jnp.concatenate([*sources_of, band_row_ids], axis=1)

        def pick(table, band):
            return lax.dynamic_index_in_dim(table, band, 0, keepdims=True)

        near, far = my_band, 1 - my_band
        near_targets = jnp.concatenate([asked, own_rows])
        targets = jnp.maximum(near_targets, 0)
        target_groups = jnp.concatenate([jnp.take(pick(by_group, near)[0], targets), band_groups[0]])
        target_kinds = jnp.concatenate(
            [jnp.take(pick(by_diag, near)[0], targets), pick(by_diag, far)[0][own_rows]]
        )
        target_groups = jnp.where(jnp.concatenate([near_targets, own_rows]) >= 0, target_groups, -1)
        nobody = jnp.full((slots,), -1, i32)
        own_groups = jnp.concatenate([nobody, groups, jnp.full((rows,), -1, i32)])
        n_blocks = slots + 2 * rows
        counts, functionals = call(
            functools.partial(count_kernel, n_func),
            (
                jax.ShapeDtypeStruct((n_tiles + 2, total_groups, n_blocks), jnp.bfloat16),
                jax.ShapeDtypeStruct((n_diag * n_func, 3 * states), jnp.bfloat16),
            ),
            [VMEM] * 11,
            (),
            4 * total_groups * n_tiles * n_dev * rows * n_blocks,
            4 << 20,
        )(
            pick(taken, near),
            pick(origin, near),
            near_targets[:, None],
            pick(taken, far),
            pick(origin, far),
            own_rows[:, None],
            target_groups[None],
            own_groups[None],
            coupling_tiles,
            diag_table,
            inverse_table,
        )
        order = groups_all.reshape(n_bands, n_rows, per_tile, depth).transpose(2, 1, 0, 3)
        group_ids = jnp.arange(total_groups, dtype=i32)
        placing = (order.reshape(-1, 1) == group_ids[None]).astype(jnp.bfloat16)
        scale = jnp.repeat(whole_diag.reshape(per_tile, depth).T, n_rhs, axis=1)
        extra = (target_kinds[None], functionals, counts, placing)
        extra_specs = [SMEM, VMEM, VMEM, VMEM]
        extra_scratch = [
            pltpu.VMEM((n_diag * n_func, n_blocks * n_rhs), f32),
            pltpu.VMEM((n_blocks * n_func, LANES), f32),
        ]
        tail = n_bands * depth

    sends = call(
        functools.partial(middle_kernel, sizes, n_ways, dense),
        (jax.ShapeDtypeStruct((n_rows, cap * n_rhs + tail, states), f32), *band_shapes),
        [SMEM] * 4 + [VMEM] * (4 + n_ways) + extra_specs,
        [sums, products, *extra_scratch],
        work * (n_tiles + n_diag),
        4 << 20,
    )(
        half_place,
        diag_row,
        requests,
        band_tiles,
        arrived_blocks,
        *arrived_bands,
        right_side,
        inverse_table,
        coupling_tiles,
        *extra,
    )
    arrived_blocks, arrived_bands = exchange(sends)

    if dense:
        part = jax.ShapeDtypeStruct((depth, LANES), f32)
        mine, other = call(part_kernel, (part, part), [VMEM])(arrived_blocks)
        other = lax.ppermute(other, "band", [(0, 1), (1, 0)])
    second = call(
        functools.partial(last_kernel, sizes, n_ways),
        jax.ShapeDtypeStruct(block, f32),
        [SMEM] * 2 + [VMEM] * (3 + n_ways),
        [sums, products],
        work * n_diag,
        4 << 20,
    )(slot_place, diag_row, arrived_blocks, *arrived_bands, right_side, inverse_table)
    if dense:
        return call(
            functools.partial(final_kernel, sizes), jax.ShapeDtypeStruct(block, f32), [VMEM] * 4
        )(mine, other, scale, second)

    n_all = n_tiles + n_diag + 1
    code = jnp.maximum(codes.reshape(-1) - 1, 0)
    band_of_mine = lax.dynamic_index_in_dim(groups_all, my_band, 0, keepdims=False).reshape(-1)
    entry_group = jnp.concatenate(
        [jnp.take(band_of_mine, jnp.maximum(asked, 0)), band_groups.reshape(-1), groups, groups]
    )
    entry_func = jnp.concatenate(
        [
            (code % rows) * n_all + (code // rows) % n_tiles,
            (own[None] * n_all + band_tiles).reshape(-1),
            own * n_all + n_tiles + diag_index,
            own * n_all + n_tiles + n_diag,
        ]
    )
    entry_valid = jnp.concatenate([asked >= 0, band_valid.reshape(-1), jnp.ones((2 * rows,), bool)])
    functionals = jnp.concatenate(
        [jnp.sum(coupling_tiles, axis=1), -jnp.sum(diag_table, axis=1)], axis=0
    )
    weights = jnp.einsum("fp,rcp->rfc", functionals, second, precision=HIGH)
    weights = jnp.concatenate([weights, jnp.sum(right_side, axis=2)[:, None]], axis=1)
    chosen = jnp.take(weights.reshape(rows * n_all, n_rhs), entry_func, axis=0)
    chosen = jnp.where(entry_valid[:, None], chosen, 0.0)
    partial = jax.ops.segment_sum(chosen, entry_group, num_segments=total_groups)
    whole = lax.psum(partial, ("band", "rows"))
    correction = jnp.take(whole, groups, axis=0) / whole_diag[:, None]
    return second + correction[:, :, None]


def solution(mesh):
    in_specs = (
        P(("band", "rows"), None, None),
        P(("band", "rows"), None, None),
        P(),
        P(),
        P(),
        P(("band", "rows")),
        P(("band", "rows"), None),
        P(("band", "rows"), None),
        P(("band", "rows"), None),
        P(("band", "rows"), None),
    )
    out_specs = P(("band", "rows"), None, None)
    return jax.shard_map(
        on_device, mesh=mesh, in_specs=in_specs, out_specs=out_specs, check_vma=False
    )
```

time: 100 us -> 93.7 us (0.937); the launches traced: 99.8 us -> 91.9 us
  waiting for transfers between devices: 49.7 us -> 35.7 us
  local copies, waits for them, and re-layouts: 7.65 us -> 14.2 us
  starting transfers between devices: 28.4 us -> 23.9 us
  Pallas kernels: 11.8 us -> 15.8 us
    all_to_all x1 -> x0, starting transfers between devices: 6.77 us -> none  [on_device(): lax.all_to_all(parts.reshape(n_dev, depth, LANES), ('band', 'rows'), spli...]
    all_to_all x1 -> x0, waiting for transfers between devices: 6.71 us -> none  [on_device(): lax.all_to_all(parts.reshape(n_dev, depth, LANES), ('band', 'rows'), spli...]
    ppermute x2, waiting for transfers between devices: 12.4 us -> 6.56 us  [to_bands(): return (lax.ppermute(sends[0], 'band', [(0, 1), (1, 0)]),)]
    ppermute x1, waiting for transfers between devices: 8.26 us -> 3.08 us  [on_device(): lax.ppermute(start_iterate, 'rows', [(i, (i + half) % n_rows) for i in ra...]
    pallas_call x2 -> x5, Pallas kernels: 6.44 us -> 11.6 us  [the longest x1 5.25 us: on_device(): call(functools.partial(middle_kernel, sizes, n_ways, dense), (jax.ShapeDt...]
    gather x0 -> x3, local copies, waits for them, and re-layouts: none -> 3.94 us  [the longest x1 1.61 us: on_device(): jnp.take(pick(by_group, near)[0], targets)]
    all_to_all x2, waiting for transfers between devices: 17.7 us -> 21.5 us  [exchange(): lax.all_to_all(sends[0], 'rows', split_axis=0, concat_axis=0, tiled=True,...]
    unnamed x39 -> x38, local copies, waits for them, and re-layouts: 5.51 us -> 7.59 us
  transfers between devices with their start and end apart: 7 -> 7, of which waited for: 7 -> 5; matrix products, arithmetic and copies ran while one was open for 4% -> 9% of each run, Pallas kernels for 0% -> 6%
where the time goes in v3:
time: 93.7 us; the launch traced here: 91.9 us
  waiting for transfers between devices  35.7 us (38%)
  starting transfers between devices  23.9 us (26%)
  Pallas kernels  15.8 us (17%)
  local copies, waits for them, and re-layouts  14.2 us (15%)
  other arithmetic  1.91 us (2%)
    all_to_all x2, waiting for transfers between devices, exchange(): lax.all_to_all(sends[0], 'rows', split_axis=0, concat_axis=0, tiled=True,...  21.5 us
    all_to_all x2, starting transfers between devices, exchange(): lax.all_to_all(sends[0], 'rows', split_axis=0, concat_axis=0, tiled=True,...  9.12 us
    unnamed x38, local copies, waits for them, and re-layouts  7.59 us
    all_to_all x1, starting transfers between devices, on_device(): lax.all_to_all(payload, ('band', 'rows'), split_axis=0, concat_axis=0, ti...  7.3 us
    ppermute x2, waiting for transfers between devices, to_bands(): return (lax.ppermute(sends[0], 'band', [(0, 1), (1, 0)]),)  6.56 us
    pallas_call x1, Pallas kernels, on_device(): call(functools.partial(middle_kernel, sizes, n_ways, dense), (jax.ShapeDt...  5.25 us
    all_to_all x1, waiting for transfers between devices, on_device(): lax.all_to_all(payload, ('band', 'rows'), split_axis=0, concat_axis=0, ti...  3.78 us
    pallas_call x1, Pallas kernels, on_device(): call(functools.partial(count_kernel, n_func), (jax.ShapeDtypeStruct((n_ti...  3.67 us
  transfers between devices with their start and end apart: 7, of which 5 were waited for; matrix products, arithmetic and copies ran while one was open for 9% of the time, Pallas kernels for 6%

profile of v3, /device:TPU:0, one launch (start us, length us, event | category | flops | bytes accessed | tf_op | source)
XLA Modules:
  0.0 91.9 jit_solution(1273738708210044891)
XLA Ops:
  3.4 1.0 %shard_map.100 = (s32[32,1,384]{2,1,0:T(1,128)}, s32[2,32]{1,0:T(2,128)S(1)}) custom-call(s32[2,32]{1,0:T(2,128)S(1)} %bitcast.55, s32[2,32]{1,0:T(2,128)S(1)} %bitcast.56, s32[4,32]{1,0:T(4,128)S(1)} %bitcast.54, s32[1,32]{1,0:T(1,128)S(1)} %bitcast.47, s32[1,32]{1,0:T(1,128)S(1)} %bitcast.51), custom_call_target="tpu_custom_call" | custom-call | tf_op jit(solution)/shard_map/pallas_call | solution.py:378
  4.4 7.3 %all-to-all-start = ((s32[32,1,384]{2,1,0:T(1,128)}), s32[32,1,384]{2,1,0:T(1,128)S(1)}, u32[]{:S(2)}, u32[]{:S(2)}) async-start(s32[32,1,384]{2,1,0:T(1,128)} %get-tuple-element.17), calls=%async_computation | async-start | bytes 98304 | tf_op jit(solution)/shard_map/all_to_all | solution.py:386
  11.7 2.7 %collective-permute-start = (f32[32,16,128]{2,1,0:T(8,128)}, f32[32,16,128]{2,1,0:T(8,128)S(1)}, u32[]{:S(2)}, u32[]{:S(2)}) collective-permute-start(f32[32,16,128]{2,1,0:T(8,128)} %start_ref.1), channel_id=1, source_target_pairs={{0,8},{1,9},{2,10},{3,11},{4,12},{5,13},{6,14},{7,15},{8,0},{9,1},... | collective-permute-start | bytes 786440 | tf_op jit(solution)/shard_map/ppermute | solution.py:376
  14.7 0.7 pad_add_fusion.4
  15.4 3.8 %all-to-all-done = s32[32,1,384]{2,1,0:T(1,128)S(1)} async-done(((s32[32,1,384]{2,1,0:T(1,128)}), s32[32,1,384]{2,1,0:T(1,128)S(1)}, u32[]{:S(2)}, u32[]{:S(2)}) %all-to-all-start) | async-done | bytes 49184 | tf_op jit(solution)/shard_map/all_to_all | solution.py:386
  19.8 1.6 %gather_fusion.2 = s32[160]{0:T(256)S(1)} fusion(s32[512]{0:T(512)S(1)} %bitcast.59, s32[1024]{0:T(1024)S(1)} %pad_clamp_fusion.1), kind=kCustom, calls=%fused_computation.1.clone | custom fusion | bytes 1920 | tf_op jit(solution)/shard_map/jit(_take)/gather | solution.py:483
  21.5 1.6 %gather_fusion.1 = s32[160]{0:T(256)S(1)} fusion(s32[512]{0:T(512)S(1)} %bitcast.58, s32[1024]{0:T(1024)S(1)} %pad_clamp_fusion.1), kind=kCustom, calls=%fused_computation.clone | custom fusion | bytes 1920 | tf_op jit(solution)/shard_map/jit(_take)/gather | solution.py:485
  24.7 3.1 %collective-permute-done.mirror_ref = f32[32,16,128]{2,1,0:T(8,128)S(1)} collective-permute-done((f32[32,16,128]{2,1,0:T(8,128)}, f32[32,16,128]{2,1,0:T(8,128)S(1)}, u32[]{:S(2)}, u32[]{:S(2)}) %collective-permute-start) | collective-permute-done | bytes 262176 | tf_op jit(solution)/shard_map/ppermute | solution.py:376
  27.7 1.3 %shard_map.101.product_ref = f32[8,1024,128]{2,1,0:T(8,128)S(1)} custom-call(f32[32,16,128]{2,1,0:T(8,128)S(1)} %copy-done.7, f32[32,16,128]{2,1,0:T(8,128)S(1)} %collective-permute-done.mirror_ref, f32[8,128,128]{2,1,0:T(8,128)S(1)} %copy-done), custom_call_target="tpu_custom_call" | custom-call | flops 805306368 | bytes 4194304 | tf_op jit(solution)/shard_map/pallas_call | solution.py:425
  29.0 2.2 %shard_map.102 = (f32[8,256,128]{2,1,0:T(8,128)}, f32[32,16,128]{2,1,0:T(8,128)}) custom-call(f32[8,1024,128]{2,1,0:T(8,128)S(1)} %shard_map.101.product_ref, s32[16,128]{1,0:T(8,128)S(1)} %dynamic-slice_bitcast_fusion.request_ref.refs_2_, s32[1,32]{1,0:T(1,128)S(1)} %get-tuple-element.35.tiles_ref.refs_3_), custom_call_target="tpu_custom_call" | custom-call | bytes 4194304 | tf_op jit(solution)/shard_map/pallas_call | solution.py:433
  31.3 3.7 %all-to-all-start.1 = ((f32[8,256,128]{2,1,0:T(8,128)}), f32[8,256,128]{2,1,0:T(8,128)S(1)}, u32[]{:S(2)}, u32[]{:S(2)}) async-start(f32[8,256,128]{2,1,0:T(8,128)} %get-tuple-element.18), calls=%async_computation.1 | async-start | bytes 2097152 | tf_op jit(solution)/shard_map/all_to_all | solution.py:444
  35.1 3.7 %shard_map.103 = (bf16[10,256,192]{2,1,0:T(8,128)(2,1)S(1)}, bf16[128,384]{1,0:T(8,128)(2,1)S(1)}) custom-call(s32[1,1536]{1,0:T(1,128)S(1)} %get-tuple-element.50.refs_0_, s32[1,1536]{1,0:T(1,128)S(1)} %get-tuple-element.39.refs_1_, s32[160,1]{1,0:T(8,128)S(1)} %copy.25.refs_2_, s32[1,1536]{1,0:T(1,128)S(1)} %get-tuple-element.51.refs_3_, ...), custom_call_target="tpu_custom_call" | custom-call | flops 1610612736 | bytes 4194304 | tf_op jit(solution)/shard_map/pallas_call | solution.py:491
  38.8 1.1 %copy-done.2 = bf16[10,256,192]{2,1,0:T(8,128)(2,1)} copy-done((bf16[10,256,192]{2,1,0:T(8,128)(2,1)}, bf16[10,256,192]{2,1,0:T(8,128)(2,1)S(1)}, u32[]{:S(2)}) %copy-start.2) | copy-done | bytes 983064
  40.6 1.7 %collective-permute-start.1 = (f32[32,16,128]{2,1,0:T(8,128)}, f32[32,16,128]{2,1,0:T(8,128)}, u32[]{:S(2)}, u32[]{:S(2)}) collective-permute-start(f32[32,16,128]{2,1,0:T(8,128)} %get-tuple-element.19), channel_id=1, source_target_pairs={{0,16},{16,0},{1,17},{17,1},{2,18},{18,2},{3,19},{19,3},{4,20},{20... | collective-permute-start | bytes 786440 | tf_op jit(solution)/shard_map/ppermute | solution.py:336
  43.0 6.6 %collective-permute-done.1.refs_5_ = f32[32,16,128]{2,1,0:T(8,128)} collective-permute-done((f32[32,16,128]{2,1,0:T(8,128)}, f32[32,16,128]{2,1,0:T(8,128)}, u32[]{:S(2)}, u32[]{:S(2)}) %collective-permute-start.1) | collective-permute-done | bytes 262176 | tf_op jit(solution)/shard_map/ppermute | solution.py:336
  49.5 1.3 %copy-done.3 = bf16[10,256,192]{2,1,0:T(8,128)(2,1)S(1)} copy-done((bf16[10,256,192]{2,1,0:T(8,128)(2,1)S(1)}, bf16[10,256,192]{2,1,0:T(8,128)(2,1)}, u32[]{:S(2)}) %copy-start.3) | copy-done | bytes 983064
  50.8 5.3 %shard_map.104 = (f32[16,136,128]{2,1,0:T(8,128)S(1)}, f32[32,16,128]{2,1,0:T(8,128)S(1)}) custom-call(s32[2,32]{1,0:T(2,128)S(1)} %fusion.9.refs_0_, s32[1,32]{1,0:T(1,128)S(1)} %bitcast.48, s32[16,128]{1,0:T(8,128)S(1)} %dynamic-slice_bitcast_fusion.request_ref.refs_2_, s32[1,32]{1,0:T(1,128)S(1)} %get-tuple-element.35.tiles_ref.refs_3_, ...), custom_call_target="tpu_custom_call" | custom-call | flops 805306368 | bytes 4194304 | tf_op jit(solution)/shard_map/pallas_call | solution.py:526
  56.1 1.0 %copy-done.4 = f32[16,136,128]{2,1,0:T(8,128)} copy-done((f32[16,136,128]{2,1,0:T(8,128)}, f32[16,136,128]{2,1,0:T(8,128)S(1)}, u32[]{:S(2)}) %copy-start.4) | copy-done | bytes 1114136
  57.8 5.4 %all-to-all-start.2 = ((f32[16,136,128]{2,1,0:T(8,128)}), f32[16,136,128]{2,1,0:T(8,128)S(1)}, u32[]{:S(2)}, u32[]{:S(2)}) async-start(f32[16,136,128]{2,1,0:T(8,128)} %copy-done.4), calls=%async_computation.2 | async-start | bytes 2228224 | tf_op jit(solution)/shard_map/all_to_all | solution.py:444
  63.3 1.6 %collective-permute-start.3 = (f32[32,16,128]{2,1,0:T(8,128)S(1)}, f32[32,16,128]{2,1,0:T(8,128)S(1)}, u32[]{:S(2)}, u32[]{:S(2)}) collective-permute-start(f32[32,16,128]{2,1,0:T(8,128)S(1)} %copy-done.16), channel_id=1, source_target_pairs={{0,16},{16,0},{1,17},{17,1},{2,18},{18,2},{3,19},{19,3},{4,20},{20... | collective-permute-start | bytes 786440 | tf_op jit(solution)/shard_map/ppermute | solution.py:336
  65.8 21.5 %all-to-all-done.2.arrived_ref.refs_2_ = f32[16,136,128]{2,1,0:T(8,128)S(1)} async-done(((f32[16,136,128]{2,1,0:T(8,128)}), f32[16,136,128]{2,1,0:T(8,128)S(1)}, u32[]{:S(2)}, u32[]{:S(2)}) %all-to-all-start.2) | async-done | bytes 1114144 | tf_op jit(solution)/shard_map/all_to_all | solution.py:444
  87.3 1.6 %collective-permute-start.2 = (f32[4,128]{1,0:T(4,128)S(1)}, f32[4,128]{1,0:T(4,128)S(1)}, u32[]{:S(2)}, u32[]{:S(2)}) collective-permute-start(f32[4,128]{1,0:T(4,128)S(1)} %get-tuple-element.24), channel_id=1, source_target_pairs={{0,16},{16,0},{1,17},{17,1},{2,18},{18,2},{3,19},{19,3},{4,20},{20... | collective-permute-start | bytes 6152 | tf_op jit(solution)/shard_map/ppermute | solution.py:550
  88.9 1.4 %shard_map.106.second_ref = f32[32,16,128]{2,1,0:T(8,128)S(1)} custom-call(s32[2,32]{1,0:T(2,128)S(1)} %get-tuple-element.16.refs_0_, s32[1,32]{1,0:T(1,128)S(1)} %bitcast.49, f32[16,136,128]{2,1,0:T(8,128)S(1)} %all-to-all-done.2.arrived_ref.refs_2_, f32[32,16,128]{2,1,0:T(8,128)S(1)} %collective-permute-done.3.refs_3_, f32[32,16,128]{2,1,0:T(8,128)S(1)} %copy-done.5, ...), custom_call_target="tpu_custom_call" | custom-call | flops 402653184 | bytes 4194304 | tf_op jit(solution)/shard_map/pallas_call | solution.py:551
  91.0 1.0 %shard_map.107 = f32[32,16,128]{2,1,0:T(8,128)} custom-call(f32[4,128]{1,0:T(4,128)S(1)} %get-tuple-element.23.mine_ref, f32[4,128]{1,0:T(4,128)S(1)} %collective-permute-done.2.other_ref, f32[4,128]{1,0:T(4,128)S(1)} %reshape.170.scale_ref, f32[32,16,128]{2,1,0:T(8,128)S(1)} %shard_map.106.second_ref), custom_call_target="tpu_custom_call" | custom-call | tf_op jit(solution)/shard_map/pallas_call | solution.py:560
  (94 shorter events, 9.5 us)
Async XLA Ops:
  0.0 0.7 copy-start.8
  1.3 0.7 copy-start.12
  2.0 0.7 copy-start.13
  2.7 0.7 copy-start.14
  4.4 14.8 %all-to-all-start = ((s32[32,1,384]{2,1,0:T(1,128)}), s32[32,1,384]{2,1,0:T(1,128)S(1)}, u32[]{:S(2)}, u32[]{:S(2)}) async-start(s32[32,1,384]{2,1,0:T(1,128)} %get-tuple-element.17), calls=%async_computation | async-start | bytes 98304 | tf_op jit(solution)/shard_map/all_to_all | solution.py:386
  11.7 16.1 %collective-permute-start = (f32[32,16,128]{2,1,0:T(8,128)}, f32[32,16,128]{2,1,0:T(8,128)S(1)}, u32[]{:S(2)}, u32[]{:S(2)}) collective-permute-start(f32[32,16,128]{2,1,0:T(8,128)} %start_ref.1), channel_id=1, source_target_pairs={{0,8},{1,9},{2,10},{3,11},{4,12},{5,13},{6,14},{7,15},{8,0},{9,1},... | collective-permute-start | bytes 786440 | tf_op jit(solution)/shard_map/ppermute | solution.py:376
  19.8 7.9 %copy-start = (f32[8,128,128]{2,1,0:T(8,128)S(1)}, f32[8,128,128]{2,1,0:T(8,128)}, u32[]{:S(2)}) copy-start(f32[8,128,128]{2,1,0:T(8,128)} %refs_8_.3) | copy-start | bytes 1572868
  19.8 7.9 %copy-start.7 = (f32[32,16,128]{2,1,0:T(8,128)S(1)}, f32[32,16,128]{2,1,0:T(8,128)}, u32[]{:S(2)}) copy-start(f32[32,16,128]{2,1,0:T(8,128)} %start_ref.1) | copy-start | bytes 786436
  31.3 3.8 %copy-start.1 = (f32[8,128,128]{2,1,0:T(8,128)S(1)}, f32[8,128,128]{2,1,0:T(8,128)}, u32[]{:S(2)}) copy-start(f32[8,128,128]{2,1,0:T(8,128)} %refs_5_.1) | copy-start | bytes 1572868
  31.3 3.8 %copy-start.6 = (f32[8,128,128]{2,1,0:T(8,128)S(1)}, f32[8,128,128]{2,1,0:T(8,128)}, u32[]{:S(2)}) copy-start(f32[8,128,128]{2,1,0:T(8,128)} %refs_9_.1) | copy-start | bytes 1572868
  31.3 18.2 %all-to-all-start.1 = ((f32[8,256,128]{2,1,0:T(8,128)}), f32[8,256,128]{2,1,0:T(8,128)S(1)}, u32[]{:S(2)}, u32[]{:S(2)}) async-start(f32[8,256,128]{2,1,0:T(8,128)} %get-tuple-element.18), calls=%async_computation.1 | async-start | bytes 2097152 | tf_op jit(solution)/shard_map/all_to_all | solution.py:444
  35.1 14.4 %copy-start.5 = (f32[32,16,128]{2,1,0:T(8,128)S(1)}, f32[32,16,128]{2,1,0:T(8,128)}, u32[]{:S(2)}) copy-start(f32[32,16,128]{2,1,0:T(8,128)} %refs_4_.1) | copy-start | bytes 786436
  35.1 14.4 %copy-start.9 = (s32[32]{0:T(128)S(1)}, s32[32]{0:T(128)}, u32[]{:S(2)}) copy-start(s32[32]{0:T(128)} %param.17) | copy-start | bytes 388
  38.8 1.1 %copy-start.2 = (bf16[10,256,192]{2,1,0:T(8,128)(2,1)}, bf16[10,256,192]{2,1,0:T(8,128)(2,1)S(1)}, u32[]{:S(2)}) copy-start(bf16[10,256,192]{2,1,0:T(8,128)(2,1)S(1)} %get-tuple-element.21.refs_11_) | copy-start | bytes 2949124
  40.6 9.0 %collective-permute-start.1 = (f32[32,16,128]{2,1,0:T(8,128)}, f32[32,16,128]{2,1,0:T(8,128)}, u32[]{:S(2)}, u32[]{:S(2)}) collective-permute-start(f32[32,16,128]{2,1,0:T(8,128)} %get-tuple-element.19), channel_id=1, source_target_pairs={{0,16},{16,0},{1,17},{17,1},{2,18},{18,2},{3,19},{19,3},{4,20},{20... | collective-permute-start | bytes 786440 | tf_op jit(solution)/shard_map/ppermute | solution.py:336
  49.5 1.3 %copy-start.3 = (bf16[10,256,192]{2,1,0:T(8,128)(2,1)S(1)}, bf16[10,256,192]{2,1,0:T(8,128)(2,1)}, u32[]{:S(2)}) copy-start(bf16[10,256,192]{2,1,0:T(8,128)(2,1)} %copy-done.2) | copy-start | bytes 2949124
  56.1 1.0 %copy-start.4 = (f32[16,136,128]{2,1,0:T(8,128)}, f32[16,136,128]{2,1,0:T(8,128)S(1)}, u32[]{:S(2)}) copy-start(f32[16,136,128]{2,1,0:T(8,128)S(1)} %get-tuple-element.22) | copy-start | bytes 3342340
  57.1 0.7 copy-start.15
  57.8 5.4 %copy-start.16 = (f32[32,16,128]{2,1,0:T(8,128)S(1)}, f32[32,16,128]{2,1,0:T(8,128)}, u32[]{:S(2)}) copy-start(f32[32,16,128]{2,1,0:T(8,128)} %copy-done.15) | copy-start | bytes 786436
  57.8 7.2 %copy-start.17 = (s32[2,16,32]{2,1,0:T(8,128)S(1)}, s32[2,16,32]{2,1,0:T(8,128)}, u32[]{:S(2)}) copy-start(s32[2,16,32]{2,1,0:T(8,128)} %get-tuple-element.32) | copy-start | bytes 12292
  57.8 7.4 %copy-start.11 = (s32[32,1]{0,1:T(1,128)S(1)}, s32[32,1]{0,1:T(1,128)}, u32[]{:S(2)}) copy-start(s32[32,1]{0,1:T(1,128)} %param.21) | copy-start | bytes 388
  57.8 29.5 %all-to-all-start.2 = ((f32[16,136,128]{2,1,0:T(8,128)}), f32[16,136,128]{2,1,0:T(8,128)S(1)}, u32[]{:S(2)}, u32[]{:S(2)}) async-start(f32[16,136,128]{2,1,0:T(8,128)} %copy-done.4), calls=%async_computation.2 | async-start | bytes 2228224 | tf_op jit(solution)/shard_map/all_to_all | solution.py:444
  63.3 25.6 %collective-permute-start.3 = (f32[32,16,128]{2,1,0:T(8,128)S(1)}, f32[32,16,128]{2,1,0:T(8,128)S(1)}, u32[]{:S(2)}, u32[]{:S(2)}) collective-permute-start(f32[32,16,128]{2,1,0:T(8,128)S(1)} %copy-done.16), channel_id=1, source_target_pairs={{0,16},{16,0},{1,17},{17,1},{2,18},{18,2},{3,19},{19,3},{4,20},{20... | collective-permute-start | bytes 786440 | tf_op jit(solution)/shard_map/ppermute | solution.py:336
  87.3 3.6 %collective-permute-start.2 = (f32[4,128]{1,0:T(4,128)S(1)}, f32[4,128]{1,0:T(4,128)S(1)}, u32[]{:S(2)}, u32[]{:S(2)}) collective-permute-start(f32[4,128]{1,0:T(4,128)S(1)} %get-tuple-element.24), channel_id=1, source_target_pairs={{0,16},{16,0},{1,17},{17,1},{2,18},{18,2},{3,19},{19,3},{4,20},{20... | collective-permute-start | bytes 6152 | tf_op jit(solution)/shard_map/ppermute | solution.py:550
  (1 other events, 0.7 us)

commit v4 on v3

v4 whole, which is shorter than its diff:
```python
import functools

import jax
import jax.numpy as jnp
from jax import lax
from jax.experimental import pallas as pl
from jax.experimental.pallas import tpu as pltpu
from jax.sharding import PartitionSpec as P

AGG_DEV = 8
LANES = 128
DENSE_LIMIT = 1 << 19

VMEM = pl.BlockSpec(memory_space=pltpu.VMEM)
SMEM = pl.BlockSpec(memory_space=pltpu.SMEM)
HBM = pl.BlockSpec(memory_space=pltpu.HBM)
ANY = pl.BlockSpec(memory_space=pl.ANY)
HIGH = lax.Precision.HIGHEST


def params():
    return pltpu.CompilerParams(vmem_limit_bytes=24 * 1024 * 1024)


def call(kernel, out_shape, in_specs, out_specs, scratch=(), flops=0, moved=0):
    def shaped(shape, spec):
        return pltpu.HBM(shape.shape, shape.dtype) if spec is HBM else shape

    if isinstance(out_shape, (tuple, list)):
        out_shape = [shaped(*pair) for pair in zip(out_shape, out_specs)]
    else:
        out_shape = shaped(out_shape, out_specs)
    run = pl.pallas_call(
        kernel,
        out_shape=out_shape,
        in_specs=in_specs,
        out_specs=out_specs,
        scratch_shapes=list(scratch),
        compiler_params=params(),
        cost_estimate=pl.CostEstimate(flops=flops, bytes_accessed=moved, transcendentals=0),
    )

    def apply(*args):
        pinned = [
            pltpu.with_memory_space_constraint(arg, pltpu.HBM) if spec is HBM else arg
            for arg, spec in zip(args, in_specs)
        ]
        return run(*pinned)

    return apply


def below(value, bound):
    return value & (bound - 1) if bound & (bound - 1) == 0 else lax.rem(value, bound)


def over(value, bound):
    if bound & (bound - 1) == 0:
        return lax.shift_right_logical(value, bound.bit_length() - 1)
    return lax.div(value, bound)


def halves(value):
    high = value.astype(jnp.bfloat16)
    low = (value - high.astype(jnp.float32)).astype(jnp.bfloat16)
    return high, low


def left_operand(value):
    high, low = halves(value)
    return jnp.concatenate([high, low, high], axis=1)


def right_operand(value):
    high, low = halves(value)
    return jnp.concatenate([high, high, low], axis=1)


def dot_nt(left, right):
    return lax.dot_general(
        left, right, (((1,), (1,)), ((), ())), preferred_element_type=jnp.float32
    )


def table_products(value, table_ref, out_ref, done=None):
    left = left_operand(value)
    count, width = table_ref.shape[0], table_ref.shape[1]
    n_rhs = out_ref.shape[1]
    rows = left.shape[0] // n_rhs
    for first in range(0, count, 2):
        last = min(first + 2, count)
        right = right_operand(table_ref[first:last].reshape((last - first) * width, -1))
        product = dot_nt(left, right)
        for t in range(first, last):
            part = product[:, (t - first) * width : (t - first + 1) * width]
            out_ref[t * rows : (t + 1) * rows] = part.reshape(rows, n_rhs, width)
        if done is not None:
            done(first * rows, (last - first) * rows)


def started(copies):
    for copy in copies:
        copy.start()
    return copies


def finish(copies):
    for copy in copies:
        copy.wait()


def request_kernel(sizes, *refs):
    rows, n_rows, cap, n_tiles, n_diag = sizes
    inputs, payload_ref, held, sems = refs[:5], refs[5], refs[6:11], refs[11]
    finish(
        started([pltpu.make_async_copy(i, h, sems.at[n]) for n, (i, h) in enumerate(zip(inputs, held))])
    )
    owner_ref, local_ref, tile_ref, diag_ref, group_ref = held
    width_k = owner_ref.shape[0]
    half = n_rows // 2
    row_of = lax.broadcasted_iota(jnp.int32, (rows, rows), 0)
    col_of = lax.broadcasted_iota(jnp.int32, (rows, rows), 1)
    lane = lax.broadcasted_iota(jnp.int32, (rows, LANES), 1)
    owners = lax.broadcasted_iota(jnp.int32, (n_rows, rows), 0)

    def column(row):
        return jnp.sum(jnp.where(row_of == col_of, row, 0), axis=1, keepdims=True)

    def owner_row(k):
        return owner_ref[k : k + 1, :]

    row_ids = lax.broadcasted_iota(jnp.int32, (1, rows), 1)
    owner_columns = [column(owner_row(k)) for k in range(width_k)]
    lists = jnp.zeros((n_rows, LANES), jnp.float32)
    places, half_places = [], []
    for k in range(width_k):
        rank = jnp.zeros((1, rows), jnp.int32)
        for other in range(k + 1):
            match = owner_columns[other] == owner_row(k)
            if other == k:
                match = match & (row_of < col_of)
            rank = rank + jnp.sum(jnp.where(match, 1, 0), axis=0, keepdims=True)
        places.append(owner_row(k) * cap + rank)
        same = (owner_row(k) >= half) == (lax.axis_index("rows") >= half)
        holder = jnp.where(owner_row(k) >= half, owner_row(k) - half, owner_row(k))
        half_places.append(holder * (2 * cap) + rank + jnp.where(same, 0, cap))
        taker = row_ids + rows * (diag_ref[...] + n_diag)
        code = local_ref[k : k + 1, :] + rows * (tile_ref[k : k + 1, :] + n_tiles * taker)
        code, rank = column(code), column(rank)
        mirror = jnp.where(owner_row(k) >= half, owner_row(k) - half, owner_row(k) + half)
        for owner, base in ((owner_row(k), 0), (mirror, LANES // 2)):
            by_rank = jnp.where(lane == rank + base, code, 0).astype(jnp.float32)
            mine = jnp.where(owners == owner, 1.0, 0.0)
            lists = lists + jnp.dot(
                mine, by_rank, precision=HIGH, preferred_element_type=jnp.float32
            )
    lists = (lists + 0.5).astype(jnp.int32)
    common = [group_ref[...], diag_ref[...]]
    common += [tile_ref[k : k + 1, :] for k in range(width_k + 2)]
    common += [owner_row(k) * rows + local_ref[k : k + 1, :] for k in range(width_k)]
    common += half_places + places
    spare = payload_ref.shape[2] - LANES - len(common) * rows
    if spare:
        common.append(jnp.zeros((1, spare), jnp.int32))
    common = jnp.concatenate(common, axis=1)
    for device in range(n_rows):
        line = jnp.concatenate([lists[device : device + 1, :], common], axis=1)
        for band in range(payload_ref.shape[0] // n_rows):
            payload_ref[band * n_rows + device] = line


def metadata_copies(meta_ref, request_ref, near_ref, sems):
    n_rows, n_near = request_ref.shape[0], near_ref.shape[0]
    band, row = lax.axis_index("band"), lax.axis_index("rows")
    last = meta_ref.shape[0] // n_rows - 1
    if n_near == 1:
        nexts = [last - band]
    else:
        nexts = [jnp.minimum(band + 1, last), jnp.maximum(band - 1, 0)]
    copies = [
        pltpu.make_async_copy(meta_ref.at[pl.ds(band * n_rows, n_rows)], request_ref, sems.at[0])
    ]
    for n, other in enumerate(nexts):
        source = meta_ref.at[pl.ds(other * n_rows + row, 1)]
        copies.append(pltpu.make_async_copy(source, near_ref.at[pl.ds(n, 1)], sems.at[1 + n]))
    return copies


def band_field(rows, width_k, way, n_ways):
    field = LANES + (2 + width_k) * rows
    if n_ways == 1:
        return field + jnp.where(lax.axis_index("band") == 0, 0, rows)
    return field + way * rows


def pack_bands(sizes, width_k, product_ref, near_ref, band_refs):
    rows = sizes[0]
    for way, band_ref in enumerate(band_refs):
        field = band_field(rows, width_k, way, len(band_refs))
        for row in range(rows):
            band_ref[row] = product_ref[near_ref[way, 0, field + row] * rows + row]


def product_kernel(start_ref, mirror_ref, tile_ref, product_out, product_ref, sems):
    copies = []
    for side, ref in enumerate((start_ref, mirror_ref)):
        held = product_ref.at[side]

        def done(first, count):
            place = pl.ds(first, count)
            copy = pltpu.make_async_copy(
                held.at[place], product_out.at[side, place], sems.at[len(copies)]
            )
            copies.extend(started([copy]))

        rows, n_rhs, states = ref.shape
        table_products(ref[...].reshape(rows * n_rhs, states), tile_ref, held, done)
    finish(copies)


def first_kernel(sizes, width_k, n_band, *refs):
    rows, n_rows, cap, n_tiles, n_rhs = sizes
    product_ref, meta_ref, send_out = refs[:3]
    band_out, refs = refs[3 : 3 + n_band], refs[3 + n_band :]
    request_ref, near_ref, meta_sems, send_sems = refs
    finish(started(metadata_copies(meta_ref, request_ref, near_ref, meta_sems)))
    half = n_rows // 2
    base = jnp.where(lax.axis_index("rows") >= half, half, 0)
    for device in range(half):
        for slot in range(2 * cap):
            side, rank = slot // cap, slot % cap
            code = request_ref[base + device, 0, side * (LANES // 2) + rank]
            pltpu.make_async_copy(
                product_ref.at[side, below(code, rows * n_tiles)],
                send_out.at[device, slot],
                send_sems.at[0],
            ).start()
    for way, out in enumerate(band_out):
        field = band_field(rows, width_k, way, n_band)
        for row in range(rows):
            block = near_ref[way, 0, field + row] * rows + row
            pltpu.make_async_copy(
                product_ref.at[0, block], out.at[row], send_sems.at[1 + way]
            ).start()
    for n, out in enumerate((send_out, *band_out)):
        pltpu.make_async_copy(out, out, send_sems.at[n]).wait()


def place(place_ref, values, n_rhs):
    per_tile = LANES // n_rhs
    length = place_ref.shape[0] // per_tile
    parts, rest = [], values
    for _ in range(3):
        part = rest.astype(jnp.bfloat16)
        rest = rest - part.astype(jnp.float32)
        parts.append(part)
    parts = jnp.concatenate(parts, axis=1)
    lane = lax.broadcasted_iota(jnp.int32, (length, LANES), 1)
    result = jnp.zeros((length, LANES), jnp.float32)
    for spot in range(per_tile):
        chosen = jnp.dot(
            place_ref[spot * length : (spot + 1) * length, :],
            parts,
            preferred_element_type=jnp.float32,
        )
        chosen = chosen[:, :LANES] + chosen[:, LANES : 2 * LANES] + chosen[:, 2 * LANES :]
        result = jnp.where((lane >= spot * n_rhs) & (lane < (spot + 1) * n_rhs), chosen, result)
    return result


def one_hot(ids, row):
    return jnp.where(ids == row, 1.0, 0.0).astype(jnp.bfloat16)


def count_kernel(sizes, width_k, n_func, *refs):
    rows, n_rows, cap, n_tiles, n_rhs = sizes
    field_ref, list_ref, tile_ref, table_ref, inverse_ref = refs[:5]
    count_out, functional_out, placing_out, scale_ref = refs[5:9]
    count_ref, functional_ref, placing_ref, sems = refs[9:]
    n_groups, n_blocks = count_ref.shape[1:]
    slots, band_rows = n_rows * cap, n_rows * rows
    copies = []

    def send(source, target):
        copies.extend(started([pltpu.make_async_copy(source, target, sems.at[len(copies)])]))

    sums = jnp.sum(tile_ref[...], axis=1)
    line = lax.broadcasted_iota(jnp.int32, (n_func, sums.shape[1]), 0)
    sums = jnp.concatenate([sums, jnp.zeros((n_func - n_tiles, sums.shape[1]), jnp.float32)], axis=0)
    n_diag = inverse_ref.shape[0]
    totals = []
    for d in range(n_diag):
        minus = -jnp.sum(table_ref[d], axis=0, keepdims=True)
        totals.append(-jnp.sum(minus, axis=1, keepdims=True))
        wanted = jnp.where(line == n_tiles, minus, sums)
        high, low = halves(inverse_ref[d])
        right = jnp.concatenate([high, high, low], axis=0)
        solved = jnp.dot(left_operand(wanted), right, preferred_element_type=jnp.float32)
        solved = jnp.where(line == n_tiles + 1, 1.0, solved)
        functional_ref[d * n_func : (d + 1) * n_func, :] = left_operand(solved)
    send(functional_ref, functional_out)

    lists = list_ref[...]
    asker = lax.broadcasted_iota(jnp.int32, lists.shape, 0)
    codes = asker * rows + below(over(lists, rows * n_tiles), rows)
    codes = jnp.where(lists > 0, codes, -1).astype(jnp.float32)
    spread = lax.broadcasted_iota(jnp.int32, (slots, n_rows), 0)
    spread = lax.div(spread, cap) == lax.broadcasted_iota(jnp.int32, (slots, n_rows), 1)
    codes = jnp.dot(
        jnp.where(spread, 1.0, 0.0), codes, precision=HIGH, preferred_element_type=jnp.float32
    )
    rank = lax.rem(lax.broadcasted_iota(jnp.int32, codes.shape, 0), cap)
    lane = lax.broadcasted_iota(jnp.int32, codes.shape, 1)
    asked = jnp.sum(jnp.where(rank == lane, codes, 0.0), axis=1, keepdims=True)
    asked = jnp.where(asked < 0.0, asked - 0.5, asked + 0.5).astype(jnp.int32)
    own = lax.axis_index("rows") * rows + lax.broadcasted_iota(jnp.int32, (rows, 1), 0)
    band = lax.axis_index("band")

    def field(n, which):
        return field_ref[n, pl.ds(which, 1), :]

    row_ids = lax.broadcasted_iota(jnp.int32, (1, band_rows), 1)
    sides = []
    for which, targets in ((band, jnp.concatenate([asked, own], axis=0)), (1 - band, own)):
        across = jnp.where(which == 0, field(2 + width_k, 1), field(3 + width_k, 0))
        takers = [field(2 + k, which) * n_groups + field(0, which) for k in range(width_k)]
        takers.append(across * n_groups + field(0, 1 - which))
        takers = jnp.concatenate(takers, axis=1)
        origins = [field(4 + width_k + k, which) for k in range(width_k)] + [row_ids]
        hits = one_hot(targets, jnp.concatenate(origins, axis=1))
        sides.append((takers, hits, field(0, which)))
    for t in range(n_tiles):
        found = []
        for takers, hits, _ in sides:
            ids = lax.broadcasted_iota(jnp.int32, (n_groups, takers.shape[1]), 0) + t * n_groups
            found.append(dot_nt(one_hot(ids, takers), hits))
        count_ref[t] = jnp.concatenate(found, axis=1).astype(jnp.bfloat16)
        send(count_ref.at[t], count_out.at[t])
    ids = lax.broadcasted_iota(jnp.int32, (n_groups, band_rows), 0)
    found = [dot_nt(one_hot(ids, groups), hits[:, -band_rows:]) for _, hits, groups in sides]
    found = jnp.concatenate(found, axis=1)
    count_ref[n_tiles] = found.astype(jnp.bfloat16)
    send(count_ref.at[n_tiles], count_out.at[n_tiles])
    block = lax.broadcasted_iota(jnp.int32, found.shape, 1)
    mine = (block >= slots) & (block < slots + rows)
    count_ref[n_tiles + 1] = jnp.where(mine, found, 0.0).astype(jnp.bfloat16)
    send(count_ref.at[n_tiles + 1], count_out.at[n_tiles + 1])

    per_tile = LANES // n_rhs
    depth = rows // per_tile
    length = n_rows * 2 * depth
    order = lax.broadcasted_iota(jnp.int32, (per_tile * length, 1), 0)
    spot, order = lax.div(order, length), lax.rem(order, length)
    device, order = lax.div(order, 2 * depth), lax.rem(order, 2 * depth)
    side, order = lax.div(order, depth), lax.rem(order, depth)
    order = side * band_rows + device * rows + spot * depth + order
    member = [one_hot(ids, field(0, which)) for which in range(2)]
    placing = jnp.zeros(placing_ref.shape, jnp.float32)
    for which in range(2):
        placing = placing + dot_nt(one_hot(order, row_ids + which * band_rows), member[which])
    placing_ref[...] = placing.astype(jnp.bfloat16)
    send(placing_ref, placing_out)
    whole = jnp.zeros((n_groups, 1), jnp.float32)
    for which in range(2):
        sums = jnp.zeros((1, band_rows), jnp.float32)
        for d in range(n_diag):
            sums = jnp.where(field(1, which) == d, totals[d], sums)
        weighted = jnp.where(ids == field(0, which), sums, 0.0)
        whole = whole + jnp.sum(weighted, axis=1, keepdims=True)
    scale = place(placing_ref, jnp.broadcast_to(whole, (n_groups, LANES)), n_rhs)
    mine = jnp.zeros(scale_ref.shape, jnp.float32)
    here = lax.axis_index("rows") * 2 + band
    for n in range(2 * n_rows):
        mine = jnp.where(here == n, scale[n * depth : (n + 1) * depth, :], mine)
    scale_ref[...] = mine
    finish(copies)


def gather_solve(
    sizes, slots, diags, arrived_ref, later, terms, inverse_ref, sum_ref, product_ref
):
    rows, n_rows, cap, n_tiles, n_rhs = sizes
    per = n_rows * cap // arrived_ref.shape[0]
    for row in range(rows):
        total = None
        for slot in slots(row):
            start = pl.multiple_of(below(slot, per) * n_rhs, n_rhs)
            block = arrived_ref[over(slot, per), pl.ds(start, n_rhs), :]
            total = block if total is None else total + block
        sum_ref[pl.ds(row * n_rhs, n_rhs), :] = total
    finish(later)
    total = sum_ref[...]
    for term in terms:
        total = total + term[...].reshape(total.shape)
    table_products(total, inverse_ref, product_ref)
    for row in range(rows):
        sum_ref[pl.ds(row * n_rhs, n_rhs), :] = product_ref[diags(row) * rows + row]


def middle_kernel(sizes, width_k, n_band, dense, *refs):
    meta_ref, arrived_ref, inverse_ref, tile_ref = refs[:4]
    terms_in, refs = refs[4 : 5 + n_band], refs[5 + n_band :]
    extra, refs = (refs[:3], refs[3:]) if dense else ((), refs)
    send_out, band_out, refs = refs[0], refs[1 : 1 + n_band], refs[1 + n_band :]
    sum_ref, product_ref, request_ref, near_ref, send_ref = refs[:5]
    terms, band_refs, refs = refs[5 : 6 + n_band], refs[6 + n_band : 6 + 2 * n_band], refs[6 + 2 * n_band :]
    term_sems, meta_sems, send_sems, refs = *refs[:3], refs[3:]
    right_ref = terms[0]
    rows, n_rows, cap, n_tiles, n_rhs = sizes
    body = cap * n_rhs
    metadata = started(metadata_copies(meta_ref, request_ref, near_ref, meta_sems))
    pairs = enumerate(zip(terms_in, terms))
    later = started([pltpu.make_async_copy(i, h, term_sems.at[n]) for n, (i, h) in pairs])
    fetched = []
    if dense:
        held, extra_sems, value_ref, spread_ref = refs[:3], refs[3], refs[4], refs[5]
        n_diag = inverse_ref.shape[0]
        pairs = enumerate(zip(extra, held))
        fetched = started([pltpu.make_async_copy(i, h, extra_sems.at[n]) for n, (i, h) in pairs])
    finish(metadata)
    mine = lax.axis_index("rows")

    def slots(row):
        field = LANES + (4 + 2 * width_k) * rows + row
        return [request_ref[mine, 0, field + k * rows] for k in range(width_k)]

    def diags(row):
        return request_ref[mine, 0, LANES + rows + row]

    gather_solve(sizes, slots, diags, arrived_ref, later, terms, inverse_ref, sum_ref, product_ref)
    table_products(sum_ref[...], tile_ref, product_ref)
    copies = []

    def send(source, target):
        copies.extend(started([pltpu.make_async_copy(source, target, send_sems.at[len(copies)])]))

    for owner in range(n_rows):
        for rank in range(cap):
            block = product_ref[below(request_ref[owner, 0, rank], rows * n_tiles)]
            send_ref[owner, rank * n_rhs : (rank + 1) * n_rhs, :] = block
        if not dense:
            send(send_ref.at[owner], send_out.at[owner])
        else:
            send(send_ref.at[owner, pl.ds(0, body)], send_out.at[owner, pl.ds(0, body)])
    pack_bands(sizes, width_k, product_ref, near_ref, band_refs)
    for ref, out in zip(band_refs, band_out):
        send(ref, out)
    if dense:
        finish(fetched)
        kinds = []
        for owner in range(n_rows):
            for rank in range(cap):
                code = over(request_ref[owner, 0, rank], rows * n_tiles * rows)
                kinds.append(below(code, n_diag))
        kinds += [diags(row) for row in range(rows)]
        kinds += [near_ref[0, 0, LANES + rows + row] for row in range(rows)]
        result = coarse_parts(
            sizes, kinds, held, right_ref, send_ref, band_refs, value_ref, spread_ref
        )
        depth = result.shape[0] // n_rows
        for owner in range(n_rows):
            send_ref[owner, body:, :] = result[owner * depth : (owner + 1) * depth, :]
        send(send_ref.at[:, pl.ds(body, depth)], send_out.at[:, pl.ds(body, depth)])
    finish(copies)


def coarse_parts(sizes, kinds, held, right_ref, send_ref, band_refs, value_ref, spread_ref):
    functional_ref, count_ref, place_ref = held
    rows, n_rows, cap, n_tiles, n_rhs = sizes
    body = cap * n_rhs
    n_func = spread_ref.shape[0] // count_ref.shape[2]
    per_tile = LANES // n_rhs
    functional = functional_ref[...]
    done = 0
    for owner in range(0, n_rows, 2):
        values = [send_ref[owner + more, :body, :] for more in range(2)]
        values = jnp.concatenate(values, axis=0)
        value_ref[:, done : done + 2 * body] = dot_nt(functional, right_operand(values))
        done += 2 * body
    for ref in (right_ref, *band_refs):
        values = ref[...].reshape(rows * n_rhs, -1)
        value_ref[:, done : done + rows * n_rhs] = dot_nt(functional, right_operand(values))
        done += rows * n_rhs
    lane = lax.broadcasted_iota(jnp.int32, (n_func, LANES), 1)
    for block, kind in enumerate(kinds):
        tile, spot = block // per_tile, block % per_tile
        start = pl.multiple_of(kind * n_func, n_func)
        piece = value_ref[pl.ds(start, n_func), tile * LANES : (tile + 1) * LANES]
        piece = jnp.where((lane >= spot * n_rhs) & (lane < (spot + 1) * n_rhs), piece, 0.0)
        spread_ref[block * n_func : (block + 1) * n_func, :] = piece
    partial = jnp.zeros((count_ref.shape[1], 2 * LANES), jnp.float32)
    for t in range(count_ref.shape[0]):
        values = spread_ref[pl.ds(t, done // n_rhs, stride=n_func), :]
        partial = partial + jnp.dot(
            count_ref[t],
            jnp.concatenate(halves(values), axis=1),
            preferred_element_type=jnp.float32,
        )
    partial = partial[:, :LANES] + partial[:, LANES:]
    source = lax.broadcasted_iota(jnp.int32, (LANES, LANES), 0)
    target = lax.broadcasted_iota(jnp.int32, (LANES, LANES), 1)
    same = jnp.where(lax.rem(source, n_rhs) == lax.rem(target, n_rhs), 1.0, 0.0)
    same = same.astype(jnp.bfloat16)
    same = jnp.concatenate([same, same], axis=0)
    partial = jnp.dot(
        jnp.concatenate(halves(partial), axis=1), same, preferred_element_type=jnp.float32
    )
    return place(place_ref, partial, n_rhs)


def part_kernel(arrived_ref, mine_ref, other_ref):
    depth = mine_ref.shape[0]
    body = arrived_ref.shape[1] - 2 * depth
    total = arrived_ref[0, body:, :]
    for source in range(1, arrived_ref.shape[0]):
        total = total + arrived_ref[source, body:, :]
    upper = lax.axis_index("band") == 0
    mine_ref[...] = jnp.where(upper, total[:depth], total[depth:])
    other_ref[...] = jnp.where(upper, total[depth:], total[:depth])


def last_kernel(sizes, width_k, n_band, *refs):
    meta_ref, arrived_ref, inverse_ref = refs[:3]
    terms_in, refs = refs[3 : 4 + n_band], refs[4 + n_band :]
    second_ref, sum_ref, product_ref, mine_ref = refs[:4]
    terms, (term_sems, meta_sem) = refs[4 : 5 + n_band], refs[5 + n_band :]
    rows, n_rows = sizes[:2]
    place = lax.axis_index("band") * n_rows + lax.axis_index("rows")
    metadata = pltpu.make_async_copy(meta_ref.at[pl.ds(place, 1)], mine_ref, meta_sem)
    metadata.start()
    pairs = enumerate(zip(terms_in, terms))
    later = started([pltpu.make_async_copy(i, h, term_sems.at[n]) for n, (i, h) in pairs])
    metadata.wait()

    def slots(row):
        field = LANES + (4 + 3 * width_k) * rows + row
        return [mine_ref[0, 0, field + k * rows] for k in range(width_k)]

    def diags(row):
        return mine_ref[0, 0, LANES + rows + row]

    gather_solve(sizes, slots, diags, arrived_ref, later, terms, inverse_ref, sum_ref, product_ref)
    second_ref[...] = sum_ref[...].reshape(second_ref.shape)


def final_kernel(sizes, mine_ref, other_ref, scale_ref, second_ref, out_ref):
    rows, n_rhs = sizes[0], sizes[4]
    depth = scale_ref.shape[0]
    correction = (mine_ref[...] + other_ref[...]) / scale_ref[...]
    padded = jnp.concatenate([correction, jnp.zeros((8 - depth, LANES), jnp.float32)], axis=0)
    turned = padded.T
    for row in range(rows):
        spot, place = row // depth, row % depth
        column = turned[spot * n_rhs : (spot + 1) * n_rhs, place : place + 1]
        out_ref[row] = second_ref[row] + column


def shifted(value, axis, steps):
    count = lax.axis_size(axis)
    initial, last = (max(0, -steps), min(count, count - steps))
    return lax.ppermute(value, axis, [(source, source + steps) for source in range(initial, last)])


def to_bands(sends):
    if len(sends) == 1:
        return (lax.ppermute(sends[0], "band", [(0, 1), (1, 0)]),)
    return shifted(sends[0], "band", 1), shifted(sends[1], "band", -1)


def on_device(
    start_iterate,
    right_side,
    diag_table,
    inverse_table,
    coupling_tiles,
    diag_index,
    tile_index,
    source_owner,
    source_local,
    aggregate_map,
):
    rows, n_rhs, states = start_iterate.shape
    width_k = source_owner.shape[1]
    n_tiles, n_diag = coupling_tiles.shape[0], inverse_table.shape[0]
    n_rows, n_bands = lax.axis_size("rows"), lax.axis_size("band")
    n_dev = n_rows * n_bands
    cap = max(2, 2 * width_k * rows // n_rows)
    slots = n_rows * cap
    total_groups = AGG_DEV * n_dev
    per_tile = LANES // n_rhs
    depth = rows // per_tile
    n_func = 16
    dense = (
        n_bands == 2
        and n_dev * rows * total_groups <= DENSE_LIMIT
        and depth == 4
        and n_diag * n_func == LANES
        and n_tiles + 2 <= n_func
    )
    sizes = (rows, n_rows, cap, n_tiles, n_rhs)
    f32, i32 = jnp.float32, jnp.int32
    my_band = lax.axis_index("band")
    my_row = lax.axis_index("rows")

    half = n_rows // 2
    mirror = lax.ppermute(start_iterate, "rows", [(i, (i + half) % n_rows) for i in range(n_rows)])
    wide = LANES + -(-(4 + 4 * width_k) * rows // LANES) * LANES
    index_shapes = [(width_k, rows), (width_k, rows), (width_k + 2, rows), (1, rows), (1, rows)]
    payload = call(
        functools.partial(request_kernel, (rows, n_rows, cap, n_tiles, n_diag)),
        jax.ShapeDtypeStruct((n_dev, 1, wide), i32),
        [HBM] * 5,
        VMEM,
        [*[pltpu.VMEM(shape, i32) for shape in index_shapes], pltpu.SemaphoreType.DMA((5,))],
    )(source_owner.T, source_local.T, tile_index.T, diag_index[None], aggregate_map.T)
    meta = lax.all_to_all(payload, ("band", "rows"), split_axis=0, concat_axis=0, tiled=True)

    n_ways = 1 if n_bands == 2 else 2
    block = (rows, n_rhs, states)
    band_shapes = [jax.ShapeDtypeStruct(block, f32)] * n_ways
    band_scratch = [pltpu.VMEM(block, f32)] * n_ways
    term_scratch = [pltpu.VMEM(block, f32)] * (1 + n_ways)
    term_sems = pltpu.SemaphoreType.DMA((1 + n_ways,))
    meta_scratch = [pltpu.SMEM((n_rows, 1, wide), i32), pltpu.SMEM((n_ways, 1, wide), i32)]
    meta_sems = pltpu.SemaphoreType.DMA((1 + n_ways,))
    flat = rows * n_rhs
    sums = pltpu.VMEM((flat, states), f32)
    products = pltpu.VMEM((max(n_tiles, n_diag) * rows, n_rhs, states), f32)
    work = 6 * flat * states * states
    made_shape = (2, n_tiles * rows, n_rhs, states)
    made = call(
        product_kernel,
        jax.ShapeDtypeStruct(made_shape, f32),
        [VMEM] * 3,
        HBM,
        [pltpu.VMEM(made_shape, f32), pltpu.SemaphoreType.DMA((2 * n_tiles,))],
        2 * work * n_tiles,
        4 << 20,
    )(start_iterate, mirror, coupling_tiles)
    packed, *bands = call(
        functools.partial(first_kernel, sizes, width_k, n_ways),
        (jax.ShapeDtypeStruct((half, 2 * cap, n_rhs, states), f32), *band_shapes),
        [HBM, ANY],
        [HBM] * (1 + n_ways),
        [*meta_scratch, meta_sems, pltpu.SemaphoreType.DMA((1 + n_ways,))],
        0,
        4 << 20,
    )(made, meta)
    sends = (packed.reshape(half, 2 * cap * n_rhs, states), *bands)
    halves_of_rows = [list(range(half)), list(range(half, n_rows))]
    late, *sends = lax.optimization_barrier((meta, *sends))

    def exchange(sends, groups=None):
        arrived = lax.all_to_all(
            sends[0], "rows", split_axis=0, concat_axis=0, tiled=True, axis_index_groups=groups
        )
        return arrived, to_bands(sends[1:])

    arrived_blocks, arrived_bands = exchange(sends, halves_of_rows)

    late = late.reshape(n_bands, n_rows, wide)
    requests = lax.dynamic_index_in_dim(late[:, :, :LANES], my_band, 0, keepdims=False)
    common = late[:, :, LANES:]
    extra, extra_scratch, tail = (), [], 0
    if dense:
        fields = common[:, :, : (4 + 2 * width_k) * rows].reshape(n_bands, n_rows, -1, rows).transpose(2, 0, 1, 3)
        fields = fields.reshape(-1, n_bands, n_rows * rows)
        n_blocks = slots + 2 * rows
        length = n_dev * depth
        extra_shapes = [
            ((n_diag * n_func, 3 * states), jnp.bfloat16),
            ((n_tiles + 2, total_groups, n_blocks), jnp.bfloat16),
            ((per_tile * length, total_groups), jnp.bfloat16),
        ]
        functional_shape, count_shape, placing_shape = extra_shapes
        counts, functionals, placing, scale = call(
            functools.partial(count_kernel, sizes, width_k, n_func),
            (
                jax.ShapeDtypeStruct(*count_shape),
                jax.ShapeDtypeStruct(*functional_shape),
                jax.ShapeDtypeStruct(*placing_shape),
                jax.ShapeDtypeStruct((depth, LANES), f32),
            ),
            [VMEM] * 5,
            [HBM, HBM, HBM, VMEM],
            [
                pltpu.VMEM(*count_shape),
                pltpu.VMEM(*functional_shape),
                pltpu.VMEM(*placing_shape),
                pltpu.SemaphoreType.DMA((n_tiles + 4,)),
            ],
            4 * total_groups * n_tiles * n_dev * rows * n_blocks,
            4 << 20,
        )(fields, requests, coupling_tiles, diag_table, inverse_table)
        extra = (functionals, counts, placing)
        extra_scratch = [
            *[pltpu.VMEM(*shape) for shape in extra_shapes],
            pltpu.SemaphoreType.DMA((3,)),
            pltpu.VMEM((n_diag * n_func, n_blocks * n_rhs), f32),
            pltpu.VMEM((n_blocks * n_func, LANES), f32),
        ]
        tail = n_bands * depth

    send_shape = (n_rows, cap * n_rhs + tail, states)
    sends = call(
        functools.partial(middle_kernel, sizes, width_k, n_ways, dense),
        (jax.ShapeDtypeStruct(send_shape, f32), *band_shapes),
        [HBM] + [VMEM] * 3 + [HBM] + [ANY] * n_ways + [HBM] * len(extra),
        [HBM] * (1 + n_ways),
        [
            sums,
            products,
            *meta_scratch,
            pltpu.VMEM(send_shape, f32),
            *term_scratch,
            *band_scratch,
            term_sems,
            meta_sems,
            pltpu.SemaphoreType.DMA((n_rows + n_ways + 1,)),
            *extra_scratch,
        ],
        work * (n_tiles + n_diag),
        4 << 20,
    )(
        meta,
        arrived_blocks,
        inverse_table,
        coupling_tiles,
        right_side,
        *arrived_bands,
        *extra,
    )
    arrived_blocks, arrived_bands = exchange(sends)

    if dense:
        part = jax.ShapeDtypeStruct((depth, LANES), f32)
        mine, other = call(part_kernel, (part, part), [VMEM], [VMEM] * 2)(arrived_blocks)
        other = lax.ppermute(other, "band", [(0, 1), (1, 0)])
    second = call(
        functools.partial(last_kernel, sizes, width_k, n_ways),
        jax.ShapeDtypeStruct(block, f32),
        [HBM] + [VMEM] * 2 + [HBM] + [ANY] * n_ways,
        VMEM,
        [
            sums,
            products,
            pltpu.SMEM((1, 1, wide), i32),
            *term_scratch,
            term_sems,
            pltpu.SemaphoreType.DMA,
        ],
        work * n_diag,
        4 << 20,
    )(meta, arrived_blocks, inverse_table, right_side, *arrived_bands)
    if dense:
        return call(
            functools.partial(final_kernel, sizes),
            jax.ShapeDtypeStruct(block, f32),
            [VMEM] * 4,
            VMEM,
        )(mine, other, scale, second)

    groups = aggregate_map[:, 0]
    own = jnp.arange(rows, dtype=i32)
    groups_all = common[:, :, :rows]
    diags_all = common[:, :, rows : 2 * rows]
    codes = requests[:, :cap]
    asked = lax.broadcasted_iota(i32, codes.shape, 0) * rows + codes // (rows * n_tiles) % rows
    asked = jnp.where(codes > 0, asked, -1).reshape(-1)
    table_sums = jnp.sum(diag_table, axis=(1, 2))
    diag_onehot = diags_all.reshape(-1, 1) == jnp.arange(n_diag, dtype=i32)[None]
    block_sums = jnp.sum(jnp.where(diag_onehot, table_sums[None], 0.0), axis=1)
    whole_diag = jnp.sum(
        jnp.where(groups[:, None] == groups_all.reshape(-1)[None], block_sums[None], 0.0), axis=1
    )
    here = lax.dynamic_index_in_dim(common, my_row, 1, keepdims=False)
    above = lax.dynamic_index_in_dim(here, jnp.minimum(my_band + 1, n_bands - 1), 0, keepdims=False)
    below = lax.dynamic_index_in_dim(here, jnp.maximum(my_band - 1, 0), 0, keepdims=False)
    place_of = (2 + width_k) * rows
    band_tiles = jnp.stack([above[place_of : place_of + rows], below[place_of + rows : place_of + 2 * rows]])
    band_groups = jnp.stack([above[:rows], below[:rows]])
    band_valid = jnp.stack([my_band + 1 < n_bands, my_band > 0])
    band_valid = jnp.broadcast_to(band_valid[:, None], (2, rows))
    n_all = n_tiles + n_diag + 1
    code = codes.reshape(-1)
    band_of_mine = lax.dynamic_index_in_dim(groups_all, my_band, 0, keepdims=False).reshape(-1)
    entry_group = jnp.concatenate(
        [jnp.take(band_of_mine, jnp.maximum(asked, 0)), band_groups.reshape(-1), groups, groups]
    )
    entry_func = jnp.concatenate(
        [
            (code % rows) * n_all + (code // rows) % n_tiles,
            (own[None] * n_all + band_tiles).reshape(-1),
            own * n_all + n_tiles + diag_index,
            own * n_all + n_tiles + n_diag,
        ]
    )
    entry_valid = jnp.concatenate([asked >= 0, band_valid.reshape(-1), jnp.ones((2 * rows,), bool)])
    functionals = jnp.concatenate(
        [jnp.sum(coupling_tiles, axis=1), -jnp.sum(diag_table, axis=1)], axis=0
    )
    weights = jnp.einsum("fp,rcp->rfc", functionals, second, precision=HIGH)
    weights = jnp.concatenate([weights, jnp.sum(right_side, axis=2)[:, None]], axis=1)
    chosen = jnp.take(weights.reshape(rows * n_all, n_rhs), entry_func, axis=0)
    chosen = jnp.where(entry_valid[:, None], chosen, 0.0)
    partial = jax.ops.segment_sum(chosen, entry_group, num_segments=total_groups)
    whole = lax.psum(partial, ("band", "rows"))
    correction = jnp.take(whole, groups, axis=0) / whole_diag[:, None]
    return second + correction[:, :, None]


def solution(mesh):
    in_specs = (
        P(("band", "rows"), None, None),
        P(("band", "rows"), None, None),
        P(),
        P(),
        P(),
        P(("band", "rows")),
        P(("band", "rows"), None),
        P(("band", "rows"), None),
        P(("band", "rows"), None),
        P(("band", "rows"), None),
    )
    out_specs = P(("band", "rows"), None, None)
    return jax.shard_map(
        on_device, mesh=mesh, in_specs=in_specs, out_specs=out_specs, check_vma=False
    )
```

time: 93.7 us -> 124 us (1.32)
  Pallas kernels: 15.8 us -> 61.6 us
  local copies, waits for them, and re-layouts: 14.2 us -> 2.27 us
  starting transfers between devices: 23.9 us -> 21.4 us
  other arithmetic: 1.91 us -> 0 us
    pallas_call x8, Pallas kernels: 15.8 us -> 61.6 us  [apply(): return run(*pinned)]
    all_to_all x2, waiting for transfers between devices: 21.5 us -> 27.8 us  [exchange(): lax.all_to_all(sends[0], 'rows', split_axis=0, concat_axis=0, tiled=True,...]
    ppermute x2, waiting for transfers between devices: 6.56 us -> 1 us  [to_bands(): return (lax.ppermute(sends[0], 'band', [(0, 1), (1, 0)]),)]
    unnamed x38 -> x17, local copies, waits for them, and re-layouts: 7.59 us -> 2.03 us
    ppermute x1, waiting for transfers between devices: 3.08 us -> 7.58 us  [on_device(): lax.ppermute(start_iterate, 'rows', [(i, (i + half) % n_rows) for i in ra...]
    gather x3 -> x0, local copies, waits for them, and re-layouts: 3.94 us -> none  [the longest x1 1.61 us: on_device(): jnp.take(pick(by_group, near)[0], targets)]
    all_to_all x1, waiting for transfers between devices: 3.78 us -> 0.01 us  [on_device(): lax.all_to_all(payload, ('band', 'rows'), split_axis=0, concat_axis=0, ti...]
    all_to_all x1, starting transfers between devices: 7.3 us -> 3.83 us  [on_device(): lax.all_to_all(payload, ('band', 'rows'), split_axis=0, concat_axis=0, ti...]
  transfers between devices with their start and end apart: 7 -> 7, of which waited for: 5 -> 5; matrix products, arithmetic and copies ran while one was open for 9% -> 0% of each run, Pallas kernels for 6% -> 10%
where the time goes in v4:
time: 124 us; the launch traced here: 122 us
  Pallas kernels  61.6 us (50%)
  waiting for transfers between devices  36.7 us (30%)
  starting transfers between devices  21.4 us (17%)
  local copies, waits for them, and re-layouts  2.27 us (2%)
    pallas_call x8, Pallas kernels, apply(): return run(*pinned)  61.6 us
    all_to_all x2, waiting for transfers between devices, exchange(): lax.all_to_all(sends[0], 'rows', split_axis=0, concat_axis=0, tiled=True,...  27.8 us
    all_to_all x2, starting transfers between devices, exchange(): lax.all_to_all(sends[0], 'rows', split_axis=0, concat_axis=0, tiled=True,...  8.66 us
    ppermute x1, waiting for transfers between devices, on_device(): lax.ppermute(start_iterate, 'rows', [(i, (i + half) % n_rows) for i in ra...  7.58 us
    ppermute x1, starting transfers between devices, on_device(): lax.ppermute(start_iterate, 'rows', [(i, (i + half) % n_rows) for i in ra...  4.04 us
    all_to_all x1, starting transfers between devices, on_device(): lax.all_to_all(payload, ('band', 'rows'), split_axis=0, concat_axis=0, ti...  3.83 us
    ppermute x2, starting transfers between devices, to_bands(): return (lax.ppermute(sends[0], 'band', [(0, 1), (1, 0)]),)  3.24 us
  transfers between devices with their start and end apart: 7, of which 5 were waited for; matrix products, arithmetic and copies ran while one was open for 0% of the time, Pallas kernels for 10%

profile of v4, /device:TPU:0, one launch (start us, length us, event | category | flops | bytes accessed | tf_op | source)
XLA Modules:
  0.0 122.2 jit_solution(1823779450901852608)
XLA Ops:
  0.0 4.0 %collective-permute-start = (f32[32,16,128]{2,1,0:T(8,128)}, f32[32,16,128]{2,1,0:T(8,128)S(1)}, u32[]{:S(2)}, u32[]{:S(2)}) collective-permute-start(f32[32,16,128]{2,1,0:T(8,128)} %start_ref.1), channel_id=1, source_target_pairs={{0,8},{1,9},{2,10},{3,11},{4,12},{5,13},{6,14},{7,15},{8,0},{9,1},... | collective-permute-start | bytes 786440 | tf_op jit(solution)/shard_map/ppermute | solution.py:606
  4.0 1.8 %shard_map.100 = s32[32,1,512]{2,1,0:T(1,128)} custom-call(s32[2,32]{1,0:T(2,128)} %bitcast.19, s32[2,32]{1,0:T(2,128)} %bitcast.20, s32[4,32]{1,0:T(4,128)} %bitcast.18, s32[1,32]{1,0:T(1,128)} %bitcast.21, s32[1,32]{1,0:T(1,128)} %bitcast.22), custom_call_target="tpu_custom_call" | custom-call | tf_op jit(solution)/shard_map/pallas_call | solution.py:48
  5.8 3.8 %all-to-all-start = ((s32[32,1,512]{2,1,0:T(1,128)}), s32[32,1,512]{2,1,0:T(1,128)S(1)}, u32[]{:S(2)}, u32[]{:S(2)}) async-start(s32[32,1,512]{2,1,0:T(1,128)} %shard_map.100), calls=%async_computation | async-start | bytes 131072 | tf_op jit(solution)/shard_map/all_to_all | solution.py:616
  9.7 7.6 %collective-permute-done.mirror_ref = f32[32,16,128]{2,1,0:T(8,128)S(1)} collective-permute-done((f32[32,16,128]{2,1,0:T(8,128)}, f32[32,16,128]{2,1,0:T(8,128)S(1)}, u32[]{:S(2)}, u32[]{:S(2)}) %collective-permute-start) | collective-permute-done | bytes 262176 | tf_op jit(solution)/shard_map/ppermute | solution.py:606
  17.3 1.0 copy-done
  18.3 0.9 copy-done.4
  19.3 2.6 %shard_map.101.refs_0_ = f32[2,256,16,128]{3,2,1,0:T(8,128)} custom-call(f32[32,16,128]{2,1,0:T(8,128)S(1)} %copy-done.4, f32[32,16,128]{2,1,0:T(8,128)S(1)} %collective-permute-done.mirror_ref, f32[8,128,128]{2,1,0:T(8,128)S(1)} %copy-done), custom_call_target="tpu_custom_call" | custom-call | flops 805306368 | bytes 4194304 | tf_op jit(solution)/shard_map/pallas_call | solution.py:48
  21.8 42.0 %shard_map.102 = (f32[8,16,16,128]{3,2,1,0:T(8,128)}, f32[32,16,128]{2,1,0:T(8,128)}) custom-call(f32[2,256,16,128]{3,2,1,0:T(8,128)} %shard_map.101.refs_0_, s32[32,1,512]{2,1,0:T(1,128)S(1)} %all-to-all-done.refs_1_.refs_0_), custom_call_target="tpu_custom_call" | custom-call | bytes 4194304 | tf_op jit(solution)/shard_map/pallas_call | solution.py:48
  63.9 0.0 copy-start.6
  63.9 3.7 %all-to-all-start.1 = ((f32[8,256,128]{2,1,0:T(8,128)}), f32[8,256,128]{2,1,0:T(8,128)S(1)}, u32[]{:S(2)}, u32[]{:S(2)}) async-start(f32[8,256,128]{2,1,0:T(8,128)} %bitcast.14), calls=%async_computation.1 | async-start | bytes 2097152 | tf_op jit(solution)/shard_map/all_to_all | solution.py:654
  67.7 0.1 reshape.14
  67.8 0.1 reshape.15.refs_0_
  67.9 1.7 %collective-permute-start.1 = (f32[32,16,128]{2,1,0:T(8,128)S(1)}, f32[32,16,128]{2,1,0:T(8,128)S(1)}, u32[]{:S(2)}, u32[]{:S(2)}) collective-permute-start(f32[32,16,128]{2,1,0:T(8,128)S(1)} %copy-done.6), channel_id=1, source_target_pairs={{0,16},{16,0},{1,17},{17,1},{2,18},{18,2},{3,19},{19,3},{4,20},{20... | collective-permute-start | bytes 786440 | tf_op jit(solution)/shard_map/ppermute | solution.py:566
  69.6 6.0 %shard_map.103 = (bf16[10,256,192]{2,1,0:T(8,128)(2,1)}, bf16[128,384]{1,0:T(8,128)(2,1)}, bf16[1024,256]{1,0:T(8,128)(2,1)}, f32[4,128]{1,0:T(4,128)S(1)}) custom-call(s32[8,2,512]{2,1,0:T(2,128)S(1)} %reshape.15.refs_0_, s32[16,128]{1,0:T(8,128)S(1)} %dynamic-slice_bitcast_fusion.refs_1_, f32[8,128,128]{2,1,0:T(8,128)S(1)} %copy-done.1, ...), custom_call_target="tpu_custom_call" | custom-call | flops 1610612736 | bytes 4194304 | tf_op jit(solution)/shard_map/pallas_call | solution.py:48
  75.6 1.0 collective-permute-done.1.refs_5_
  76.6 5.4 %all-to-all-done.1.refs_1_ = f32[8,256,128]{2,1,0:T(8,128)S(1)} async-done(((f32[8,256,128]{2,1,0:T(8,128)}), f32[8,256,128]{2,1,0:T(8,128)S(1)}, u32[]{:S(2)}, u32[]{:S(2)}) %all-to-all-start.1) | async-done | bytes 1048608 | tf_op jit(solution)/shard_map/all_to_all | solution.py:654
  82.0 6.6 %shard_map.104 = (f32[16,136,128]{2,1,0:T(8,128)}, f32[32,16,128]{2,1,0:T(8,128)}) custom-call(s32[32,1,512]{2,1,0:T(1,128)} %copy-done.3, f32[8,256,128]{2,1,0:T(8,128)S(1)} %all-to-all-done.1.refs_1_, f32[8,128,128]{2,1,0:T(8,128)S(1)} %copy-done.2, f32[8,128,128]{2,1,0:T(8,128)S(1)} %copy-done.1, f32[32,16,128]{2,1,0:T(8,128)} %refs_3_.5, ...), custom_call_target="tpu_custom_call" | custom-call | flops 805306368 | bytes 4194304 | tf_op jit(solution)/shard_map/pallas_call | solution.py:48
  88.6 5.0 %all-to-all-start.2 = ((f32[16,136,128]{2,1,0:T(8,128)}), f32[16,136,128]{2,1,0:T(8,128)S(1)}, u32[]{:S(2)}, u32[]{:S(2)}) async-start(f32[16,136,128]{2,1,0:T(8,128)} %get-tuple-element.26), calls=%async_computation.2 | async-start | bytes 2228224 | tf_op jit(solution)/shard_map/all_to_all | solution.py:654
  93.6 1.6 %collective-permute-start.3 = (f32[32,16,128]{2,1,0:T(8,128)S(1)}, f32[32,16,128]{2,1,0:T(8,128)S(1)}, u32[]{:S(2)}, u32[]{:S(2)}) collective-permute-start(f32[32,16,128]{2,1,0:T(8,128)S(1)} %copy-done.7), channel_id=1, source_target_pairs={{0,16},{16,0},{1,17},{17,1},{2,18},{18,2},{3,19},{19,3},{4,20},{20... | collective-permute-start | bytes 786440 | tf_op jit(solution)/shard_map/ppermute | solution.py:566
  95.1 22.4 %all-to-all-done.2.arrived_ref.refs_1_ = f32[16,136,128]{2,1,0:T(8,128)S(1)} async-done(((f32[16,136,128]{2,1,0:T(8,128)}), f32[16,136,128]{2,1,0:T(8,128)S(1)}, u32[]{:S(2)}, u32[]{:S(2)}) %all-to-all-start.2) | async-done | bytes 1114144 | tf_op jit(solution)/shard_map/all_to_all | solution.py:654
  117.6 1.6 %collective-permute-start.2 = (f32[4,128]{1,0:T(4,128)S(1)}, f32[4,128]{1,0:T(4,128)S(1)}, u32[]{:S(2)}, u32[]{:S(2)}) collective-permute-start(f32[4,128]{1,0:T(4,128)S(1)} %get-tuple-element.28), channel_id=1, source_target_pairs={{0,16},{16,0},{1,17},{17,1},{2,18},{18,2},{3,19},{19,3},{4,20},{20... | collective-permute-start | bytes 6152 | tf_op jit(solution)/shard_map/ppermute | solution.py:738
  119.2 1.7 %shard_map.106.second_ref = f32[32,16,128]{2,1,0:T(8,128)S(1)} custom-call(s32[32,1,512]{2,1,0:T(1,128)} %copy-done.3, f32[16,136,128]{2,1,0:T(8,128)S(1)} %all-to-all-done.2.arrived_ref.refs_1_, f32[8,128,128]{2,1,0:T(8,128)S(1)} %copy-done.2, f32[32,16,128]{2,1,0:T(8,128)} %refs_3_.5, f32[32,16,128]{2,1,0:T(8,128)S(1)} %collective-permute-done.3.refs_4_), custom_call_target="tpu_custom_call" | custom-call | flops 402653184 | bytes 4194304 | tf_op jit(solution)/shard_map/pallas_call | solution.py:48
  120.9 0.3 collective-permute-done.2.other_ref
  121.2 1.0 shard_map.107
  (21 shorter events, 0.1 us)
Async XLA Ops:
  0.0 17.3 %collective-permute-start = (f32[32,16,128]{2,1,0:T(8,128)}, f32[32,16,128]{2,1,0:T(8,128)S(1)}, u32[]{:S(2)}, u32[]{:S(2)}) collective-permute-start(f32[32,16,128]{2,1,0:T(8,128)} %start_ref.1), channel_id=1, source_target_pairs={{0,8},{1,9},{2,10},{3,11},{4,12},{5,13},{6,14},{7,15},{8,0},{9,1},... | collective-permute-start | bytes 786440 | tf_op jit(solution)/shard_map/ppermute | solution.py:606
  5.8 16.0 %all-to-all-start = ((s32[32,1,512]{2,1,0:T(1,128)}), s32[32,1,512]{2,1,0:T(1,128)S(1)}, u32[]{:S(2)}, u32[]{:S(2)}) async-start(s32[32,1,512]{2,1,0:T(1,128)} %shard_map.100), calls=%async_computation | async-start | bytes 131072 | tf_op jit(solution)/shard_map/all_to_all | solution.py:616
  17.3 1.0 copy-start
  18.3 0.9 copy-start.4
  21.8 45.8 %copy-start.3 = (s32[32,1,512]{2,1,0:T(1,128)}, s32[32,1,512]{2,1,0:T(1,128)S(1)}, u32[]{:S(2)}) copy-start(s32[32,1,512]{2,1,0:T(1,128)S(1)} %all-to-all-done.refs_1_.refs_0_) | copy-start | bytes 196612
  63.9 4.1 %copy-start.6 = (f32[32,16,128]{2,1,0:T(8,128)S(1)}, f32[32,16,128]{2,1,0:T(8,128)}, u32[]{:S(2)}) copy-start(f32[32,16,128]{2,1,0:T(8,128)} %get-tuple-element.21) | copy-start | bytes 786436
  63.9 5.7 %copy-start.1 = (f32[8,128,128]{2,1,0:T(8,128)S(1)}, f32[8,128,128]{2,1,0:T(8,128)}, u32[]{:S(2)}) copy-start(f32[8,128,128]{2,1,0:T(8,128)} %refs_3_.4) | copy-start | bytes 1572868
  63.9 5.7 %copy-start.2 = (f32[8,128,128]{2,1,0:T(8,128)S(1)}, f32[8,128,128]{2,1,0:T(8,128)}, u32[]{:S(2)}) copy-start(f32[8,128,128]{2,1,0:T(8,128)} %refs_2_.5) | copy-start | bytes 1572868
  63.9 5.7 %copy-start.5 = (f32[8,128,128]{2,1,0:T(8,128)S(1)}, f32[8,128,128]{2,1,0:T(8,128)}, u32[]{:S(2)}) copy-start(f32[8,128,128]{2,1,0:T(8,128)} %refs_3_.3) | copy-start | bytes 1572868
  63.9 18.1 %all-to-all-start.1 = ((f32[8,256,128]{2,1,0:T(8,128)}), f32[8,256,128]{2,1,0:T(8,128)S(1)}, u32[]{:S(2)}, u32[]{:S(2)}) async-start(f32[8,256,128]{2,1,0:T(8,128)} %bitcast.14), calls=%async_computation.1 | async-start | bytes 2097152 | tf_op jit(solution)/shard_map/all_to_all | solution.py:654
  67.9 8.7 %collective-permute-start.1 = (f32[32,16,128]{2,1,0:T(8,128)S(1)}, f32[32,16,128]{2,1,0:T(8,128)S(1)}, u32[]{:S(2)}, u32[]{:S(2)}) collective-permute-start(f32[32,16,128]{2,1,0:T(8,128)S(1)} %copy-done.6), channel_id=1, source_target_pairs={{0,16},{16,0},{1,17},{17,1},{2,18},{18,2},{3,19},{19,3},{4,20},{20... | collective-permute-start | bytes 786440 | tf_op jit(solution)/shard_map/ppermute | solution.py:566
  88.6 5.0 %copy-start.7 = (f32[32,16,128]{2,1,0:T(8,128)S(1)}, f32[32,16,128]{2,1,0:T(8,128)}, u32[]{:S(2)}) copy-start(f32[32,16,128]{2,1,0:T(8,128)} %get-tuple-element.30) | copy-start | bytes 786436
  88.6 29.0 %all-to-all-start.2 = ((f32[16,136,128]{2,1,0:T(8,128)}), f32[16,136,128]{2,1,0:T(8,128)S(1)}, u32[]{:S(2)}, u32[]{:S(2)}) async-start(f32[16,136,128]{2,1,0:T(8,128)} %get-tuple-element.26), calls=%async_computation.2 | async-start | bytes 2228224 | tf_op jit(solution)/shard_map/all_to_all | solution.py:654
  93.6 25.6 %collective-permute-start.3 = (f32[32,16,128]{2,1,0:T(8,128)S(1)}, f32[32,16,128]{2,1,0:T(8,128)S(1)}, u32[]{:S(2)}, u32[]{:S(2)}) collective-permute-start(f32[32,16,128]{2,1,0:T(8,128)S(1)} %copy-done.7), channel_id=1, source_target_pairs={{0,16},{16,0},{1,17},{17,1},{2,18},{18,2},{3,19},{19,3},{4,20},{20... | collective-permute-start | bytes 786440 | tf_op jit(solution)/shard_map/ppermute | solution.py:566
  117.6 3.6 %collective-permute-start.2 = (f32[4,128]{1,0:T(4,128)S(1)}, f32[4,128]{1,0:T(4,128)S(1)}, u32[]{:S(2)}, u32[]{:S(2)}) collective-permute-start(f32[4,128]{1,0:T(4,128)S(1)} %get-tuple-element.28), channel_id=1, source_target_pairs={{0,16},{16,0},{1,17},{17,1},{2,18},{18,2},{3,19},{19,3},{4,20},{20... | collective-permute-start | bytes 6152 | tf_op jit(solution)/shard_map/ppermute | solution.py:738

commit v5 on v4

--- a/solution.py
+++ b/solution.py
@@ -220,30 +220,33 @@
 
 def first_kernel(sizes, width_k, n_band, *refs):
     rows, n_rows, cap, n_tiles, n_rhs = sizes
-    product_ref, meta_ref, send_out = refs[:3]
+    product_in, meta_ref, send_out = refs[:3]
     band_out, refs = refs[3 : 3 + n_band], refs[3 + n_band :]
-    request_ref, near_ref, meta_sems, send_sems = refs
+    product_ref, request_ref, near_ref, send_ref = refs[:4]
+    band_refs, (load_sems, meta_sems, send_sems) = refs[4 : 4 + n_band], refs[4 + n_band :]
+    loads = []
+    for side in range(2):
+        for tile in range(n_tiles):
+            place = pl.ds(tile * rows, rows)
+            source, target = product_in.at[side, place], product_ref.at[side, place]
+            loads.append(pltpu.make_async_copy(source, target, load_sems.at[len(loads)]))
+    started(loads)
     finish(started(metadata_copies(meta_ref, request_ref, near_ref, meta_sems)))
+    finish(loads)
     half = n_rows // 2
     base = jnp.where(lax.axis_index("rows") >= half, half, 0)
+    copies = []
     for device in range(half):
         for slot in range(2 * cap):
             side, rank = slot // cap, slot % cap
             code = request_ref[base + device, 0, side * (LANES // 2) + rank]
-            pltpu.make_async_copy(
-                product_ref.at[side, below(code, rows * n_tiles)],
-                send_out.at[device, slot],
-                send_sems.at[0],
-            ).start()
-    for way, out in enumerate(band_out):
-        field = band_field(rows, width_k, way, n_band)
-        for row in range(rows):
-            block = near_ref[way, 0, field + row] * rows + row
-            pltpu.make_async_copy(
-                product_ref.at[0, block], out.at[row], send_sems.at[1 + way]
-            ).start()
-    for n, out in enumerate((send_out, *band_out)):
-        pltpu.make_async_copy(out, out, send_sems.at[n]).wait()
+            send_ref[device, slot] = product_ref[side, below(code, rows * n_tiles)]
+        copy = pltpu.make_async_copy(send_ref.at[device], send_out.at[device], send_sems.at[device])
+        copies += started([copy])
+    pack_bands(sizes, width_k, product_ref.at[0], near_ref, band_refs)
+    for n, (ref, out) in enumerate(zip(band_refs, band_out)):
+        copies += started([pltpu.make_async_copy(ref, out, send_sems.at[half + n])])
+    finish(copies)
 
 
 def place(place_ref, values, n_rhs):
@@ -642,7 +645,15 @@
         (jax.ShapeDtypeStruct((half, 2 * cap, n_rhs, states), f32), *band_shapes),
         [HBM, ANY],
         [HBM] * (1 + n_ways),
-        [*meta_scratch, meta_sems, pltpu.SemaphoreType.DMA((1 + n_ways,))],
+        [
+            pltpu.VMEM(made_shape, f32),
+            *meta_scratch,
+            pltpu.VMEM((half, 2 * cap, n_rhs, states), f32),
+            *band_scratch,
+            pltpu.SemaphoreType.DMA((2 * n_tiles,)),
+            meta_sems,
+            pltpu.SemaphoreType.DMA((half + n_ways,)),
+        ],
         0,
         4 << 20,
     )(made, meta)

time: 124 us -> 85.5 us (0.69)
  the two profiles are of different devices: /device:TPU:0 before, /device:TPU:16 now
where the time goes in v5:
time: 85.5 us; the launch traced here: 85 us
  waiting for transfers between devices  37 us (43%)
  Pallas kernels  23.1 us (27%)
  starting transfers between devices  22.5 us (26%)
  local copies, waits for them, and re-layouts  2.27 us (3%)
    all_to_all x2, waiting for transfers between devices, exchange(): lax.all_to_all(sends[0], 'rows', split_axis=0, concat_axis=0, tiled=True,...  30.4 us
    pallas_call x8, Pallas kernels, apply(): return run(*pinned)  23.1 us
    all_to_all x2, starting transfers between devices, exchange(): lax.all_to_all(sends[0], 'rows', split_axis=0, concat_axis=0, tiled=True,...  11.2 us
    all_to_all x1, starting transfers between devices, on_device(): lax.all_to_all(payload, ('band', 'rows'), split_axis=0, concat_axis=0, ti...  6.5 us
    ppermute x1, waiting for transfers between devices, on_device(): lax.ppermute(start_iterate, 'rows', [(i, (i + half) % n_rows) for i in ra...  4.56 us
    ppermute x2, starting transfers between devices, to_bands(): return (lax.ppermute(sends[0], 'band', [(0, 1), (1, 0)]),)  3.16 us
    unnamed x17, local copies, waits for them, and re-layouts  2.03 us
  transfers between devices with their start and end apart: 7, of which 6 were waited for; matrix products, arithmetic and copies ran while one was open for 0% of the time, Pallas kernels for 14%

profile of v5, /device:TPU:16, one launch (start us, length us, event | category | flops | bytes accessed | tf_op | source)
XLA Modules:
  0.0 85.0 jit_solution(14857622903530144830)
XLA Ops:
  0.0 1.8 %shard_map.100 = s32[32,1,512]{2,1,0:T(1,128)} custom-call(s32[2,32]{1,0:T(2,128)} %bitcast.19, s32[2,32]{1,0:T(2,128)} %bitcast.20, s32[4,32]{1,0:T(4,128)} %bitcast.18, s32[1,32]{1,0:T(1,128)} %bitcast.21, s32[1,32]{1,0:T(1,128)} %bitcast.22), custom_call_target="tpu_custom_call" | custom-call | tf_op jit(solution)/shard_map/pallas_call | solution.py:48
  1.8 6.5 %all-to-all-start = ((s32[32,1,512]{2,1,0:T(1,128)}), s32[32,1,512]{2,1,0:T(1,128)S(1)}, u32[]{:S(2)}, u32[]{:S(2)}) async-start(s32[32,1,512]{2,1,0:T(1,128)} %shard_map.100), calls=%async_computation | async-start | bytes 131072 | tf_op jit(solution)/shard_map/all_to_all | solution.py:619
  8.3 4.6 %collective-permute-done.mirror_ref = f32[32,16,128]{2,1,0:T(8,128)S(1)} collective-permute-done((f32[32,16,128]{2,1,0:T(8,128)}, f32[32,16,128]{2,1,0:T(8,128)S(1)}, u32[]{:S(2)}, u32[]{:S(2)}) %collective-permute-start) | collective-permute-done | bytes 262176 | tf_op jit(solution)/shard_map/ppermute | solution.py:609
  12.9 1.0 %copy-done = f32[8,128,128]{2,1,0:T(8,128)S(1)} copy-done((f32[8,128,128]{2,1,0:T(8,128)S(1)}, f32[8,128,128]{2,1,0:T(8,128)}, u32[]{:S(2)}) %copy-start) | copy-done | bytes 524312
  13.9 0.9 %copy-done.4 = f32[32,16,128]{2,1,0:T(8,128)S(1)} copy-done((f32[32,16,128]{2,1,0:T(8,128)S(1)}, f32[32,16,128]{2,1,0:T(8,128)}, u32[]{:S(2)}) %copy-start.4) | copy-done | bytes 262168
  14.9 2.6 %shard_map.101.refs_0_ = f32[2,256,16,128]{3,2,1,0:T(8,128)} custom-call(f32[32,16,128]{2,1,0:T(8,128)S(1)} %copy-done.4, f32[32,16,128]{2,1,0:T(8,128)S(1)} %collective-permute-done.mirror_ref, f32[8,128,128]{2,1,0:T(8,128)S(1)} %copy-done), custom_call_target="tpu_custom_call" | custom-call | flops 805306368 | bytes 4194304 | tf_op jit(solution)/shard_map/pallas_call | solution.py:48
  17.4 0.6 all-to-all-done.refs_1_.refs_0_
  18.0 3.4 %shard_map.102 = (f32[8,16,16,128]{3,2,1,0:T(8,128)}, f32[32,16,128]{2,1,0:T(8,128)}) custom-call(f32[2,256,16,128]{3,2,1,0:T(8,128)} %shard_map.101.refs_0_, s32[32,1,512]{2,1,0:T(1,128)S(1)} %all-to-all-done.refs_1_.refs_0_), custom_call_target="tpu_custom_call" | custom-call | bytes 4194304 | tf_op jit(solution)/shard_map/pallas_call | solution.py:48
  21.5 0.0 copy-start.2
  21.5 6.0 %all-to-all-start.1 = ((f32[8,256,128]{2,1,0:T(8,128)}), f32[8,256,128]{2,1,0:T(8,128)S(1)}, u32[]{:S(2)}, u32[]{:S(2)}) async-start(f32[8,256,128]{2,1,0:T(8,128)} %bitcast.14), calls=%async_computation.1 | async-start | bytes 2097152 | tf_op jit(solution)/shard_map/all_to_all | solution.py:665
  27.5 0.1 reshape.14
  27.6 0.1 reshape.15.refs_0_
  27.8 1.6 %collective-permute-start.1 = (f32[32,16,128]{2,1,0:T(8,128)S(1)}, f32[32,16,128]{2,1,0:T(8,128)S(1)}, u32[]{:S(2)}, u32[]{:S(2)}) collective-permute-start(f32[32,16,128]{2,1,0:T(8,128)S(1)} %copy-done.6), channel_id=1, source_target_pairs={{0,16},{16,0},{1,17},{17,1},{2,18},{18,2},{3,19},{19,3},{4,20},{20... | collective-permute-start | bytes 786440 | tf_op jit(solution)/shard_map/ppermute | solution.py:569
  29.4 6.0 %shard_map.103 = (bf16[10,256,192]{2,1,0:T(8,128)(2,1)}, bf16[128,384]{1,0:T(8,128)(2,1)}, bf16[1024,256]{1,0:T(8,128)(2,1)}, f32[4,128]{1,0:T(4,128)S(1)}) custom-call(s32[8,2,512]{2,1,0:T(2,128)S(1)} %reshape.15.refs_0_, s32[16,128]{1,0:T(8,128)S(1)} %dynamic-slice_bitcast_fusion.refs_1_, f32[8,128,128]{2,1,0:T(8,128)S(1)} %copy-done.1, ...), custom_call_target="tpu_custom_call" | custom-call | flops 1610612736 | bytes 4194304 | tf_op jit(solution)/shard_map/pallas_call | solution.py:48
  35.4 1.2 %collective-permute-done.1.refs_5_ = f32[32,16,128]{2,1,0:T(8,128)S(1)} collective-permute-done((f32[32,16,128]{2,1,0:T(8,128)S(1)}, f32[32,16,128]{2,1,0:T(8,128)S(1)}, u32[]{:S(2)}, u32[]{:S(2)}) %collective-permute-start.1) | collective-permute-done | bytes 262176 | tf_op jit(solution)/shard_map/ppermute | solution.py:569
  36.5 5.4 %all-to-all-done.1.refs_1_ = f32[8,256,128]{2,1,0:T(8,128)S(1)} async-done(((f32[8,256,128]{2,1,0:T(8,128)}), f32[8,256,128]{2,1,0:T(8,128)S(1)}, u32[]{:S(2)}, u32[]{:S(2)}) %all-to-all-start.1) | async-done | bytes 1048608 | tf_op jit(solution)/shard_map/all_to_all | solution.py:665
  41.9 6.6 %shard_map.104 = (f32[16,136,128]{2,1,0:T(8,128)}, f32[32,16,128]{2,1,0:T(8,128)}) custom-call(s32[32,1,512]{2,1,0:T(1,128)} %copy-done.3, f32[8,256,128]{2,1,0:T(8,128)S(1)} %all-to-all-done.1.refs_1_, f32[8,128,128]{2,1,0:T(8,128)S(1)} %copy-done.2, f32[8,128,128]{2,1,0:T(8,128)S(1)} %copy-done.1, f32[32,16,128]{2,1,0:T(8,128)} %refs_3_.5, ...), custom_call_target="tpu_custom_call" | custom-call | flops 805306368 | bytes 4194304 | tf_op jit(solution)/shard_map/pallas_call | solution.py:48
  48.5 5.3 %all-to-all-start.2 = ((f32[16,136,128]{2,1,0:T(8,128)}), f32[16,136,128]{2,1,0:T(8,128)S(1)}, u32[]{:S(2)}, u32[]{:S(2)}) async-start(f32[16,136,128]{2,1,0:T(8,128)} %get-tuple-element.26), calls=%async_computation.2 | async-start | bytes 2228224 | tf_op jit(solution)/shard_map/all_to_all | solution.py:665
  53.8 1.6 %collective-permute-start.3 = (f32[32,16,128]{2,1,0:T(8,128)S(1)}, f32[32,16,128]{2,1,0:T(8,128)S(1)}, u32[]{:S(2)}, u32[]{:S(2)}) collective-permute-start(f32[32,16,128]{2,1,0:T(8,128)S(1)} %copy-done.7), channel_id=1, source_target_pairs={{0,16},{16,0},{1,17},{17,1},{2,18},{18,2},{3,19},{19,3},{4,20},{20... | collective-permute-start | bytes 786440 | tf_op jit(solution)/shard_map/ppermute | solution.py:569
  55.4 25.0 %all-to-all-done.2.arrived_ref.refs_1_ = f32[16,136,128]{2,1,0:T(8,128)S(1)} async-done(((f32[16,136,128]{2,1,0:T(8,128)}), f32[16,136,128]{2,1,0:T(8,128)S(1)}, u32[]{:S(2)}, u32[]{:S(2)}) %all-to-all-start.2) | async-done | bytes 1114144 | tf_op jit(solution)/shard_map/all_to_all | solution.py:665
  80.4 1.6 %collective-permute-start.2 = (f32[4,128]{1,0:T(4,128)S(1)}, f32[4,128]{1,0:T(4,128)S(1)}, u32[]{:S(2)}, u32[]{:S(2)}) collective-permute-start(f32[4,128]{1,0:T(4,128)S(1)} %get-tuple-element.28), channel_id=1, source_target_pairs={{0,16},{16,0},{1,17},{17,1},{2,18},{18,2},{3,19},{19,3},{4,20},{20... | collective-permute-start | bytes 6152 | tf_op jit(solution)/shard_map/ppermute | solution.py:749
  82.0 1.7 %shard_map.106.second_ref = f32[32,16,128]{2,1,0:T(8,128)S(1)} custom-call(s32[32,1,512]{2,1,0:T(1,128)} %copy-done.3, f32[16,136,128]{2,1,0:T(8,128)S(1)} %all-to-all-done.2.arrived_ref.refs_1_, f32[8,128,128]{2,1,0:T(8,128)S(1)} %copy-done.2, f32[32,16,128]{2,1,0:T(8,128)} %refs_3_.5, f32[32,16,128]{2,1,0:T(8,128)S(1)} %collective-permute-done.3.refs_4_), custom_call_target="tpu_custom_call" | custom-call | flops 402653184 | bytes 4194304 | tf_op jit(solution)/shard_map/pallas_call | solution.py:48
  83.7 0.3 collective-permute-done.2.other_ref
  84.0 1.0 %shard_map.107 = f32[32,16,128]{2,1,0:T(8,128)} custom-call(f32[4,128]{1,0:T(4,128)S(1)} %get-tuple-element.27.mine_ref, f32[4,128]{1,0:T(4,128)S(1)} %collective-permute-done.2.other_ref, f32[4,128]{1,0:T(4,128)S(1)} %get-tuple-element.29.scale_ref, f32[32,16,128]{2,1,0:T(8,128)S(1)} %shard_map.106.second_ref), custom_call_target="tpu_custom_call" | custom-call | tf_op jit(solution)/shard_map/pallas_call | solution.py:48
  (21 shorter events, 0.1 us)
Async XLA Ops:
  0.0 12.9 %collective-permute-start = (f32[32,16,128]{2,1,0:T(8,128)}, f32[32,16,128]{2,1,0:T(8,128)S(1)}, u32[]{:S(2)}, u32[]{:S(2)}) collective-permute-start(f32[32,16,128]{2,1,0:T(8,128)} %start_ref.1), channel_id=1, source_target_pairs={{0,8},{1,9},{2,10},{3,11},{4,12},{5,13},{6,14},{7,15},{8,0},{9,1},... | collective-permute-start | bytes 786440 | tf_op jit(solution)/shard_map/ppermute | solution.py:609
  1.8 16.2 %all-to-all-start = ((s32[32,1,512]{2,1,0:T(1,128)}), s32[32,1,512]{2,1,0:T(1,128)S(1)}, u32[]{:S(2)}, u32[]{:S(2)}) async-start(s32[32,1,512]{2,1,0:T(1,128)} %shard_map.100), calls=%async_computation | async-start | bytes 131072 | tf_op jit(solution)/shard_map/all_to_all | solution.py:619
  12.9 1.0 %copy-start = (f32[8,128,128]{2,1,0:T(8,128)S(1)}, f32[8,128,128]{2,1,0:T(8,128)}, u32[]{:S(2)}) copy-start(f32[8,128,128]{2,1,0:T(8,128)} %refs_3_.4) | copy-start | bytes 1572868
  13.9 0.9 %copy-start.4 = (f32[32,16,128]{2,1,0:T(8,128)S(1)}, f32[32,16,128]{2,1,0:T(8,128)}, u32[]{:S(2)}) copy-start(f32[32,16,128]{2,1,0:T(8,128)} %start_ref.1) | copy-start | bytes 786436
  18.0 9.5 %copy-start.3 = (s32[32,1,512]{2,1,0:T(1,128)}, s32[32,1,512]{2,1,0:T(1,128)S(1)}, u32[]{:S(2)}) copy-start(s32[32,1,512]{2,1,0:T(1,128)S(1)} %all-to-all-done.refs_1_.refs_0_) | copy-start | bytes 196612
  21.5 6.3 %copy-start.6 = (f32[32,16,128]{2,1,0:T(8,128)S(1)}, f32[32,16,128]{2,1,0:T(8,128)}, u32[]{:S(2)}) copy-start(f32[32,16,128]{2,1,0:T(8,128)} %get-tuple-element.21) | copy-start | bytes 786436
  21.5 7.9 %copy-start.1 = (f32[8,128,128]{2,1,0:T(8,128)S(1)}, f32[8,128,128]{2,1,0:T(8,128)}, u32[]{:S(2)}) copy-start(f32[8,128,128]{2,1,0:T(8,128)} %refs_3_.4) | copy-start | bytes 1572868
  21.5 7.9 %copy-start.2 = (f32[8,128,128]{2,1,0:T(8,128)S(1)}, f32[8,128,128]{2,1,0:T(8,128)}, u32[]{:S(2)}) copy-start(f32[8,128,128]{2,1,0:T(8,128)} %refs_2_.5) | copy-start | bytes 1572868
  21.5 7.9 %copy-start.5 = (f32[8,128,128]{2,1,0:T(8,128)S(1)}, f32[8,128,128]{2,1,0:T(8,128)}, u32[]{:S(2)}) copy-start(f32[8,128,128]{2,1,0:T(8,128)} %refs_3_.3) | copy-start | bytes 1572868
  21.5 20.4 %all-to-all-start.1 = ((f32[8,256,128]{2,1,0:T(8,128)}), f32[8,256,128]{2,1,0:T(8,128)S(1)}, u32[]{:S(2)}, u32[]{:S(2)}) async-start(f32[8,256,128]{2,1,0:T(8,128)} %bitcast.14), calls=%async_computation.1 | async-start | bytes 2097152 | tf_op jit(solution)/shard_map/all_to_all | solution.py:665
  27.8 8.8 %collective-permute-start.1 = (f32[32,16,128]{2,1,0:T(8,128)S(1)}, f32[32,16,128]{2,1,0:T(8,128)S(1)}, u32[]{:S(2)}, u32[]{:S(2)}) collective-permute-start(f32[32,16,128]{2,1,0:T(8,128)S(1)} %copy-done.6), channel_id=1, source_target_pairs={{0,16},{16,0},{1,17},{17,1},{2,18},{18,2},{3,19},{19,3},{4,20},{20... | collective-permute-start | bytes 786440 | tf_op jit(solution)/shard_map/ppermute | solution.py:569
  48.5 5.3 %copy-start.7 = (f32[32,16,128]{2,1,0:T(8,128)S(1)}, f32[32,16,128]{2,1,0:T(8,128)}, u32[]{:S(2)}) copy-start(f32[32,16,128]{2,1,0:T(8,128)} %get-tuple-element.30) | copy-start | bytes 786436
  48.5 31.8 %all-to-all-start.2 = ((f32[16,136,128]{2,1,0:T(8,128)}), f32[16,136,128]{2,1,0:T(8,128)S(1)}, u32[]{:S(2)}, u32[]{:S(2)}) async-start(f32[16,136,128]{2,1,0:T(8,128)} %get-tuple-element.26), calls=%async_computation.2 | async-start | bytes 2228224 | tf_op jit(solution)/shard_map/all_to_all | solution.py:665
  53.8 28.2 %collective-permute-start.3 = (f32[32,16,128]{2,1,0:T(8,128)S(1)}, f32[32,16,128]{2,1,0:T(8,128)S(1)}, u32[]{:S(2)}, u32[]{:S(2)}) collective-permute-start(f32[32,16,128]{2,1,0:T(8,128)S(1)} %copy-done.7), channel_id=1, source_target_pairs={{0,16},{16,0},{1,17},{17,1},{2,18},{18,2},{3,19},{19,3},{4,20},{20... | collective-permute-start | bytes 786440 | tf_op jit(solution)/shard_map/ppermute | solution.py:569
  80.4 3.6 %collective-permute-start.2 = (f32[4,128]{1,0:T(4,128)S(1)}, f32[4,128]{1,0:T(4,128)S(1)}, u32[]{:S(2)}, u32[]{:S(2)}) collective-permute-start(f32[4,128]{1,0:T(4,128)S(1)} %get-tuple-element.28), channel_id=1, source_target_pairs={{0,16},{16,0},{1,17},{17,1},{2,18},{18,2},{3,19},{19,3},{4,20},{20... | collective-permute-start | bytes 6152 | tf_op jit(solution)/shard_map/ppermute | solution.py:749

commit v6 on v5

--- a/solution.py
+++ b/solution.py
@@ -82,13 +82,15 @@
     )
 
 
-def table_products(value, table_ref, out_ref, done=None):
+def table_products(value, table_ref, out_ref, done=None, loads=None):
     left = left_operand(value)
     count, width = table_ref.shape[0], table_ref.shape[1]
     n_rhs = out_ref.shape[1]
     rows = left.shape[0] // n_rhs
     for first in range(0, count, 2):
         last = min(first + 2, count)
+        if loads is not None:
+            loads[first // 2].wait()
         right = right_operand(table_ref[first:last].reshape((last - first) * width, -1))
         product = dot_nt(left, right)
         for t in range(first, last):
@@ -201,37 +203,50 @@
             band_ref[row] = product_ref[near_ref[way, 0, field + row] * rows + row]
 
 
-def product_kernel(start_ref, mirror_ref, tile_ref, product_out, product_ref, sems):
+def table_loads(table_in, table_ref, sems):
     copies = []
-    for side, ref in enumerate((start_ref, mirror_ref)):
-        held = product_ref.at[side]
-
-        def done(first, count):
-            place = pl.ds(first, count)
-            copy = pltpu.make_async_copy(
-                held.at[place], product_out.at[side, place], sems.at[len(copies)]
-            )
-            copies.extend(started([copy]))
-
-        rows, n_rhs, states = ref.shape
-        table_products(ref[...].reshape(rows * n_rhs, states), tile_ref, held, done)
+    for first in range(0, table_in.shape[0], 2):
+        place = pl.ds(first, min(2, table_in.shape[0] - first))
+        source, target = table_in.at[place], table_ref.at[place]
+        copies.append(pltpu.make_async_copy(source, target, sems.at[first // 2]))
+    return started(copies)
+
+
+def product_kernel(start_in, tile_in, product_out, start_ref, tile_ref, product_ref, sems, tile_sems):
+    start = pltpu.make_async_copy(start_in, start_ref, sems.at[0])
+    start.start()
+    loads = table_loads(tile_in, tile_ref, tile_sems)
+    start.wait()
+    copies = []
+
+    def done(first, count):
+        place = pl.ds(first, count)
+        source, target = product_ref.at[place], product_out.at[place]
+        copies.extend(started([pltpu.make_async_copy(source, target, sems.at[1 + len(copies)])]))
+
+    rows, n_rhs, states = start_ref.shape
+    values = start_ref[...].reshape(rows * n_rhs, states)
+    table_products(values, tile_ref, product_ref, done, loads)
     finish(copies)
 
 
 def first_kernel(sizes, width_k, n_band, *refs):
     rows, n_rows, cap, n_tiles, n_rhs = sizes
-    product_in, meta_ref, send_out = refs[:3]
-    band_out, refs = refs[3 : 3 + n_band], refs[3 + n_band :]
-    product_ref, request_ref, near_ref, send_ref = refs[:4]
-    band_refs, (load_sems, meta_sems, send_sems) = refs[4 : 4 + n_band], refs[4 + n_band :]
+    product_in, mirror_ref, tile_in, meta_ref, send_out = refs[:5]
+    band_out, refs = refs[5 : 5 + n_band], refs[5 + n_band :]
+    product_ref, tile_ref, request_ref, near_ref, send_ref = refs[:5]
+    band_refs, (load_sems, tile_sems, meta_sems, send_sems) = refs[5 : 5 + n_band], refs[5 + n_band :]
+    tile_loads = table_loads(tile_in, tile_ref, tile_sems)
+    metadata = started(metadata_copies(meta_ref, request_ref, near_ref, meta_sems))
     loads = []
-    for side in range(2):
-        for tile in range(n_tiles):
-            place = pl.ds(tile * rows, rows)
-            source, target = product_in.at[side, place], product_ref.at[side, place]
-            loads.append(pltpu.make_async_copy(source, target, load_sems.at[len(loads)]))
+    for tile in range(n_tiles):
+        place = pl.ds(tile * rows, rows)
+        source, target = product_in.at[place], product_ref.at[0, place]
+        loads.append(pltpu.make_async_copy(source, target, load_sems.at[tile]))
     started(loads)
-    finish(started(metadata_copies(meta_ref, request_ref, near_ref, meta_sems)))
+    values = mirror_ref[...].reshape(rows * n_rhs, -1)
+    table_products(values, tile_ref, product_ref.at[1], None, tile_loads)
+    finish(metadata)
     finish(loads)
     half = n_rows // 2
     base = jnp.where(lax.axis_index("rows") >= half, half, 0)
@@ -606,7 +621,6 @@
     my_row = lax.axis_index("rows")
 
     half = n_rows // 2
-    mirror = lax.ppermute(start_iterate, "rows", [(i, (i + half) % n_rows) for i in range(n_rows)])
     wide = LANES + -(-(4 + 4 * width_k) * rows // LANES) * LANES
     index_shapes = [(width_k, rows), (width_k, rows), (width_k + 2, rows), (1, rows), (1, rows)]
     payload = call(
@@ -616,6 +630,8 @@
         VMEM,
         [*[pltpu.VMEM(shape, i32) for shape in index_shapes], pltpu.SemaphoreType.DMA((5,))],
     )(source_owner.T, source_local.T, tile_index.T, diag_index[None], aggregate_map.T)
+    payload, to_mirror = lax.optimization_barrier((payload, start_iterate))
+    mirror = lax.ppermute(to_mirror, "rows", [(i, (i + half) % n_rows) for i in range(n_rows)])
     meta = lax.all_to_all(payload, ("band", "rows"), split_axis=0, concat_axis=0, tiled=True)
 
     n_ways = 1 if n_bands == 2 else 2
@@ -630,33 +646,43 @@
     sums = pltpu.VMEM((flat, states), f32)
     products = pltpu.VMEM((max(n_tiles, n_diag) * rows, n_rhs, states), f32)
     work = 6 * flat * states * states
-    made_shape = (2, n_tiles * rows, n_rhs, states)
+    made_shape = (n_tiles * rows, n_rhs, states)
+    table_scratch = [pltpu.VMEM(coupling_tiles.shape, f32)]
+    table_sems = pltpu.SemaphoreType.DMA((-(-n_tiles // 2),))
     made = call(
         product_kernel,
         jax.ShapeDtypeStruct(made_shape, f32),
-        [VMEM] * 3,
+        [HBM, HBM],
         HBM,
-        [pltpu.VMEM(made_shape, f32), pltpu.SemaphoreType.DMA((2 * n_tiles,))],
-        2 * work * n_tiles,
+        [
+            pltpu.VMEM(block, f32),
+            *table_scratch,
+            pltpu.VMEM(made_shape, f32),
+            pltpu.SemaphoreType.DMA((1 + n_tiles,)),
+            table_sems,
+        ],
+        work * n_tiles,
         4 << 20,
-    )(start_iterate, mirror, coupling_tiles)
+    )(start_iterate, coupling_tiles)
     packed, *bands = call(
         functools.partial(first_kernel, sizes, width_k, n_ways),
         (jax.ShapeDtypeStruct((half, 2 * cap, n_rhs, states), f32), *band_shapes),
-        [HBM, ANY],
+        [HBM, VMEM, HBM, ANY],
         [HBM] * (1 + n_ways),
         [
-            pltpu.VMEM(made_shape, f32),
+            pltpu.VMEM((2, *made_shape), f32),
+            *table_scratch,
             *meta_scratch,
             pltpu.VMEM((half, 2 * cap, n_rhs, states), f32),
             *band_scratch,
-            pltpu.SemaphoreType.DMA((2 * n_tiles,)),
+            pltpu.SemaphoreType.DMA((n_tiles,)),
+            table_sems,
             meta_sems,
             pltpu.SemaphoreType.DMA((half + n_ways,)),
         ],
-        0,
+        work * n_tiles,
         4 << 20,
-    )(made, meta)
+    )(made, mirror, coupling_tiles, meta)
     sends = (packed.reshape(half, 2 * cap * n_rhs, states), *bands)
     halves_of_rows = [list(range(half)), list(range(half, n_rows))]
     late, *sends = lax.optimization_barrier((meta, *sends))

time: 85.5 us -> 85.9 us (level)
  waiting for transfers between devices: 37 us -> 42.3 us
  starting transfers between devices: 22.5 us -> 17.3 us
  Pallas kernels: 23.1 us -> 25.4 us
  local copies, waits for them, and re-layouts: 2.27 us -> 0.28 us
    all_to_all x1, waiting for transfers between devices: 0.56 us -> 7.53 us  [on_device(): lax.all_to_all(payload, ('band', 'rows'), split_axis=0, concat_axis=0, ti...]
    ppermute x1, waiting for transfers between devices: 4.56 us -> 0.01 us  [on_device(): lax.ppermute(to_mirror, 'rows', [(i, (i + half) % n_rows) for i in range(...]
    pallas_call x8, Pallas kernels: 23.1 us -> 25.4 us  [apply(): return run(*pinned)]
    all_to_all x2, starting transfers between devices: 11.2 us -> 8.98 us  [exchange(): lax.all_to_all(sends[0], 'rows', split_axis=0, concat_axis=0, tiled=True,...]
    unnamed x17 -> x13, local copies, waits for them, and re-layouts: 2.03 us -> 0.04 us
    ppermute x2, starting transfers between devices: 3.16 us -> 1.17 us  [to_bands(): return (lax.ppermute(sends[0], 'band', [(0, 1), (1, 0)]),)]
    all_to_all x2, waiting for transfers between devices: 30.4 us -> 31.4 us  [exchange(): lax.all_to_all(sends[0], 'rows', split_axis=0, concat_axis=0, tiled=True,...]
    ppermute x1, waiting for transfers between devices: 0.32 us -> 1.32 us  [on_device(): other = lax.ppermute(other, 'band', [(0, 1), (1, 0)])]
  transfers between devices with their start and end apart: 7 -> 7, of which waited for: 6 -> 5; matrix products, arithmetic and copies ran while one was open for 0% -> 0% of each run, Pallas kernels for 14% -> 14%
where the time goes in v6:
time: 85.9 us; the launch traced here: 85.5 us
  waiting for transfers between devices  42.3 us (49%)
  Pallas kernels  25.4 us (30%)
  starting transfers between devices  17.3 us (20%)
    all_to_all x2, waiting for transfers between devices, exchange(): lax.all_to_all(sends[0], 'rows', split_axis=0, concat_axis=0, tiled=True,...  31.4 us
    pallas_call x8, Pallas kernels, apply(): return run(*pinned)  25.4 us
    all_to_all x2, starting transfers between devices, exchange(): lax.all_to_all(sends[0], 'rows', split_axis=0, concat_axis=0, tiled=True,...  8.98 us
    all_to_all x1, waiting for transfers between devices, on_device(): lax.all_to_all(payload, ('band', 'rows'), split_axis=0, concat_axis=0, ti...  7.53 us
    all_to_all x1, starting transfers between devices, on_device(): lax.all_to_all(payload, ('band', 'rows'), split_axis=0, concat_axis=0, ti...  6.48 us
    ppermute x2, waiting for transfers between devices, to_bands(): return (lax.ppermute(sends[0], 'band', [(0, 1), (1, 0)]),)  2.07 us
  transfers between devices with their start and end apart: 7, of which 5 were waited for; matrix products, arithmetic and copies ran while one was open for 0% of the time, Pallas kernels for 14%

profile of v6, /device:TPU:16, one launch (start us, length us, event | category | flops | bytes accessed | tf_op | source)
XLA Modules:
  0.0 85.5 jit_solution(15815610081943404513)
XLA Ops:
  0.0 1.8 %shard_map.100 = s32[32,1,512]{2,1,0:T(1,128)} custom-call(s32[2,32]{1,0:T(2,128)} %bitcast.19, s32[2,32]{1,0:T(2,128)} %bitcast.20, s32[4,32]{1,0:T(4,128)} %bitcast.18, s32[1,32]{1,0:T(1,128)} %bitcast.21, s32[1,32]{1,0:T(1,128)} %bitcast.22), custom_call_target="tpu_custom_call" | custom-call | tf_op jit(solution)/shard_map/pallas_call | solution.py:48
  1.8 0.1 collective-permute-start
  1.9 6.5 %all-to-all-start = ((s32[32,1,512]{2,1,0:T(1,128)}), s32[32,1,512]{2,1,0:T(1,128)S(1)}, u32[]{:S(2)}, u32[]{:S(2)}) async-start(s32[32,1,512]{2,1,0:T(1,128)} %shard_map.100), calls=%async_computation | async-start | bytes 131072 | tf_op jit(solution)/shard_map/all_to_all | solution.py:635
  8.4 3.9 %shard_map.101.refs_0_ = f32[256,16,128]{2,1,0:T(8,128)} custom-call(f32[32,16,128]{2,1,0:T(8,128)} %start_in.1, f32[8,128,128]{2,1,0:T(8,128)} %refs_3_.4), custom_call_target="tpu_custom_call" | custom-call | flops 402653184 | bytes 4194304 | tf_op jit(solution)/shard_map/pallas_call | solution.py:48
  12.3 7.5 %all-to-all-done.refs_3_.refs_0_ = s32[32,1,512]{2,1,0:T(1,128)S(1)} async-done(((s32[32,1,512]{2,1,0:T(1,128)}), s32[32,1,512]{2,1,0:T(1,128)S(1)}, u32[]{:S(2)}, u32[]{:S(2)}) %all-to-all-start) | async-done | bytes 65568 | tf_op jit(solution)/shard_map/all_to_all | solution.py:635
  19.9 4.4 %shard_map.102 = (f32[8,16,16,128]{3,2,1,0:T(8,128)}, f32[32,16,128]{2,1,0:T(8,128)}) custom-call(f32[256,16,128]{2,1,0:T(8,128)} %shard_map.101.refs_0_, f32[32,16,128]{2,1,0:T(8,128)S(1)} %collective-permute-done.refs_1_, f32[8,128,128]{2,1,0:T(8,128)} %refs_3_.4, s32[32,1,512]{2,1,0:T(1,128)S(1)} %all-to-all-done.refs_3_.refs_0_), custom_call_target="tpu_custom_call" | custom-call | flops 402653184 | bytes 4194304 | tf_op jit(solution)/shard_map/pallas_call | solution.py:48
  24.2 0.0 copy-start.4
  24.3 0.0 copy-start
  24.3 3.7 %all-to-all-start.1 = ((f32[8,256,128]{2,1,0:T(8,128)}), f32[8,256,128]{2,1,0:T(8,128)S(1)}, u32[]{:S(2)}, u32[]{:S(2)}) async-start(f32[8,256,128]{2,1,0:T(8,128)} %bitcast.14), calls=%async_computation.1 | async-start | bytes 2097152 | tf_op jit(solution)/shard_map/all_to_all | solution.py:691
  28.0 0.1 reshape.14
  28.2 0.1 reshape.15.refs_0_
  28.3 0.6 collective-permute-start.1
  28.9 6.0 %shard_map.103 = (bf16[10,256,192]{2,1,0:T(8,128)(2,1)}, bf16[128,384]{1,0:T(8,128)(2,1)}, bf16[1024,256]{1,0:T(8,128)(2,1)}, f32[4,128]{1,0:T(4,128)S(1)}) custom-call(s32[8,2,512]{2,1,0:T(2,128)S(1)} %reshape.15.refs_0_, s32[16,128]{1,0:T(8,128)S(1)} %dynamic-slice_bitcast_fusion.refs_1_, f32[8,128,128]{2,1,0:T(8,128)S(1)} %copy-done, ...), custom_call_target="tpu_custom_call" | custom-call | flops 1610612736 | bytes 4194304 | tf_op jit(solution)/shard_map/pallas_call | solution.py:48
  34.9 2.1 %collective-permute-done.1.refs_5_ = f32[32,16,128]{2,1,0:T(8,128)S(1)} collective-permute-done((f32[32,16,128]{2,1,0:T(8,128)S(1)}, f32[32,16,128]{2,1,0:T(8,128)S(1)}, u32[]{:S(2)}, u32[]{:S(2)}) %collective-permute-start.1) | collective-permute-done | bytes 262176 | tf_op jit(solution)/shard_map/ppermute | solution.py:584
  37.0 5.4 %all-to-all-done.1.refs_1_ = f32[8,256,128]{2,1,0:T(8,128)S(1)} async-done(((f32[8,256,128]{2,1,0:T(8,128)}), f32[8,256,128]{2,1,0:T(8,128)S(1)}, u32[]{:S(2)}, u32[]{:S(2)}) %all-to-all-start.1) | async-done | bytes 1048608 | tf_op jit(solution)/shard_map/all_to_all | solution.py:691
  42.4 6.6 %shard_map.104 = (f32[16,136,128]{2,1,0:T(8,128)}, f32[32,16,128]{2,1,0:T(8,128)}) custom-call(s32[32,1,512]{2,1,0:T(1,128)} %copy-done.2, f32[8,256,128]{2,1,0:T(8,128)S(1)} %all-to-all-done.1.refs_1_, f32[8,128,128]{2,1,0:T(8,128)S(1)} %copy-done.1, f32[8,128,128]{2,1,0:T(8,128)S(1)} %copy-done, f32[32,16,128]{2,1,0:T(8,128)} %refs_3_.5, ...), custom_call_target="tpu_custom_call" | custom-call | flops 805306368 | bytes 4194304 | tf_op jit(solution)/shard_map/pallas_call | solution.py:48
  49.0 0.0 copy-start.5
  49.0 5.3 %all-to-all-start.2 = ((f32[16,136,128]{2,1,0:T(8,128)}), f32[16,136,128]{2,1,0:T(8,128)S(1)}, u32[]{:S(2)}, u32[]{:S(2)}) async-start(f32[16,136,128]{2,1,0:T(8,128)} %get-tuple-element.30), calls=%async_computation.2 | async-start | bytes 2228224 | tf_op jit(solution)/shard_map/all_to_all | solution.py:691
  54.3 0.6 collective-permute-start.3
  54.8 26.0 %all-to-all-done.2.arrived_ref.refs_1_ = f32[16,136,128]{2,1,0:T(8,128)S(1)} async-done(((f32[16,136,128]{2,1,0:T(8,128)}), f32[16,136,128]{2,1,0:T(8,128)S(1)}, u32[]{:S(2)}, u32[]{:S(2)}) %all-to-all-start.2) | async-done | bytes 1114144 | tf_op jit(solution)/shard_map/all_to_all | solution.py:691
  80.9 0.6 collective-permute-start.2
  81.4 1.7 %shard_map.106.second_ref = f32[32,16,128]{2,1,0:T(8,128)S(1)} custom-call(s32[32,1,512]{2,1,0:T(1,128)} %copy-done.2, f32[16,136,128]{2,1,0:T(8,128)S(1)} %all-to-all-done.2.arrived_ref.refs_1_, f32[8,128,128]{2,1,0:T(8,128)S(1)} %copy-done.1, f32[32,16,128]{2,1,0:T(8,128)} %refs_3_.5, f32[32,16,128]{2,1,0:T(8,128)S(1)} %collective-permute-done.3.refs_4_), custom_call_target="tpu_custom_call" | custom-call | flops 402653184 | bytes 4194304 | tf_op jit(solution)/shard_map/pallas_call | solution.py:48
  83.2 1.3 %collective-permute-done.2.other_ref = f32[4,128]{1,0:T(4,128)S(1)} collective-permute-done((f32[4,128]{1,0:T(4,128)S(1)}, f32[4,128]{1,0:T(4,128)S(1)}, u32[]{:S(2)}, u32[]{:S(2)}) %collective-permute-start.2) | collective-permute-done | bytes 2080 | tf_op jit(solution)/shard_map/ppermute | solution.py:775
  84.5 1.0 %shard_map.107 = f32[32,16,128]{2,1,0:T(8,128)} custom-call(f32[4,128]{1,0:T(4,128)S(1)} %get-tuple-element.31.mine_ref, f32[4,128]{1,0:T(4,128)S(1)} %collective-permute-done.2.other_ref, f32[4,128]{1,0:T(4,128)S(1)} %get-tuple-element.33.scale_ref, f32[32,16,128]{2,1,0:T(8,128)S(1)} %shard_map.106.second_ref), custom_call_target="tpu_custom_call" | custom-call | tf_op jit(solution)/shard_map/pallas_call | solution.py:48
  (17 shorter events, 0.1 us)
Async XLA Ops:
  1.8 18.1 %collective-permute-start = (f32[32,16,128]{2,1,0:T(8,128)}, f32[32,16,128]{2,1,0:T(8,128)S(1)}, u32[]{:S(2)}, u32[]{:S(2)}) collective-permute-start(f32[32,16,128]{2,1,0:T(8,128)} %start_in.1), channel_id=1, source_target_pairs={{0,8},{1,9},{2,10},{3,11},{4,12},{5,13},{6,14},{7,15},{8,0},{9,1},... | collective-permute-start | bytes 786440 | tf_op jit(solution)/shard_map/ppermute | solution.py:634
  1.9 18.0 %all-to-all-start = ((s32[32,1,512]{2,1,0:T(1,128)}), s32[32,1,512]{2,1,0:T(1,128)S(1)}, u32[]{:S(2)}, u32[]{:S(2)}) async-start(s32[32,1,512]{2,1,0:T(1,128)} %shard_map.100), calls=%async_computation | async-start | bytes 131072 | tf_op jit(solution)/shard_map/all_to_all | solution.py:635
  19.9 8.1 %copy-start.2 = (s32[32,1,512]{2,1,0:T(1,128)}, s32[32,1,512]{2,1,0:T(1,128)S(1)}, u32[]{:S(2)}) copy-start(s32[32,1,512]{2,1,0:T(1,128)S(1)} %all-to-all-done.refs_3_.refs_0_) | copy-start | bytes 196612
  24.2 4.1 %copy-start.4 = (f32[32,16,128]{2,1,0:T(8,128)S(1)}, f32[32,16,128]{2,1,0:T(8,128)}, u32[]{:S(2)}) copy-start(f32[32,16,128]{2,1,0:T(8,128)} %get-tuple-element.25) | copy-start | bytes 786436
  24.3 4.7 %copy-start = (f32[8,128,128]{2,1,0:T(8,128)S(1)}, f32[8,128,128]{2,1,0:T(8,128)}, u32[]{:S(2)}) copy-start(f32[8,128,128]{2,1,0:T(8,128)} %refs_3_.4) | copy-start | bytes 1572868
  24.3 4.6 %copy-start.1 = (f32[8,128,128]{2,1,0:T(8,128)S(1)}, f32[8,128,128]{2,1,0:T(8,128)}, u32[]{:S(2)}) copy-start(f32[8,128,128]{2,1,0:T(8,128)} %refs_2_.7) | copy-start | bytes 1572868
  24.3 4.6 %copy-start.3 = (f32[8,128,128]{2,1,0:T(8,128)S(1)}, f32[8,128,128]{2,1,0:T(8,128)}, u32[]{:S(2)}) copy-start(f32[8,128,128]{2,1,0:T(8,128)} %refs_3_.3) | copy-start | bytes 1572868
  24.3 18.1 %all-to-all-start.1 = ((f32[8,256,128]{2,1,0:T(8,128)}), f32[8,256,128]{2,1,0:T(8,128)S(1)}, u32[]{:S(2)}, u32[]{:S(2)}) async-start(f32[8,256,128]{2,1,0:T(8,128)} %bitcast.14), calls=%async_computation.1 | async-start | bytes 2097152 | tf_op jit(solution)/shard_map/all_to_all | solution.py:691
  28.3 8.7 %collective-permute-start.1 = (f32[32,16,128]{2,1,0:T(8,128)S(1)}, f32[32,16,128]{2,1,0:T(8,128)S(1)}, u32[]{:S(2)}, u32[]{:S(2)}) collective-permute-start(f32[32,16,128]{2,1,0:T(8,128)S(1)} %copy-done.4), channel_id=1, source_target_pairs={{0,16},{16,0},{1,17},{17,1},{2,18},{18,2},{3,19},{19,3},{4,20},{20... | collective-permute-start | bytes 786440 | tf_op jit(solution)/shard_map/ppermute | solution.py:584
  49.0 5.3 %copy-start.5 = (f32[32,16,128]{2,1,0:T(8,128)S(1)}, f32[32,16,128]{2,1,0:T(8,128)}, u32[]{:S(2)}) copy-start(f32[32,16,128]{2,1,0:T(8,128)} %get-tuple-element.34) | copy-start | bytes 786436
  49.0 31.9 %all-to-all-start.2 = ((f32[16,136,128]{2,1,0:T(8,128)}), f32[16,136,128]{2,1,0:T(8,128)S(1)}, u32[]{:S(2)}, u32[]{:S(2)}) async-start(f32[16,136,128]{2,1,0:T(8,128)} %get-tuple-element.30), calls=%async_computation.2 | async-start | bytes 2228224 | tf_op jit(solution)/shard_map/all_to_all | solution.py:691
  54.3 27.2 %collective-permute-start.3 = (f32[32,16,128]{2,1,0:T(8,128)S(1)}, f32[32,16,128]{2,1,0:T(8,128)S(1)}, u32[]{:S(2)}, u32[]{:S(2)}) collective-permute-start(f32[32,16,128]{2,1,0:T(8,128)S(1)} %copy-done.5), channel_id=1, source_target_pairs={{0,16},{16,0},{1,17},{17,1},{2,18},{18,2},{3,19},{19,3},{4,20},{20... | collective-permute-start | bytes 786440 | tf_op jit(solution)/shard_map/ppermute | solution.py:584
  80.9 3.6 %collective-permute-start.2 = (f32[4,128]{1,0:T(4,128)S(1)}, f32[4,128]{1,0:T(4,128)S(1)}, u32[]{:S(2)}, u32[]{:S(2)}) collective-permute-start(f32[4,128]{1,0:T(4,128)S(1)} %get-tuple-element.32), channel_id=1, source_target_pairs={{0,16},{16,0},{1,17},{17,1},{2,18},{18,2},{3,19},{19,3},{4,20},{20... | collective-permute-start | bytes 6152 | tf_op jit(solution)/shard_map/ppermute | solution.py:775

commit v7 on v6

--- a/solution.py
+++ b/solution.py
@@ -113,7 +113,7 @@
 
 def request_kernel(sizes, *refs):
     rows, n_rows, cap, n_tiles, n_diag = sizes
-    inputs, payload_ref, held, sems = refs[:5], refs[5], refs[6:11], refs[11]
+    inputs, (list_ref, index_ref, place_ref), held, sems = refs[:5], refs[5:8], refs[8:13], refs[13]
     finish(
         started([pltpu.make_async_copy(i, h, sems.at[n]) for n, (i, h) in enumerate(zip(inputs, held))])
     )
@@ -157,39 +157,31 @@
                 mine, by_rank, precision=HIGH, preferred_element_type=jnp.float32
             )
     lists = (lists + 0.5).astype(jnp.int32)
-    common = [group_ref[...], diag_ref[...]]
-    common += [tile_ref[k : k + 1, :] for k in range(width_k + 2)]
-    common += [owner_row(k) * rows + local_ref[k : k + 1, :] for k in range(width_k)]
-    common += half_places + places
-    spare = payload_ref.shape[2] - LANES - len(common) * rows
-    if spare:
-        common.append(jnp.zeros((1, spare), jnp.int32))
-    common = jnp.concatenate(common, axis=1)
-    for device in range(n_rows):
-        line = jnp.concatenate([lists[device : device + 1, :], common], axis=1)
-        for band in range(payload_ref.shape[0] // n_rows):
-            payload_ref[band * n_rows + device] = line
-
-
-def metadata_copies(meta_ref, request_ref, near_ref, sems):
-    n_rows, n_near = request_ref.shape[0], near_ref.shape[0]
-    band, row = lax.axis_index("band"), lax.axis_index("rows")
-    last = meta_ref.shape[0] // n_rows - 1
-    if n_near == 1:
-        nexts = [last - band]
-    else:
-        nexts = [jnp.minimum(band + 1, last), jnp.maximum(band - 1, 0)]
-    copies = [
-        pltpu.make_async_copy(meta_ref.at[pl.ds(band * n_rows, n_rows)], request_ref, sems.at[0])
-    ]
-    for n, other in enumerate(nexts):
-        source = meta_ref.at[pl.ds(other * n_rows + row, 1)]
-        copies.append(pltpu.make_async_copy(source, near_ref.at[pl.ds(n, 1)], sems.at[1 + n]))
-    return copies
+    upper = lax.axis_index("rows") >= half
+    lists = jnp.where(upper, lists[half:], lists[:half])
+
+    def joined(parts, wide):
+        spare = wide - len(parts) * rows
+        if spare:
+            parts = [*parts, jnp.zeros((1, spare), jnp.int32)]
+        return jnp.concatenate(parts, axis=1)
+
+    index = [group_ref[...], diag_ref[...]]
+    index += [tile_ref[k : k + 1, :] for k in range(width_k + 2)]
+    index += [owner_row(k) * rows + local_ref[k : k + 1, :] for k in range(width_k)]
+    index = joined(index, index_ref.shape[2])
+    index_ref[0] = index
+    place_ref[0] = joined(half_places + places, place_ref.shape[2])
+    for device in range(half):
+        list_ref[device] = jnp.concatenate([lists[device : device + 1, :], index], axis=1)
+
+
+def copies_of(pairs, sems):
+    return started([pltpu.make_async_copy(i, h, sems.at[n]) for n, (i, h) in enumerate(pairs)])
 
 
 def band_field(rows, width_k, way, n_ways):
-    field = LANES + (2 + width_k) * rows
+    field = (2 + width_k) * rows
     if n_ways == 1:
         return field + jnp.where(lax.axis_index("band") == 0, 0, rows)
     return field + way * rows
@@ -232,43 +224,39 @@
 
 def first_kernel(sizes, width_k, n_band, *refs):
     rows, n_rows, cap, n_tiles, n_rhs = sizes
-    product_in, mirror_ref, tile_in, meta_ref, send_out = refs[:5]
-    band_out, refs = refs[5 : 5 + n_band], refs[5 + n_band :]
-    product_ref, tile_ref, request_ref, near_ref, send_ref = refs[:5]
-    band_refs, (load_sems, tile_sems, meta_sems, send_sems) = refs[5 : 5 + n_band], refs[5 + n_band :]
-    tile_loads = table_loads(tile_in, tile_ref, tile_sems)
-    metadata = started(metadata_copies(meta_ref, request_ref, near_ref, meta_sems))
-    loads = []
-    for tile in range(n_tiles):
-        place = pl.ds(tile * rows, rows)
-        source, target = product_in.at[place], product_ref.at[0, place]
-        loads.append(pltpu.make_async_copy(source, target, load_sems.at[tile]))
-    started(loads)
+    product_in, mirror_ref, tile_ref, list_in, near_in, send_out = refs[:6]
+    band_out, refs = refs[6 : 6 + n_band], refs[6 + n_band :]
+    product_ref, list_ref, near_ref, send_ref = refs[:4]
+    band_refs, (load_sems, meta_sems, send_sems) = refs[4 : 4 + n_band], refs[4 + n_band :]
+    list_in = list_in.at[:, :, pl.ds(0, LANES)]
+    metadata = copies_of(((list_in, list_ref), (near_in, near_ref)), meta_sems)
+    places = [pl.ds(tile * rows, rows) for tile in range(n_tiles)]
+    loads = [(product_in.at[place], product_ref.at[0, place]) for place in places]
+    loads = copies_of(loads, load_sems)
     values = mirror_ref[...].reshape(rows * n_rhs, -1)
-    table_products(values, tile_ref, product_ref.at[1], None, tile_loads)
+    table_products(values, tile_ref, product_ref.at[1])
     finish(metadata)
     finish(loads)
+    copies = []
+    pack_bands(sizes, width_k, product_ref.at[0], near_ref, band_refs)
     half = n_rows // 2
-    base = jnp.where(lax.axis_index("rows") >= half, half, 0)
-    copies = []
+    for n, (ref, out) in enumerate(zip(band_refs, band_out)):
+        copies += started([pltpu.make_async_copy(ref, out, send_sems.at[half + n])])
     for device in range(half):
         for slot in range(2 * cap):
             side, rank = slot // cap, slot % cap
-            code = request_ref[base + device, 0, side * (LANES // 2) + rank]
+            code = list_ref[device, 0, side * (LANES // 2) + rank]
             send_ref[device, slot] = product_ref[side, below(code, rows * n_tiles)]
         copy = pltpu.make_async_copy(send_ref.at[device], send_out.at[device], send_sems.at[device])
         copies += started([copy])
-    pack_bands(sizes, width_k, product_ref.at[0], near_ref, band_refs)
-    for n, (ref, out) in enumerate(zip(band_refs, band_out)):
-        copies += started([pltpu.make_async_copy(ref, out, send_sems.at[half + n])])
     finish(copies)
 
 
-def place(place_ref, values, n_rhs):
+def place(place_ref, values, n_rhs, n_parts):
     per_tile = LANES // n_rhs
     length = place_ref.shape[0] // per_tile
     parts, rest = [], values
-    for _ in range(3):
+    for _ in range(n_parts):
         part = rest.astype(jnp.bfloat16)
         rest = rest - part.astype(jnp.float32)
         parts.append(part)
@@ -281,7 +269,7 @@
             parts,
             preferred_element_type=jnp.float32,
         )
-        chosen = chosen[:, :LANES] + chosen[:, LANES : 2 * LANES] + chosen[:, 2 * LANES :]
+        chosen = sum(chosen[:, n * LANES : (n + 1) * LANES] for n in range(n_parts))
         result = jnp.where((lane >= spot * n_rhs) & (lane < (spot + 1) * n_rhs), chosen, result)
     return result
 
@@ -292,9 +280,9 @@
 
 def count_kernel(sizes, width_k, n_func, *refs):
     rows, n_rows, cap, n_tiles, n_rhs = sizes
-    field_ref, list_ref, tile_ref, table_ref, inverse_ref = refs[:5]
-    count_out, functional_out, placing_out, scale_ref = refs[5:9]
-    count_ref, functional_ref, placing_ref, sems = refs[9:]
+    field_ref, list_ref, mirror_list_ref, tile_ref, table_ref, inverse_ref = refs[:6]
+    count_out, functional_out, placing_out, scale_ref = refs[6:10]
+    count_ref, functional_ref, placing_ref, sems = refs[10:]
     n_groups, n_blocks = count_ref.shape[1:]
     slots, band_rows = n_rows * cap, n_rows * rows
     copies = []
@@ -318,35 +306,44 @@
         functional_ref[d * n_func : (d + 1) * n_func, :] = left_operand(solved)
     send(functional_ref, functional_out)
 
-    lists = list_ref[...]
-    asker = lax.broadcasted_iota(jnp.int32, lists.shape, 0)
-    codes = asker * rows + below(over(lists, rows * n_tiles), rows)
-    codes = jnp.where(lists > 0, codes, -1).astype(jnp.float32)
-    spread = lax.broadcasted_iota(jnp.int32, (slots, n_rows), 0)
-    spread = lax.div(spread, cap) == lax.broadcasted_iota(jnp.int32, (slots, n_rows), 1)
-    codes = jnp.dot(
-        jnp.where(spread, 1.0, 0.0), codes, precision=HIGH, preferred_element_type=jnp.float32
-    )
-    rank = lax.rem(lax.broadcasted_iota(jnp.int32, codes.shape, 0), cap)
-    lane = lax.broadcasted_iota(jnp.int32, codes.shape, 1)
-    asked = jnp.sum(jnp.where(rank == lane, codes, 0.0), axis=1, keepdims=True)
-    asked = jnp.where(asked < 0.0, asked - 0.5, asked + 0.5).astype(jnp.int32)
+    half = n_rows // 2
+    upper = lax.axis_index("rows") >= half
+    asked = []
+    for ref, first, lanes in (
+        (list_ref, jnp.where(upper, half, 0), 0),
+        (mirror_list_ref, jnp.where(upper, 0, half), LANES // 2),
+    ):
+        lists = ref[...]
+        asker = first + lax.broadcasted_iota(jnp.int32, lists.shape, 0)
+        codes = asker * rows + below(over(lists, rows * n_tiles), rows)
+        codes = jnp.where(lists > 0, codes, -1).astype(jnp.float32)
+        spread = lax.broadcasted_iota(jnp.int32, (slots // 2, half), 0)
+        spread = lax.div(spread, cap) == lax.broadcasted_iota(jnp.int32, (slots // 2, half), 1)
+        codes = jnp.dot(
+            jnp.where(spread, 1.0, 0.0), codes, precision=HIGH, preferred_element_type=jnp.float32
+        )
+        rank = lax.rem(lax.broadcasted_iota(jnp.int32, codes.shape, 0), cap)
+        lane = lax.broadcasted_iota(jnp.int32, codes.shape, 1)
+        codes = jnp.sum(jnp.where(rank + lanes == lane, codes, 0.0), axis=1, keepdims=True)
+        asked.append(jnp.where(codes < 0.0, codes - 0.5, codes + 0.5).astype(jnp.int32))
+    asked = jnp.concatenate(asked, axis=0)
     own = lax.axis_index("rows") * rows + lax.broadcasted_iota(jnp.int32, (rows, 1), 0)
     band = lax.axis_index("band")
 
-    def field(n, which):
-        return field_ref[n, pl.ds(which, 1), :]
+    def field(n, side):
+        return field_ref[n, side : side + 1, :]
 
     row_ids = lax.broadcasted_iota(jnp.int32, (1, band_rows), 1)
     sides = []
-    for which, targets in ((band, jnp.concatenate([asked, own], axis=0)), (1 - band, own)):
-        across = jnp.where(which == 0, field(2 + width_k, 1), field(3 + width_k, 0))
-        takers = [field(2 + k, which) * n_groups + field(0, which) for k in range(width_k)]
-        takers.append(across * n_groups + field(0, 1 - which))
+    for side, targets in ((0, jnp.concatenate([asked, own], axis=0)), (1, own)):
+        first = band == side
+        across = jnp.where(first, field(2 + width_k, 1 - side), field(3 + width_k, 1 - side))
+        takers = [field(2 + k, side) * n_groups + field(0, side) for k in range(width_k)]
+        takers.append(across * n_groups + field(0, 1 - side))
         takers = jnp.concatenate(takers, axis=1)
-        origins = [field(4 + width_k + k, which) for k in range(width_k)] + [row_ids]
+        origins = [field(4 + width_k + k, side) for k in range(width_k)] + [row_ids]
         hits = one_hot(targets, jnp.concatenate(origins, axis=1))
-        sides.append((takers, hits, field(0, which)))
+        sides.append((takers, hits, field(0, side)))
     for t in range(n_tiles):
         found = []
         for takers, hits, _ in sides:
@@ -372,20 +369,22 @@
     device, order = lax.div(order, 2 * depth), lax.rem(order, 2 * depth)
     side, order = lax.div(order, depth), lax.rem(order, depth)
     order = side * band_rows + device * rows + spot * depth + order
-    member = [one_hot(ids, field(0, which)) for which in range(2)]
+    member = [
+        one_hot(ids, jnp.where(band == which, field(0, 0), field(0, 1))) for which in range(2)
+    ]
     placing = jnp.zeros(placing_ref.shape, jnp.float32)
     for which in range(2):
         placing = placing + dot_nt(one_hot(order, row_ids + which * band_rows), member[which])
     placing_ref[...] = placing.astype(jnp.bfloat16)
     send(placing_ref, placing_out)
     whole = jnp.zeros((n_groups, 1), jnp.float32)
-    for which in range(2):
+    for side in range(2):
         sums = jnp.zeros((1, band_rows), jnp.float32)
         for d in range(n_diag):
-            sums = jnp.where(field(1, which) == d, totals[d], sums)
-        weighted = jnp.where(ids == field(0, which), sums, 0.0)
+            sums = jnp.where(field(1, side) == d, totals[d], sums)
+        weighted = jnp.where(ids == field(0, side), sums, 0.0)
         whole = whole + jnp.sum(weighted, axis=1, keepdims=True)
-    scale = place(placing_ref, jnp.broadcast_to(whole, (n_groups, LANES)), n_rhs)
+    scale = place(placing_ref, jnp.broadcast_to(whole, (n_groups, LANES)), n_rhs, 3)
     mine = jnp.zeros(scale_ref.shape, jnp.float32)
     here = lax.axis_index("rows") * 2 + band
     for n in range(2 * n_rows):
@@ -416,34 +415,33 @@
 
 
 def middle_kernel(sizes, width_k, n_band, dense, *refs):
-    meta_ref, arrived_ref, inverse_ref, tile_ref = refs[:4]
-    terms_in, refs = refs[4 : 5 + n_band], refs[5 + n_band :]
+    metadata_in, arrived_ref, inverse_ref, tile_ref = list(refs[:5]), *refs[5:8]
+    for n in (2, 3):
+        metadata_in[n] = metadata_in[n].at[:, :, pl.ds(0, LANES)]
+    terms_in, refs = refs[8 : 9 + n_band], refs[9 + n_band :]
     extra, refs = (refs[:3], refs[3:]) if dense else ((), refs)
     send_out, band_out, refs = refs[0], refs[1 : 1 + n_band], refs[1 + n_band :]
-    sum_ref, product_ref, request_ref, near_ref, send_ref = refs[:5]
-    terms, band_refs, refs = refs[5 : 6 + n_band], refs[6 + n_band : 6 + 2 * n_band], refs[6 + 2 * n_band :]
+    metadata, sum_ref, product_ref, send_ref = refs[:5], *refs[5:8]
+    place_ref, index_ref, list_ref, mirror_list_ref, near_ref = metadata
+    terms, band_refs, refs = refs[8 : 9 + n_band], refs[9 + n_band : 9 + 2 * n_band], refs[9 + 2 * n_band :]
     term_sems, meta_sems, send_sems, refs = *refs[:3], refs[3:]
     right_ref = terms[0]
     rows, n_rows, cap, n_tiles, n_rhs = sizes
-    body = cap * n_rhs
-    metadata = started(metadata_copies(meta_ref, request_ref, near_ref, meta_sems))
-    pairs = enumerate(zip(terms_in, terms))
-    later = started([pltpu.make_async_copy(i, h, term_sems.at[n]) for n, (i, h) in pairs])
+    body, half = cap * n_rhs, n_rows // 2
+    metadata = copies_of(zip(metadata_in, metadata), meta_sems)
+    later = copies_of(zip(terms_in, terms), term_sems)
     fetched = []
     if dense:
-        held, extra_sems, value_ref, spread_ref = refs[:3], refs[3], refs[4], refs[5]
+        held, extra_sems, value_ref, spread_ref, result_ref = refs[:3], *refs[3:]
         n_diag = inverse_ref.shape[0]
-        pairs = enumerate(zip(extra, held))
-        fetched = started([pltpu.make_async_copy(i, h, extra_sems.at[n]) for n, (i, h) in pairs])
+        fetched = copies_of(zip(extra, held), extra_sems)
     finish(metadata)
-    mine = lax.axis_index("rows")
 
     def slots(row):
-        field = LANES + (4 + 2 * width_k) * rows + row
-        return [request_ref[mine, 0, field + k * rows] for k in range(width_k)]
+        return [place_ref[0, 0, k * rows + row] for k in range(width_k)]
 
     def diags(row):
-        return request_ref[mine, 0, LANES + rows + row]
+        return index_ref[0, 0, rows + row]
 
     gather_solve(sizes, slots, diags, arrived_ref, later, terms, inverse_ref, sum_ref, product_ref)
     table_products(sum_ref[...], tile_ref, product_ref)
@@ -452,33 +450,34 @@
     def send(source, target):
         copies.extend(started([pltpu.make_async_copy(source, target, send_sems.at[len(copies)])]))
 
-    for owner in range(n_rows):
-        for rank in range(cap):
-            block = product_ref[below(request_ref[owner, 0, rank], rows * n_tiles)]
-            send_ref[owner, rank * n_rhs : (rank + 1) * n_rhs, :] = block
-        if not dense:
-            send(send_ref.at[owner], send_out.at[owner])
-        else:
-            send(send_ref.at[owner, pl.ds(0, body)], send_out.at[owner, pl.ds(0, body)])
     pack_bands(sizes, width_k, product_ref, near_ref, band_refs)
     for ref, out in zip(band_refs, band_out):
         send(ref, out)
+    upper = lax.axis_index("rows") >= half
+    codes, order = [], 0
+    for ref, first, lanes in (
+        (list_ref, jnp.where(upper, half, 0), 0),
+        (mirror_list_ref, jnp.where(upper, 0, half), LANES // 2),
+    ):
+        for device in range(half):
+            for rank in range(cap):
+                code = ref[device, 0, lanes + rank]
+                codes.append(code)
+                block = product_ref[below(code, rows * n_tiles)]
+                send_ref[order, rank * n_rhs : (rank + 1) * n_rhs, :] = block
+            target = send_out.at[first + device]
+            send(send_ref.at[order], target.at[pl.ds(0, body)] if dense else target)
+            order += 1
     if dense:
         finish(fetched)
-        kinds = []
-        for owner in range(n_rows):
-            for rank in range(cap):
-                code = over(request_ref[owner, 0, rank], rows * n_tiles * rows)
-                kinds.append(below(code, n_diag))
+        kinds = [below(over(code, rows * n_tiles * rows), n_diag) for code in codes]
         kinds += [diags(row) for row in range(rows)]
-        kinds += [near_ref[0, 0, LANES + rows + row] for row in range(rows)]
+        kinds += [near_ref[0, 0, rows + row] for row in range(rows)]
         result = coarse_parts(
             sizes, kinds, held, right_ref, send_ref, band_refs, value_ref, spread_ref
         )
-        depth = result.shape[0] // n_rows
-        for owner in range(n_rows):
-            send_ref[owner, body:, :] = result[owner * depth : (owner + 1) * depth, :]
-        send(send_ref.at[:, pl.ds(body, depth)], send_out.at[:, pl.ds(body, depth)])
+        result_ref[...] = result.reshape(result_ref.shape)
+        send(result_ref, send_out.at[:, pl.ds(body, result_ref.shape[1])])
     finish(copies)
 
 
@@ -491,7 +490,7 @@
     functional = functional_ref[...]
     done = 0
     for owner in range(0, n_rows, 2):
-        values = [send_ref[owner + more, :body, :] for more in range(2)]
+        values = [send_ref[owner + more] for more in range(2)]
         values = jnp.concatenate(values, axis=0)
         value_ref[:, done : done + 2 * body] = dot_nt(functional, right_operand(values))
         done += 2 * body
@@ -523,7 +522,7 @@
     partial = jnp.dot(
         jnp.concatenate(halves(partial), axis=1), same, preferred_element_type=jnp.float32
     )
-    return place(place_ref, partial, n_rhs)
+    return place(place_ref, partial, n_rhs, 2)
 
 
 def part_kernel(arrived_ref, mine_ref, other_ref):
@@ -538,24 +537,21 @@
 
 
 def last_kernel(sizes, width_k, n_band, *refs):
-    meta_ref, arrived_ref, inverse_ref = refs[:3]
-    terms_in, refs = refs[3 : 4 + n_band], refs[4 + n_band :]
-    second_ref, sum_ref, product_ref, mine_ref = refs[:4]
-    terms, (term_sems, meta_sem) = refs[4 : 5 + n_band], refs[5 + n_band :]
-    rows, n_rows = sizes[:2]
-    place = lax.axis_index("band") * n_rows + lax.axis_index("rows")
-    metadata = pltpu.make_async_copy(meta_ref.at[pl.ds(place, 1)], mine_ref, meta_sem)
-    metadata.start()
-    pairs = enumerate(zip(terms_in, terms))
-    later = started([pltpu.make_async_copy(i, h, term_sems.at[n]) for n, (i, h) in pairs])
-    metadata.wait()
+    metadata_in, arrived_ref, inverse_ref = refs[:2], *refs[2:4]
+    terms_in, refs = refs[4 : 5 + n_band], refs[5 + n_band :]
+    second_ref, metadata, sum_ref, product_ref = refs[0], refs[1:3], *refs[3:5]
+    place_ref, index_ref = metadata
+    terms, (term_sems, meta_sems) = refs[5 : 6 + n_band], refs[6 + n_band :]
+    rows = sizes[0]
+    metadata = copies_of(zip(metadata_in, metadata), meta_sems)
+    later = copies_of(zip(terms_in, terms), term_sems)
+    finish(metadata)
 
     def slots(row):
-        field = LANES + (4 + 3 * width_k) * rows + row
-        return [mine_ref[0, 0, field + k * rows] for k in range(width_k)]
+        return [place_ref[0, 0, (width_k + k) * rows + row] for k in range(width_k)]
 
     def diags(row):
-        return mine_ref[0, 0, LANES + rows + row]
+        return index_ref[0, 0, rows + row]
 
     gather_solve(sizes, slots, diags, arrived_ref, later, terms, inverse_ref, sum_ref, product_ref)
     second_ref[...] = sum_ref[...].reshape(second_ref.shape)
@@ -621,18 +617,31 @@
     my_row = lax.axis_index("rows")
 
     half = n_rows // 2
-    wide = LANES + -(-(4 + 4 * width_k) * rows // LANES) * LANES
+    wide = -(-(4 + 2 * width_k) * rows // LANES) * LANES
+    place_wide = -(-2 * width_k * rows // LANES) * LANES
     index_shapes = [(width_k, rows), (width_k, rows), (width_k + 2, rows), (1, rows), (1, rows)]
-    payload = call(
+    halves_of_rows = [list(range(half)), list(range(half, n_rows))]
+    to_mirror = [(i, (i + half) % n_rows) for i in range(n_rows)]
+    mirror = lax.ppermute(start_iterate, "rows", to_mirror)
+    lists, index, places = call(
         functools.partial(request_kernel, (rows, n_rows, cap, n_tiles, n_diag)),
-        jax.ShapeDtypeStruct((n_dev, 1, wide), i32),
+        (
+            jax.ShapeDtypeStruct((half, 1, LANES + wide), i32),
+            jax.ShapeDtypeStruct((1, 1, wide), i32),
+            jax.ShapeDtypeStruct((1, 1, place_wide), i32),
+        ),
         [HBM] * 5,
-        VMEM,
+        [VMEM] * 3,
         [*[pltpu.VMEM(shape, i32) for shape in index_shapes], pltpu.SemaphoreType.DMA((5,))],
     )(source_owner.T, source_local.T, tile_index.T, diag_index[None], aggregate_map.T)
-    payload, to_mirror = lax.optimization_barrier((payload, start_iterate))
-    mirror = lax.ppermute(to_mirror, "rows", [(i, (i + half) % n_rows) for i in range(n_rows)])
-    meta = lax.all_to_all(payload, ("band", "rows"), split_axis=0, concat_axis=0, tiled=True)
+    lists = lax.all_to_all(
+        lists, "rows", split_axis=0, concat_axis=0, tiled=True, axis_index_groups=halves_of_rows
+    )
+    if n_bands == 2:
+        near = lax.ppermute(index, "band", [(0, 1), (1, 0)])
+    else:
+        ways = [[(b, (b + step) % n_bands) for b in range(n_bands)] for step in (-1, 1)]
+        near = jnp.concatenate([lax.ppermute(index, "band", way) for way in ways], axis=0)
 
     n_ways = 1 if n_bands == 2 else 2
     block = (rows, n_rhs, states)
@@ -640,8 +649,9 @@
     band_scratch = [pltpu.VMEM(block, f32)] * n_ways
     term_scratch = [pltpu.VMEM(block, f32)] * (1 + n_ways)
     term_sems = pltpu.SemaphoreType.DMA((1 + n_ways,))
-    meta_scratch = [pltpu.SMEM((n_rows, 1, wide), i32), pltpu.SMEM((n_ways, 1, wide), i32)]
-    meta_sems = pltpu.SemaphoreType.DMA((1 + n_ways,))
+    list_scratch = pltpu.SMEM((half, 1, LANES), i32)
+    near_scratch = pltpu.SMEM((n_ways, 1, wide), i32)
+    row_scratch = [pltpu.SMEM((1, 1, place_wide), i32), pltpu.SMEM((1, 1, wide), i32)]
     flat = rows * n_rhs
     sums = pltpu.VMEM((flat, states), f32)
     products = pltpu.VMEM((max(n_tiles, n_diag) * rows, n_rhs, states), f32)
@@ -667,26 +677,24 @@
     packed, *bands = call(
         functools.partial(first_kernel, sizes, width_k, n_ways),
         (jax.ShapeDtypeStruct((half, 2 * cap, n_rhs, states), f32), *band_shapes),
-        [HBM, VMEM, HBM, ANY],
+        [HBM, VMEM, VMEM, ANY, ANY],
         [HBM] * (1 + n_ways),
         [
             pltpu.VMEM((2, *made_shape), f32),
-            *table_scratch,
-            *meta_scratch,
+            list_scratch,
+            near_scratch,
             pltpu.VMEM((half, 2 * cap, n_rhs, states), f32),
             *band_scratch,
             pltpu.SemaphoreType.DMA((n_tiles,)),
-            table_sems,
-            meta_sems,
+            pltpu.SemaphoreType.DMA((2,)),
             pltpu.SemaphoreType.DMA((half + n_ways,)),
         ],
         work * n_tiles,
         4 << 20,
-    )(made, mirror, coupling_tiles, meta)
+    )(made, mirror, coupling_tiles, lists, near)
+    packed, late = lax.optimization_barrier((packed, lists))
     sends = (packed.reshape(half, 2 * cap * n_rhs, states), *bands)
     halves_of_rows = [list(range(half)), list(range(half, n_rows))]
-    late, *sends = lax.optimization_barrier((meta, *sends))
-
     def exchange(sends, groups=None):
         arrived = lax.all_to_all(
             sends[0], "rows", split_axis=0, concat_axis=0, tiled=True, axis_index_groups=groups
@@ -695,13 +703,18 @@
 
     arrived_blocks, arrived_bands = exchange(sends, halves_of_rows)
 
-    late = late.reshape(n_bands, n_rows, wide)
-    requests = lax.dynamic_index_in_dim(late[:, :, :LANES], my_band, 0, keepdims=False)
-    common = late[:, :, LANES:]
+    mirror_lists = lax.ppermute(late, "rows", to_mirror)
     extra, extra_scratch, tail = (), [], 0
     if dense:
-        fields = common[:, :, : (4 + 2 * width_k) * rows].reshape(n_bands, n_rows, -1, rows).transpose(2, 0, 1, 3)
-        fields = fields.reshape(-1, n_bands, n_rows * rows)
+        across = lax.ppermute(late, "band", [(0, 1), (1, 0)])
+        corner = [(b * n_rows + i, (1 - b) * n_rows + j) for b in range(2) for i, j in to_mirror]
+        corner = lax.ppermute(late, ("band", "rows"), corner)
+        near_half = jnp.stack([late, across])[:, :, 0, LANES:]
+        far_half = jnp.stack([mirror_lists, corner])[:, :, 0, LANES:]
+        upper = my_row >= half
+        fields = [jnp.where(upper, far_half, near_half), jnp.where(upper, near_half, far_half)]
+        fields = jnp.concatenate(fields, axis=1).reshape(2, n_rows, -1, rows).transpose(2, 0, 1, 3)
+        fields = fields.reshape(-1, 2, n_rows * rows)
         n_blocks = slots + 2 * rows
         length = n_dev * depth
         extra_shapes = [
@@ -718,7 +731,7 @@
                 jax.ShapeDtypeStruct(*placing_shape),
                 jax.ShapeDtypeStruct((depth, LANES), f32),
             ),
-            [VMEM] * 5,
+            [VMEM] * 6,
             [HBM, HBM, HBM, VMEM],
             [
                 pltpu.VMEM(*count_shape),
@@ -728,13 +741,14 @@
             ],
             4 * total_groups * n_tiles * n_dev * rows * n_blocks,
             4 << 20,
-        )(fields, requests, coupling_tiles, diag_table, inverse_table)
+        )(fields, late[:, 0, :LANES], mirror_lists[:, 0, :LANES], coupling_tiles, diag_table, inverse_table)
         extra = (functionals, counts, placing)
         extra_scratch = [
             *[pltpu.VMEM(*shape) for shape in extra_shapes],
             pltpu.SemaphoreType.DMA((3,)),
             pltpu.VMEM((n_diag * n_func, n_blocks * n_rhs), f32),
             pltpu.VMEM((n_blocks * n_func, LANES), f32),
+            pltpu.VMEM((n_rows, n_bands * depth, LANES), f32),
         ]
         tail = n_bands * depth
 
@@ -742,24 +756,31 @@
     sends = call(
         functools.partial(middle_kernel, sizes, width_k, n_ways, dense),
         (jax.ShapeDtypeStruct(send_shape, f32), *band_shapes),
-        [HBM] + [VMEM] * 3 + [HBM] + [ANY] * n_ways + [HBM] * len(extra),
+        [ANY] * 5 + [VMEM] * 3 + [HBM] + [ANY] * n_ways + [HBM] * len(extra),
         [HBM] * (1 + n_ways),
         [
+            *row_scratch,
+            list_scratch,
+            list_scratch,
+            near_scratch,
             sums,
             products,
-            *meta_scratch,
-            pltpu.VMEM(send_shape, f32),
+            pltpu.VMEM((n_rows, cap * n_rhs, states), f32),
             *term_scratch,
             *band_scratch,
             term_sems,
-            meta_sems,
+            pltpu.SemaphoreType.DMA((5,)),
             pltpu.SemaphoreType.DMA((n_rows + n_ways + 1,)),
             *extra_scratch,
         ],
         work * (n_tiles + n_diag),
         4 << 20,
     )(
-        meta,
+        places,
+        index,
+        lists,
+        mirror_lists,
+        near,
         arrived_blocks,
         inverse_table,
         coupling_tiles,
@@ -776,19 +797,19 @@
     second = call(
         functools.partial(last_kernel, sizes, width_k, n_ways),
         jax.ShapeDtypeStruct(block, f32),
-        [HBM] + [VMEM] * 2 + [HBM] + [ANY] * n_ways,
+        [ANY] * 2 + [VMEM] * 2 + [HBM] + [ANY] * n_ways,
         VMEM,
         [
+            *row_scratch,
             sums,
             products,
-            pltpu.SMEM((1, 1, wide), i32),
             *term_scratch,
             term_sems,
-            pltpu.SemaphoreType.DMA,
+            pltpu.SemaphoreType.DMA((2,)),
         ],
         work * n_diag,
         4 << 20,
-    )(meta, arrived_blocks, inverse_table, right_side, *arrived_bands)
+    )(places, index, arrived_blocks, inverse_table, right_side, *arrived_bands)
     if dense:
         return call(
             functools.partial(final_kernel, sizes),
@@ -799,10 +820,14 @@
 
     groups = aggregate_map[:, 0]
     own = jnp.arange(rows, dtype=i32)
-    groups_all = common[:, :, :rows]
-    diags_all = common[:, :, rows : 2 * rows]
-    codes = requests[:, :cap]
-    asked = lax.broadcasted_iota(i32, codes.shape, 0) * rows + codes // (rows * n_tiles) % rows
+    index_all = lax.all_gather(index, ("band", "rows"), axis=0, tiled=True)
+    index_all = index_all.reshape(n_bands, n_rows, wide)
+    groups_all, diags_all = index_all[:, :, :rows], index_all[:, :, rows : 2 * rows]
+    lanes = LANES // 2
+    codes = jnp.concatenate([lists[:, 0, :cap], mirror_lists[:, 0, lanes : lanes + cap]], axis=0)
+    asker = jnp.arange(n_rows, dtype=i32)
+    asker = jnp.where(my_row < half, asker, (asker + half) % n_rows)
+    asked = asker[:, None] * rows + codes // (rows * n_tiles) % rows
     asked = jnp.where(codes > 0, asked, -1).reshape(-1)
     table_sums = jnp.sum(diag_table, axis=(1, 2))
     diag_onehot = diags_all.reshape(-1, 1) == jnp.arange(n_diag, dtype=i32)[None]
@@ -810,9 +835,7 @@
     whole_diag = jnp.sum(
         jnp.where(groups[:, None] == groups_all.reshape(-1)[None], block_sums[None], 0.0), axis=1
     )
-    here = lax.dynamic_index_in_dim(common, my_row, 1, keepdims=False)
-    above = lax.dynamic_index_in_dim(here, jnp.minimum(my_band + 1, n_bands - 1), 0, keepdims=False)
-    below = lax.dynamic_index_in_dim(here, jnp.maximum(my_band - 1, 0), 0, keepdims=False)
+    above, below = near[0, 0], near[-1, 0]
     place_of = (2 + width_k) * rows
     band_tiles = jnp.stack([above[place_of : place_of + rows], below[place_of + rows : place_of + 2 * rows]])
     band_groups = jnp.stack([above[:rows], below[:rows]])

time: 85.9 us -> 86.3 us (level)
  starting transfers between devices: 17.3 us -> 26.5 us
  waiting for transfers between devices: 42.3 us -> 35.9 us
  Pallas kernels: 25.4 us -> 22.9 us
    ppermute x1 -> x5, waiting for transfers between devices: 0.01 us -> 8.91 us  [the longest x1 8.54 us: on_device(): corner = lax.ppermute(late, ('band', 'rows'), corner)]
    all_to_all x1, waiting for transfers between devices: 7.53 us -> 0.01 us  [on_device(): lax.all_to_all(lists, 'rows', split_axis=0, concat_axis=0, tiled=True, ax...]
    ppermute x1 -> x5, starting transfers between devices: 0.07 us -> 5.97 us  [the longest x1 2.54 us: on_device(): mirror_lists = lax.ppermute(late, 'rows', to_mirror)]
    all_to_all x2, waiting for transfers between devices: 31.4 us -> 25.8 us  [exchange(): lax.all_to_all(sends[0], 'rows', split_axis=0, concat_axis=0, tiled=True,...]
    all_to_all x2, starting transfers between devices: 8.98 us -> 13.4 us  [exchange(): lax.all_to_all(sends[0], 'rows', split_axis=0, concat_axis=0, tiled=True,...]
    pallas_call x8, Pallas kernels: 25.4 us -> 22.9 us  [apply(): return run(*pinned)]
    all_to_all x1, starting transfers between devices: 6.48 us -> 4.12 us  [on_device(): lax.all_to_all(lists, 'rows', split_axis=0, concat_axis=0, tiled=True, ax...]
    ppermute x2, waiting for transfers between devices: 2.07 us -> 0.01 us  [to_bands(): return (lax.ppermute(sends[0], 'band', [(0, 1), (1, 0)]),)]
  transfers between devices with their start and end apart: 7 -> 11, of which waited for: 5 -> 4; matrix products, arithmetic and copies ran while one was open for 0% -> 0% of each run, Pallas kernels for 14% -> 15%
where the time goes in v7:
time: 86.3 us; the launch traced here: 85.9 us
  waiting for transfers between devices  35.9 us (42%)
  starting transfers between devices  26.5 us (31%)
  Pallas kernels  22.9 us (27%)
    all_to_all x2, waiting for transfers between devices, exchange(): lax.all_to_all(sends[0], 'rows', split_axis=0, concat_axis=0, tiled=True,...  25.8 us
    pallas_call x8, Pallas kernels, apply(): return run(*pinned)  22.9 us
    all_to_all x2, starting transfers between devices, exchange(): lax.all_to_all(sends[0], 'rows', split_axis=0, concat_axis=0, tiled=True,...  13.4 us
    ppermute x1, waiting for transfers between devices, on_device(): corner = lax.ppermute(late, ('band', 'rows'), corner)  8.54 us
    all_to_all x1, starting transfers between devices, on_device(): lax.all_to_all(lists, 'rows', split_axis=0, concat_axis=0, tiled=True, ax...  4.12 us
    ppermute x1, starting transfers between devices, on_device(): mirror_lists = lax.ppermute(late, 'rows', to_mirror)  2.54 us
    ppermute x2, starting transfers between devices, to_bands(): return (lax.ppermute(sends[0], 'band', [(0, 1), (1, 0)]),)  2.28 us
  transfers between devices with their start and end apart: 11, of which 4 were waited for; matrix products, arithmetic and copies ran while one was open for 0% of the time, Pallas kernels for 15%

profile of v7, /device:TPU:16, one launch (start us, length us, event | category | flops | bytes accessed | tf_op | source)
XLA Modules:
  0.0 85.9 jit_solution(4921252387990528908)
XLA Ops:
  0.0 1.8 %shard_map.100 = (s32[8,1,384]{2,1,0:T(1,128)}, s32[1,1,256]{2,1,0:T(1,128)S(1)}, s32[1,1,128]{2,1,0:T(1,128)S(1)}) custom-call(s32[2,32]{1,0:T(2,128)} %bitcast.24, s32[2,32]{1,0:T(2,128)} %bitcast.25, s32[4,32]{1,0:T(4,128)} %bitcast.23, s32[1,32]{1,0:T(1,128)} %bitcast.26, s32[1,32]{1,0:T(1,128)} %bitcast.27), custom_call_target="tpu_custom_call" | custom-call | tf_op jit(solution)/shard_map/pallas_call | solution.py:48
  1.8 4.1 %all-to-all-start = ((s32[8,1,384]{2,1,0:T(1,128)}), s32[8,1,384]{2,1,0:T(1,128)S(1)}, u32[]{:S(2)}, u32[]{:S(2)}) async-start(s32[8,1,384]{2,1,0:T(1,128)} %get-tuple-element.22), calls=%async_computation | async-start | bytes 24576 | tf_op jit(solution)/shard_map/all_to_all | solution.py:637
  5.9 1.6 %collective-permute-start.1 = (s32[1,1,256]{2,1,0:T(1,128)S(1)}, s32[1,1,256]{2,1,0:T(1,128)S(1)}, u32[]{:S(2)}, u32[]{:S(2)}) collective-permute-start(s32[1,1,256]{2,1,0:T(1,128)S(1)} %get-tuple-element.21.refs_1_), channel_id=1, source_target_pairs={{0,16},{16,0},{1,17},{17,1},{2,18},{18,2},{3,19},{19,3},{4,20},{20... | collective-permute-start | bytes 3080 | tf_op jit(solution)/shard_map/ppermute | solution.py:641
  7.5 3.9 %shard_map.101.refs_0_ = f32[256,16,128]{2,1,0:T(8,128)} custom-call(f32[32,16,128]{2,1,0:T(8,128)} %start_in.1, f32[8,128,128]{2,1,0:T(8,128)} %refs_7_.1), custom_call_target="tpu_custom_call" | custom-call | flops 402653184 | bytes 4194304 | tf_op jit(solution)/shard_map/pallas_call | solution.py:48
  11.5 0.4 collective-permute-done.refs_1_
  11.8 2.7 %shard_map.102 = (f32[8,16,16,128]{3,2,1,0:T(8,128)}, f32[32,16,128]{2,1,0:T(8,128)}) custom-call(f32[256,16,128]{2,1,0:T(8,128)} %shard_map.101.refs_0_, f32[32,16,128]{2,1,0:T(8,128)S(1)} %collective-permute-done.refs_1_, f32[8,128,128]{2,1,0:T(8,128)S(1)} %copy-done, s32[8,1,384]{2,1,0:T(1,128)S(1)} %all-to-all-done.refs_3_.refs_2_, ...), custom_call_target="tpu_custom_call" | custom-call | flops 402653184 | bytes 4194304 | tf_op jit(solution)/shard_map/pallas_call | solution.py:48
  14.6 6.8 %all-to-all-start.1 = ((f32[8,256,128]{2,1,0:T(8,128)}), f32[8,256,128]{2,1,0:T(8,128)S(1)}, u32[]{:S(2)}, u32[]{:S(2)}) async-start(f32[8,256,128]{2,1,0:T(8,128)} %bitcast.20), calls=%async_computation.1 | async-start | bytes 2097152 | tf_op jit(solution)/shard_map/all_to_all | solution.py:699
  21.4 1.5 %collective-permute-start.5 = (s32[8,1,384]{2,1,0:T(1,128)S(1)}, s32[8,1,384]{2,1,0:T(1,128)S(1)}, u32[]{:S(2)}, u32[]{:S(2)}) collective-permute-start(s32[8,1,384]{2,1,0:T(1,128)S(1)} %all-to-all-done.refs_3_.refs_2_), channel_id=1, source_target_pairs={{0,16},{16,0},{1,17},{17,1},{2,18},{18,2},{3,19},{19,3},{4,20},{20... | collective-permute-start | bytes 36872 | tf_op jit(solution)/shard_map/ppermute | solution.py:709
  22.9 0.3 collective-permute-start.4
  23.2 2.5 %collective-permute-start.2 = (s32[8,1,384]{2,1,0:T(1,128)S(1)}, s32[8,1,384]{2,1,0:T(1,128)S(1)}, u32[]{:S(2)}, u32[]{:S(2)}) collective-permute-start(s32[8,1,384]{2,1,0:T(1,128)S(1)} %all-to-all-done.refs_3_.refs_2_), channel_id=1, source_target_pairs={{0,8},{1,9},{2,10},{3,11},{4,12},{5,13},{6,14},{7,15},{8,0},{9,1},... | collective-permute-start | bytes 36872 | tf_op jit(solution)/shard_map/ppermute | solution.py:706
  25.8 1.5 %collective-permute-start.3 = (f32[32,16,128]{2,1,0:T(8,128)S(1)}, f32[32,16,128]{2,1,0:T(8,128)S(1)}, u32[]{:S(2)}, u32[]{:S(2)}) collective-permute-start(f32[32,16,128]{2,1,0:T(8,128)S(1)} %copy-done.3), channel_id=1, source_target_pairs={{0,16},{16,0},{1,17},{17,1},{2,18},{18,2},{3,19},{19,3},{4,20},{20... | collective-permute-start | bytes 786440 | tf_op jit(solution)/shard_map/ppermute | solution.py:580
  27.3 8.5 %collective-permute-done.4 = s32[8,1,384]{2,1,0:T(1,128)S(1)} collective-permute-done((s32[8,1,384]{2,1,0:T(1,128)S(1)}, s32[8,1,384]{2,1,0:T(1,128)S(1)}, u32[]{:S(2)}, u32[]{:S(2)}) %collective-permute-start.4) | collective-permute-done | bytes 12320 | tf_op jit(solution)/shard_map/ppermute | solution.py:711
  35.8 0.1 fusion
  35.9 0.1 select_n.22
  36.1 0.1 reshape.18.refs_0_
  36.3 5.8 %shard_map.103 = (bf16[10,256,192]{2,1,0:T(8,128)(2,1)}, bf16[128,384]{1,0:T(8,128)(2,1)}, bf16[1024,256]{1,0:T(8,128)(2,1)}, f32[4,128]{1,0:T(4,128)S(1)}) custom-call(s32[8,2,512]{2,1,0:T(2,128)S(1)} %reshape.18.refs_0_, s32[8,128]{1,0:T(8,128)S(1)} %bitcast.18, s32[8,128]{1,0:T(8,128)S(1)} %bitcast.19, f32[8,128,128]{2,1,0:T(8,128)S(1)} %copy-done, ...), custom_call_target="tpu_custom_call" | custom-call | flops 1610612736 | bytes 4194304 | tf_op jit(solution)/shard_map/pallas_call | solution.py:48
  42.1 5.9 %shard_map.104 = (f32[16,136,128]{2,1,0:T(8,128)}, f32[32,16,128]{2,1,0:T(8,128)}) custom-call(s32[1,1,128]{2,1,0:T(1,128)S(1)} %get-tuple-element.20.refs_0_, s32[1,1,256]{2,1,0:T(1,128)S(1)} %get-tuple-element.21.refs_1_, s32[8,1,384]{2,1,0:T(1,128)S(1)} %all-to-all-done.refs_3_.refs_2_, s32[8,1,384]{2,1,0:T(1,128)S(1)} %collective-permute-done.2.refs_3_, ...), custom_call_target="tpu_custom_call" | custom-call | flops 805306368 | bytes 4194304 | tf_op jit(solution)/shard_map/pallas_call | solution.py:48
  48.0 6.6 %all-to-all-start.2 = ((f32[16,136,128]{2,1,0:T(8,128)}), f32[16,136,128]{2,1,0:T(8,128)S(1)}, u32[]{:S(2)}, u32[]{:S(2)}) async-start(f32[16,136,128]{2,1,0:T(8,128)} %get-tuple-element.30), calls=%async_computation.2 | async-start | bytes 2228224 | tf_op jit(solution)/shard_map/all_to_all | solution.py:699
  54.7 0.8 collective-permute-start.7
  55.4 25.8 %all-to-all-done.2.arrived_ref.refs_2_ = f32[16,136,128]{2,1,0:T(8,128)S(1)} async-done(((f32[16,136,128]{2,1,0:T(8,128)}), f32[16,136,128]{2,1,0:T(8,128)S(1)}, u32[]{:S(2)}, u32[]{:S(2)}) %all-to-all-start.2) | async-done | bytes 1114144 | tf_op jit(solution)/shard_map/all_to_all | solution.py:699
  81.2 0.8 collective-permute-start.6
  82.0 1.8 %shard_map.106.second_ref = f32[32,16,128]{2,1,0:T(8,128)S(1)} custom-call(s32[1,1,128]{2,1,0:T(1,128)S(1)} %get-tuple-element.20.refs_0_, s32[1,1,256]{2,1,0:T(1,128)S(1)} %get-tuple-element.21.refs_1_, f32[16,136,128]{2,1,0:T(8,128)S(1)} %all-to-all-done.2.arrived_ref.refs_2_, f32[8,128,128]{2,1,0:T(8,128)S(1)} %copy-done.1, f32[32,16,128]{2,1,0:T(8,128)} %refs_4_.3, ...), custom_call_target="tpu_custom_call" | custom-call | flops 402653184 | bytes 4194304 | tf_op jit(solution)/shard_map/pallas_call | solution.py:48
  83.8 1.1 %collective-permute-done.6.other_ref = f32[4,128]{1,0:T(4,128)S(1)} collective-permute-done((f32[4,128]{1,0:T(4,128)S(1)}, f32[4,128]{1,0:T(4,128)S(1)}, u32[]{:S(2)}, u32[]{:S(2)}) %collective-permute-start.6) | collective-permute-done | bytes 2080 | tf_op jit(solution)/shard_map/ppermute | solution.py:796
  84.9 1.0 %shard_map.107 = f32[32,16,128]{2,1,0:T(8,128)} custom-call(f32[4,128]{1,0:T(4,128)S(1)} %get-tuple-element.31.mine_ref, f32[4,128]{1,0:T(4,128)S(1)} %collective-permute-done.6.other_ref, f32[4,128]{1,0:T(4,128)S(1)} %get-tuple-element.33.scale_ref, f32[32,16,128]{2,1,0:T(8,128)S(1)} %shard_map.106.second_ref), custom_call_target="tpu_custom_call" | custom-call | tf_op jit(solution)/shard_map/pallas_call | solution.py:48
  (24 shorter events, 0.2 us)
Async XLA Ops:
  0.0 11.8 %collective-permute-start = (f32[32,16,128]{2,1,0:T(8,128)}, f32[32,16,128]{2,1,0:T(8,128)S(1)}, u32[]{:S(2)}, u32[]{:S(2)}) collective-permute-start(f32[32,16,128]{2,1,0:T(8,128)} %start_in.1), channel_id=1, source_target_pairs={{0,8},{1,9},{2,10},{3,11},{4,12},{5,13},{6,14},{7,15},{8,0},{9,1},... | collective-permute-start | bytes 786440 | tf_op jit(solution)/shard_map/ppermute | solution.py:625
  1.8 9.7 %all-to-all-start = ((s32[8,1,384]{2,1,0:T(1,128)}), s32[8,1,384]{2,1,0:T(1,128)S(1)}, u32[]{:S(2)}, u32[]{:S(2)}) async-start(s32[8,1,384]{2,1,0:T(1,128)} %get-tuple-element.22), calls=%async_computation | async-start | bytes 24576 | tf_op jit(solution)/shard_map/all_to_all | solution.py:637
  5.9 5.9 %copy-start = (f32[8,128,128]{2,1,0:T(8,128)S(1)}, f32[8,128,128]{2,1,0:T(8,128)}, u32[]{:S(2)}) copy-start(f32[8,128,128]{2,1,0:T(8,128)} %refs_7_.1) | copy-start | bytes 1572868
  5.9 5.5 %collective-permute-start.1 = (s32[1,1,256]{2,1,0:T(1,128)S(1)}, s32[1,1,256]{2,1,0:T(1,128)S(1)}, u32[]{:S(2)}, u32[]{:S(2)}) collective-permute-start(s32[1,1,256]{2,1,0:T(1,128)S(1)} %get-tuple-element.21.refs_1_), channel_id=1, source_target_pairs={{0,16},{16,0},{1,17},{17,1},{2,18},{18,2},{3,19},{19,3},{4,20},{20... | collective-permute-start | bytes 3080 | tf_op jit(solution)/shard_map/ppermute | solution.py:641
  14.6 11.2 %copy-start.3 = (f32[32,16,128]{2,1,0:T(8,128)S(1)}, f32[32,16,128]{2,1,0:T(8,128)}, u32[]{:S(2)}) copy-start(f32[32,16,128]{2,1,0:T(8,128)} %get-tuple-element.26) | copy-start | bytes 786436
  14.6 21.7 %copy-start.1 = (f32[8,128,128]{2,1,0:T(8,128)S(1)}, f32[8,128,128]{2,1,0:T(8,128)}, u32[]{:S(2)}) copy-start(f32[8,128,128]{2,1,0:T(8,128)} %refs_3_.3) | copy-start | bytes 1572868
  14.6 21.7 %copy-start.2 = (f32[8,128,128]{2,1,0:T(8,128)S(1)}, f32[8,128,128]{2,1,0:T(8,128)}, u32[]{:S(2)}) copy-start(f32[8,128,128]{2,1,0:T(8,128)} %refs_4_.2) | copy-start | bytes 1572868
  14.6 27.5 %all-to-all-start.1 = ((f32[8,256,128]{2,1,0:T(8,128)}), f32[8,256,128]{2,1,0:T(8,128)S(1)}, u32[]{:S(2)}, u32[]{:S(2)}) async-start(f32[8,256,128]{2,1,0:T(8,128)} %bitcast.20), calls=%async_computation.1 | async-start | bytes 2097152 | tf_op jit(solution)/shard_map/all_to_all | solution.py:699
  21.4 5.9 %collective-permute-start.5 = (s32[8,1,384]{2,1,0:T(1,128)S(1)}, s32[8,1,384]{2,1,0:T(1,128)S(1)}, u32[]{:S(2)}, u32[]{:S(2)}) collective-permute-start(s32[8,1,384]{2,1,0:T(1,128)S(1)} %all-to-all-done.refs_3_.refs_2_), channel_id=1, source_target_pairs={{0,16},{16,0},{1,17},{17,1},{2,18},{18,2},{3,19},{19,3},{4,20},{20... | collective-permute-start | bytes 36872 | tf_op jit(solution)/shard_map/ppermute | solution.py:709
  22.9 12.9 %collective-permute-start.4 = (s32[8,1,384]{2,1,0:T(1,128)S(1)}, s32[8,1,384]{2,1,0:T(1,128)S(1)}, u32[]{:S(2)}, u32[]{:S(2)}) collective-permute-start(s32[8,1,384]{2,1,0:T(1,128)S(1)} %all-to-all-done.refs_3_.refs_2_), channel_id=1, source_target_pairs={{0,24},{1,25},{2,26},{3,27},{4,28},{5,29},{6,30},{7,31},{8,16},{9,... | collective-permute-start | bytes 36872 | tf_op jit(solution)/shard_map/ppermute | solution.py:711
  23.2 12.6 %collective-permute-start.2 = (s32[8,1,384]{2,1,0:T(1,128)S(1)}, s32[8,1,384]{2,1,0:T(1,128)S(1)}, u32[]{:S(2)}, u32[]{:S(2)}) collective-permute-start(s32[8,1,384]{2,1,0:T(1,128)S(1)} %all-to-all-done.refs_3_.refs_2_), channel_id=1, source_target_pairs={{0,8},{1,9},{2,10},{3,11},{4,12},{5,13},{6,14},{7,15},{8,0},{9,1},... | collective-permute-start | bytes 36872 | tf_op jit(solution)/shard_map/ppermute | solution.py:706
  25.8 16.3 %collective-permute-start.3 = (f32[32,16,128]{2,1,0:T(8,128)S(1)}, f32[32,16,128]{2,1,0:T(8,128)S(1)}, u32[]{:S(2)}, u32[]{:S(2)}) collective-permute-start(f32[32,16,128]{2,1,0:T(8,128)S(1)} %copy-done.3), channel_id=1, source_target_pairs={{0,16},{16,0},{1,17},{17,1},{2,18},{18,2},{3,19},{19,3},{4,20},{20... | collective-permute-start | bytes 786440 | tf_op jit(solution)/shard_map/ppermute | solution.py:580
  48.0 6.6 %copy-start.4 = (f32[32,16,128]{2,1,0:T(8,128)S(1)}, f32[32,16,128]{2,1,0:T(8,128)}, u32[]{:S(2)}) copy-start(f32[32,16,128]{2,1,0:T(8,128)} %get-tuple-element.34) | copy-start | bytes 786436
  48.0 33.2 %all-to-all-start.2 = ((f32[16,136,128]{2,1,0:T(8,128)}), f32[16,136,128]{2,1,0:T(8,128)S(1)}, u32[]{:S(2)}, u32[]{:S(2)}) async-start(f32[16,136,128]{2,1,0:T(8,128)} %get-tuple-element.30), calls=%async_computation.2 | async-start | bytes 2228224 | tf_op jit(solution)/shard_map/all_to_all | solution.py:699
  54.7 27.4 %collective-permute-start.7 = (f32[32,16,128]{2,1,0:T(8,128)S(1)}, f32[32,16,128]{2,1,0:T(8,128)S(1)}, u32[]{:S(2)}, u32[]{:S(2)}) collective-permute-start(f32[32,16,128]{2,1,0:T(8,128)S(1)} %copy-done.4), channel_id=1, source_target_pairs={{0,16},{16,0},{1,17},{17,1},{2,18},{18,2},{3,19},{19,3},{4,20},{20... | collective-permute-start | bytes 786440 | tf_op jit(solution)/shard_map/ppermute | solution.py:580
  81.2 3.6 %collective-permute-start.6 = (f32[4,128]{1,0:T(4,128)S(1)}, f32[4,128]{1,0:T(4,128)S(1)}, u32[]{:S(2)}, u32[]{:S(2)}) collective-permute-start(f32[4,128]{1,0:T(4,128)S(1)} %get-tuple-element.32), channel_id=1, source_target_pairs={{0,16},{16,0},{1,17},{17,1},{2,18},{18,2},{3,19},{19,3},{4,20},{20... | collective-permute-start | bytes 6152 | tf_op jit(solution)/shard_map/ppermute | solution.py:796

commit v8 on v7

--- a/solution.py
+++ b/solution.py
@@ -180,6 +180,13 @@
     return started([pltpu.make_async_copy(i, h, sems.at[n]) for n, (i, h) in enumerate(pairs)])
 
 
+def near_rows(near_in, near_ref):
+    if near_ref.shape[0] != 1:
+        return near_in
+    row = lax.rem(lax.axis_index("rows"), near_in.shape[0])
+    return near_in.at[pl.ds(row, 1), :, pl.ds(LANES, near_ref.shape[2])]
+
+
 def band_field(rows, width_k, way, n_ways):
     field = (2 + width_k) * rows
     if n_ways == 1:
@@ -229,6 +236,7 @@
     product_ref, list_ref, near_ref, send_ref = refs[:4]
     band_refs, (load_sems, meta_sems, send_sems) = refs[4 : 4 + n_band], refs[4 + n_band :]
     list_in = list_in.at[:, :, pl.ds(0, LANES)]
+    near_in = near_rows(near_in, near_ref)
     metadata = copies_of(((list_in, list_ref), (near_in, near_ref)), meta_sems)
     places = [pl.ds(tile * rows, rows) for tile in range(n_tiles)]
     loads = [(product_in.at[place], product_ref.at[0, place]) for place in places]
@@ -416,13 +424,14 @@
 
 def middle_kernel(sizes, width_k, n_band, dense, *refs):
     metadata_in, arrived_ref, inverse_ref, tile_ref = list(refs[:5]), *refs[5:8]
-    for n in (2, 3):
-        metadata_in[n] = metadata_in[n].at[:, :, pl.ds(0, LANES)]
     terms_in, refs = refs[8 : 9 + n_band], refs[9 + n_band :]
     extra, refs = (refs[:3], refs[3:]) if dense else ((), refs)
     send_out, band_out, refs = refs[0], refs[1 : 1 + n_band], refs[1 + n_band :]
     metadata, sum_ref, product_ref, send_ref = refs[:5], *refs[5:8]
     place_ref, index_ref, list_ref, mirror_list_ref, near_ref = metadata
+    for n in (2, 3):
+        metadata_in[n] = metadata_in[n].at[:, :, pl.ds(0, LANES)]
+    metadata_in[4] = near_rows(metadata_in[4], near_ref)
     terms, band_refs, refs = refs[8 : 9 + n_band], refs[9 + n_band : 9 + 2 * n_band], refs[9 + 2 * n_band :]
     term_sems, meta_sems, send_sems, refs = *refs[:3], refs[3:]
     right_ref = terms[0]
@@ -638,7 +647,7 @@
         lists, "rows", split_axis=0, concat_axis=0, tiled=True, axis_index_groups=halves_of_rows
     )
     if n_bands == 2:
-        near = lax.ppermute(index, "band", [(0, 1), (1, 0)])
+        near = lax.ppermute(lists, "band", [(0, 1), (1, 0)])
     else:
         ways = [[(b, (b + step) % n_bands) for b in range(n_bands)] for step in (-1, 1)]
         near = jnp.concatenate([lax.ppermute(index, "band", way) for way in ways], axis=0)
@@ -692,7 +701,6 @@
         work * n_tiles,
         4 << 20,
     )(made, mirror, coupling_tiles, lists, near)
-    packed, late = lax.optimization_barrier((packed, lists))
     sends = (packed.reshape(half, 2 * cap * n_rhs, states), *bands)
     halves_of_rows = [list(range(half)), list(range(half, n_rows))]
     def exchange(sends, groups=None):
@@ -703,17 +711,17 @@
 
     arrived_blocks, arrived_bands = exchange(sends, halves_of_rows)
 
-    mirror_lists = lax.ppermute(late, "rows", to_mirror)
+    if not dense:
+        mirror_lists = lax.ppermute(lists, "rows", to_mirror)
     extra, extra_scratch, tail = (), [], 0
     if dense:
-        across = lax.ppermute(late, "band", [(0, 1), (1, 0)])
-        corner = [(b * n_rows + i, (1 - b) * n_rows + j) for b in range(2) for i, j in to_mirror]
-        corner = lax.ppermute(late, ("band", "rows"), corner)
-        near_half = jnp.stack([late, across])[:, :, 0, LANES:]
-        far_half = jnp.stack([mirror_lists, corner])[:, :, 0, LANES:]
+        near_half = jnp.concatenate([lists, near], axis=1)
+        far_half = lax.ppermute(near_half, "rows", to_mirror)
+        mirror_lists = far_half[:, :1]
+        near_half, far_half = near_half[:, :, LANES:], far_half[:, :, LANES:]
         upper = my_row >= half
         fields = [jnp.where(upper, far_half, near_half), jnp.where(upper, near_half, far_half)]
-        fields = jnp.concatenate(fields, axis=1).reshape(2, n_rows, -1, rows).transpose(2, 0, 1, 3)
+        fields = jnp.concatenate(fields, axis=0).reshape(n_rows, 2, -1, rows).transpose(2, 1, 0, 3)
         fields = fields.reshape(-1, 2, n_rows * rows)
         n_blocks = slots + 2 * rows
         length = n_dev * depth
@@ -741,7 +749,7 @@
             ],
             4 * total_groups * n_tiles * n_dev * rows * n_blocks,
             4 << 20,
-        )(fields, late[:, 0, :LANES], mirror_lists[:, 0, :LANES], coupling_tiles, diag_table, inverse_table)
+        )(fields, lists[:, 0, :LANES], mirror_lists[:, 0, :LANES], coupling_tiles, diag_table, inverse_table)
         extra = (functionals, counts, placing)
         extra_scratch = [
             *[pltpu.VMEM(*shape) for shape in extra_shapes],

time: 86.3 us -> 91.1 us (1.056)
  the two profiles are of different devices: /device:TPU:16 before, /device:TPU:0 now
where the time goes in v8:
time: 91.1 us; the launch traced here: 89.4 us
  waiting for transfers between devices  38.7 us (42%)
  Pallas kernels  22.3 us (24%)
  starting transfers between devices  16.7 us (18%)
  blocking collectives  11.1 us (12%)
    all_to_all x2, waiting for transfers between devices, exchange(): lax.all_to_all(sends[0], 'rows', split_axis=0, concat_axis=0, tiled=True,...  23.3 us
    pallas_call x8, Pallas kernels, apply(): return run(*pinned)  22.3 us
    ppermute x1, waiting for transfers between devices, on_device(): far_half = lax.ppermute(near_half, 'rows', to_mirror)  12.7 us
    all_to_all x1, blocking collectives, on_device(): lax.all_to_all(lists, 'rows', split_axis=0, concat_axis=0, tiled=True, ax...  11.1 us
    all_to_all x2, starting transfers between devices, exchange(): lax.all_to_all(sends[0], 'rows', split_axis=0, concat_axis=0, tiled=True,...  9.13 us
    ppermute x1, starting transfers between devices, on_device(): mirror = lax.ppermute(start_iterate, 'rows', to_mirror)  4.04 us
  transfers between devices with their start and end apart: 8, of which 4 were waited for; matrix products, arithmetic and copies ran while one was open for 0% of the time, Pallas kernels for 14%

profile of v8, /device:TPU:0, one launch (start us, length us, event | category | flops | bytes accessed | tf_op | source)
XLA Modules:
  0.0 89.4 jit_solution(8788080607882208975)
XLA Ops:
  0.0 4.0 %collective-permute-start.2 = (f32[32,16,128]{2,1,0:T(8,128)}, f32[32,16,128]{2,1,0:T(8,128)S(1)}, u32[]{:S(2)}, u32[]{:S(2)}) collective-permute-start(f32[32,16,128]{2,1,0:T(8,128)} %start_in.1), channel_id=1, source_target_pairs={{0,8},{1,9},{2,10},{3,11},{4,12},{5,13},{6,14},{7,15},{8,0},{9,1},... | collective-permute-start | bytes 786440 | tf_op jit(solution)/shard_map/ppermute | solution.py:634
  4.0 1.2 %shard_map.100 = (s32[8,1,384]{2,1,0:T(1,128)S(1)}, s32[1,1,256]{2,1,0:T(1,128)S(1)}, s32[1,1,128]{2,1,0:T(1,128)S(1)}) custom-call(s32[2,32]{1,0:T(2,128)} %bitcast.16, s32[2,32]{1,0:T(2,128)} %bitcast.17, s32[4,32]{1,0:T(4,128)} %bitcast.15, s32[1,32]{1,0:T(1,128)} %bitcast.18, s32[1,32]{1,0:T(1,128)} %bitcast.19), custom_call_target="tpu_custom_call" | custom-call | tf_op jit(solution)/shard_map/pallas_call | solution.py:48
  5.2 11.1 %all_to_all.15.refs_3_.refs_2_ = s32[8,1,384]{2,1,0:T(1,128)S(1)} all-to-all(s32[8,1,384]{2,1,0:T(1,128)S(1)} %get-tuple-element.20), channel_id=1, replica_groups={{0,1,2,3,4,5,6,7},{8,9,10,11,12,13,14,15},{16,17,18,19,20,21,22,23},{24..., dimensions={0} | all-to-all | bytes 24576 | tf_op jit(solution)/shard_map/all_to_all | solution.py:646
  16.3 1.6 %collective-permute-start = (s32[8,1,384]{2,1,0:T(1,128)S(1)}, s32[8,1,384]{2,1,0:T(1,128)S(1)}, u32[]{:S(2)}, u32[]{:S(2)}) collective-permute-start(s32[8,1,384]{2,1,0:T(1,128)S(1)} %all_to_all.15.refs_3_.refs_2_), channel_id=1, source_target_pairs={{0,16},{16,0},{1,17},{17,1},{2,18},{18,2},{3,19},{19,3},{4,20},{20... | collective-permute-start | bytes 36872 | tf_op jit(solution)/shard_map/ppermute | solution.py:650
  17.9 3.9 %shard_map.101.refs_0_ = f32[256,16,128]{2,1,0:T(8,128)} custom-call(f32[32,16,128]{2,1,0:T(8,128)} %start_in.1, f32[8,128,128]{2,1,0:T(8,128)} %refs_7_.1), custom_call_target="tpu_custom_call" | custom-call | flops 402653184 | bytes 4194304 | tf_op jit(solution)/shard_map/pallas_call | solution.py:48
  21.9 2.7 %shard_map.102 = (f32[8,16,16,128]{3,2,1,0:T(8,128)}, f32[32,16,128]{2,1,0:T(8,128)}) custom-call(f32[256,16,128]{2,1,0:T(8,128)} %shard_map.101.refs_0_, f32[32,16,128]{2,1,0:T(8,128)S(1)} %collective-permute-done.2.refs_1_, f32[8,128,128]{2,1,0:T(8,128)S(1)} %copy-done, s32[8,1,384]{2,1,0:T(1,128)S(1)} %all_to_all.15.refs_3_.refs_2_, ...), custom_call_target="tpu_custom_call" | custom-call | flops 402653184 | bytes 4194304 | tf_op jit(solution)/shard_map/pallas_call | solution.py:48
  24.6 0.0 copy-start.3
  24.6 0.0 copy-start.1
  24.6 3.7 %all-to-all-start.1 = ((f32[8,256,128]{2,1,0:T(8,128)}), f32[8,256,128]{2,1,0:T(8,128)S(1)}, u32[]{:S(2)}, u32[]{:S(2)}) async-start(f32[8,256,128]{2,1,0:T(8,128)} %bitcast.13), calls=%async_computation.1 | async-start | bytes 2097152 | tf_op jit(solution)/shard_map/all_to_all | solution.py:707
  28.4 0.1 collective-permute-start.1
  28.5 12.7 %collective-permute-done.1 = s32[8,2,384]{2,1,0:T(2,128)S(1)} collective-permute-done((s32[8,2,384]{2,1,0:T(2,128)S(1)}, s32[8,2,384]{2,1,0:T(2,128)S(1)}, u32[]{:S(2)}, u32[]{:S(2)}) %collective-permute-start.1) | collective-permute-done | bytes 24608 | tf_op jit(solution)/shard_map/ppermute | solution.py:719
  41.2 0.5 collective-permute-start.3
  41.7 0.1 reshape.10
  41.9 0.1 reshape.11.refs_0_
  42.1 5.8 %shard_map.103 = (bf16[10,256,192]{2,1,0:T(8,128)(2,1)}, bf16[128,384]{1,0:T(8,128)(2,1)}, bf16[1024,256]{1,0:T(8,128)(2,1)}, f32[4,128]{1,0:T(4,128)S(1)}) custom-call(s32[8,2,512]{2,1,0:T(2,128)S(1)} %reshape.11.refs_0_, s32[8,128]{1,0:T(8,128)S(1)} %bitcast.11, s32[8,128]{1,0:T(8,128)S(1)} %bitcast.12, f32[8,128,128]{2,1,0:T(8,128)S(1)} %copy-done, ...), custom_call_target="tpu_custom_call" | custom-call | flops 1610612736 | bytes 4194304 | tf_op jit(solution)/shard_map/pallas_call | solution.py:48
  47.9 1.5 %collective-permute-done.3.refs_9_ = f32[32,16,128]{2,1,0:T(8,128)S(1)} collective-permute-done((f32[32,16,128]{2,1,0:T(8,128)S(1)}, f32[32,16,128]{2,1,0:T(8,128)S(1)}, u32[]{:S(2)}, u32[]{:S(2)}) %collective-permute-start.3) | collective-permute-done | bytes 262176 | tf_op jit(solution)/shard_map/ppermute | solution.py:589
  49.3 5.9 %shard_map.104 = (f32[16,136,128]{2,1,0:T(8,128)}, f32[32,16,128]{2,1,0:T(8,128)}) custom-call(s32[1,1,128]{2,1,0:T(1,128)S(1)} %get-tuple-element.18.refs_0_, s32[1,1,256]{2,1,0:T(1,128)S(1)} %get-tuple-element.19.refs_1_, s32[8,1,384]{2,1,0:T(1,128)S(1)} %all_to_all.15.refs_3_.refs_2_, s32[8,1,384]{2,1,0:T(1,128)S(1)} %slice.21.refs_3_, ...), custom_call_target="tpu_custom_call" | custom-call | flops 805306368 | bytes 4194304 | tf_op jit(solution)/shard_map/pallas_call | solution.py:48
  55.3 5.4 %all-to-all-start.2 = ((f32[16,136,128]{2,1,0:T(8,128)}), f32[16,136,128]{2,1,0:T(8,128)S(1)}, u32[]{:S(2)}, u32[]{:S(2)}) async-start(f32[16,136,128]{2,1,0:T(8,128)} %get-tuple-element.26), calls=%async_computation.2 | async-start | bytes 2228224 | tf_op jit(solution)/shard_map/all_to_all | solution.py:707
  60.7 0.7 collective-permute-start.5
  61.4 23.3 %all-to-all-done.2.arrived_ref.refs_2_ = f32[16,136,128]{2,1,0:T(8,128)S(1)} async-done(((f32[16,136,128]{2,1,0:T(8,128)}), f32[16,136,128]{2,1,0:T(8,128)S(1)}, u32[]{:S(2)}, u32[]{:S(2)}) %all-to-all-start.2) | async-done | bytes 1114144 | tf_op jit(solution)/shard_map/all_to_all | solution.py:707
  84.7 0.7 collective-permute-start.4
  85.4 1.8 %shard_map.106.second_ref = f32[32,16,128]{2,1,0:T(8,128)S(1)} custom-call(s32[1,1,128]{2,1,0:T(1,128)S(1)} %get-tuple-element.18.refs_0_, s32[1,1,256]{2,1,0:T(1,128)S(1)} %get-tuple-element.19.refs_1_, f32[16,136,128]{2,1,0:T(8,128)S(1)} %all-to-all-done.2.arrived_ref.refs_2_, f32[8,128,128]{2,1,0:T(8,128)S(1)} %copy-done.1, f32[32,16,128]{2,1,0:T(8,128)} %refs_4_.3, ...), custom_call_target="tpu_custom_call" | custom-call | flops 402653184 | bytes 4194304 | tf_op jit(solution)/shard_map/pallas_call | solution.py:48
  87.2 1.2 %collective-permute-done.4.other_ref = f32[4,128]{1,0:T(4,128)S(1)} collective-permute-done((f32[4,128]{1,0:T(4,128)S(1)}, f32[4,128]{1,0:T(4,128)S(1)}, u32[]{:S(2)}, u32[]{:S(2)}) %collective-permute-start.4) | collective-permute-done | bytes 2080 | tf_op jit(solution)/shard_map/ppermute | solution.py:804
  88.4 1.0 %shard_map.107 = f32[32,16,128]{2,1,0:T(8,128)} custom-call(f32[4,128]{1,0:T(4,128)S(1)} %get-tuple-element.27.mine_ref, f32[4,128]{1,0:T(4,128)S(1)} %collective-permute-done.4.other_ref, f32[4,128]{1,0:T(4,128)S(1)} %get-tuple-element.29.scale_ref, f32[32,16,128]{2,1,0:T(8,128)S(1)} %shard_map.106.second_ref), custom_call_target="tpu_custom_call" | custom-call | tf_op jit(solution)/shard_map/pallas_call | solution.py:48
  (20 shorter events, 0.2 us)
Async XLA Ops:
  0.0 21.8 %collective-permute-start.2 = (f32[32,16,128]{2,1,0:T(8,128)}, f32[32,16,128]{2,1,0:T(8,128)S(1)}, u32[]{:S(2)}, u32[]{:S(2)}) collective-permute-start(f32[32,16,128]{2,1,0:T(8,128)} %start_in.1), channel_id=1, source_target_pairs={{0,8},{1,9},{2,10},{3,11},{4,12},{5,13},{6,14},{7,15},{8,0},{9,1},... | collective-permute-start | bytes 786440 | tf_op jit(solution)/shard_map/ppermute | solution.py:634
  16.3 5.5 %copy-start = (f32[8,128,128]{2,1,0:T(8,128)S(1)}, f32[8,128,128]{2,1,0:T(8,128)}, u32[]{:S(2)}) copy-start(f32[8,128,128]{2,1,0:T(8,128)} %refs_7_.1) | copy-start | bytes 1572868
  16.3 5.5 %collective-permute-start = (s32[8,1,384]{2,1,0:T(1,128)S(1)}, s32[8,1,384]{2,1,0:T(1,128)S(1)}, u32[]{:S(2)}, u32[]{:S(2)}) collective-permute-start(s32[8,1,384]{2,1,0:T(1,128)S(1)} %all_to_all.15.refs_3_.refs_2_), channel_id=1, source_target_pairs={{0,16},{16,0},{1,17},{17,1},{2,18},{18,2},{3,19},{19,3},{4,20},{20... | collective-permute-start | bytes 36872 | tf_op jit(solution)/shard_map/ppermute | solution.py:650
  24.6 16.6 %copy-start.3 = (f32[32,16,128]{2,1,0:T(8,128)S(1)}, f32[32,16,128]{2,1,0:T(8,128)}, u32[]{:S(2)}) copy-start(f32[32,16,128]{2,1,0:T(8,128)} %get-tuple-element.22) | copy-start | bytes 786436
  24.6 17.4 %copy-start.1 = (f32[8,128,128]{2,1,0:T(8,128)S(1)}, f32[8,128,128]{2,1,0:T(8,128)}, u32[]{:S(2)}) copy-start(f32[8,128,128]{2,1,0:T(8,128)} %refs_3_.3) | copy-start | bytes 1572868
  24.6 17.4 %copy-start.2 = (f32[8,128,128]{2,1,0:T(8,128)S(1)}, f32[8,128,128]{2,1,0:T(8,128)}, u32[]{:S(2)}) copy-start(f32[8,128,128]{2,1,0:T(8,128)} %refs_4_.2) | copy-start | bytes 1572868
  24.6 24.7 %all-to-all-start.1 = ((f32[8,256,128]{2,1,0:T(8,128)}), f32[8,256,128]{2,1,0:T(8,128)S(1)}, u32[]{:S(2)}, u32[]{:S(2)}) async-start(f32[8,256,128]{2,1,0:T(8,128)} %bitcast.13), calls=%async_computation.1 | async-start | bytes 2097152 | tf_op jit(solution)/shard_map/all_to_all | solution.py:707
  28.4 12.8 %collective-permute-start.1 = (s32[8,2,384]{2,1,0:T(2,128)S(1)}, s32[8,2,384]{2,1,0:T(2,128)S(1)}, u32[]{:S(2)}, u32[]{:S(2)}) collective-permute-start(s32[8,2,384]{2,1,0:T(2,128)S(1)} %pad_add_fusion.1), channel_id=1, source_target_pairs={{0,8},{1,9},{2,10},{3,11},{4,12},{5,13},{6,14},{7,15},{8,0},{9,1},... | collective-permute-start | bytes 73736 | tf_op jit(solution)/shard_map/ppermute | solution.py:719
  41.2 8.2 %collective-permute-start.3 = (f32[32,16,128]{2,1,0:T(8,128)S(1)}, f32[32,16,128]{2,1,0:T(8,128)S(1)}, u32[]{:S(2)}, u32[]{:S(2)}) collective-permute-start(f32[32,16,128]{2,1,0:T(8,128)S(1)} %copy-done.3), channel_id=1, source_target_pairs={{0,16},{16,0},{1,17},{17,1},{2,18},{18,2},{3,19},{19,3},{4,20},{20... | collective-permute-start | bytes 786440 | tf_op jit(solution)/shard_map/ppermute | solution.py:589
  55.2 5.5 %copy-start.4 = (f32[32,16,128]{2,1,0:T(8,128)S(1)}, f32[32,16,128]{2,1,0:T(8,128)}, u32[]{:S(2)}) copy-start(f32[32,16,128]{2,1,0:T(8,128)} %get-tuple-element.30) | copy-start | bytes 786436
  55.3 29.5 %all-to-all-start.2 = ((f32[16,136,128]{2,1,0:T(8,128)}), f32[16,136,128]{2,1,0:T(8,128)S(1)}, u32[]{:S(2)}, u32[]{:S(2)}) async-start(f32[16,136,128]{2,1,0:T(8,128)} %get-tuple-element.26), calls=%async_computation.2 | async-start | bytes 2228224 | tf_op jit(solution)/shard_map/all_to_all | solution.py:707
  60.7 24.7 %collective-permute-start.5 = (f32[32,16,128]{2,1,0:T(8,128)S(1)}, f32[32,16,128]{2,1,0:T(8,128)S(1)}, u32[]{:S(2)}, u32[]{:S(2)}) collective-permute-start(f32[32,16,128]{2,1,0:T(8,128)S(1)} %copy-done.4), channel_id=1, source_target_pairs={{0,16},{16,0},{1,17},{17,1},{2,18},{18,2},{3,19},{19,3},{4,20},{20... | collective-permute-start | bytes 786440 | tf_op jit(solution)/shard_map/ppermute | solution.py:589
  84.7 3.6 %collective-permute-start.4 = (f32[4,128]{1,0:T(4,128)S(1)}, f32[4,128]{1,0:T(4,128)S(1)}, u32[]{:S(2)}, u32[]{:S(2)}) collective-permute-start(f32[4,128]{1,0:T(4,128)S(1)} %get-tuple-element.28), channel_id=1, source_target_pairs={{0,16},{16,0},{1,17},{17,1},{2,18},{18,2},{3,19},{19,3},{4,20},{20... | collective-permute-start | bytes 6152 | tf_op jit(solution)/shard_map/ppermute | solution.py:804

commit v9 on v7

--- a/solution.py
+++ b/solution.py
@@ -157,8 +157,6 @@
                 mine, by_rank, precision=HIGH, preferred_element_type=jnp.float32
             )
     lists = (lists + 0.5).astype(jnp.int32)
-    upper = lax.axis_index("rows") >= half
-    lists = jnp.where(upper, lists[half:], lists[:half])
 
     def joined(parts, wide):
         spare = wide - len(parts) * rows
@@ -172,7 +170,7 @@
     index = joined(index, index_ref.shape[2])
     index_ref[0] = index
     place_ref[0] = joined(half_places + places, place_ref.shape[2])
-    for device in range(half):
+    for device in range(n_rows):
         list_ref[device] = jnp.concatenate([lists[device : device + 1, :], index], axis=1)
 
 
@@ -228,7 +226,9 @@
     band_out, refs = refs[6 : 6 + n_band], refs[6 + n_band :]
     product_ref, list_ref, near_ref, send_ref = refs[:4]
     band_refs, (load_sems, meta_sems, send_sems) = refs[4 : 4 + n_band], refs[4 + n_band :]
-    list_in = list_in.at[:, :, pl.ds(0, LANES)]
+    half = n_rows // 2
+    base = jnp.where(lax.axis_index("rows") >= half, half, 0)
+    list_in = list_in.at[pl.ds(base, half), :, pl.ds(0, LANES)]
     metadata = copies_of(((list_in, list_ref), (near_in, near_ref)), meta_sems)
     places = [pl.ds(tile * rows, rows) for tile in range(n_tiles)]
     loads = [(product_in.at[place], product_ref.at[0, place]) for place in places]
@@ -239,7 +239,6 @@
     finish(loads)
     copies = []
     pack_bands(sizes, width_k, product_ref.at[0], near_ref, band_refs)
-    half = n_rows // 2
     for n, (ref, out) in enumerate(zip(band_refs, band_out)):
         copies += started([pltpu.make_async_copy(ref, out, send_sems.at[half + n])])
     for device in range(half):
@@ -280,9 +279,9 @@
 
 def count_kernel(sizes, width_k, n_func, *refs):
     rows, n_rows, cap, n_tiles, n_rhs = sizes
-    field_ref, list_ref, mirror_list_ref, tile_ref, table_ref, inverse_ref = refs[:6]
-    count_out, functional_out, placing_out, scale_ref = refs[6:10]
-    count_ref, functional_ref, placing_ref, sems = refs[10:]
+    field_ref, list_ref, tile_ref, table_ref, inverse_ref = refs[:5]
+    count_out, functional_out, placing_out, scale_ref = refs[5:9]
+    count_ref, functional_ref, placing_ref, sems = refs[9:]
     n_groups, n_blocks = count_ref.shape[1:]
     slots, band_rows = n_rows * cap, n_rows * rows
     copies = []
@@ -306,27 +305,19 @@
         functional_ref[d * n_func : (d + 1) * n_func, :] = left_operand(solved)
     send(functional_ref, functional_out)
 
-    half = n_rows // 2
-    upper = lax.axis_index("rows") >= half
-    asked = []
-    for ref, first, lanes in (
-        (list_ref, jnp.where(upper, half, 0), 0),
-        (mirror_list_ref, jnp.where(upper, 0, half), LANES // 2),
-    ):
-        lists = ref[...]
-        asker = first + lax.broadcasted_iota(jnp.int32, lists.shape, 0)
-        codes = asker * rows + below(over(lists, rows * n_tiles), rows)
-        codes = jnp.where(lists > 0, codes, -1).astype(jnp.float32)
-        spread = lax.broadcasted_iota(jnp.int32, (slots // 2, half), 0)
-        spread = lax.div(spread, cap) == lax.broadcasted_iota(jnp.int32, (slots // 2, half), 1)
-        codes = jnp.dot(
-            jnp.where(spread, 1.0, 0.0), codes, precision=HIGH, preferred_element_type=jnp.float32
-        )
-        rank = lax.rem(lax.broadcasted_iota(jnp.int32, codes.shape, 0), cap)
-        lane = lax.broadcasted_iota(jnp.int32, codes.shape, 1)
-        codes = jnp.sum(jnp.where(rank + lanes == lane, codes, 0.0), axis=1, keepdims=True)
-        asked.append(jnp.where(codes < 0.0, codes - 0.5, codes + 0.5).astype(jnp.int32))
-    asked = jnp.concatenate(asked, axis=0)
+    lists = list_ref[...]
+    asker = lax.broadcasted_iota(jnp.int32, lists.shape, 0)
+    codes = asker * rows + below(over(lists, rows * n_tiles), rows)
+    codes = jnp.where(lists > 0, codes, -1).astype(jnp.float32)
+    spread = lax.broadcasted_iota(jnp.int32, (slots, n_rows), 0)
+    spread = lax.div(spread, cap) == lax.broadcasted_iota(jnp.int32, (slots, n_rows), 1)
+    codes = jnp.dot(
+        jnp.where(spread, 1.0, 0.0), codes, precision=HIGH, preferred_element_type=jnp.float32
+    )
+    rank = lax.rem(lax.broadcasted_iota(jnp.int32, codes.shape, 0), cap)
+    lane = lax.broadcasted_iota(jnp.int32, codes.shape, 1)
+    asked = jnp.sum(jnp.where(rank == lane, codes, 0.0), axis=1, keepdims=True)
+    asked = jnp.where(asked < 0.0, asked - 0.5, asked + 0.5).astype(jnp.int32)
     own = lax.axis_index("rows") * rows + lax.broadcasted_iota(jnp.int32, (rows, 1), 0)
     band = lax.axis_index("band")
 
@@ -415,19 +406,18 @@
 
 
 def middle_kernel(sizes, width_k, n_band, dense, *refs):
-    metadata_in, arrived_ref, inverse_ref, tile_ref = list(refs[:5]), *refs[5:8]
-    for n in (2, 3):
-        metadata_in[n] = metadata_in[n].at[:, :, pl.ds(0, LANES)]
-    terms_in, refs = refs[8 : 9 + n_band], refs[9 + n_band :]
+    metadata_in, arrived_ref, inverse_ref, tile_ref = list(refs[:4]), *refs[4:7]
+    metadata_in[2] = metadata_in[2].at[:, :, pl.ds(0, LANES)]
+    terms_in, refs = refs[7 : 8 + n_band], refs[8 + n_band :]
     extra, refs = (refs[:3], refs[3:]) if dense else ((), refs)
     send_out, band_out, refs = refs[0], refs[1 : 1 + n_band], refs[1 + n_band :]
-    metadata, sum_ref, product_ref, send_ref = refs[:5], *refs[5:8]
-    place_ref, index_ref, list_ref, mirror_list_ref, near_ref = metadata
-    terms, band_refs, refs = refs[8 : 9 + n_band], refs[9 + n_band : 9 + 2 * n_band], refs[9 + 2 * n_band :]
+    metadata, sum_ref, product_ref, send_ref = refs[:4], *refs[4:7]
+    place_ref, index_ref, list_ref, near_ref = metadata
+    terms, band_refs, refs = refs[7 : 8 + n_band], refs[8 + n_band : 8 + 2 * n_band], refs[8 + 2 * n_band :]
     term_sems, meta_sems, send_sems, refs = *refs[:3], refs[3:]
     right_ref = terms[0]
     rows, n_rows, cap, n_tiles, n_rhs = sizes
-    body, half = cap * n_rhs, n_rows // 2
+    body = cap * n_rhs
     metadata = copies_of(zip(metadata_in, metadata), meta_sems)
     later = copies_of(zip(terms_in, terms), term_sems)
     fetched = []
@@ -453,21 +443,15 @@
     pack_bands(sizes, width_k, product_ref, near_ref, band_refs)
     for ref, out in zip(band_refs, band_out):
         send(ref, out)
-    upper = lax.axis_index("rows") >= half
-    codes, order = [], 0
-    for ref, first, lanes in (
-        (list_ref, jnp.where(upper, half, 0), 0),
-        (mirror_list_ref, jnp.where(upper, 0, half), LANES // 2),
-    ):
-        for device in range(half):
-            for rank in range(cap):
-                code = ref[device, 0, lanes + rank]
-                codes.append(code)
-                block = product_ref[below(code, rows * n_tiles)]
-                send_ref[order, rank * n_rhs : (rank + 1) * n_rhs, :] = block
-            target = send_out.at[first + device]
-            send(send_ref.at[order], target.at[pl.ds(0, body)] if dense else target)
-            order += 1
+    codes = []
+    for owner in range(n_rows):
+        for rank in range(cap):
+            code = list_ref[owner, 0, rank]
+            codes.append(code)
+            block = product_ref[below(code, rows * n_tiles)]
+            send_ref[owner, rank * n_rhs : (rank + 1) * n_rhs, :] = block
+        target = send_out.at[owner]
+        send(send_ref.at[owner], target.at[pl.ds(0, body)] if dense else target)
     if dense:
         finish(fetched)
         kinds = [below(over(code, rows * n_tiles * rows), n_diag) for code in codes]
@@ -626,7 +610,7 @@
     lists, index, places = call(
         functools.partial(request_kernel, (rows, n_rows, cap, n_tiles, n_diag)),
         (
-            jax.ShapeDtypeStruct((half, 1, LANES + wide), i32),
+            jax.ShapeDtypeStruct((n_rows, 1, LANES + wide), i32),
             jax.ShapeDtypeStruct((1, 1, wide), i32),
             jax.ShapeDtypeStruct((1, 1, place_wide), i32),
         ),
@@ -634,9 +618,7 @@
         [VMEM] * 3,
         [*[pltpu.VMEM(shape, i32) for shape in index_shapes], pltpu.SemaphoreType.DMA((5,))],
     )(source_owner.T, source_local.T, tile_index.T, diag_index[None], aggregate_map.T)
-    lists = lax.all_to_all(
-        lists, "rows", split_axis=0, concat_axis=0, tiled=True, axis_index_groups=halves_of_rows
-    )
+    lists = lax.all_to_all(lists, "rows", split_axis=0, concat_axis=0, tiled=True)
     if n_bands == 2:
         near = lax.ppermute(index, "band", [(0, 1), (1, 0)])
     else:
@@ -693,6 +675,9 @@
         4 << 20,
     )(made, mirror, coupling_tiles, lists, near)
     packed, late = lax.optimization_barrier((packed, lists))
+    if dense:
+        across = lax.ppermute(late, "band", [(0, 1), (1, 0)])
+        across, *bands = lax.optimization_barrier((across, *bands))
     sends = (packed.reshape(half, 2 * cap * n_rhs, states), *bands)
     halves_of_rows = [list(range(half)), list(range(half, n_rows))]
     def exchange(sends, groups=None):
@@ -703,17 +688,10 @@
 
     arrived_blocks, arrived_bands = exchange(sends, halves_of_rows)
 
-    mirror_lists = lax.ppermute(late, "rows", to_mirror)
     extra, extra_scratch, tail = (), [], 0
     if dense:
-        across = lax.ppermute(late, "band", [(0, 1), (1, 0)])
-        corner = [(b * n_rows + i, (1 - b) * n_rows + j) for b in range(2) for i, j in to_mirror]
-        corner = lax.ppermute(late, ("band", "rows"), corner)
-        near_half = jnp.stack([late, across])[:, :, 0, LANES:]
-        far_half = jnp.stack([mirror_lists, corner])[:, :, 0, LANES:]
-        upper = my_row >= half
-        fields = [jnp.where(upper, far_half, near_half), jnp.where(upper, near_half, far_half)]
-        fields = jnp.concatenate(fields, axis=1).reshape(2, n_rows, -1, rows).transpose(2, 0, 1, 3)
+        fields = jnp.stack([late, across])[:, :, 0, LANES:]
+        fields = fields.reshape(2, n_rows, -1, rows).transpose(2, 0, 1, 3)
         fields = fields.reshape(-1, 2, n_rows * rows)
         n_blocks = slots + 2 * rows
         length = n_dev * depth
@@ -731,7 +709,7 @@
                 jax.ShapeDtypeStruct(*placing_shape),
                 jax.ShapeDtypeStruct((depth, LANES), f32),
             ),
-            [VMEM] * 6,
+            [VMEM] * 5,
             [HBM, HBM, HBM, VMEM],
             [
                 pltpu.VMEM(*count_shape),
@@ -741,7 +719,7 @@
             ],
             4 * total_groups * n_tiles * n_dev * rows * n_blocks,
             4 << 20,
-        )(fields, late[:, 0, :LANES], mirror_lists[:, 0, :LANES], coupling_tiles, diag_table, inverse_table)
+        )(fields, late[:, 0, :LANES], coupling_tiles, diag_table, inverse_table)
         extra = (functionals, counts, placing)
         extra_scratch = [
             *[pltpu.VMEM(*shape) for shape in extra_shapes],
@@ -756,12 +734,11 @@
     sends = call(
         functools.partial(middle_kernel, sizes, width_k, n_ways, dense),
         (jax.ShapeDtypeStruct(send_shape, f32), *band_shapes),
-        [ANY] * 5 + [VMEM] * 3 + [HBM] + [ANY] * n_ways + [HBM] * len(extra),
+        [ANY] * 4 + [VMEM] * 3 + [HBM] + [ANY] * n_ways + [HBM] * len(extra),
         [HBM] * (1 + n_ways),
         [
             *row_scratch,
-            list_scratch,
-            list_scratch,
+            pltpu.SMEM((n_rows, 1, LANES), i32),
             near_scratch,
             sums,
             products,
@@ -769,7 +746,7 @@
             *term_scratch,
             *band_scratch,
             term_sems,
-            pltpu.SemaphoreType.DMA((5,)),
+            pltpu.SemaphoreType.DMA((4,)),
             pltpu.SemaphoreType.DMA((n_rows + n_ways + 1,)),
             *extra_scratch,
         ],
@@ -779,7 +756,6 @@
         places,
         index,
         lists,
-        mirror_lists,
         near,
         arrived_blocks,
         inverse_table,
@@ -823,11 +799,8 @@
     index_all = lax.all_gather(index, ("band", "rows"), axis=0, tiled=True)
     index_all = index_all.reshape(n_bands, n_rows, wide)
     groups_all, diags_all = index_all[:, :, :rows], index_all[:, :, rows : 2 * rows]
-    lanes = LANES // 2
-    codes = jnp.concatenate([lists[:, 0, :cap], mirror_lists[:, 0, lanes : lanes + cap]], axis=0)
-    asker = jnp.arange(n_rows, dtype=i32)
-    asker = jnp.where(my_row < half, asker, (asker + half) % n_rows)
-    asked = asker[:, None] * rows + codes // (rows * n_tiles) % rows
+    codes = lists[:, 0, :cap]
+    asked = jnp.arange(n_rows, dtype=i32)[:, None] * rows + codes // (rows * n_tiles) % rows
     asked = jnp.where(codes > 0, asked, -1).reshape(-1)
     table_sums = jnp.sum(diag_table, axis=(1, 2))
     diag_onehot = diags_all.reshape(-1, 1) == jnp.arange(n_diag, dtype=i32)[None]

time: 86.3 us -> 80 us (0.927)
  waiting for transfers between devices: 35.9 us -> 32.4 us
  starting transfers between devices: 26.5 us -> 23.5 us
    ppermute x2 -> x0, waiting for transfers between devices: 8.54 us -> none  [the longest x1 8.54 us: on_device(): corner = lax.ppermute(late, ('band', 'rows'), corner)]
    all_to_all x2, starting transfers between devices: 13.4 us -> 8.96 us  [exchange(): lax.all_to_all(sends[0], 'rows', split_axis=0, concat_axis=0, tiled=True,...]
    ppermute x2 -> x0, starting transfers between devices: 2.87 us -> none  [the longest x1 2.54 us: on_device(): mirror_lists = lax.ppermute(late, 'rows', to_mirror)]
    all_to_all x1, starting transfers between devices: 4.12 us -> 6.73 us  [on_device(): lax.all_to_all(lists, 'rows', split_axis=0, concat_axis=0, tiled=True)]
    ppermute x1, waiting for transfers between devices: 0.01 us -> 2.31 us  [on_device(): across = lax.ppermute(late, 'band', [(0, 1), (1, 0)])]
    all_to_all x1, waiting for transfers between devices: 0.01 us -> 2.16 us  [on_device(): lax.all_to_all(lists, 'rows', split_axis=0, concat_axis=0, tiled=True)]
    all_to_all x2, waiting for transfers between devices: 25.8 us -> 27.6 us  [exchange(): lax.all_to_all(sends[0], 'rows', split_axis=0, concat_axis=0, tiled=True,...]
  transfers between devices with their start and end apart: 11 -> 9, of which waited for: 4 -> 5; matrix products, arithmetic and copies ran while one was open for 0% -> 0% of each run, Pallas kernels for 15% -> 17%
where the time goes in v9:
time: 80 us; the launch traced here: 79.5 us
  waiting for transfers between devices  32.4 us (40%)
  starting transfers between devices  23.5 us (29%)
  Pallas kernels  23.1 us (29%)
    all_to_all x2, waiting for transfers between devices, exchange(): lax.all_to_all(sends[0], 'rows', split_axis=0, concat_axis=0, tiled=True,...  27.6 us
    pallas_call x8, Pallas kernels, apply(): return run(*pinned)  23.1 us
    all_to_all x2, starting transfers between devices, exchange(): lax.all_to_all(sends[0], 'rows', split_axis=0, concat_axis=0, tiled=True,...  8.96 us
    all_to_all x1, starting transfers between devices, on_device(): lax.all_to_all(lists, 'rows', split_axis=0, concat_axis=0, tiled=True)  6.73 us
    ppermute x2, starting transfers between devices, to_bands(): return (lax.ppermute(sends[0], 'band', [(0, 1), (1, 0)]),)  3.1 us
    ppermute x1, waiting for transfers between devices, on_device(): across = lax.ppermute(late, 'band', [(0, 1), (1, 0)])  2.31 us
    all_to_all x1, waiting for transfers between devices, on_device(): lax.all_to_all(lists, 'rows', split_axis=0, concat_axis=0, tiled=True)  2.16 us
  transfers between devices with their start and end apart: 9, of which 5 were waited for; matrix products, arithmetic and copies ran while one was open for 0% of the time, Pallas kernels for 17%

profile of v9, /device:TPU:16, one launch (start us, length us, event | category | flops | bytes accessed | tf_op | source)
XLA Modules:
  0.0 79.5 jit_solution(303449778260806880)
XLA Ops:
  0.0 1.8 %shard_map.100 = (s32[16,1,384]{2,1,0:T(1,128)}, s32[1,1,256]{2,1,0:T(1,128)S(1)}, s32[1,1,128]{2,1,0:T(1,128)S(1)}) custom-call(s32[2,32]{1,0:T(2,128)} %bitcast.18, s32[2,32]{1,0:T(2,128)} %bitcast.19, s32[4,32]{1,0:T(4,128)} %bitcast.17, s32[1,32]{1,0:T(1,128)} %bitcast.20, s32[1,32]{1,0:T(1,128)} %bitcast.21), custom_call_target="tpu_custom_call" | custom-call | tf_op jit(solution)/shard_map/pallas_call | solution.py:48
  1.8 6.7 %all-to-all-start = ((s32[16,1,384]{2,1,0:T(1,128)}), s32[16,1,384]{2,1,0:T(1,128)S(1)}, u32[]{:S(2)}, u32[]{:S(2)}) async-start(s32[16,1,384]{2,1,0:T(1,128)} %get-tuple-element.24), calls=%async_computation | async-start | bytes 49152 | tf_op jit(solution)/shard_map/all_to_all | solution.py:621
  8.5 1.6 %collective-permute-start = (s32[1,1,256]{2,1,0:T(1,128)S(1)}, s32[1,1,256]{2,1,0:T(1,128)S(1)}, u32[]{:S(2)}, u32[]{:S(2)}) collective-permute-start(s32[1,1,256]{2,1,0:T(1,128)S(1)} %get-tuple-element.23.refs_1_), channel_id=1, source_target_pairs={{0,16},{16,0},{1,17},{17,1},{2,18},{18,2},{3,19},{19,3},{4,20},{20... | collective-permute-start | bytes 3080 | tf_op jit(solution)/shard_map/ppermute | solution.py:623
  10.1 3.9 %shard_map.101.refs_0_ = f32[256,16,128]{2,1,0:T(8,128)} custom-call(f32[32,16,128]{2,1,0:T(8,128)} %start_in.1, f32[8,128,128]{2,1,0:T(8,128)} %refs_6_.1), custom_call_target="tpu_custom_call" | custom-call | flops 402653184 | bytes 4194304 | tf_op jit(solution)/shard_map/pallas_call | solution.py:48
  14.1 2.2 %all-to-all-done.refs_3_.refs_2_ = s32[16,1,384]{2,1,0:T(1,128)S(1)} async-done(((s32[16,1,384]{2,1,0:T(1,128)}), s32[16,1,384]{2,1,0:T(1,128)S(1)}, u32[]{:S(2)}, u32[]{:S(2)}) %all-to-all-start) | async-done | bytes 24608 | tf_op jit(solution)/shard_map/all_to_all | solution.py:621
  16.2 2.7 %shard_map.102 = (f32[8,16,16,128]{3,2,1,0:T(8,128)}, f32[32,16,128]{2,1,0:T(8,128)}) custom-call(f32[256,16,128]{2,1,0:T(8,128)} %shard_map.101.refs_0_, f32[32,16,128]{2,1,0:T(8,128)S(1)} %collective-permute-done.1.refs_1_, f32[8,128,128]{2,1,0:T(8,128)S(1)} %copy-done, s32[16,1,384]{2,1,0:T(1,128)S(1)} %all-to-all-done.refs_3_.refs_2_, ...), custom_call_target="tpu_custom_call" | custom-call | flops 402653184 | bytes 4194304 | tf_op jit(solution)/shard_map/pallas_call | solution.py:48
  19.0 0.0 copy-start.3
  19.0 3.7 %all-to-all-start.1 = ((f32[8,256,128]{2,1,0:T(8,128)}), f32[8,256,128]{2,1,0:T(8,128)S(1)}, u32[]{:S(2)}, u32[]{:S(2)}) async-start(f32[8,256,128]{2,1,0:T(8,128)} %bitcast.14), calls=%async_computation.1 | async-start | bytes 2097152 | tf_op jit(solution)/shard_map/all_to_all | solution.py:684
  22.7 1.6 %collective-permute-start.2 = (s32[16,1,384]{2,1,0:T(1,128)S(1)}, s32[16,1,384]{2,1,0:T(1,128)S(1)}, u32[]{:S(2)}, u32[]{:S(2)}) collective-permute-start(s32[16,1,384]{2,1,0:T(1,128)S(1)} %all-to-all-done.refs_3_.refs_2_), channel_id=1, source_target_pairs={{0,16},{16,0},{1,17},{17,1},{2,18},{18,2},{3,19},{19,3},{4,20},{20... | collective-permute-start | bytes 73736 | tf_op jit(solution)/shard_map/ppermute | solution.py:679
  24.3 2.3 %collective-permute-done.2 = s32[16,1,384]{2,1,0:T(1,128)S(1)} collective-permute-done((s32[16,1,384]{2,1,0:T(1,128)S(1)}, s32[16,1,384]{2,1,0:T(1,128)S(1)}, u32[]{:S(2)}, u32[]{:S(2)}) %collective-permute-start.2) | collective-permute-done | bytes 24608 | tf_op jit(solution)/shard_map/ppermute | solution.py:679
  26.6 1.5 %collective-permute-start.3 = (f32[32,16,128]{2,1,0:T(8,128)S(1)}, f32[32,16,128]{2,1,0:T(8,128)S(1)}, u32[]{:S(2)}, u32[]{:S(2)}) collective-permute-start(f32[32,16,128]{2,1,0:T(8,128)S(1)} %copy-done.3), channel_id=1, source_target_pairs={{0,16},{16,0},{1,17},{17,1},{2,18},{18,2},{3,19},{19,3},{4,20},{20... | collective-permute-start | bytes 786440 | tf_op jit(solution)/shard_map/ppermute | solution.py:564
  28.1 0.1 fusion
  28.2 0.1 reshape_squeeze.3
  28.3 0.1 reshape.7.refs_0_
  28.5 6.0 %shard_map.103 = (bf16[10,256,192]{2,1,0:T(8,128)(2,1)}, bf16[128,384]{1,0:T(8,128)(2,1)}, bf16[1024,256]{1,0:T(8,128)(2,1)}, f32[4,128]{1,0:T(4,128)S(1)}) custom-call(s32[8,2,512]{2,1,0:T(2,128)S(1)} %reshape.7.refs_0_, s32[16,128]{1,0:T(8,128)S(1)} %bitcast.13, f32[8,128,128]{2,1,0:T(8,128)S(1)} %copy-done, f32[8,128,128]{2,1,0:T(8,128)S(1)} %copy-done.2, ...), custom_call_target="tpu_custom_call" | custom-call | flops 1610612736 | bytes 4194304 | tf_op jit(solution)/shard_map/pallas_call | solution.py:48
  34.5 2.6 %all-to-all-done.1.refs_4_ = f32[8,256,128]{2,1,0:T(8,128)S(1)} async-done(((f32[8,256,128]{2,1,0:T(8,128)}), f32[8,256,128]{2,1,0:T(8,128)S(1)}, u32[]{:S(2)}, u32[]{:S(2)}) %all-to-all-start.1) | async-done | bytes 1048608 | tf_op jit(solution)/shard_map/all_to_all | solution.py:684
  37.1 5.9 %shard_map.104 = (f32[16,136,128]{2,1,0:T(8,128)}, f32[32,16,128]{2,1,0:T(8,128)}) custom-call(s32[1,1,128]{2,1,0:T(1,128)S(1)} %get-tuple-element.22.refs_0_, s32[1,1,256]{2,1,0:T(1,128)S(1)} %get-tuple-element.23.refs_1_, s32[16,1,384]{2,1,0:T(1,128)S(1)} %all-to-all-done.refs_3_.refs_2_, s32[1,1,256]{2,1,0:T(1,128)S(1)} %collective-permute-done.refs_4_.refs_3_, ...), custom_call_target="tpu_custom_call" | custom-call | flops 805306368 | bytes 4194304 | tf_op jit(solution)/shard_map/pallas_call | solution.py:48
  43.0 5.3 %all-to-all-start.2 = ((f32[16,136,128]{2,1,0:T(8,128)}), f32[16,136,128]{2,1,0:T(8,128)S(1)}, u32[]{:S(2)}, u32[]{:S(2)}) async-start(f32[16,136,128]{2,1,0:T(8,128)} %get-tuple-element.34), calls=%async_computation.2 | async-start | bytes 2228224 | tf_op jit(solution)/shard_map/all_to_all | solution.py:684
  48.3 1.6 %collective-permute-start.5 = (f32[32,16,128]{2,1,0:T(8,128)S(1)}, f32[32,16,128]{2,1,0:T(8,128)S(1)}, u32[]{:S(2)}, u32[]{:S(2)}) collective-permute-start(f32[32,16,128]{2,1,0:T(8,128)S(1)} %copy-done.4), channel_id=1, source_target_pairs={{0,16},{16,0},{1,17},{17,1},{2,18},{18,2},{3,19},{19,3},{4,20},{20... | collective-permute-start | bytes 786440 | tf_op jit(solution)/shard_map/ppermute | solution.py:564
  49.9 25.0 %all-to-all-done.2.arrived_ref.refs_2_ = f32[16,136,128]{2,1,0:T(8,128)S(1)} async-done(((f32[16,136,128]{2,1,0:T(8,128)}), f32[16,136,128]{2,1,0:T(8,128)S(1)}, u32[]{:S(2)}, u32[]{:S(2)}) %all-to-all-start.2) | async-done | bytes 1114144 | tf_op jit(solution)/shard_map/all_to_all | solution.py:684
  74.9 1.6 %collective-permute-start.4 = (f32[4,128]{1,0:T(4,128)S(1)}, f32[4,128]{1,0:T(4,128)S(1)}, u32[]{:S(2)}, u32[]{:S(2)}) collective-permute-start(f32[4,128]{1,0:T(4,128)S(1)} %get-tuple-element.36), channel_id=1, source_target_pairs={{0,16},{16,0},{1,17},{17,1},{2,18},{18,2},{3,19},{19,3},{4,20},{20... | collective-permute-start | bytes 6152 | tf_op jit(solution)/shard_map/ppermute | solution.py:772
  76.5 1.8 %shard_map.106.second_ref = f32[32,16,128]{2,1,0:T(8,128)S(1)} custom-call(s32[1,1,128]{2,1,0:T(1,128)S(1)} %get-tuple-element.22.refs_0_, s32[1,1,256]{2,1,0:T(1,128)S(1)} %get-tuple-element.23.refs_1_, f32[16,136,128]{2,1,0:T(8,128)S(1)} %all-to-all-done.2.arrived_ref.refs_2_, f32[8,128,128]{2,1,0:T(8,128)S(1)} %copy-done.1, f32[32,16,128]{2,1,0:T(8,128)} %refs_4_.3, ...), custom_call_target="tpu_custom_call" | custom-call | flops 402653184 | bytes 4194304 | tf_op jit(solution)/shard_map/pallas_call | solution.py:48
  78.2 0.3 collective-permute-done.4.other_ref
  78.5 1.0 %shard_map.107 = f32[32,16,128]{2,1,0:T(8,128)} custom-call(f32[4,128]{1,0:T(4,128)S(1)} %get-tuple-element.35.mine_ref, f32[4,128]{1,0:T(4,128)S(1)} %collective-permute-done.4.other_ref, f32[4,128]{1,0:T(4,128)S(1)} %get-tuple-element.37.scale_ref, f32[32,16,128]{2,1,0:T(8,128)S(1)} %shard_map.106.second_ref), custom_call_target="tpu_custom_call" | custom-call | tf_op jit(solution)/shard_map/pallas_call | solution.py:48
  (17 shorter events, 0.1 us)
Async XLA Ops:
  0.0 16.2 %collective-permute-start.1 = (f32[32,16,128]{2,1,0:T(8,128)}, f32[32,16,128]{2,1,0:T(8,128)S(1)}, u32[]{:S(2)}, u32[]{:S(2)}) collective-permute-start(f32[32,16,128]{2,1,0:T(8,128)} %start_in.1), channel_id=1, source_target_pairs={{0,8},{1,9},{2,10},{3,11},{4,12},{5,13},{6,14},{7,15},{8,0},{9,1},... | collective-permute-start | bytes 786440 | tf_op jit(solution)/shard_map/ppermute | solution.py:609
  1.8 14.4 %all-to-all-start = ((s32[16,1,384]{2,1,0:T(1,128)}), s32[16,1,384]{2,1,0:T(1,128)S(1)}, u32[]{:S(2)}, u32[]{:S(2)}) async-start(s32[16,1,384]{2,1,0:T(1,128)} %get-tuple-element.24), calls=%async_computation | async-start | bytes 49152 | tf_op jit(solution)/shard_map/all_to_all | solution.py:621
  8.5 7.7 %copy-start = (f32[8,128,128]{2,1,0:T(8,128)S(1)}, f32[8,128,128]{2,1,0:T(8,128)}, u32[]{:S(2)}) copy-start(f32[8,128,128]{2,1,0:T(8,128)} %refs_6_.1) | copy-start | bytes 1572868
  8.5 5.5 %collective-permute-start = (s32[1,1,256]{2,1,0:T(1,128)S(1)}, s32[1,1,256]{2,1,0:T(1,128)S(1)}, u32[]{:S(2)}, u32[]{:S(2)}) collective-permute-start(s32[1,1,256]{2,1,0:T(1,128)S(1)} %get-tuple-element.23.refs_1_), channel_id=1, source_target_pairs={{0,16},{16,0},{1,17},{17,1},{2,18},{18,2},{3,19},{19,3},{4,20},{20... | collective-permute-start | bytes 3080 | tf_op jit(solution)/shard_map/ppermute | solution.py:623
  19.0 7.6 %copy-start.3 = (f32[32,16,128]{2,1,0:T(8,128)S(1)}, f32[32,16,128]{2,1,0:T(8,128)}, u32[]{:S(2)}) copy-start(f32[32,16,128]{2,1,0:T(8,128)} %get-tuple-element.29) | copy-start | bytes 786436
  19.0 9.5 %copy-start.1 = (f32[8,128,128]{2,1,0:T(8,128)S(1)}, f32[8,128,128]{2,1,0:T(8,128)}, u32[]{:S(2)}) copy-start(f32[8,128,128]{2,1,0:T(8,128)} %refs_3_.3) | copy-start | bytes 1572868
  19.0 9.5 %copy-start.2 = (f32[8,128,128]{2,1,0:T(8,128)S(1)}, f32[8,128,128]{2,1,0:T(8,128)}, u32[]{:S(2)}) copy-start(f32[8,128,128]{2,1,0:T(8,128)} %refs_3_.2) | copy-start | bytes 1572868
  19.0 18.1 %all-to-all-start.1 = ((f32[8,256,128]{2,1,0:T(8,128)}), f32[8,256,128]{2,1,0:T(8,128)S(1)}, u32[]{:S(2)}, u32[]{:S(2)}) async-start(f32[8,256,128]{2,1,0:T(8,128)} %bitcast.14), calls=%async_computation.1 | async-start | bytes 2097152 | tf_op jit(solution)/shard_map/all_to_all | solution.py:684
  22.7 3.9 %collective-permute-start.2 = (s32[16,1,384]{2,1,0:T(1,128)S(1)}, s32[16,1,384]{2,1,0:T(1,128)S(1)}, u32[]{:S(2)}, u32[]{:S(2)}) collective-permute-start(s32[16,1,384]{2,1,0:T(1,128)S(1)} %all-to-all-done.refs_3_.refs_2_), channel_id=1, source_target_pairs={{0,16},{16,0},{1,17},{17,1},{2,18},{18,2},{3,19},{19,3},{4,20},{20... | collective-permute-start | bytes 73736 | tf_op jit(solution)/shard_map/ppermute | solution.py:679
  26.6 7.8 %collective-permute-start.3 = (f32[32,16,128]{2,1,0:T(8,128)S(1)}, f32[32,16,128]{2,1,0:T(8,128)S(1)}, u32[]{:S(2)}, u32[]{:S(2)}) collective-permute-start(f32[32,16,128]{2,1,0:T(8,128)S(1)} %copy-done.3), channel_id=1, source_target_pairs={{0,16},{16,0},{1,17},{17,1},{2,18},{18,2},{3,19},{19,3},{4,20},{20... | collective-permute-start | bytes 786440 | tf_op jit(solution)/shard_map/ppermute | solution.py:564
  43.0 5.3 %copy-start.4 = (f32[32,16,128]{2,1,0:T(8,128)S(1)}, f32[32,16,128]{2,1,0:T(8,128)}, u32[]{:S(2)}) copy-start(f32[32,16,128]{2,1,0:T(8,128)} %get-tuple-element.38) | copy-start | bytes 786436
  43.0 31.8 %all-to-all-start.2 = ((f32[16,136,128]{2,1,0:T(8,128)}), f32[16,136,128]{2,1,0:T(8,128)S(1)}, u32[]{:S(2)}, u32[]{:S(2)}) async-start(f32[16,136,128]{2,1,0:T(8,128)} %get-tuple-element.34), calls=%async_computation.2 | async-start | bytes 2228224 | tf_op jit(solution)/shard_map/all_to_all | solution.py:684
  48.3 28.2 %collective-permute-start.5 = (f32[32,16,128]{2,1,0:T(8,128)S(1)}, f32[32,16,128]{2,1,0:T(8,128)S(1)}, u32[]{:S(2)}, u32[]{:S(2)}) collective-permute-start(f32[32,16,128]{2,1,0:T(8,128)S(1)} %copy-done.4), channel_id=1, source_target_pairs={{0,16},{16,0},{1,17},{17,1},{2,18},{18,2},{3,19},{19,3},{4,20},{20... | collective-permute-start | bytes 786440 | tf_op jit(solution)/shard_map/ppermute | solution.py:564
  74.9 3.6 %collective-permute-start.4 = (f32[4,128]{1,0:T(4,128)S(1)}, f32[4,128]{1,0:T(4,128)S(1)}, u32[]{:S(2)}, u32[]{:S(2)}) collective-permute-start(f32[4,128]{1,0:T(4,128)S(1)} %get-tuple-element.36), channel_id=1, source_target_pairs={{0,16},{16,0},{1,17},{17,1},{2,18},{18,2},{3,19},{19,3},{4,20},{20... | collective-permute-start | bytes 6152 | tf_op jit(solution)/shard_map/ppermute | solution.py:772

commit v10 on v9

--- a/solution.py
+++ b/solution.py
@@ -10,6 +10,7 @@
 AGG_DEV = 8
 LANES = 128
 DENSE_LIMIT = 1 << 19
+BEHIND_SWAP = 100
 
 VMEM = pl.BlockSpec(memory_space=pltpu.VMEM)
 SMEM = pl.BlockSpec(memory_space=pltpu.SMEM)
@@ -262,12 +263,9 @@
     parts = jnp.concatenate(parts, axis=1)
     lane = lax.broadcasted_iota(jnp.int32, (length, LANES), 1)
     result = jnp.zeros((length, LANES), jnp.float32)
+    placed = jnp.dot(place_ref[...], parts, preferred_element_type=jnp.float32)
     for spot in range(per_tile):
-        chosen = jnp.dot(
-            place_ref[spot * length : (spot + 1) * length, :],
-            parts,
-            preferred_element_type=jnp.float32,
-        )
+        chosen = placed[spot * length : (spot + 1) * length]
         chosen = sum(chosen[:, n * LANES : (n + 1) * LANES] for n in range(n_parts))
         result = jnp.where((lane >= spot * n_rhs) & (lane < (spot + 1) * n_rhs), chosen, result)
     return result
@@ -282,7 +280,7 @@
     field_ref, list_ref, tile_ref, table_ref, inverse_ref = refs[:5]
     count_out, functional_out, placing_out, scale_ref = refs[5:9]
     count_ref, functional_ref, placing_ref, sems = refs[9:]
-    n_groups, n_blocks = count_ref.shape[1:]
+    n_groups, n_blocks = count_ref.shape[0], count_ref.shape[1] // (n_tiles + 2)
     slots, band_rows = n_rows * cap, n_rows * rows
     copies = []
 
@@ -335,22 +333,21 @@
         origins = [field(4 + width_k + k, side) for k in range(width_k)] + [row_ids]
         hits = one_hot(targets, jnp.concatenate(origins, axis=1))
         sides.append((takers, hits, field(0, side)))
+    pieces = []
     for t in range(n_tiles):
         found = []
         for takers, hits, _ in sides:
             ids = lax.broadcasted_iota(jnp.int32, (n_groups, takers.shape[1]), 0) + t * n_groups
             found.append(dot_nt(one_hot(ids, takers), hits))
-        count_ref[t] = jnp.concatenate(found, axis=1).astype(jnp.bfloat16)
-        send(count_ref.at[t], count_out.at[t])
+        pieces += found
     ids = lax.broadcasted_iota(jnp.int32, (n_groups, band_rows), 0)
     found = [dot_nt(one_hot(ids, groups), hits[:, -band_rows:]) for _, hits, groups in sides]
     found = jnp.concatenate(found, axis=1)
-    count_ref[n_tiles] = found.astype(jnp.bfloat16)
-    send(count_ref.at[n_tiles], count_out.at[n_tiles])
     block = lax.broadcasted_iota(jnp.int32, found.shape, 1)
     mine = (block >= slots) & (block < slots + rows)
-    count_ref[n_tiles + 1] = jnp.where(mine, found, 0.0).astype(jnp.bfloat16)
-    send(count_ref.at[n_tiles + 1], count_out.at[n_tiles + 1])
+    pieces += [found, jnp.where(mine, found, 0.0)]
+    count_ref[...] = jnp.concatenate(pieces, axis=1).astype(jnp.bfloat16)
+    send(count_ref, count_out)
 
     per_tile = LANES // n_rhs
     depth = rows // per_tile
@@ -384,18 +381,10 @@
     finish(copies)
 
 
-def gather_solve(
-    sizes, slots, diags, arrived_ref, later, terms, inverse_ref, sum_ref, product_ref
-):
+def gather_solve(sizes, fetch, diags, later, terms, inverse_ref, sum_ref, product_ref):
     rows, n_rows, cap, n_tiles, n_rhs = sizes
-    per = n_rows * cap // arrived_ref.shape[0]
     for row in range(rows):
-        total = None
-        for slot in slots(row):
-            start = pl.multiple_of(below(slot, per) * n_rhs, n_rhs)
-            block = arrived_ref[over(slot, per), pl.ds(start, n_rhs), :]
-            total = block if total is None else total + block
-        sum_ref[pl.ds(row * n_rhs, n_rhs), :] = total
+        sum_ref[pl.ds(row * n_rhs, n_rhs), :] = fetch(row)
     finish(later)
     total = sum_ref[...]
     for term in terms:
@@ -405,152 +394,210 @@
         sum_ref[pl.ds(row * n_rhs, n_rhs), :] = product_ref[diags(row) * rows + row]
 
 
-def middle_kernel(sizes, width_k, n_band, dense, *refs):
-    metadata_in, arrived_ref, inverse_ref, tile_ref = list(refs[:4]), *refs[4:7]
-    metadata_in[2] = metadata_in[2].at[:, :, pl.ds(0, LANES)]
-    terms_in, refs = refs[7 : 8 + n_band], refs[8 + n_band :]
-    extra, refs = (refs[:3], refs[3:]) if dense else ((), refs)
-    send_out, band_out, refs = refs[0], refs[1 : 1 + n_band], refs[1 + n_band :]
-    metadata, sum_ref, product_ref, send_ref = refs[:4], *refs[4:7]
-    place_ref, index_ref, list_ref, near_ref = metadata
-    terms, band_refs, refs = refs[7 : 8 + n_band], refs[8 + n_band : 8 + 2 * n_band], refs[8 + 2 * n_band :]
-    term_sems, meta_sems, send_sems, refs = *refs[:3], refs[3:]
-    right_ref = terms[0]
+def arrived_blocks_of(sizes, width_k, place_ref, field, arrived_ref):
     rows, n_rows, cap, n_tiles, n_rhs = sizes
-    body = cap * n_rhs
-    metadata = copies_of(zip(metadata_in, metadata), meta_sems)
-    later = copies_of(zip(terms_in, terms), term_sems)
-    fetched = []
-    if dense:
-        held, extra_sems, value_ref, spread_ref, result_ref = refs[:3], *refs[3:]
-        n_diag = inverse_ref.shape[0]
-        fetched = copies_of(zip(extra, held), extra_sems)
-    finish(metadata)
-
-    def slots(row):
-        return [place_ref[0, 0, k * rows + row] for k in range(width_k)]
-
-    def diags(row):
-        return index_ref[0, 0, rows + row]
-
-    gather_solve(sizes, slots, diags, arrived_ref, later, terms, inverse_ref, sum_ref, product_ref)
-    table_products(sum_ref[...], tile_ref, product_ref)
-    copies = []
-
-    def send(source, target):
-        copies.extend(started([pltpu.make_async_copy(source, target, send_sems.at[len(copies)])]))
-
-    pack_bands(sizes, width_k, product_ref, near_ref, band_refs)
-    for ref, out in zip(band_refs, band_out):
-        send(ref, out)
-    codes = []
-    for owner in range(n_rows):
-        for rank in range(cap):
-            code = list_ref[owner, 0, rank]
-            codes.append(code)
-            block = product_ref[below(code, rows * n_tiles)]
-            send_ref[owner, rank * n_rhs : (rank + 1) * n_rhs, :] = block
-        target = send_out.at[owner]
-        send(send_ref.at[owner], target.at[pl.ds(0, body)] if dense else target)
-    if dense:
-        finish(fetched)
-        kinds = [below(over(code, rows * n_tiles * rows), n_diag) for code in codes]
-        kinds += [diags(row) for row in range(rows)]
-        kinds += [near_ref[0, 0, rows + row] for row in range(rows)]
-        result = coarse_parts(
-            sizes, kinds, held, right_ref, send_ref, band_refs, value_ref, spread_ref
-        )
-        result_ref[...] = result.reshape(result_ref.shape)
-        send(result_ref, send_out.at[:, pl.ds(body, result_ref.shape[1])])
-    finish(copies)
-
-
-def coarse_parts(sizes, kinds, held, right_ref, send_ref, band_refs, value_ref, spread_ref):
-    functional_ref, count_ref, place_ref = held
-    rows, n_rows, cap, n_tiles, n_rhs = sizes
-    body = cap * n_rhs
-    n_func = spread_ref.shape[0] // count_ref.shape[2]
-    per_tile = LANES // n_rhs
-    functional = functional_ref[...]
-    done = 0
-    for owner in range(0, n_rows, 2):
-        values = [send_ref[owner + more] for more in range(2)]
-        values = jnp.concatenate(values, axis=0)
-        value_ref[:, done : done + 2 * body] = dot_nt(functional, right_operand(values))
-        done += 2 * body
-    for ref in (right_ref, *band_refs):
-        values = ref[...].reshape(rows * n_rhs, -1)
-        value_ref[:, done : done + rows * n_rhs] = dot_nt(functional, right_operand(values))
-        done += rows * n_rhs
-    lane = lax.broadcasted_iota(jnp.int32, (n_func, LANES), 1)
-    for block, kind in enumerate(kinds):
-        tile, spot = block // per_tile, block % per_tile
-        start = pl.multiple_of(kind * n_func, n_func)
-        piece = value_ref[pl.ds(start, n_func), tile * LANES : (tile + 1) * LANES]
-        piece = jnp.where((lane >= spot * n_rhs) & (lane < (spot + 1) * n_rhs), piece, 0.0)
-        spread_ref[block * n_func : (block + 1) * n_func, :] = piece
-    partial = jnp.zeros((count_ref.shape[1], 2 * LANES), jnp.float32)
-    for t in range(count_ref.shape[0]):
-        values = spread_ref[pl.ds(t, done // n_rhs, stride=n_func), :]
-        partial = partial + jnp.dot(
-            count_ref[t],
-            jnp.concatenate(halves(values), axis=1),
-            preferred_element_type=jnp.float32,
-        )
-    partial = partial[:, :LANES] + partial[:, LANES:]
-    source = lax.broadcasted_iota(jnp.int32, (LANES, LANES), 0)
-    target = lax.broadcasted_iota(jnp.int32, (LANES, LANES), 1)
-    same = jnp.where(lax.rem(source, n_rhs) == lax.rem(target, n_rhs), 1.0, 0.0)
-    same = same.astype(jnp.bfloat16)
-    same = jnp.concatenate([same, same], axis=0)
-    partial = jnp.dot(
-        jnp.concatenate(halves(partial), axis=1), same, preferred_element_type=jnp.float32
-    )
-    return place(place_ref, partial, n_rhs, 2)
-
-
-def part_kernel(arrived_ref, mine_ref, other_ref):
-    depth = mine_ref.shape[0]
-    body = arrived_ref.shape[1] - 2 * depth
-    total = arrived_ref[0, body:, :]
-    for source in range(1, arrived_ref.shape[0]):
-        total = total + arrived_ref[source, body:, :]
-    upper = lax.axis_index("band") == 0
-    mine_ref[...] = jnp.where(upper, total[:depth], total[depth:])
-    other_ref[...] = jnp.where(upper, total[depth:], total[:depth])
-
-
-def last_kernel(sizes, width_k, n_band, *refs):
+    per = n_rows * cap // arrived_ref.shape[0]
+
+    def fetch(row):
+        total = None
+        for k in range(width_k):
+            slot = place_ref[0, 0, (field + k) * rows + row]
+            start = pl.multiple_of(below(slot, per) * n_rhs, n_rhs)
+            block = arrived_ref[over(slot, per), pl.ds(start, n_rhs), :]
+            total = block if total is None else total + block
+        return total
+
+    return fetch
+
+
+def solve_kernel(sizes, width_k, n_band, field, *refs):
     metadata_in, arrived_ref, inverse_ref = refs[:2], *refs[2:4]
     terms_in, refs = refs[4 : 5 + n_band], refs[5 + n_band :]
-    second_ref, metadata, sum_ref, product_ref = refs[0], refs[1:3], *refs[3:5]
+    out_ref, metadata, sum_ref, product_ref = refs[0], refs[1:3], *refs[3:5]
     place_ref, index_ref = metadata
     terms, (term_sems, meta_sems) = refs[5 : 6 + n_band], refs[6 + n_band :]
     rows = sizes[0]
     metadata = copies_of(zip(metadata_in, metadata), meta_sems)
     later = copies_of(zip(terms_in, terms), term_sems)
     finish(metadata)
-
-    def slots(row):
-        return [place_ref[0, 0, (width_k + k) * rows + row] for k in range(width_k)]
+    fetch = arrived_blocks_of(sizes, width_k, place_ref, field, arrived_ref)
 
     def diags(row):
         return index_ref[0, 0, rows + row]
 
-    gather_solve(sizes, slots, diags, arrived_ref, later, terms, inverse_ref, sum_ref, product_ref)
-    second_ref[...] = sum_ref[...].reshape(second_ref.shape)
-
-
-def final_kernel(sizes, mine_ref, other_ref, scale_ref, second_ref, out_ref):
-    rows, n_rhs = sizes[0], sizes[4]
+    gather_solve(sizes, fetch, diags, later, terms, inverse_ref, sum_ref, product_ref)
+    out_ref[...] = sum_ref[...].reshape(out_ref.shape)
+
+
+def pack_kernel(sizes, width_k, n_band, *refs):
+    rows, n_rows, cap, n_tiles, n_rhs = sizes
+    list_in, near_in, first_ref, tile_ref, send_out = refs[:5]
+    band_out, refs = refs[5 : 5 + n_band], refs[5 + n_band :]
+    list_ref, near_ref, product_ref, send_ref = refs[:4]
+    band_refs, (meta_sems, send_sems) = refs[4 : 4 + n_band], refs[4 + n_band :]
+    list_in = list_in.at[:, :, pl.ds(0, LANES)]
+    metadata = copies_of(((list_in, list_ref), (near_in, near_ref)), meta_sems)
+    table_products(first_ref[...].reshape(rows * n_rhs, -1), tile_ref, product_ref)
+    finish(metadata)
+    pack_bands(sizes, width_k, product_ref, near_ref, band_refs)
+    for owner in range(n_rows):
+        for rank in range(cap):
+            block = product_ref[below(list_ref[owner, 0, rank], rows * n_tiles)]
+            send_ref[owner, rank * n_rhs : (rank + 1) * n_rhs, :] = block
+    finish(copies_of(zip((send_ref, *band_refs), (send_out, *band_out)), send_sems))
+
+
+def own_kernel(sizes, width_k, *refs):
+    rows, n_rows, cap, n_tiles, n_rhs = sizes
+    metadata_in, first_ref, tile_ref, right_in, extra = list(refs[:3]), *refs[3:6], refs[6:9]
+    send_out, band_out, metadata, product_ref, send_ref, right_ref, band_ref = refs[9], refs[10], refs[11:14], *refs[14:18]
+    held, value_ref, spread_ref, result_ref, meta_sems, load_sems, send_sems = refs[18:21], *refs[21:]
+    index_ref, list_ref, near_ref = metadata
+    metadata_in[1] = metadata_in[1].at[:, :, pl.ds(0, LANES)]
+    metadata = copies_of(zip(metadata_in, metadata), meta_sems)
+    fetched = copies_of(zip((right_in, *extra), (right_ref, *held)), load_sems)
+    table_products(first_ref[...].reshape(rows * n_rhs, -1), tile_ref, product_ref)
+    finish(metadata)
+    copies = []
+
+    def send(source, target):
+        copies.extend(started([pltpu.make_async_copy(source, target, send_sems.at[len(copies)])]))
+
+    pack_bands(sizes, width_k, product_ref, near_ref, (band_ref,))
+    send(band_ref, band_out)
+    body, half = cap * n_rhs, n_rows // 2
+    upper = lax.axis_index("rows") >= half
+    mine, others = jnp.where(upper, half, 0), jnp.where(upper, 0, half)
+    for first in (mine, others):
+        for device in range(half):
+            owner = first + device
+            for rank in range(cap):
+                block = product_ref[below(list_ref[owner, 0, rank], rows * n_tiles)]
+                send_ref[owner, rank * n_rhs : (rank + 1) * n_rhs, :] = block
+            if first is mine:
+                send(send_ref.at[owner], send_out.at[device, pl.ds(0, body)])
+    finish(fetched)
+    functional_ref, count_ref, place_ref = held
+    n_blocks = n_rows * cap + 2 * rows
+    n_func = spread_ref.shape[0] // n_blocks
+    n_diag = functional_ref.shape[0] // n_func
+    functional = functional_ref[...]
+    per_tile = LANES // n_rhs
+    lane = lax.broadcasted_iota(jnp.int32, (n_func, LANES), 1)
+
+    def spread(first, values, kinds):
+        wide = values.shape[0]
+        value_ref[:, first * n_rhs : first * n_rhs + wide] = dot_nt(functional, right_operand(values))
+        for block, kind in enumerate(kinds, first):
+            tile, spot = block // per_tile, block % per_tile
+            start = pl.multiple_of(kind * n_func, n_func)
+            piece = value_ref[pl.ds(start, n_func), tile * LANES : (tile + 1) * LANES]
+            piece = jnp.where((lane >= spot * n_rhs) & (lane < (spot + 1) * n_rhs), piece, 0.0)
+            spread_ref[block * n_func : (block + 1) * n_func, :] = piece
+
+    for owner in range(0, n_rows, 2):
+        kinds = []
+        for more in range(2):
+            for rank in range(cap):
+                code = list_ref[owner + more, 0, rank]
+                kinds.append(below(over(code, rows * n_tiles * rows), n_diag))
+        values = jnp.concatenate([send_ref[owner], send_ref[owner + 1]], axis=0)
+        spread(owner * cap, values, kinds)
+    done = n_rows * cap
+    kinds = [index_ref[0, 0, rows + row] for row in range(rows)]
+    spread(done, right_ref[...].reshape(rows * n_rhs, -1), kinds)
+    kinds = [near_ref[0, 0, rows + row] for row in range(rows)]
+    spread(done + rows, band_ref[...].reshape(rows * n_rhs, -1), kinds)
+    result = coarse_parts(n_rhs, n_blocks, count_ref, place_ref, spread_ref)
+    result_ref[...] = result.reshape(result_ref.shape)
+    depth = result_ref.shape[1]
+    for n, first in enumerate((mine, others)):
+        target = send_out.at[:, pl.ds(body + n * depth, depth)]
+        send(result_ref.at[pl.ds(first, half)], target)
+    finish(copies)
+
+
+def mirror_kernel(sizes, list_in, mirror_ref, tile_ref, send_out, list_ref, product_ref, send_ref, sems):
+    rows, n_rows, cap, n_tiles, n_rhs = sizes
+    half = n_rows // 2
+    base = jnp.where(lax.axis_index("rows") >= half, half, 0)
+    list_in = list_in.at[pl.ds(base, half), :, pl.ds(0, LANES)]
+    metadata = started([pltpu.make_async_copy(list_in, list_ref, sems.at[half])])
+    table_products(mirror_ref[...].reshape(rows * n_rhs, -1), tile_ref, product_ref)
+    finish(metadata)
+    copies = []
+    for device in range(half):
+        for rank in range(cap):
+            code = list_ref[device, 0, LANES // 2 + rank]
+            block = product_ref[below(code, rows * n_tiles)]
+            send_ref[device, rank * n_rhs : (rank + 1) * n_rhs, :] = block
+        copy = pltpu.make_async_copy(send_ref.at[device], send_out.at[device], sems.at[device])
+        copies += started([copy])
+    finish(copies)
+
+
+def coarse_parts(n_rhs, n_blocks, count_ref, place_ref, spread_ref):
+    n_func = spread_ref.shape[0] // n_blocks
+    values = [
+        spread_ref[pl.ds(t, n_blocks, stride=n_func), :] for t in range(count_ref.shape[1] // n_blocks)
+    ]
+    values = jnp.concatenate(values, axis=0)
+    partial = jnp.dot(
+        count_ref[...], jnp.concatenate(halves(values), axis=1), preferred_element_type=jnp.float32
+    )
+    partial = partial[:, :LANES] + partial[:, LANES:]
+    shift = LANES // 2
+    while shift >= n_rhs:
+        partial = partial + pltpu.roll(partial, shift, axis=1)
+        shift //= 2
+    return place(place_ref, partial, n_rhs, 2)
+
+
+def part_kernel(arrived_ref, keep_ref, give_ref):
+    depth = keep_ref.shape[0] // 2
+    body = arrived_ref.shape[1] - 4 * depth
+    total = arrived_ref[0, body:, :]
+    for source in range(1, arrived_ref.shape[0]):
+        total = total + arrived_ref[source, body:, :]
+    lower = lax.axis_index("band") == 0
+    for n in range(2):
+        zero, one = (total[(2 * n + m) * depth : (2 * n + m + 1) * depth] for m in range(2))
+        keep_ref[n * depth : (n + 1) * depth] = jnp.where(lower, zero, one)
+        give_ref[n * depth : (n + 1) * depth] = jnp.where(lower, one, zero)
+
+
+def final_kernel(sizes, width_k, *refs):
+    rows, n_rows, cap, n_tiles, n_rhs = sizes
+    metadata_in, own_ref, mirror_ref, inverse_ref, terms_in = refs[:2], *refs[2:5], refs[5:7]
+    near_ref, far_ref, scale_ref, out_ref = refs[7:11]
+    metadata, sum_ref, product_ref, terms, term_sems, meta_sems = refs[11:13], *refs[13:15], refs[15:17], *refs[17:]
+    place_ref, index_ref = metadata
+    metadata = copies_of(zip(metadata_in, metadata), meta_sems)
+    later = copies_of(zip(terms_in, terms), term_sems)
+    finish(metadata)
+
+    def fetch(row):
+        total = None
+        for k in range(width_k):
+            slot = place_ref[0, 0, k * rows + row]
+            holder, slot = over(slot, 2 * cap), below(slot, 2 * cap)
+            start = pl.ds(pl.multiple_of(below(slot, cap) * n_rhs, n_rhs), n_rhs)
+            block = jnp.where(slot < cap, own_ref[holder, start, :], mirror_ref[holder, start, :])
+            total = block if total is None else total + block
+        return total
+
+    def diags(row):
+        return index_ref[0, 0, rows + row]
+
     depth = scale_ref.shape[0]
-    correction = (mine_ref[...] + other_ref[...]) / scale_ref[...]
+    correction = (near_ref[...] + far_ref[...]) / scale_ref[...]
     padded = jnp.concatenate([correction, jnp.zeros((8 - depth, LANES), jnp.float32)], axis=0)
     turned = padded.T
+    gather_solve(sizes, fetch, diags, later, terms, inverse_ref, sum_ref, product_ref)
     for row in range(rows):
         spot, place = row // depth, row % depth
         column = turned[spot * n_rhs : (spot + 1) * n_rhs, place : place + 1]
-        out_ref[row] = second_ref[row] + column
+        out_ref[row] = sum_ref[pl.ds(row * n_rhs, n_rhs), :] + column
 
 
 def shifted(value, axis, steps):
@@ -688,7 +735,6 @@
 
     arrived_blocks, arrived_bands = exchange(sends, halves_of_rows)
 
-    extra, extra_scratch, tail = (), [], 0
     if dense:
         fields = jnp.stack([late, across])[:, :, 0, LANES:]
         fields = fields.reshape(2, n_rows, -1, rows).transpose(2, 0, 1, 3)
@@ -697,7 +743,7 @@
         length = n_dev * depth
         extra_shapes = [
             ((n_diag * n_func, 3 * states), jnp.bfloat16),
-            ((n_tiles + 2, total_groups, n_blocks), jnp.bfloat16),
+            ((total_groups, (n_tiles + 2) * n_blocks), jnp.bfloat16),
             ((per_tile * length, total_groups), jnp.bfloat16),
         ]
         functional_shape, count_shape, placing_shape = extra_shapes
@@ -715,84 +761,127 @@
                 pltpu.VMEM(*count_shape),
                 pltpu.VMEM(*functional_shape),
                 pltpu.VMEM(*placing_shape),
-                pltpu.SemaphoreType.DMA((n_tiles + 4,)),
+                pltpu.SemaphoreType.DMA((3,)),
             ],
             4 * total_groups * n_tiles * n_dev * rows * n_blocks,
             4 << 20,
         )(fields, late[:, 0, :LANES], coupling_tiles, diag_table, inverse_table)
-        extra = (functionals, counts, placing)
         extra_scratch = [
             *[pltpu.VMEM(*shape) for shape in extra_shapes],
-            pltpu.SemaphoreType.DMA((3,)),
             pltpu.VMEM((n_diag * n_func, n_blocks * n_rhs), f32),
             pltpu.VMEM((n_blocks * n_func, LANES), f32),
             pltpu.VMEM((n_rows, n_bands * depth, LANES), f32),
         ]
-        tail = n_bands * depth
-
-    send_shape = (n_rows, cap * n_rhs + tail, states)
+
+        made = (arrived_blocks, functionals, counts, placing, scale)
+        arrived_blocks, functionals, counts, placing, scale = lax.optimization_barrier(made)
+
+    def solve(field, arrived, bands):
+        return call(
+            functools.partial(solve_kernel, sizes, width_k, n_ways, field),
+            jax.ShapeDtypeStruct(block, f32),
+            [ANY] * 2 + [VMEM] * 2 + [HBM] + [ANY] * n_ways,
+            VMEM,
+            [
+                *row_scratch,
+                sums,
+                products,
+                *term_scratch,
+                term_sems,
+                pltpu.SemaphoreType.DMA((2,)),
+            ],
+            work * n_diag,
+            4 << 20,
+        )(places, index, arrived, inverse_table, right_side, *bands)
+
+    first = solve(0, arrived_blocks, arrived_bands)
+    body = cap * n_rhs
+    full_list = pltpu.SMEM((n_rows, 1, LANES), i32)
+    if dense:
+        mirror = lax.ppermute(first, "rows", to_mirror)
+        own, band = call(
+            functools.partial(own_kernel, sizes, width_k),
+            (
+                jax.ShapeDtypeStruct((half, body + 2 * n_bands * depth, states), f32),
+                jax.ShapeDtypeStruct(block, f32),
+            ),
+            [ANY] * 3 + [VMEM] * 2 + [HBM] * 4,
+            [HBM] * 2,
+            [
+                row_scratch[1],
+                full_list,
+                near_scratch,
+                products,
+                pltpu.VMEM((n_rows, body, states), f32),
+                pltpu.VMEM(block, f32),
+                pltpu.VMEM(block, f32),
+                *extra_scratch,
+                pltpu.SemaphoreType.DMA((3,)),
+                pltpu.SemaphoreType.DMA((4,)),
+                pltpu.SemaphoreType.DMA((half + 3,)),
+            ],
+            2 * work * n_tiles,
+            4 << 20,
+        )(index, lists, near, first, coupling_tiles, right_side, functionals, counts, placing)
+        own, (band,) = exchange((own, band), halves_of_rows)
+        packed = call(
+            functools.partial(mirror_kernel, sizes),
+            jax.ShapeDtypeStruct((half, body, states), f32),
+            [ANY] + [VMEM] * 2,
+            HBM,
+            [
+                list_scratch,
+                products,
+                pltpu.VMEM((half, body, states), f32),
+                pltpu.SemaphoreType.DMA((half + 1,)),
+            ],
+            BEHIND_SWAP * work * n_tiles,
+            4 << 20,
+        )(lists, mirror, coupling_tiles)
+        packed, band = lax.optimization_barrier((packed, band))
+        swapped = lax.all_to_all(
+            packed, "rows", split_axis=0, concat_axis=0, tiled=True, axis_index_groups=halves_of_rows
+        )
+        part = jax.ShapeDtypeStruct((2 * depth, LANES), f32)
+        keep, give = call(part_kernel, (part, part), [VMEM], [VMEM] * 2)(own)
+        keep = keep + lax.ppermute(give, "band", [(0, 1), (1, 0)])
+        far = lax.ppermute(keep[depth:], "rows", to_mirror)
+        return call(
+            functools.partial(final_kernel, sizes, width_k),
+            jax.ShapeDtypeStruct(block, f32),
+            [ANY] * 2 + [VMEM] * 3 + [HBM, ANY] + [VMEM] * 3,
+            VMEM,
+            [
+                *row_scratch,
+                sums,
+                products,
+                *term_scratch,
+                term_sems,
+                pltpu.SemaphoreType.DMA((2,)),
+            ],
+            work * n_diag,
+            4 << 20,
+        )(places, index, own, swapped, inverse_table, right_side, band, keep[:depth], far, scale)
+
     sends = call(
-        functools.partial(middle_kernel, sizes, width_k, n_ways, dense),
-        (jax.ShapeDtypeStruct(send_shape, f32), *band_shapes),
-        [ANY] * 4 + [VMEM] * 3 + [HBM] + [ANY] * n_ways + [HBM] * len(extra),
+        functools.partial(pack_kernel, sizes, width_k, n_ways),
+        (jax.ShapeDtypeStruct((n_rows, body, states), f32), *band_shapes),
+        [ANY] * 2 + [VMEM] * 2,
         [HBM] * (1 + n_ways),
         [
-            *row_scratch,
-            pltpu.SMEM((n_rows, 1, LANES), i32),
+            full_list,
             near_scratch,
-            sums,
             products,
-            pltpu.VMEM((n_rows, cap * n_rhs, states), f32),
-            *term_scratch,
+            pltpu.VMEM((n_rows, body, states), f32),
             *band_scratch,
-            term_sems,
-            pltpu.SemaphoreType.DMA((4,)),
-            pltpu.SemaphoreType.DMA((n_rows + n_ways + 1,)),
-            *extra_scratch,
+            pltpu.SemaphoreType.DMA((2,)),
+            pltpu.SemaphoreType.DMA((1 + n_ways,)),
         ],
-        work * (n_tiles + n_diag),
+        work * n_tiles,
         4 << 20,
-    )(
-        places,
-        index,
-        lists,
-        near,
-        arrived_blocks,
-        inverse_table,
-        coupling_tiles,
-        right_side,
-        *arrived_bands,
-        *extra,
-    )
+    )(lists, near, first, coupling_tiles)
     arrived_blocks, arrived_bands = exchange(sends)
-
-    if dense:
-        part = jax.ShapeDtypeStruct((depth, LANES), f32)
-        mine, other = call(part_kernel, (part, part), [VMEM], [VMEM] * 2)(arrived_blocks)
-        other = lax.ppermute(other, "band", [(0, 1), (1, 0)])
-    second = call(
-        functools.partial(last_kernel, sizes, width_k, n_ways),
-        jax.ShapeDtypeStruct(block, f32),
-        [ANY] * 2 + [VMEM] * 2 + [HBM] + [ANY] * n_ways,
-        VMEM,
-        [
-            *row_scratch,
-            sums,
-            products,
-            *term_scratch,
-            term_sems,
-            pltpu.SemaphoreType.DMA((2,)),
-        ],
-        work * n_diag,
-        4 << 20,
-    )(places, index, arrived_blocks, inverse_table, right_side, *arrived_bands)
-    if dense:
-        return call(
-            functools.partial(final_kernel, sizes),
-            jax.ShapeDtypeStruct(block, f32),
-            [VMEM] * 4,
-            VMEM,
-        )(mine, other, scale, second)
+    second = solve(width_k, arrived_blocks, arrived_bands)
 
     groups = aggregate_map[:, 0]
     own = jnp.arange(rows, dtype=i32)

time: 80 us -> 76.4 us (0.955)
  the two profiles are of different devices: /device:TPU:16 before, /device:TPU:0 now
where the time goes in v10:
time: 76.4 us; the launch traced here: 75.8 us
  starting transfers between devices  31.1 us (41%)
  Pallas kernels  25.5 us (33%)
  waiting for transfers between devices  18.6 us (24%)
    pallas_call x9, Pallas kernels, apply(): return run(*pinned)  25.5 us
    all_to_all x2, starting transfers between devices, exchange(): lax.all_to_all(sends[0], 'rows', split_axis=0, concat_axis=0, tiled=True,...  7.25 us
    ppermute x1, starting transfers between devices, on_device(): mirror = lax.ppermute(start_iterate, 'rows', to_mirror)  4.04 us
    all_to_all x1, starting transfers between devices, on_device(): lax.all_to_all(lists, 'rows', split_axis=0, concat_axis=0, tiled=True)  3.9 us
    ppermute x2, waiting for transfers between devices, to_bands(): return (lax.ppermute(sends[0], 'band', [(0, 1), (1, 0)]),)  3.78 us
    all_to_all x1, starting transfers between devices, on_device(): lax.all_to_all(packed, 'rows', split_axis=0, concat_axis=0, tiled=True, a...  3.49 us
    all_to_all x2, waiting for transfers between devices, exchange(): lax.all_to_all(sends[0], 'rows', split_axis=0, concat_axis=0, tiled=True,...  3.3 us
    ppermute x2, starting transfers between devices, to_bands(): return (lax.ppermute(sends[0], 'band', [(0, 1), (1, 0)]),)  3.11 us
  transfers between devices with their start and end apart: 12, of which 9 were waited for; matrix products, arithmetic and copies ran while one was open for 0% of the time, Pallas kernels for 25%

profile of v10, /device:TPU:0, one launch (start us, length us, event | category | flops | bytes accessed | tf_op | source)
XLA Modules:
  0.0 75.8 jit_solution(4143653563299990276)
XLA Ops:
  0.0 4.0 %collective-permute-start.1 = (f32[32,16,128]{2,1,0:T(8,128)}, f32[32,16,128]{2,1,0:T(8,128)S(1)}, u32[]{:S(2)}, u32[]{:S(2)}) collective-permute-start(f32[32,16,128]{2,1,0:T(8,128)} %start_in.1), channel_id=1, source_target_pairs={{0,8},{1,9},{2,10},{3,11},{4,12},{5,13},{6,14},{7,15},{8,0},{9,1},... | collective-permute-start | bytes 786440 | tf_op jit(solution)/shard_map/ppermute | solution.py:656
  4.0 1.8 %shard_map.100 = (s32[16,1,384]{2,1,0:T(1,128)}, s32[1,1,256]{2,1,0:T(1,128)S(1)}, s32[1,1,128]{2,1,0:T(1,128)S(1)}) custom-call(s32[2,32]{1,0:T(2,128)} %bitcast.18, s32[2,32]{1,0:T(2,128)} %bitcast.19, s32[4,32]{1,0:T(4,128)} %bitcast.17, s32[1,32]{1,0:T(1,128)} %bitcast.20, s32[1,32]{1,0:T(1,128)} %bitcast.21), custom_call_target="tpu_custom_call" | custom-call | tf_op jit(solution)/shard_map/pallas_call | solution.py:49
  5.8 3.9 %all-to-all-start = ((s32[16,1,384]{2,1,0:T(1,128)}), s32[16,1,384]{2,1,0:T(1,128)S(1)}, u32[]{:S(2)}, u32[]{:S(2)}) async-start(s32[16,1,384]{2,1,0:T(1,128)} %get-tuple-element.31), calls=%async_computation | async-start | bytes 49152 | tf_op jit(solution)/shard_map/all_to_all | solution.py:668
  9.7 1.6 %collective-permute-start = (s32[1,1,256]{2,1,0:T(1,128)S(1)}, s32[1,1,256]{2,1,0:T(1,128)S(1)}, u32[]{:S(2)}, u32[]{:S(2)}) collective-permute-start(s32[1,1,256]{2,1,0:T(1,128)S(1)} %get-tuple-element.30.refs_1_.refs_0_), channel_id=1, source_target_pairs={{0,16},{16,0},{1,17},{17,1},{2,18},{18,2},{3,19},{19,3},{4,20},{20... | collective-permute-start | bytes 3080 | tf_op jit(solution)/shard_map/ppermute | solution.py:670
  11.3 3.9 %shard_map.101.refs_0_ = f32[256,16,128]{2,1,0:T(8,128)} custom-call(f32[32,16,128]{2,1,0:T(8,128)} %start_in.1, f32[8,128,128]{2,1,0:T(8,128)} %tile_ref.1), custom_call_target="tpu_custom_call" | custom-call | flops 402653184 | bytes 4194304 | tf_op jit(solution)/shard_map/pallas_call | solution.py:49
  15.2 2.4 %all-to-all-done.refs_3_.refs_1_.list_in = s32[16,1,384]{2,1,0:T(1,128)S(1)} async-done(((s32[16,1,384]{2,1,0:T(1,128)}), s32[16,1,384]{2,1,0:T(1,128)S(1)}, u32[]{:S(2)}, u32[]{:S(2)}) %all-to-all-start) | async-done | bytes 24608 | tf_op jit(solution)/shard_map/all_to_all | solution.py:668
  17.6 2.7 %shard_map.102 = (f32[8,16,16,128]{3,2,1,0:T(8,128)}, f32[32,16,128]{2,1,0:T(8,128)}) custom-call(f32[256,16,128]{2,1,0:T(8,128)} %shard_map.101.refs_0_, f32[32,16,128]{2,1,0:T(8,128)S(1)} %collective-permute-done.1.refs_1_, f32[8,128,128]{2,1,0:T(8,128)S(1)} %copy-done.1, s32[16,1,384]{2,1,0:T(1,128)S(1)} %all-to-all-done.refs_3_.refs_1_.list_in, ...), custom_call_target="tpu_custom_call" | custom-call | flops 402653184 | bytes 4194304 | tf_op jit(solution)/shard_map/pallas_call | solution.py:49
  20.4 3.7 %all-to-all-start.1 = ((f32[8,256,128]{2,1,0:T(8,128)}), f32[8,256,128]{2,1,0:T(8,128)S(1)}, u32[]{:S(2)}, u32[]{:S(2)}) async-start(f32[8,256,128]{2,1,0:T(8,128)} %bitcast.14), calls=%async_computation.1 | async-start | bytes 2097152 | tf_op jit(solution)/shard_map/all_to_all | solution.py:731
  25.7 2.3 %collective-permute-done.2 = s32[16,1,384]{2,1,0:T(1,128)S(1)} collective-permute-done((s32[16,1,384]{2,1,0:T(1,128)S(1)}, s32[16,1,384]{2,1,0:T(1,128)S(1)}, u32[]{:S(2)}, u32[]{:S(2)}) %collective-permute-start.2) | collective-permute-done | bytes 24608 | tf_op jit(solution)/shard_map/ppermute | solution.py:726
  29.8 6.0 %shard_map.103 = (bf16[256,1920]{1,0:T(8,128)(2,1)}, bf16[128,384]{1,0:T(8,128)(2,1)}, bf16[1024,256]{1,0:T(8,128)(2,1)}, f32[4,128]{1,0:T(4,128)S(1)}) custom-call(s32[8,2,512]{2,1,0:T(2,128)S(1)} %reshape.7.refs_0_, s32[16,128]{1,0:T(8,128)S(1)} %bitcast.13, f32[8,128,128]{2,1,0:T(8,128)S(1)} %copy-done.1, f32[8,128,128]{2,1,0:T(8,128)S(1)} %copy-done.2, ...), custom_call_target="tpu_custom_call" | custom-call | flops 1610612736 | bytes 4194304 | tf_op jit(solution)/shard_map/pallas_call | solution.py:49
  35.8 2.7 %all-to-all-done.1.refs_2_ = f32[8,256,128]{2,1,0:T(8,128)S(1)} async-done(((f32[8,256,128]{2,1,0:T(8,128)}), f32[8,256,128]{2,1,0:T(8,128)S(1)}, u32[]{:S(2)}, u32[]{:S(2)}) %all-to-all-start.1) | async-done | bytes 1048608 | tf_op jit(solution)/shard_map/all_to_all | solution.py:731
  38.5 1.8 %shard_map.104.refs_3_ = f32[32,16,128]{2,1,0:T(8,128)S(1)} custom-call(s32[1,1,128]{2,1,0:T(1,128)S(1)} %get-tuple-element.29.refs_0_, s32[1,1,256]{2,1,0:T(1,128)S(1)} %get-tuple-element.30.refs_1_.refs_0_, f32[8,256,128]{2,1,0:T(8,128)S(1)} %all-to-all-done.1.refs_2_, f32[8,128,128]{2,1,0:T(8,128)S(1)} %copy-done, f32[32,16,128]{2,1,0:T(8,128)} %refs_5_.3, ...), custom_call_target="tpu_custom_call" | custom-call | flops 402653184 | bytes 4194304 | tf_op jit(solution)/shard_map/pallas_call | solution.py:49
  40.2 2.7 %collective-permute-start.4 = (f32[32,16,128]{2,1,0:T(8,128)S(1)}, f32[32,16,128]{2,1,0:T(8,128)S(1)}, u32[]{:S(2)}, u32[]{:S(2)}) collective-permute-start(f32[32,16,128]{2,1,0:T(8,128)S(1)} %shard_map.104.refs_3_), channel_id=1, source_target_pairs={{0,8},{1,9},{2,10},{3,11},{4,12},{5,13},{6,14},{7,15},{8,0},{9,1},... | collective-permute-start | bytes 786440 | tf_op jit(solution)/shard_map/ppermute | solution.py:801
  43.0 5.0 %shard_map.105 = (f32[8,144,128]{2,1,0:T(8,128)}, f32[32,16,128]{2,1,0:T(8,128)}) custom-call(s32[1,1,256]{2,1,0:T(1,128)S(1)} %get-tuple-element.30.refs_1_.refs_0_, s32[16,1,384]{2,1,0:T(1,128)S(1)} %all-to-all-done.refs_3_.refs_1_.list_in, s32[1,1,256]{2,1,0:T(1,128)S(1)} %collective-permute-done.refs_4_.refs_2_, f32[32,16,128]{2,1,0:T(8,128)S(1)} %shard_map.104.refs_3_, ...), custom_call_target="tpu_custom_call" | custom-call | flops 805306368 | bytes 4194304 | tf_op jit(solution)/shard_map/pallas_call | solution.py:49
  48.0 3.5 %all-to-all-start.2 = ((f32[8,144,128]{2,1,0:T(8,128)}), f32[8,144,128]{2,1,0:T(8,128)S(1)}, u32[]{:S(2)}, u32[]{:S(2)}) async-start(f32[8,144,128]{2,1,0:T(8,128)} %get-tuple-element.46), calls=%async_computation.2 | async-start | bytes 1179648 | tf_op jit(solution)/shard_map/all_to_all | solution.py:731
  51.6 1.6 %collective-permute-start.5 = (f32[32,16,128]{2,1,0:T(8,128)}, f32[32,16,128]{2,1,0:T(8,128)S(1)}, u32[]{:S(2)}, u32[]{:S(2)}) collective-permute-start(f32[32,16,128]{2,1,0:T(8,128)} %get-tuple-element.47), channel_id=1, source_target_pairs={{0,16},{16,0},{1,17},{17,1},{2,18},{18,2},{3,19},{19,3},{4,20},{20... | collective-permute-start | bytes 786440 | tf_op jit(solution)/shard_map/ppermute | solution.py:611
  54.7 1.9 %shard_map.106 = f32[8,128,128]{2,1,0:T(8,128)} custom-call(s32[16,1,384]{2,1,0:T(1,128)S(1)} %all-to-all-done.refs_3_.refs_1_.list_in, f32[32,16,128]{2,1,0:T(8,128)S(1)} %collective-permute-done.4.mirror_ref, f32[8,128,128]{2,1,0:T(8,128)S(1)} %copy-done.1), custom_call_target="tpu_custom_call" | custom-call | flops 40265318400 | bytes 4194304 | tf_op jit(solution)/shard_map/pallas_call | solution.py:49
  56.6 3.8 %collective-permute-done.5.refs_6_ = f32[32,16,128]{2,1,0:T(8,128)S(1)} collective-permute-done((f32[32,16,128]{2,1,0:T(8,128)}, f32[32,16,128]{2,1,0:T(8,128)S(1)}, u32[]{:S(2)}, u32[]{:S(2)}) %collective-permute-start.5) | collective-permute-done | bytes 262176 | tf_op jit(solution)/shard_map/ppermute | solution.py:611
  61.0 3.5 %all-to-all-start.3 = ((f32[8,128,128]{2,1,0:T(8,128)}), f32[8,128,128]{2,1,0:T(8,128)S(1)}, u32[]{:S(2)}, u32[]{:S(2)}) async-start(f32[8,128,128]{2,1,0:T(8,128)} %shard_map.106), calls=%async_computation.3 | async-start | bytes 1048576 | tf_op jit(solution)/shard_map/all_to_all | solution.py:842
  64.6 1.6 %collective-permute-start.6 = (f32[8,128]{1,0:T(8,128)S(1)}, f32[8,128]{1,0:T(8,128)S(1)}, u32[]{:S(2)}, u32[]{:S(2)}) collective-permute-start(f32[8,128]{1,0:T(8,128)S(1)} %get-tuple-element.51), channel_id=1, source_target_pairs={{0,16},{16,0},{1,17},{17,1},{2,18},{18,2},{3,19},{19,3},{4,20},{20... | collective-permute-start | bytes 12296 | tf_op jit(solution)/shard_map/ppermute | solution.py:847
  66.1 2.1 %collective-permute-done.6 = f32[8,128]{1,0:T(8,128)S(1)} collective-permute-done((f32[8,128]{1,0:T(8,128)S(1)}, f32[8,128]{1,0:T(8,128)S(1)}, u32[]{:S(2)}, u32[]{:S(2)}) %collective-permute-start.6) | collective-permute-done | bytes 4128 | tf_op jit(solution)/shard_map/ppermute | solution.py:847
  68.2 1.8 %collective-permute-start.7 = (f32[4,128]{1,0:T(4,128)S(1)}, f32[4,128]{1,0:T(4,128)S(1)}, u32[]{:S(2)}, u32[]{:S(2)}) collective-permute-start(f32[4,128]{1,0:T(4,128)S(1)} %get-tuple-element.53), channel_id=1, source_target_pairs={{0,8},{1,9},{2,10},{3,11},{4,12},{5,13},{6,14},{7,15},{8,0},{9,1},... | collective-permute-start | bytes 6152 | tf_op jit(solution)/shard_map/ppermute | solution.py:848
  70.1 2.8 %collective-permute-done.7.refs_8_ = f32[4,128]{1,0:T(4,128)S(1)} collective-permute-done((f32[4,128]{1,0:T(4,128)S(1)}, f32[4,128]{1,0:T(4,128)S(1)}, u32[]{:S(2)}, u32[]{:S(2)}) %collective-permute-start.7) | collective-permute-done | bytes 2080 | tf_op jit(solution)/shard_map/ppermute | solution.py:848
  73.3 2.5 %shard_map.108 = f32[32,16,128]{2,1,0:T(8,128)} custom-call(s32[1,1,128]{2,1,0:T(1,128)S(1)} %get-tuple-element.29.refs_0_, s32[1,1,256]{2,1,0:T(1,128)S(1)} %get-tuple-element.30.refs_1_.refs_0_, f32[8,144,128]{2,1,0:T(8,128)S(1)} %all-to-all-done.2.arrived_ref.refs_2_, f32[8,128,128]{2,1,0:T(8,128)S(1)} %all-to-all-done.3.refs_3_, ...), custom_call_target="tpu_custom_call" | custom-call | flops 402653184 | bytes 4194304 | tf_op jit(solution)/shard_map/pallas_call | solution.py:49
  (24 shorter events, 6.1 us)
Async XLA Ops:
  0.0 17.6 %copy-start.1 = (f32[8,128,128]{2,1,0:T(8,128)S(1)}, f32[8,128,128]{2,1,0:T(8,128)}, u32[]{:S(2)}) copy-start(f32[8,128,128]{2,1,0:T(8,128)} %tile_ref.1) | copy-start | bytes 1572868
  0.0 17.6 %collective-permute-start.1 = (f32[32,16,128]{2,1,0:T(8,128)}, f32[32,16,128]{2,1,0:T(8,128)S(1)}, u32[]{:S(2)}, u32[]{:S(2)}) collective-permute-start(f32[32,16,128]{2,1,0:T(8,128)} %start_in.1), channel_id=1, source_target_pairs={{0,8},{1,9},{2,10},{3,11},{4,12},{5,13},{6,14},{7,15},{8,0},{9,1},... | collective-permute-start | bytes 786440 | tf_op jit(solution)/shard_map/ppermute | solution.py:656
  5.8 11.8 %all-to-all-start = ((s32[16,1,384]{2,1,0:T(1,128)}), s32[16,1,384]{2,1,0:T(1,128)S(1)}, u32[]{:S(2)}, u32[]{:S(2)}) async-start(s32[16,1,384]{2,1,0:T(1,128)} %get-tuple-element.31), calls=%async_computation | async-start | bytes 49152 | tf_op jit(solution)/shard_map/all_to_all | solution.py:668
  9.7 5.5 %collective-permute-start = (s32[1,1,256]{2,1,0:T(1,128)S(1)}, s32[1,1,256]{2,1,0:T(1,128)S(1)}, u32[]{:S(2)}, u32[]{:S(2)}) collective-permute-start(s32[1,1,256]{2,1,0:T(1,128)S(1)} %get-tuple-element.30.refs_1_.refs_0_), channel_id=1, source_target_pairs={{0,16},{16,0},{1,17},{17,1},{2,18},{18,2},{3,19},{19,3},{4,20},{20... | collective-permute-start | bytes 3080 | tf_op jit(solution)/shard_map/ppermute | solution.py:670
  20.3 7.6 %copy-start.3 = (f32[32,16,128]{2,1,0:T(8,128)S(1)}, f32[32,16,128]{2,1,0:T(8,128)}, u32[]{:S(2)}) copy-start(f32[32,16,128]{2,1,0:T(8,128)} %get-tuple-element.42) | copy-start | bytes 786436
  20.4 9.5 %copy-start = (f32[8,128,128]{2,1,0:T(8,128)S(1)}, f32[8,128,128]{2,1,0:T(8,128)}, u32[]{:S(2)}) copy-start(f32[8,128,128]{2,1,0:T(8,128)} %refs_4_.7) | copy-start | bytes 1572868
  20.4 9.5 %copy-start.2 = (f32[8,128,128]{2,1,0:T(8,128)S(1)}, f32[8,128,128]{2,1,0:T(8,128)}, u32[]{:S(2)}) copy-start(f32[8,128,128]{2,1,0:T(8,128)} %refs_3_.2) | copy-start | bytes 1572868
  20.4 18.1 %all-to-all-start.1 = ((f32[8,256,128]{2,1,0:T(8,128)}), f32[8,256,128]{2,1,0:T(8,128)S(1)}, u32[]{:S(2)}, u32[]{:S(2)}) async-start(f32[8,256,128]{2,1,0:T(8,128)} %bitcast.14), calls=%async_computation.1 | async-start | bytes 2097152 | tf_op jit(solution)/shard_map/all_to_all | solution.py:731
  24.1 3.9 %collective-permute-start.2 = (s32[16,1,384]{2,1,0:T(1,128)S(1)}, s32[16,1,384]{2,1,0:T(1,128)S(1)}, u32[]{:S(2)}, u32[]{:S(2)}) collective-permute-start(s32[16,1,384]{2,1,0:T(1,128)S(1)} %all-to-all-done.refs_3_.refs_1_.list_in), channel_id=1, source_target_pairs={{0,16},{16,0},{1,17},{17,1},{2,18},{18,2},{3,19},{19,3},{4,20},{20... | collective-permute-start | bytes 73736 | tf_op jit(solution)/shard_map/ppermute | solution.py:726
  28.0 10.5 %collective-permute-start.3 = (f32[32,16,128]{2,1,0:T(8,128)S(1)}, f32[32,16,128]{2,1,0:T(8,128)S(1)}, u32[]{:S(2)}, u32[]{:S(2)}) collective-permute-start(f32[32,16,128]{2,1,0:T(8,128)S(1)} %copy-done.3), channel_id=1, source_target_pairs={{0,16},{16,0},{1,17},{17,1},{2,18},{18,2},{3,19},{19,3},{4,20},{20... | collective-permute-start | bytes 786440 | tf_op jit(solution)/shard_map/ppermute | solution.py:611
  40.2 14.5 %collective-permute-start.4 = (f32[32,16,128]{2,1,0:T(8,128)S(1)}, f32[32,16,128]{2,1,0:T(8,128)S(1)}, u32[]{:S(2)}, u32[]{:S(2)}) collective-permute-start(f32[32,16,128]{2,1,0:T(8,128)S(1)} %shard_map.104.refs_3_), channel_id=1, source_target_pairs={{0,8},{1,9},{2,10},{3,11},{4,12},{5,13},{6,14},{7,15},{8,0},{9,1},... | collective-permute-start | bytes 786440 | tf_op jit(solution)/shard_map/ppermute | solution.py:801
  48.0 13.0 %all-to-all-start.2 = ((f32[8,144,128]{2,1,0:T(8,128)}), f32[8,144,128]{2,1,0:T(8,128)S(1)}, u32[]{:S(2)}, u32[]{:S(2)}) async-start(f32[8,144,128]{2,1,0:T(8,128)} %get-tuple-element.46), calls=%async_computation.2 | async-start | bytes 1179648 | tf_op jit(solution)/shard_map/all_to_all | solution.py:731
  51.6 8.8 %collective-permute-start.5 = (f32[32,16,128]{2,1,0:T(8,128)}, f32[32,16,128]{2,1,0:T(8,128)S(1)}, u32[]{:S(2)}, u32[]{:S(2)}) collective-permute-start(f32[32,16,128]{2,1,0:T(8,128)} %get-tuple-element.47), channel_id=1, source_target_pairs={{0,16},{16,0},{1,17},{17,1},{2,18},{18,2},{3,19},{19,3},{4,20},{20... | collective-permute-start | bytes 786440 | tf_op jit(solution)/shard_map/ppermute | solution.py:611
  61.0 12.3 %all-to-all-start.3 = ((f32[8,128,128]{2,1,0:T(8,128)}), f32[8,128,128]{2,1,0:T(8,128)S(1)}, u32[]{:S(2)}, u32[]{:S(2)}) async-start(f32[8,128,128]{2,1,0:T(8,128)} %shard_map.106), calls=%async_computation.3 | async-start | bytes 1048576 | tf_op jit(solution)/shard_map/all_to_all | solution.py:842
  64.6 3.7 %collective-permute-start.6 = (f32[8,128]{1,0:T(8,128)S(1)}, f32[8,128]{1,0:T(8,128)S(1)}, u32[]{:S(2)}, u32[]{:S(2)}) collective-permute-start(f32[8,128]{1,0:T(8,128)S(1)} %get-tuple-element.51), channel_id=1, source_target_pairs={{0,16},{16,0},{1,17},{17,1},{2,18},{18,2},{3,19},{19,3},{4,20},{20... | collective-permute-start | bytes 12296 | tf_op jit(solution)/shard_map/ppermute | solution.py:847
  68.2 4.6 %collective-permute-start.7 = (f32[4,128]{1,0:T(4,128)S(1)}, f32[4,128]{1,0:T(4,128)S(1)}, u32[]{:S(2)}, u32[]{:S(2)}) collective-permute-start(f32[4,128]{1,0:T(4,128)S(1)} %get-tuple-element.53), channel_id=1, source_target_pairs={{0,8},{1,9},{2,10},{3,11},{4,12},{5,13},{6,14},{7,15},{8,0},{9,1},... | collective-permute-start | bytes 6152 | tf_op jit(solution)/shard_map/ppermute | solution.py:848

commit v11 on v10

--- a/solution.py
+++ b/solution.py
@@ -278,8 +278,8 @@
 def count_kernel(sizes, width_k, n_func, *refs):
     rows, n_rows, cap, n_tiles, n_rhs = sizes
     field_ref, list_ref, tile_ref, table_ref, inverse_ref = refs[:5]
-    count_out, functional_out, placing_out, scale_ref = refs[5:9]
-    count_ref, functional_ref, placing_ref, sems = refs[9:]
+    count_out, functional_out, through_out, placing_out, scale_ref = refs[5:10]
+    count_ref, functional_ref, through_ref, placing_ref, sems = refs[10:]
     n_groups, n_blocks = count_ref.shape[0], count_ref.shape[1] // (n_tiles + 2)
     slots, band_rows = n_rows * cap, n_rows * rows
     copies = []
@@ -291,7 +291,7 @@
     line = lax.broadcasted_iota(jnp.int32, (n_func, sums.shape[1]), 0)
     sums = jnp.concatenate([sums, jnp.zeros((n_func - n_tiles, sums.shape[1]), jnp.float32)], axis=0)
     n_diag = inverse_ref.shape[0]
-    totals = []
+    totals, functionals = [], []
     for d in range(n_diag):
         minus = -jnp.sum(table_ref[d], axis=0, keepdims=True)
         totals.append(-jnp.sum(minus, axis=1, keepdims=True))
@@ -300,8 +300,17 @@
         right = jnp.concatenate([high, high, low], axis=0)
         solved = jnp.dot(left_operand(wanted), right, preferred_element_type=jnp.float32)
         solved = jnp.where(line == n_tiles + 1, 1.0, solved)
-        functional_ref[d * n_func : (d + 1) * n_func, :] = left_operand(solved)
+        functionals.append(solved)
+    functionals = left_operand(jnp.concatenate(functionals, axis=0))
+    functional_ref[...] = functionals
     send(functional_ref, functional_out)
+    for t in range(n_tiles):
+        high, low = halves(tile_ref[t])
+        right = jnp.concatenate([high, high, low], axis=0)
+        through = jnp.dot(functionals, right, preferred_element_type=jnp.float32)
+        place_of = pl.ds(t * n_diag * n_func, n_diag * n_func)
+        through_ref[place_of, :] = left_operand(through)
+    send(through_ref, through_out)
 
     lists = list_ref[...]
     asker = lax.broadcasted_iota(jnp.int32, lists.shape, 0)
@@ -449,9 +458,10 @@
 
 def own_kernel(sizes, width_k, *refs):
     rows, n_rows, cap, n_tiles, n_rhs = sizes
-    metadata_in, first_ref, tile_ref, right_in, extra = list(refs[:3]), *refs[3:6], refs[6:9]
-    send_out, band_out, metadata, product_ref, send_ref, right_ref, band_ref = refs[9], refs[10], refs[11:14], *refs[14:18]
-    held, value_ref, spread_ref, result_ref, meta_sems, load_sems, send_sems = refs[18:21], *refs[21:]
+    metadata_in, first_ref, tile_ref, right_in, extra = list(refs[:3]), *refs[3:6], refs[6:10]
+    send_out, band_out, metadata, product_ref, send_ref, right_ref, band_ref = refs[10], refs[11], refs[12:15], *refs[15:19]
+    held, value_ref, through_ref, spread_ref, result_ref = refs[19:23], *refs[23:27]
+    meta_sems, load_sems, send_sems = refs[27:]
     index_ref, list_ref, near_ref = metadata
     metadata_in[1] = metadata_in[1].at[:, :, pl.ds(0, LANES)]
     metadata = copies_of(zip(metadata_in, metadata), meta_sems)
@@ -468,46 +478,47 @@
     body, half = cap * n_rhs, n_rows // 2
     upper = lax.axis_index("rows") >= half
     mine, others = jnp.where(upper, half, 0), jnp.where(upper, 0, half)
-    for first in (mine, others):
-        for device in range(half):
-            owner = first + device
-            for rank in range(cap):
-                block = product_ref[below(list_ref[owner, 0, rank], rows * n_tiles)]
-                send_ref[owner, rank * n_rhs : (rank + 1) * n_rhs, :] = block
-            if first is mine:
-                send(send_ref.at[owner], send_out.at[device, pl.ds(0, body)])
+    for device in range(half):
+        for rank in range(cap):
+            block = product_ref[below(list_ref[mine + device, 0, rank], rows * n_tiles)]
+            send_ref[device, rank * n_rhs : (rank + 1) * n_rhs, :] = block
+        send(send_ref.at[device], send_out.at[device, pl.ds(0, body)])
     finish(fetched)
-    functional_ref, count_ref, place_ref = held
+    functional_ref, through_in, count_ref, place_ref = held
     n_blocks = n_rows * cap + 2 * rows
     n_func = spread_ref.shape[0] // n_blocks
     n_diag = functional_ref.shape[0] // n_func
-    functional = functional_ref[...]
     per_tile = LANES // n_rhs
+    values = right_operand(first_ref[...].reshape(rows * n_rhs, -1))
+    step = 2 * n_diag * n_func
+    for done in range(0, through_in.shape[0], step):
+        through_ref[done : done + step, :] = dot_nt(through_in[done : done + step, :], values)
+    value_ref[...] = dot_nt(
+        functional_ref[...], right_operand(right_ref[...].reshape(rows * n_rhs, -1))
+    )
     lane = lax.broadcasted_iota(jnp.int32, (n_func, LANES), 1)
 
-    def spread(first, values, kinds):
-        wide = values.shape[0]
-        value_ref[:, first * n_rhs : first * n_rhs + wide] = dot_nt(functional, right_operand(values))
-        for block, kind in enumerate(kinds, first):
-            tile, spot = block // per_tile, block % per_tile
-            start = pl.multiple_of(kind * n_func, n_func)
-            piece = value_ref[pl.ds(start, n_func), tile * LANES : (tile + 1) * LANES]
-            piece = jnp.where((lane >= spot * n_rhs) & (lane < (spot + 1) * n_rhs), piece, 0.0)
-            spread_ref[block * n_func : (block + 1) * n_func, :] = piece
-
-    for owner in range(0, n_rows, 2):
-        kinds = []
-        for more in range(2):
-            for rank in range(cap):
-                code = list_ref[owner + more, 0, rank]
-                kinds.append(below(over(code, rows * n_tiles * rows), n_diag))
-        values = jnp.concatenate([send_ref[owner], send_ref[owner + 1]], axis=0)
-        spread(owner * cap, values, kinds)
-    done = n_rows * cap
-    kinds = [index_ref[0, 0, rows + row] for row in range(rows)]
-    spread(done, right_ref[...].reshape(rows * n_rhs, -1), kinds)
-    kinds = [near_ref[0, 0, rows + row] for row in range(rows)]
-    spread(done + rows, band_ref[...].reshape(rows * n_rhs, -1), kinds)
+    def spread(block, ref, kind, row):
+        start = pl.multiple_of(kind * n_func, n_func)
+        tile = pl.multiple_of(over(row, per_tile) * LANES, LANES)
+        piece = ref[pl.ds(start, n_func), pl.ds(tile, LANES)]
+        low = below(row, per_tile) * n_rhs
+        piece = jnp.where((lane >= low) & (lane < low + n_rhs), piece, 0.0)
+        spread_ref[block * n_func : (block + 1) * n_func, :] = piece
+
+    for owner in range(n_rows):
+        for rank in range(cap):
+            code = list_ref[owner, 0, rank]
+            tile = below(over(code, rows), n_tiles)
+            kind = below(over(code, rows * n_tiles * rows), n_diag)
+            spread(owner * cap + rank, through_ref, tile * n_diag + kind, below(code, rows))
+    field = band_field(rows, width_k, 0, 1)
+    for row in range(rows):
+        done = n_rows * cap + row
+        place_of = jnp.int32(row)
+        spread(done, value_ref, index_ref[0, 0, rows + row], place_of)
+        kind = near_ref[0, 0, field + row] * n_diag + near_ref[0, 0, rows + row]
+        spread(done + rows, through_ref, kind, place_of)
     result = coarse_parts(n_rhs, n_blocks, count_ref, place_ref, spread_ref)
     result_ref[...] = result.reshape(result_ref.shape)
     depth = result_ref.shape[1]
@@ -743,38 +754,43 @@
         length = n_dev * depth
         extra_shapes = [
             ((n_diag * n_func, 3 * states), jnp.bfloat16),
+            ((n_tiles * n_diag * n_func, 3 * states), jnp.bfloat16),
             ((total_groups, (n_tiles + 2) * n_blocks), jnp.bfloat16),
             ((per_tile * length, total_groups), jnp.bfloat16),
         ]
-        functional_shape, count_shape, placing_shape = extra_shapes
-        counts, functionals, placing, scale = call(
+        functional_shape, through_shape, count_shape, placing_shape = extra_shapes
+        counts, functionals, through, placing, scale = call(
             functools.partial(count_kernel, sizes, width_k, n_func),
             (
                 jax.ShapeDtypeStruct(*count_shape),
                 jax.ShapeDtypeStruct(*functional_shape),
+                jax.ShapeDtypeStruct(*through_shape),
                 jax.ShapeDtypeStruct(*placing_shape),
                 jax.ShapeDtypeStruct((depth, LANES), f32),
             ),
             [VMEM] * 5,
-            [HBM, HBM, HBM, VMEM],
+            [HBM] * 4 + [VMEM],
             [
                 pltpu.VMEM(*count_shape),
                 pltpu.VMEM(*functional_shape),
+                pltpu.VMEM(*through_shape),
                 pltpu.VMEM(*placing_shape),
-                pltpu.SemaphoreType.DMA((3,)),
+                pltpu.SemaphoreType.DMA((4,)),
             ],
             4 * total_groups * n_tiles * n_dev * rows * n_blocks,
             4 << 20,
         )(fields, late[:, 0, :LANES], coupling_tiles, diag_table, inverse_table)
         extra_scratch = [
             *[pltpu.VMEM(*shape) for shape in extra_shapes],
-            pltpu.VMEM((n_diag * n_func, n_blocks * n_rhs), f32),
+            pltpu.VMEM((n_diag * n_func, flat), f32),
+            pltpu.VMEM((n_tiles * n_diag * n_func, flat), f32),
             pltpu.VMEM((n_blocks * n_func, LANES), f32),
             pltpu.VMEM((n_rows, n_bands * depth, LANES), f32),
         ]
 
-        made = (arrived_blocks, functionals, counts, placing, scale)
-        arrived_blocks, functionals, counts, placing, scale = lax.optimization_barrier(made)
+        made = (arrived_blocks, functionals, through, counts, placing, scale)
+        made = lax.optimization_barrier(made)
+        arrived_blocks, functionals, through, counts, placing, scale = made
 
     def solve(field, arrived, bands):
         return call(
@@ -805,24 +821,35 @@
                 jax.ShapeDtypeStruct((half, body + 2 * n_bands * depth, states), f32),
                 jax.ShapeDtypeStruct(block, f32),
             ),
-            [ANY] * 3 + [VMEM] * 2 + [HBM] * 4,
+            [ANY] * 3 + [VMEM] * 2 + [HBM] * 5,
             [HBM] * 2,
             [
                 row_scratch[1],
                 full_list,
                 near_scratch,
                 products,
-                pltpu.VMEM((n_rows, body, states), f32),
+                pltpu.VMEM((half, body, states), f32),
                 pltpu.VMEM(block, f32),
                 pltpu.VMEM(block, f32),
                 *extra_scratch,
                 pltpu.SemaphoreType.DMA((3,)),
-                pltpu.SemaphoreType.DMA((4,)),
+                pltpu.SemaphoreType.DMA((5,)),
                 pltpu.SemaphoreType.DMA((half + 3,)),
             ],
             2 * work * n_tiles,
             4 << 20,
-        )(index, lists, near, first, coupling_tiles, right_side, functionals, counts, placing)
+        )(
+            index,
+            lists,
+            near,
+            first,
+            coupling_tiles,
+            right_side,
+            functionals,
+            through,
+            counts,
+            placing,
+        )
         own, (band,) = exchange((own, band), halves_of_rows)
         packed = call(
             functools.partial(mirror_kernel, sizes),

time: 76.4 us -> 78 us (1.021)
  Pallas kernels: 25.5 us -> 27.3 us
  starting transfers between devices: 31.1 us -> 29.9 us
  waiting for transfers between devices: 18.6 us -> 19.5 us
    pallas_call x9, Pallas kernels: 25.5 us -> 27.3 us  [apply(): return run(*pinned)]
    ppermute x2, waiting for transfers between devices: 3.78 us -> 5.29 us  [to_bands(): return (lax.ppermute(sends[0], 'band', [(0, 1), (1, 0)]),)]
    ppermute x1, waiting for transfers between devices: 1.53 us -> 0.02 us  [on_device(): mirror = lax.ppermute(first, 'rows', to_mirror)]
    ppermute x1, starting transfers between devices: 1.84 us -> 0.45 us  [on_device(): far = lax.ppermute(keep[depth:], 'rows', to_mirror)]
    ppermute x1, waiting for transfers between devices: 2.75 us -> 4.14 us  [on_device(): far = lax.ppermute(keep[depth:], 'rows', to_mirror)]
  transfers between devices with their start and end apart: 12 -> 12, of which waited for: 9 -> 8; matrix products, arithmetic and copies ran while one was open for 0% -> 0% of each run, Pallas kernels for 25% -> 26%
where the time goes in v11:
time: 78 us; the launch traced here: 77.4 us
  starting transfers between devices  29.9 us (38%)
  Pallas kernels  27.3 us (35%)
  waiting for transfers between devices  19.5 us (25%)
    pallas_call x9, Pallas kernels, apply(): return run(*pinned)  27.3 us
    all_to_all x2, starting transfers between devices, exchange(): lax.all_to_all(sends[0], 'rows', split_axis=0, concat_axis=0, tiled=True,...  7.43 us
    ppermute x2, waiting for transfers between devices, to_bands(): return (lax.ppermute(sends[0], 'band', [(0, 1), (1, 0)]),)  5.29 us
    ppermute x1, waiting for transfers between devices, on_device(): far = lax.ppermute(keep[depth:], 'rows', to_mirror)  4.14 us
    ppermute x1, starting transfers between devices, on_device(): mirror = lax.ppermute(start_iterate, 'rows', to_mirror)  4.04 us
    all_to_all x1, starting transfers between devices, on_device(): lax.all_to_all(lists, 'rows', split_axis=0, concat_axis=0, tiled=True)  3.9 us
    all_to_all x1, starting transfers between devices, on_device(): lax.all_to_all(packed, 'rows', split_axis=0, concat_axis=0, tiled=True, a...  3.49 us
    ppermute x2, starting transfers between devices, to_bands(): return (lax.ppermute(sends[0], 'band', [(0, 1), (1, 0)]),)  3.1 us
  transfers between devices with their start and end apart: 12, of which 8 were waited for; matrix products, arithmetic and copies ran while one was open for 0% of the time, Pallas kernels for 26%

profile of v11, /device:TPU:0, one launch (start us, length us, event | category | flops | bytes accessed | tf_op | source)
XLA Modules:
  0.0 77.4 jit_solution(5168793067827350101)
XLA Ops:
  0.0 4.0 %collective-permute-start.1 = (f32[32,16,128]{2,1,0:T(8,128)}, f32[32,16,128]{2,1,0:T(8,128)S(1)}, u32[]{:S(2)}, u32[]{:S(2)}) collective-permute-start(f32[32,16,128]{2,1,0:T(8,128)} %start_in.1), channel_id=1, source_target_pairs={{0,8},{1,9},{2,10},{3,11},{4,12},{5,13},{6,14},{7,15},{8,0},{9,1},... | collective-permute-start | bytes 786440 | tf_op jit(solution)/shard_map/ppermute | solution.py:667
  4.0 1.8 %shard_map.100 = (s32[16,1,384]{2,1,0:T(1,128)}, s32[1,1,256]{2,1,0:T(1,128)S(1)}, s32[1,1,128]{2,1,0:T(1,128)S(1)}) custom-call(s32[2,32]{1,0:T(2,128)} %bitcast.18, s32[2,32]{1,0:T(2,128)} %bitcast.19, s32[4,32]{1,0:T(4,128)} %bitcast.17, s32[1,32]{1,0:T(1,128)} %bitcast.20, s32[1,32]{1,0:T(1,128)} %bitcast.21), custom_call_target="tpu_custom_call" | custom-call | tf_op jit(solution)/shard_map/pallas_call | solution.py:49
  5.8 3.9 %all-to-all-start = ((s32[16,1,384]{2,1,0:T(1,128)}), s32[16,1,384]{2,1,0:T(1,128)S(1)}, u32[]{:S(2)}, u32[]{:S(2)}) async-start(s32[16,1,384]{2,1,0:T(1,128)} %get-tuple-element.33), calls=%async_computation | async-start | bytes 49152 | tf_op jit(solution)/shard_map/all_to_all | solution.py:679
  9.7 1.6 %collective-permute-start = (s32[1,1,256]{2,1,0:T(1,128)S(1)}, s32[1,1,256]{2,1,0:T(1,128)S(1)}, u32[]{:S(2)}, u32[]{:S(2)}) collective-permute-start(s32[1,1,256]{2,1,0:T(1,128)S(1)} %get-tuple-element.32.refs_1_.refs_0_), channel_id=1, source_target_pairs={{0,16},{16,0},{1,17},{17,1},{2,18},{18,2},{3,19},{19,3},{4,20},{20... | collective-permute-start | bytes 3080 | tf_op jit(solution)/shard_map/ppermute | solution.py:681
  11.3 3.9 %shard_map.101.refs_0_ = f32[256,16,128]{2,1,0:T(8,128)} custom-call(f32[32,16,128]{2,1,0:T(8,128)} %start_in.1, f32[8,128,128]{2,1,0:T(8,128)} %tile_ref.1), custom_call_target="tpu_custom_call" | custom-call | flops 402653184 | bytes 4194304 | tf_op jit(solution)/shard_map/pallas_call | solution.py:49
  15.2 2.4 %all-to-all-done.refs_3_.refs_1_.list_in = s32[16,1,384]{2,1,0:T(1,128)S(1)} async-done(((s32[16,1,384]{2,1,0:T(1,128)}), s32[16,1,384]{2,1,0:T(1,128)S(1)}, u32[]{:S(2)}, u32[]{:S(2)}) %all-to-all-start) | async-done | bytes 24608 | tf_op jit(solution)/shard_map/all_to_all | solution.py:679
  17.6 2.7 %shard_map.102 = (f32[8,16,16,128]{3,2,1,0:T(8,128)}, f32[32,16,128]{2,1,0:T(8,128)}) custom-call(f32[256,16,128]{2,1,0:T(8,128)} %shard_map.101.refs_0_, f32[32,16,128]{2,1,0:T(8,128)S(1)} %collective-permute-done.1.refs_1_, f32[8,128,128]{2,1,0:T(8,128)S(1)} %copy-done, s32[16,1,384]{2,1,0:T(1,128)S(1)} %all-to-all-done.refs_3_.refs_1_.list_in, ...), custom_call_target="tpu_custom_call" | custom-call | flops 402653184 | bytes 4194304 | tf_op jit(solution)/shard_map/pallas_call | solution.py:49
  20.4 3.9 %all-to-all-start.1 = ((f32[8,256,128]{2,1,0:T(8,128)}), f32[8,256,128]{2,1,0:T(8,128)S(1)}, u32[]{:S(2)}, u32[]{:S(2)}) async-start(f32[8,256,128]{2,1,0:T(8,128)} %bitcast.14), calls=%async_computation.1 | async-start | bytes 2097152 | tf_op jit(solution)/shard_map/all_to_all | solution.py:742
  24.3 1.6 %collective-permute-start.2 = (s32[16,1,384]{2,1,0:T(1,128)S(1)}, s32[16,1,384]{2,1,0:T(1,128)S(1)}, u32[]{:S(2)}, u32[]{:S(2)}) collective-permute-start(s32[16,1,384]{2,1,0:T(1,128)S(1)} %all-to-all-done.refs_3_.refs_1_.list_in), channel_id=1, source_target_pairs={{0,16},{16,0},{1,17},{17,1},{2,18},{18,2},{3,19},{19,3},{4,20},{20... | collective-permute-start | bytes 73736 | tf_op jit(solution)/shard_map/ppermute | solution.py:737
  25.9 2.3 %collective-permute-done.2 = s32[16,1,384]{2,1,0:T(1,128)S(1)} collective-permute-done((s32[16,1,384]{2,1,0:T(1,128)S(1)}, s32[16,1,384]{2,1,0:T(1,128)S(1)}, u32[]{:S(2)}, u32[]{:S(2)}) %collective-permute-start.2) | collective-permute-done | bytes 24608 | tf_op jit(solution)/shard_map/ppermute | solution.py:737
  30.0 6.3 %shard_map.103 = (bf16[256,1920]{1,0:T(8,128)(2,1)}, bf16[128,384]{1,0:T(8,128)(2,1)}, bf16[1024,384]{1,0:T(8,128)(2,1)}, bf16[1024,256]{1,0:T(8,128)(2,1)}, f32[4,128]{1,0:T(4,128)S(1)}) custom-call(s32[8,2,512]{2,1,0:T(2,128)S(1)} %reshape.7.refs_0_, s32[16,128]{1,0:T(8,128)S(1)} %bitcast.13, f32[8,128,128]{2,1,0:T(8,128)S(1)} %copy-done, ...), custom_call_target="tpu_custom_call" | custom-call | flops 1610612736 | bytes 4194304 | tf_op jit(solution)/shard_map/pallas_call | solution.py:49
  36.3 2.1 %all-to-all-done.1.refs_2_ = f32[8,256,128]{2,1,0:T(8,128)S(1)} async-done(((f32[8,256,128]{2,1,0:T(8,128)}), f32[8,256,128]{2,1,0:T(8,128)S(1)}, u32[]{:S(2)}, u32[]{:S(2)}) %all-to-all-start.1) | async-done | bytes 1048608 | tf_op jit(solution)/shard_map/all_to_all | solution.py:742
  38.5 1.8 %shard_map.104.refs_3_ = f32[32,16,128]{2,1,0:T(8,128)S(1)} custom-call(s32[1,1,128]{2,1,0:T(1,128)S(1)} %get-tuple-element.31.refs_0_, s32[1,1,256]{2,1,0:T(1,128)S(1)} %get-tuple-element.32.refs_1_.refs_0_, f32[8,256,128]{2,1,0:T(8,128)S(1)} %all-to-all-done.1.refs_2_, f32[8,128,128]{2,1,0:T(8,128)S(1)} %copy-done.1, f32[32,16,128]{2,1,0:T(8,128)} %refs_5_.3, ...), custom_call_target="tpu_custom_call" | custom-call | flops 402653184 | bytes 4194304 | tf_op jit(solution)/shard_map/pallas_call | solution.py:49
  40.2 2.7 %collective-permute-start.4 = (f32[32,16,128]{2,1,0:T(8,128)S(1)}, f32[32,16,128]{2,1,0:T(8,128)S(1)}, u32[]{:S(2)}, u32[]{:S(2)}) collective-permute-start(f32[32,16,128]{2,1,0:T(8,128)S(1)} %shard_map.104.refs_3_), channel_id=1, source_target_pairs={{0,8},{1,9},{2,10},{3,11},{4,12},{5,13},{6,14},{7,15},{8,0},{9,1},... | collective-permute-start | bytes 786440 | tf_op jit(solution)/shard_map/ppermute | solution.py:817
  43.0 6.5 %shard_map.105 = (f32[8,144,128]{2,1,0:T(8,128)}, f32[32,16,128]{2,1,0:T(8,128)}) custom-call(s32[1,1,256]{2,1,0:T(1,128)S(1)} %get-tuple-element.32.refs_1_.refs_0_, s32[16,1,384]{2,1,0:T(1,128)S(1)} %all-to-all-done.refs_3_.refs_1_.list_in, s32[1,1,256]{2,1,0:T(1,128)S(1)} %collective-permute-done.refs_4_.refs_2_, f32[32,16,128]{2,1,0:T(8,128)S(1)} %shard_map.104.refs_3_, ...), custom_call_target="tpu_custom_call" | custom-call | flops 805306368 | bytes 4194304 | tf_op jit(solution)/shard_map/pallas_call | solution.py:49
  49.4 3.5 %all-to-all-start.2 = ((f32[8,144,128]{2,1,0:T(8,128)}), f32[8,144,128]{2,1,0:T(8,128)S(1)}, u32[]{:S(2)}, u32[]{:S(2)}) async-start(f32[8,144,128]{2,1,0:T(8,128)} %get-tuple-element.50), calls=%async_computation.2 | async-start | bytes 1179648 | tf_op jit(solution)/shard_map/all_to_all | solution.py:742
  53.0 1.6 %collective-permute-start.5 = (f32[32,16,128]{2,1,0:T(8,128)}, f32[32,16,128]{2,1,0:T(8,128)S(1)}, u32[]{:S(2)}, u32[]{:S(2)}) collective-permute-start(f32[32,16,128]{2,1,0:T(8,128)} %get-tuple-element.51), channel_id=1, source_target_pairs={{0,16},{16,0},{1,17},{17,1},{2,18},{18,2},{3,19},{19,3},{4,20},{20... | collective-permute-start | bytes 786440 | tf_op jit(solution)/shard_map/ppermute | solution.py:622
  54.6 1.9 %shard_map.106 = f32[8,128,128]{2,1,0:T(8,128)} custom-call(s32[16,1,384]{2,1,0:T(1,128)S(1)} %all-to-all-done.refs_3_.refs_1_.list_in, f32[32,16,128]{2,1,0:T(8,128)S(1)} %collective-permute-done.4.mirror_ref, f32[8,128,128]{2,1,0:T(8,128)S(1)} %copy-done), custom_call_target="tpu_custom_call" | custom-call | flops 40265318400 | bytes 4194304 | tf_op jit(solution)/shard_map/pallas_call | solution.py:49
  56.5 5.3 %collective-permute-done.5.refs_6_ = f32[32,16,128]{2,1,0:T(8,128)S(1)} collective-permute-done((f32[32,16,128]{2,1,0:T(8,128)}, f32[32,16,128]{2,1,0:T(8,128)S(1)}, u32[]{:S(2)}, u32[]{:S(2)}) %collective-permute-start.5) | collective-permute-done | bytes 262176 | tf_op jit(solution)/shard_map/ppermute | solution.py:622
  62.5 3.5 %all-to-all-start.3 = ((f32[8,128,128]{2,1,0:T(8,128)}), f32[8,128,128]{2,1,0:T(8,128)S(1)}, u32[]{:S(2)}, u32[]{:S(2)}) async-start(f32[8,128,128]{2,1,0:T(8,128)} %shard_map.106), calls=%async_computation.3 | async-start | bytes 1048576 | tf_op jit(solution)/shard_map/all_to_all | solution.py:869
  66.0 1.6 %collective-permute-start.6 = (f32[8,128]{1,0:T(8,128)S(1)}, f32[8,128]{1,0:T(8,128)S(1)}, u32[]{:S(2)}, u32[]{:S(2)}) collective-permute-start(f32[8,128]{1,0:T(8,128)S(1)} %get-tuple-element.55), channel_id=1, source_target_pairs={{0,16},{16,0},{1,17},{17,1},{2,18},{18,2},{3,19},{19,3},{4,20},{20... | collective-permute-start | bytes 12296 | tf_op jit(solution)/shard_map/ppermute | solution.py:874
  67.6 2.1 %collective-permute-done.6 = f32[8,128]{1,0:T(8,128)S(1)} collective-permute-done((f32[8,128]{1,0:T(8,128)S(1)}, f32[8,128]{1,0:T(8,128)S(1)}, u32[]{:S(2)}, u32[]{:S(2)}) %collective-permute-start.6) | collective-permute-done | bytes 4128 | tf_op jit(solution)/shard_map/ppermute | solution.py:874
  70.1 4.1 %collective-permute-done.7.refs_8_ = f32[4,128]{1,0:T(4,128)S(1)} collective-permute-done((f32[4,128]{1,0:T(4,128)S(1)}, f32[4,128]{1,0:T(4,128)S(1)}, u32[]{:S(2)}, u32[]{:S(2)}) %collective-permute-start.7) | collective-permute-done | bytes 2080 | tf_op jit(solution)/shard_map/ppermute | solution.py:875
  74.8 2.5 %shard_map.108 = f32[32,16,128]{2,1,0:T(8,128)} custom-call(s32[1,1,128]{2,1,0:T(1,128)S(1)} %get-tuple-element.31.refs_0_, s32[1,1,256]{2,1,0:T(1,128)S(1)} %get-tuple-element.32.refs_1_.refs_0_, f32[8,144,128]{2,1,0:T(8,128)S(1)} %all-to-all-done.2.arrived_ref.refs_2_, f32[8,128,128]{2,1,0:T(8,128)S(1)} %all-to-all-done.3.refs_3_, ...), custom_call_target="tpu_custom_call" | custom-call | flops 402653184 | bytes 4194304 | tf_op jit(solution)/shard_map/pallas_call | solution.py:49
  (24 shorter events, 3.5 us)
Async XLA Ops:
  0.0 17.6 %copy-start = (f32[8,128,128]{2,1,0:T(8,128)S(1)}, f32[8,128,128]{2,1,0:T(8,128)}, u32[]{:S(2)}) copy-start(f32[8,128,128]{2,1,0:T(8,128)} %tile_ref.1) | copy-start | bytes 1572868
  0.0 17.6 %collective-permute-start.1 = (f32[32,16,128]{2,1,0:T(8,128)}, f32[32,16,128]{2,1,0:T(8,128)S(1)}, u32[]{:S(2)}, u32[]{:S(2)}) collective-permute-start(f32[32,16,128]{2,1,0:T(8,128)} %start_in.1), channel_id=1, source_target_pairs={{0,8},{1,9},{2,10},{3,11},{4,12},{5,13},{6,14},{7,15},{8,0},{9,1},... | collective-permute-start | bytes 786440 | tf_op jit(solution)/shard_map/ppermute | solution.py:667
  5.8 11.8 %all-to-all-start = ((s32[16,1,384]{2,1,0:T(1,128)}), s32[16,1,384]{2,1,0:T(1,128)S(1)}, u32[]{:S(2)}, u32[]{:S(2)}) async-start(s32[16,1,384]{2,1,0:T(1,128)} %get-tuple-element.33), calls=%async_computation | async-start | bytes 49152 | tf_op jit(solution)/shard_map/all_to_all | solution.py:679
  9.7 5.5 %collective-permute-start = (s32[1,1,256]{2,1,0:T(1,128)S(1)}, s32[1,1,256]{2,1,0:T(1,128)S(1)}, u32[]{:S(2)}, u32[]{:S(2)}) collective-permute-start(s32[1,1,256]{2,1,0:T(1,128)S(1)} %get-tuple-element.32.refs_1_.refs_0_), channel_id=1, source_target_pairs={{0,16},{16,0},{1,17},{17,1},{2,18},{18,2},{3,19},{19,3},{4,20},{20... | collective-permute-start | bytes 3080 | tf_op jit(solution)/shard_map/ppermute | solution.py:681
  20.3 7.8 %copy-start.3 = (f32[32,16,128]{2,1,0:T(8,128)S(1)}, f32[32,16,128]{2,1,0:T(8,128)}, u32[]{:S(2)}) copy-start(f32[32,16,128]{2,1,0:T(8,128)} %get-tuple-element.45) | copy-start | bytes 786436
  20.4 9.7 %copy-start.1 = (f32[8,128,128]{2,1,0:T(8,128)S(1)}, f32[8,128,128]{2,1,0:T(8,128)}, u32[]{:S(2)}) copy-start(f32[8,128,128]{2,1,0:T(8,128)} %refs_4_.7) | copy-start | bytes 1572868
  20.4 9.6 %copy-start.2 = (f32[8,128,128]{2,1,0:T(8,128)S(1)}, f32[8,128,128]{2,1,0:T(8,128)}, u32[]{:S(2)}) copy-start(f32[8,128,128]{2,1,0:T(8,128)} %refs_3_.2) | copy-start | bytes 1572868
  20.4 18.1 %all-to-all-start.1 = ((f32[8,256,128]{2,1,0:T(8,128)}), f32[8,256,128]{2,1,0:T(8,128)S(1)}, u32[]{:S(2)}, u32[]{:S(2)}) async-start(f32[8,256,128]{2,1,0:T(8,128)} %bitcast.14), calls=%async_computation.1 | async-start | bytes 2097152 | tf_op jit(solution)/shard_map/all_to_all | solution.py:742
  24.3 3.9 %collective-permute-start.2 = (s32[16,1,384]{2,1,0:T(1,128)S(1)}, s32[16,1,384]{2,1,0:T(1,128)S(1)}, u32[]{:S(2)}, u32[]{:S(2)}) collective-permute-start(s32[16,1,384]{2,1,0:T(1,128)S(1)} %all-to-all-done.refs_3_.refs_1_.list_in), channel_id=1, source_target_pairs={{0,16},{16,0},{1,17},{17,1},{2,18},{18,2},{3,19},{19,3},{4,20},{20... | collective-permute-start | bytes 73736 | tf_op jit(solution)/shard_map/ppermute | solution.py:737
  28.2 10.3 %collective-permute-start.3 = (f32[32,16,128]{2,1,0:T(8,128)S(1)}, f32[32,16,128]{2,1,0:T(8,128)S(1)}, u32[]{:S(2)}, u32[]{:S(2)}) collective-permute-start(f32[32,16,128]{2,1,0:T(8,128)S(1)} %copy-done.3), channel_id=1, source_target_pairs={{0,16},{16,0},{1,17},{17,1},{2,18},{18,2},{3,19},{19,3},{4,20},{20... | collective-permute-start | bytes 786440 | tf_op jit(solution)/shard_map/ppermute | solution.py:622
  40.2 14.4 %collective-permute-start.4 = (f32[32,16,128]{2,1,0:T(8,128)S(1)}, f32[32,16,128]{2,1,0:T(8,128)S(1)}, u32[]{:S(2)}, u32[]{:S(2)}) collective-permute-start(f32[32,16,128]{2,1,0:T(8,128)S(1)} %shard_map.104.refs_3_), channel_id=1, source_target_pairs={{0,8},{1,9},{2,10},{3,11},{4,12},{5,13},{6,14},{7,15},{8,0},{9,1},... | collective-permute-start | bytes 786440 | tf_op jit(solution)/shard_map/ppermute | solution.py:817
  49.4 13.0 %all-to-all-start.2 = ((f32[8,144,128]{2,1,0:T(8,128)}), f32[8,144,128]{2,1,0:T(8,128)S(1)}, u32[]{:S(2)}, u32[]{:S(2)}) async-start(f32[8,144,128]{2,1,0:T(8,128)} %get-tuple-element.50), calls=%async_computation.2 | async-start | bytes 1179648 | tf_op jit(solution)/shard_map/all_to_all | solution.py:742
  53.0 8.8 %collective-permute-start.5 = (f32[32,16,128]{2,1,0:T(8,128)}, f32[32,16,128]{2,1,0:T(8,128)S(1)}, u32[]{:S(2)}, u32[]{:S(2)}) collective-permute-start(f32[32,16,128]{2,1,0:T(8,128)} %get-tuple-element.51), channel_id=1, source_target_pairs={{0,16},{16,0},{1,17},{17,1},{2,18},{18,2},{3,19},{19,3},{4,20},{20... | collective-permute-start | bytes 786440 | tf_op jit(solution)/shard_map/ppermute | solution.py:622
  62.5 12.3 %all-to-all-start.3 = ((f32[8,128,128]{2,1,0:T(8,128)}), f32[8,128,128]{2,1,0:T(8,128)S(1)}, u32[]{:S(2)}, u32[]{:S(2)}) async-start(f32[8,128,128]{2,1,0:T(8,128)} %shard_map.106), calls=%async_computation.3 | async-start | bytes 1048576 | tf_op jit(solution)/shard_map/all_to_all | solution.py:869
  66.0 3.7 %collective-permute-start.6 = (f32[8,128]{1,0:T(8,128)S(1)}, f32[8,128]{1,0:T(8,128)S(1)}, u32[]{:S(2)}, u32[]{:S(2)}) collective-permute-start(f32[8,128]{1,0:T(8,128)S(1)} %get-tuple-element.55), channel_id=1, source_target_pairs={{0,16},{16,0},{1,17},{17,1},{2,18},{18,2},{3,19},{19,3},{4,20},{20... | collective-permute-start | bytes 12296 | tf_op jit(solution)/shard_map/ppermute | solution.py:874
  69.7 4.6 %collective-permute-start.7 = (f32[4,128]{1,0:T(4,128)S(1)}, f32[4,128]{1,0:T(4,128)S(1)}, u32[]{:S(2)}, u32[]{:S(2)}) collective-permute-start(f32[4,128]{1,0:T(4,128)S(1)} %get-tuple-element.57), channel_id=1, source_target_pairs={{0,8},{1,9},{2,10},{3,11},{4,12},{5,13},{6,14},{7,15},{8,0},{9,1},... | collective-permute-start | bytes 6152 | tf_op jit(solution)/shard_map/ppermute | solution.py:875

commit v12 on v10

--- a/solution.py
+++ b/solution.py
@@ -271,16 +271,31 @@
     return result
 
 
+def spread_values(n_rhs, n_func, functional_ref, blocks, kinds, value_ref, spread_ref, done):
+    per_tile = LANES // n_rhs
+    lane = lax.broadcasted_iota(jnp.int32, (n_func, LANES), 1)
+    columns = slice(done * n_rhs, done * n_rhs + blocks.shape[0])
+    value_ref[:, columns] = dot_nt(functional_ref[...], right_operand(blocks))
+    for block, kind in enumerate(kinds, done):
+        tile, spot = block // per_tile, block % per_tile
+        start = pl.multiple_of(kind * n_func, n_func)
+        piece = value_ref[pl.ds(start, n_func), tile * LANES : (tile + 1) * LANES]
+        piece = jnp.where((lane >= spot * n_rhs) & (lane < (spot + 1) * n_rhs), piece, 0.0)
+        spread_ref[block * n_func : (block + 1) * n_func, :] = piece
+
+
 def one_hot(ids, row):
     return jnp.where(ids == row, 1.0, 0.0).astype(jnp.bfloat16)
 
 
 def count_kernel(sizes, width_k, n_func, *refs):
     rows, n_rows, cap, n_tiles, n_rhs = sizes
-    field_ref, list_ref, tile_ref, table_ref, inverse_ref = refs[:5]
-    count_out, functional_out, placing_out, scale_ref = refs[5:9]
-    count_ref, functional_ref, placing_ref, sems = refs[9:]
-    n_groups, n_blocks = count_ref.shape[0], count_ref.shape[1] // (n_tiles + 2)
+    index_in, right_in, field_ref, list_ref, tile_ref, table_ref, inverse_ref = refs[:7]
+    count_out, functional_out, placing_out, partial_out, scale_ref = refs[7:12]
+    count_ref, functional_ref, placing_ref, partial_ref = refs[12:16]
+    index_ref, right_ref, value_ref, spread_ref, load_sems, sems = refs[16:]
+    loads = copies_of(((index_in, index_ref), (right_in, right_ref)), load_sems)
+    n_groups = count_ref.shape[0]
     slots, band_rows = n_rows * cap, n_rows * rows
     copies = []
 
@@ -316,6 +331,9 @@
     lane = lax.broadcasted_iota(jnp.int32, codes.shape, 1)
     asked = jnp.sum(jnp.where(rank == lane, codes, 0.0), axis=1, keepdims=True)
     asked = jnp.where(asked < 0.0, asked - 0.5, asked + 0.5).astype(jnp.int32)
+    low, high = asked[: slots // 2], asked[slots // 2 :]
+    upper = lax.axis_index("rows") >= n_rows // 2
+    asked = jnp.concatenate([jnp.where(upper, high, low), jnp.where(upper, low, high)], axis=0)
     own = lax.axis_index("rows") * rows + lax.broadcasted_iota(jnp.int32, (rows, 1), 0)
     band = lax.axis_index("band")
 
@@ -333,21 +351,31 @@
         origins = [field(4 + width_k + k, side) for k in range(width_k)] + [row_ids]
         hits = one_hot(targets, jnp.concatenate(origins, axis=1))
         sides.append((takers, hits, field(0, side)))
-    pieces = []
-    for t in range(n_tiles):
+    pieces, own_pieces = [], []
+    ids = lax.broadcasted_iota(jnp.int32, (n_groups, band_rows), 0)
+    for t in range(n_tiles + 1):
         found = []
-        for takers, hits, _ in sides:
-            ids = lax.broadcasted_iota(jnp.int32, (n_groups, takers.shape[1]), 0) + t * n_groups
-            found.append(dot_nt(one_hot(ids, takers), hits))
-        pieces += found
-    ids = lax.broadcasted_iota(jnp.int32, (n_groups, band_rows), 0)
-    found = [dot_nt(one_hot(ids, groups), hits[:, -band_rows:]) for _, hits, groups in sides]
-    found = jnp.concatenate(found, axis=1)
-    block = lax.broadcasted_iota(jnp.int32, found.shape, 1)
-    mine = (block >= slots) & (block < slots + rows)
-    pieces += [found, jnp.where(mine, found, 0.0)]
+        for takers, hits, groups in sides:
+            if t < n_tiles:
+                wide = lax.broadcasted_iota(jnp.int32, (n_groups, takers.shape[1]), 0)
+                found.append(dot_nt(one_hot(wide + t * n_groups, takers), hits))
+            else:
+                found.append(dot_nt(one_hot(ids, groups), hits[:, -band_rows:]))
+        pieces += [found[0][:, :slots], found[1]]
+        own_pieces.append(found[0][:, slots:])
     count_ref[...] = jnp.concatenate(pieces, axis=1).astype(jnp.bfloat16)
     send(count_ref, count_out)
+
+    own_counts = jnp.concatenate([*own_pieces, own_pieces[-1]], axis=1).astype(jnp.bfloat16)
+    finish(loads)
+    rights = right_ref[...].reshape(rows * n_rhs, -1)
+    kinds = [index_ref[0, 0, rows + row] for row in range(rows)]
+    spread_values(n_rhs, n_func, functional_ref, rights, kinds, value_ref, spread_ref, 0)
+    values = [spread_ref[pl.ds(t, rows, stride=n_func), :] for t in range(n_tiles + 2)]
+    values = jnp.concatenate(halves(jnp.concatenate(values, axis=0)), axis=1)
+    partial = jnp.dot(own_counts, values, preferred_element_type=jnp.float32)
+    partial_ref[...] = partial[:, :LANES] + partial[:, LANES:]
+    send(partial_ref, partial_out)
 
     per_tile = LANES // n_rhs
     depth = rows // per_tile
@@ -449,13 +477,13 @@
 
 def own_kernel(sizes, width_k, *refs):
     rows, n_rows, cap, n_tiles, n_rhs = sizes
-    metadata_in, first_ref, tile_ref, right_in, extra = list(refs[:3]), *refs[3:6], refs[6:9]
-    send_out, band_out, metadata, product_ref, send_ref, right_ref, band_ref = refs[9], refs[10], refs[11:14], *refs[14:18]
-    held, value_ref, spread_ref, result_ref, meta_sems, load_sems, send_sems = refs[18:21], *refs[21:]
-    index_ref, list_ref, near_ref = metadata
-    metadata_in[1] = metadata_in[1].at[:, :, pl.ds(0, LANES)]
+    metadata_in, first_ref, tile_ref, extra = list(refs[:2]), *refs[2:4], refs[4:8]
+    send_out, band_out, metadata, product_ref, send_ref, band_ref = refs[8], refs[9], refs[10:12], *refs[12:15]
+    held, value_ref, spread_ref, result_ref, meta_sems, load_sems, send_sems = refs[15:19], *refs[19:]
+    list_ref, near_ref = metadata
+    metadata_in[0] = metadata_in[0].at[:, :, pl.ds(0, LANES)]
     metadata = copies_of(zip(metadata_in, metadata), meta_sems)
-    fetched = copies_of(zip((right_in, *extra), (right_ref, *held)), load_sems)
+    fetched = copies_of(zip(extra, held), load_sems)
     table_products(first_ref[...].reshape(rows * n_rhs, -1), tile_ref, product_ref)
     finish(metadata)
     copies = []
@@ -468,47 +496,32 @@
     body, half = cap * n_rhs, n_rows // 2
     upper = lax.axis_index("rows") >= half
     mine, others = jnp.where(upper, half, 0), jnp.where(upper, 0, half)
-    for first in (mine, others):
-        for device in range(half):
-            owner = first + device
-            for rank in range(cap):
-                block = product_ref[below(list_ref[owner, 0, rank], rows * n_tiles)]
-                send_ref[owner, rank * n_rhs : (rank + 1) * n_rhs, :] = block
-            if first is mine:
-                send(send_ref.at[owner], send_out.at[device, pl.ds(0, body)])
     finish(fetched)
-    functional_ref, count_ref, place_ref = held
-    n_blocks = n_rows * cap + 2 * rows
+    functional_ref, count_ref, place_ref, partial_ref = held
+    n_blocks = n_rows * cap + rows
     n_func = spread_ref.shape[0] // n_blocks
     n_diag = functional_ref.shape[0] // n_func
-    functional = functional_ref[...]
-    per_tile = LANES // n_rhs
-    lane = lax.broadcasted_iota(jnp.int32, (n_func, LANES), 1)
-
-    def spread(first, values, kinds):
-        wide = values.shape[0]
-        value_ref[:, first * n_rhs : first * n_rhs + wide] = dot_nt(functional, right_operand(values))
-        for block, kind in enumerate(kinds, first):
-            tile, spot = block // per_tile, block % per_tile
-            start = pl.multiple_of(kind * n_func, n_func)
-            piece = value_ref[pl.ds(start, n_func), tile * LANES : (tile + 1) * LANES]
-            piece = jnp.where((lane >= spot * n_rhs) & (lane < (spot + 1) * n_rhs), piece, 0.0)
-            spread_ref[block * n_func : (block + 1) * n_func, :] = piece
-
-    for owner in range(0, n_rows, 2):
-        kinds = []
-        for more in range(2):
-            for rank in range(cap):
-                code = list_ref[owner + more, 0, rank]
-                kinds.append(below(over(code, rows * n_tiles * rows), n_diag))
-        values = jnp.concatenate([send_ref[owner], send_ref[owner + 1]], axis=0)
-        spread(owner * cap, values, kinds)
-    done = n_rows * cap
-    kinds = [index_ref[0, 0, rows + row] for row in range(rows)]
-    spread(done, right_ref[...].reshape(rows * n_rhs, -1), kinds)
+
+    def spread(done, blocks, kinds):
+        spread_values(n_rhs, n_func, functional_ref, blocks, kinds, value_ref, spread_ref, done)
+
     kinds = [near_ref[0, 0, rows + row] for row in range(rows)]
-    spread(done + rows, band_ref[...].reshape(rows * n_rhs, -1), kinds)
-    result = coarse_parts(n_rhs, n_blocks, count_ref, place_ref, spread_ref)
+    spread(n_rows * cap, band_ref[...].reshape(rows * n_rhs, -1), kinds)
+    kinds = []
+    for order in range(n_rows):
+        owner = order % half + (mine if order < half else others)
+        for rank in range(cap):
+            code = list_ref[owner, 0, rank]
+            kinds.append(below(over(code, rows * n_tiles * rows), n_diag))
+            block = product_ref[below(code, rows * n_tiles)]
+            send_ref[order, rank * n_rhs : (rank + 1) * n_rhs, :] = block
+        if order < half:
+            send(send_ref.at[order], send_out.at[order, pl.ds(0, body)])
+        if order % 2:
+            blocks = jnp.concatenate([send_ref[order - 1], send_ref[order]], axis=0)
+            spread((order - 1) * cap, blocks, kinds)
+            kinds = []
+    result = coarse_parts(n_rhs, n_blocks, count_ref, place_ref, partial_ref, spread_ref)
     result_ref[...] = result.reshape(result_ref.shape)
     depth = result_ref.shape[1]
     for n, first in enumerate((mine, others)):
@@ -536,7 +549,7 @@
     finish(copies)
 
 
-def coarse_parts(n_rhs, n_blocks, count_ref, place_ref, spread_ref):
+def coarse_parts(n_rhs, n_blocks, count_ref, place_ref, partial_ref, spread_ref):
     n_func = spread_ref.shape[0] // n_blocks
     values = [
         spread_ref[pl.ds(t, n_blocks, stride=n_func), :] for t in range(count_ref.shape[1] // n_blocks)
@@ -545,7 +558,7 @@
     partial = jnp.dot(
         count_ref[...], jnp.concatenate(halves(values), axis=1), preferred_element_type=jnp.float32
     )
-    partial = partial[:, :LANES] + partial[:, LANES:]
+    partial = partial[:, :LANES] + partial[:, LANES:] + partial_ref[...]
     shift = LANES // 2
     while shift >= n_rhs:
         partial = partial + pltpu.roll(partial, shift, axis=1)
@@ -566,15 +579,8 @@
         give_ref[n * depth : (n + 1) * depth] = jnp.where(lower, one, zero)
 
 
-def final_kernel(sizes, width_k, *refs):
+def half_blocks_of(sizes, width_k, place_ref, arrived_ref, far):
     rows, n_rows, cap, n_tiles, n_rhs = sizes
-    metadata_in, own_ref, mirror_ref, inverse_ref, terms_in = refs[:2], *refs[2:5], refs[5:7]
-    near_ref, far_ref, scale_ref, out_ref = refs[7:11]
-    metadata, sum_ref, product_ref, terms, term_sems, meta_sems = refs[11:13], *refs[13:15], refs[15:17], *refs[17:]
-    place_ref, index_ref = metadata
-    metadata = copies_of(zip(metadata_in, metadata), meta_sems)
-    later = copies_of(zip(terms_in, terms), term_sems)
-    finish(metadata)
 
     def fetch(row):
         total = None
@@ -582,22 +588,52 @@
             slot = place_ref[0, 0, k * rows + row]
             holder, slot = over(slot, 2 * cap), below(slot, 2 * cap)
             start = pl.ds(pl.multiple_of(below(slot, cap) * n_rhs, n_rhs), n_rhs)
-            block = jnp.where(slot < cap, own_ref[holder, start, :], mirror_ref[holder, start, :])
+            mine = slot >= cap if far else slot < cap
+            block = jnp.where(mine, arrived_ref[holder, start, :], 0.0)
             total = block if total is None else total + block
         return total
 
+    return fetch
+
+
+def base_kernel(sizes, width_k, *refs):
+    metadata_in, own_ref, inverse_ref, terms_in, out_ref = refs[:2], *refs[2:4], refs[4:6], refs[6]
+    metadata, sum_ref, product_ref, terms, term_sems, meta_sems = refs[7:9], *refs[9:11], refs[11:13], *refs[13:]
+    place_ref, index_ref = metadata
+    rows = sizes[0]
+    metadata = copies_of(zip(metadata_in, metadata), meta_sems)
+    later = copies_of(zip(terms_in, terms), term_sems)
+    finish(metadata)
+    fetch = half_blocks_of(sizes, width_k, place_ref, own_ref, False)
+
     def diags(row):
         return index_ref[0, 0, rows + row]
 
+    gather_solve(sizes, fetch, diags, later, terms, inverse_ref, sum_ref, product_ref)
+    out_ref[...] = sum_ref[...].reshape(out_ref.shape)
+
+
+def final_kernel(sizes, width_k, *refs):
+    rows, n_rows, cap, n_tiles, n_rhs = sizes
+    metadata_in, mirror_ref, inverse_ref, base_ref, near_ref, far_ref, scale_ref = refs[:2], *refs[2:8]
+    out_ref, metadata, sum_ref, product_ref, meta_sems = refs[8], refs[9:11], *refs[11:]
+    place_ref, index_ref = metadata
+    metadata = copies_of(zip(metadata_in, metadata), meta_sems)
     depth = scale_ref.shape[0]
     correction = (near_ref[...] + far_ref[...]) / scale_ref[...]
     padded = jnp.concatenate([correction, jnp.zeros((8 - depth, LANES), jnp.float32)], axis=0)
     turned = padded.T
-    gather_solve(sizes, fetch, diags, later, terms, inverse_ref, sum_ref, product_ref)
+    finish(metadata)
+    fetch = half_blocks_of(sizes, width_k, place_ref, mirror_ref, True)
+
+    def diags(row):
+        return index_ref[0, 0, rows + row]
+
+    gather_solve(sizes, fetch, diags, [], [], inverse_ref, sum_ref, product_ref)
     for row in range(rows):
         spot, place = row // depth, row % depth
         column = turned[spot * n_rhs : (spot + 1) * n_rhs, place : place + 1]
-        out_ref[row] = sum_ref[pl.ds(row * n_rhs, n_rhs), :] + column
+        out_ref[row] = (base_ref[row] + column) + sum_ref[pl.ds(row * n_rhs, n_rhs), :]
 
 
 def shifted(value, axis, steps):
@@ -739,33 +775,43 @@
         fields = jnp.stack([late, across])[:, :, 0, LANES:]
         fields = fields.reshape(2, n_rows, -1, rows).transpose(2, 0, 1, 3)
         fields = fields.reshape(-1, 2, n_rows * rows)
-        n_blocks = slots + 2 * rows
+        n_blocks = slots + rows
         length = n_dev * depth
         extra_shapes = [
             ((n_diag * n_func, 3 * states), jnp.bfloat16),
-            ((total_groups, (n_tiles + 2) * n_blocks), jnp.bfloat16),
+            ((total_groups, (n_tiles + 1) * n_blocks), jnp.bfloat16),
             ((per_tile * length, total_groups), jnp.bfloat16),
+            ((total_groups, LANES), f32),
         ]
-        functional_shape, count_shape, placing_shape = extra_shapes
-        counts, functionals, placing, scale = call(
+        functional_shape, count_shape, placing_shape, partial_shape = extra_shapes
+        counts, functionals, placing, partial, scale = call(
             functools.partial(count_kernel, sizes, width_k, n_func),
             (
                 jax.ShapeDtypeStruct(*count_shape),
                 jax.ShapeDtypeStruct(*functional_shape),
                 jax.ShapeDtypeStruct(*placing_shape),
+                jax.ShapeDtypeStruct(*partial_shape),
                 jax.ShapeDtypeStruct((depth, LANES), f32),
             ),
-            [VMEM] * 5,
-            [HBM, HBM, HBM, VMEM],
+            [ANY, HBM] + [VMEM] * 5,
+            [HBM] * 4 + [VMEM],
             [
                 pltpu.VMEM(*count_shape),
                 pltpu.VMEM(*functional_shape),
                 pltpu.VMEM(*placing_shape),
-                pltpu.SemaphoreType.DMA((3,)),
+                pltpu.VMEM(*partial_shape),
+                row_scratch[1],
+                pltpu.VMEM(block, f32),
+                pltpu.VMEM((n_diag * n_func, flat), f32),
+                pltpu.VMEM((rows * n_func, LANES), f32),
+                pltpu.SemaphoreType.DMA((2,)),
+                pltpu.SemaphoreType.DMA((4,)),
             ],
             4 * total_groups * n_tiles * n_dev * rows * n_blocks,
             4 << 20,
-        )(fields, late[:, 0, :LANES], coupling_tiles, diag_table, inverse_table)
+        )(
+            index, right_side, fields, late[:, 0, :LANES], coupling_tiles, diag_table, inverse_table
+        )
         extra_scratch = [
             *[pltpu.VMEM(*shape) for shape in extra_shapes],
             pltpu.VMEM((n_diag * n_func, n_blocks * n_rhs), f32),
@@ -773,8 +819,9 @@
             pltpu.VMEM((n_rows, n_bands * depth, LANES), f32),
         ]
 
-        made = (arrived_blocks, functionals, counts, placing, scale)
-        arrived_blocks, functionals, counts, placing, scale = lax.optimization_barrier(made)
+        made = (arrived_blocks, functionals, counts, placing, partial, scale)
+        made = lax.optimization_barrier(made)
+        arrived_blocks, functionals, counts, placing, partial, scale = made
 
     def solve(field, arrived, bands):
         return call(
@@ -805,24 +852,22 @@
                 jax.ShapeDtypeStruct((half, body + 2 * n_bands * depth, states), f32),
                 jax.ShapeDtypeStruct(block, f32),
             ),
-            [ANY] * 3 + [VMEM] * 2 + [HBM] * 4,
+            [ANY] * 2 + [VMEM] * 2 + [HBM] * 4,
             [HBM] * 2,
             [
-                row_scratch[1],
                 full_list,
                 near_scratch,
                 products,
                 pltpu.VMEM((n_rows, body, states), f32),
                 pltpu.VMEM(block, f32),
-                pltpu.VMEM(block, f32),
                 *extra_scratch,
-                pltpu.SemaphoreType.DMA((3,)),
+                pltpu.SemaphoreType.DMA((2,)),
                 pltpu.SemaphoreType.DMA((4,)),
                 pltpu.SemaphoreType.DMA((half + 3,)),
             ],
             2 * work * n_tiles,
             4 << 20,
-        )(index, lists, near, first, coupling_tiles, right_side, functionals, counts, placing)
+        )(lists, near, first, coupling_tiles, functionals, counts, placing, partial)
         own, (band,) = exchange((own, band), halves_of_rows)
         packed = call(
             functools.partial(mirror_kernel, sizes),
@@ -846,10 +891,10 @@
         keep, give = call(part_kernel, (part, part), [VMEM], [VMEM] * 2)(own)
         keep = keep + lax.ppermute(give, "band", [(0, 1), (1, 0)])
         far = lax.ppermute(keep[depth:], "rows", to_mirror)
-        return call(
-            functools.partial(final_kernel, sizes, width_k),
+        base = call(
+            functools.partial(base_kernel, sizes, width_k),
             jax.ShapeDtypeStruct(block, f32),
-            [ANY] * 2 + [VMEM] * 3 + [HBM, ANY] + [VMEM] * 3,
+            [ANY] * 2 + [VMEM] * 2 + [HBM, ANY],
             VMEM,
             [
                 *row_scratch,
@@ -861,7 +906,16 @@
             ],
             work * n_diag,
             4 << 20,
-        )(places, index, own, swapped, inverse_table, right_side, band, keep[:depth], far, scale)
+        )(places, index, own, inverse_table, right_side, band)
+        return call(
+            functools.partial(final_kernel, sizes, width_k),
+            jax.ShapeDtypeStruct(block, f32),
+            [ANY] * 2 + [VMEM] * 6,
+            VMEM,
+            [*row_scratch, sums, products, pltpu.SemaphoreType.DMA((2,))],
+            work * n_diag,
+            4 << 20,
+        )(places, index, swapped, inverse_table, base, keep[:depth], far, scale)
 
     sends = call(
         functools.partial(pack_kernel, sizes, width_k, n_ways),

time: 76.4 us -> 76.2 us (level)
  waiting for transfers between devices: 18.6 us -> 16.3 us
  Pallas kernels: 25.5 us -> 27.4 us
    pallas_call x9 -> x10, Pallas kernels: 25.5 us -> 27.4 us  [apply(): return run(*pinned)]
    ppermute x1, waiting for transfers between devices: 2.75 us -> 1.01 us  [on_device(): far = lax.ppermute(keep[depth:], 'rows', to_mirror)]
  transfers between devices with their start and end apart: 12 -> 12, of which waited for: 9 -> 9; matrix products, arithmetic and copies ran while one was open for 0% -> 0% of each run, Pallas kernels for 25% -> 28%
where the time goes in v12:
time: 76.2 us; the launch traced here: 75.6 us
  starting transfers between devices  31.3 us (41%)
  Pallas kernels  27.4 us (36%)
  waiting for transfers between devices  16.3 us (21%)
    pallas_call x10, Pallas kernels, apply(): return run(*pinned)  27.4 us
    all_to_all x2, starting transfers between devices, exchange(): lax.all_to_all(sends[0], 'rows', split_axis=0, concat_axis=0, tiled=True,...  7.43 us
    ppermute x1, starting transfers between devices, on_device(): mirror = lax.ppermute(start_iterate, 'rows', to_mirror)  4.04 us
    all_to_all x1, starting transfers between devices, on_device(): lax.all_to_all(lists, 'rows', split_axis=0, concat_axis=0, tiled=True)  3.9 us
    all_to_all x1, starting transfers between devices, on_device(): lax.all_to_all(packed, 'rows', split_axis=0, concat_axis=0, tiled=True, a...  3.49 us
    ppermute x2, waiting for transfers between devices, to_bands(): return (lax.ppermute(sends[0], 'band', [(0, 1), (1, 0)]),)  3.47 us
    ppermute x2, starting transfers between devices, to_bands(): return (lax.ppermute(sends[0], 'band', [(0, 1), (1, 0)]),)  3.1 us
    all_to_all x2, waiting for transfers between devices, exchange(): lax.all_to_all(sends[0], 'rows', split_axis=0, concat_axis=0, tiled=True,...  2.87 us
  transfers between devices with their start and end apart: 12, of which 9 were waited for; matrix products, arithmetic and copies ran while one was open for 0% of the time, Pallas kernels for 28%

profile of v12, /device:TPU:0, one launch (start us, length us, event | category | flops | bytes accessed | tf_op | source)
XLA Modules:
  0.0 75.6 jit_solution(3776652192759334617)
XLA Ops:
  0.0 4.0 %collective-permute-start = (f32[32,16,128]{2,1,0:T(8,128)}, f32[32,16,128]{2,1,0:T(8,128)S(1)}, u32[]{:S(2)}, u32[]{:S(2)}) collective-permute-start(f32[32,16,128]{2,1,0:T(8,128)} %start_in.1), channel_id=1, source_target_pairs={{0,8},{1,9},{2,10},{3,11},{4,12},{5,13},{6,14},{7,15},{8,0},{9,1},... | collective-permute-start | bytes 786440 | tf_op jit(solution)/shard_map/ppermute | solution.py:692
  4.0 1.8 %shard_map.100 = (s32[16,1,384]{2,1,0:T(1,128)}, s32[1,1,256]{2,1,0:T(1,128)S(1)}, s32[1,1,128]{2,1,0:T(1,128)S(1)}) custom-call(s32[2,32]{1,0:T(2,128)} %bitcast.18, s32[2,32]{1,0:T(2,128)} %bitcast.19, s32[4,32]{1,0:T(4,128)} %bitcast.17, s32[1,32]{1,0:T(1,128)} %bitcast.20, s32[1,32]{1,0:T(1,128)} %bitcast.21), custom_call_target="tpu_custom_call" | custom-call | tf_op jit(solution)/shard_map/pallas_call | solution.py:49
  5.8 3.9 %all-to-all-start = ((s32[16,1,384]{2,1,0:T(1,128)}), s32[16,1,384]{2,1,0:T(1,128)S(1)}, u32[]{:S(2)}, u32[]{:S(2)}) async-start(s32[16,1,384]{2,1,0:T(1,128)} %get-tuple-element.33), calls=%async_computation | async-start | bytes 49152 | tf_op jit(solution)/shard_map/all_to_all | solution.py:704
  11.3 3.9 %shard_map.101.refs_0_ = f32[256,16,128]{2,1,0:T(8,128)} custom-call(f32[32,16,128]{2,1,0:T(8,128)} %start_in.1, f32[8,128,128]{2,1,0:T(8,128)} %refs_3_.5), custom_call_target="tpu_custom_call" | custom-call | flops 402653184 | bytes 4194304 | tf_op jit(solution)/shard_map/pallas_call | solution.py:49
  15.2 2.4 %all-to-all-done.refs_3_.list_in.refs_0_ = s32[16,1,384]{2,1,0:T(1,128)S(1)} async-done(((s32[16,1,384]{2,1,0:T(1,128)}), s32[16,1,384]{2,1,0:T(1,128)S(1)}, u32[]{:S(2)}, u32[]{:S(2)}) %all-to-all-start) | async-done | bytes 24608 | tf_op jit(solution)/shard_map/all_to_all | solution.py:704
  17.6 2.7 %shard_map.102 = (f32[8,16,16,128]{3,2,1,0:T(8,128)}, f32[32,16,128]{2,1,0:T(8,128)}) custom-call(f32[256,16,128]{2,1,0:T(8,128)} %shard_map.101.refs_0_, f32[32,16,128]{2,1,0:T(8,128)S(1)} %collective-permute-done.refs_1_, f32[8,128,128]{2,1,0:T(8,128)S(1)} %copy-done.1, s32[16,1,384]{2,1,0:T(1,128)S(1)} %all-to-all-done.refs_3_.list_in.refs_0_, ...), custom_call_target="tpu_custom_call" | custom-call | flops 402653184 | bytes 4194304 | tf_op jit(solution)/shard_map/pallas_call | solution.py:49
  20.4 3.7 %all-to-all-start.1 = ((f32[8,256,128]{2,1,0:T(8,128)}), f32[8,256,128]{2,1,0:T(8,128)S(1)}, u32[]{:S(2)}, u32[]{:S(2)}) async-start(f32[8,256,128]{2,1,0:T(8,128)} %bitcast.14), calls=%async_computation.1 | async-start | bytes 2097152 | tf_op jit(solution)/shard_map/all_to_all | solution.py:767
  24.1 1.6 %collective-permute-start.2 = (s32[16,1,384]{2,1,0:T(1,128)S(1)}, s32[16,1,384]{2,1,0:T(1,128)S(1)}, u32[]{:S(2)}, u32[]{:S(2)}) collective-permute-start(s32[16,1,384]{2,1,0:T(1,128)S(1)} %all-to-all-done.refs_3_.list_in.refs_0_), channel_id=1, source_target_pairs={{0,16},{16,0},{1,17},{17,1},{2,18},{18,2},{3,19},{19,3},{4,20},{20... | collective-permute-start | bytes 73736 | tf_op jit(solution)/shard_map/ppermute | solution.py:762
  25.7 2.3 %collective-permute-done.2 = s32[16,1,384]{2,1,0:T(1,128)S(1)} collective-permute-done((s32[16,1,384]{2,1,0:T(1,128)S(1)}, s32[16,1,384]{2,1,0:T(1,128)S(1)}, u32[]{:S(2)}, u32[]{:S(2)}) %collective-permute-start.2) | collective-permute-done | bytes 24608 | tf_op jit(solution)/shard_map/ppermute | solution.py:762
  29.8 6.7 %shard_map.103 = (bf16[256,1440]{1,0:T(8,128)(2,1)}, bf16[128,384]{1,0:T(8,128)(2,1)}, bf16[1024,256]{1,0:T(8,128)(2,1)}, f32[256,128]{1,0:T(8,128)}, f32[4,128]{1,0:T(4,128)S(1)}) custom-call(s32[1,1,256]{2,1,0:T(1,128)S(1)} %get-tuple-element.32.refs_0_.refs_1_, f32[32,16,128]{2,1,0:T(8,128)} %refs_4_.5, s32[8,2,512]{2,1,0:T(2,128)S(1)} %reshape.7.refs_2_, ...), custom_call_target="tpu_custom_call" | custom-call | flops 1342177280 | bytes 4194304 | tf_op jit(solution)/shard_map/pallas_call | solution.py:49
  36.5 1.9 %all-to-all-done.1.refs_2_ = f32[8,256,128]{2,1,0:T(8,128)S(1)} async-done(((f32[8,256,128]{2,1,0:T(8,128)}), f32[8,256,128]{2,1,0:T(8,128)S(1)}, u32[]{:S(2)}, u32[]{:S(2)}) %all-to-all-start.1) | async-done | bytes 1048608 | tf_op jit(solution)/shard_map/all_to_all | solution.py:767
  38.5 1.8 %shard_map.104.refs_2_ = f32[32,16,128]{2,1,0:T(8,128)S(1)} custom-call(s32[1,1,128]{2,1,0:T(1,128)S(1)} %get-tuple-element.31.refs_0_, s32[1,1,256]{2,1,0:T(1,128)S(1)} %get-tuple-element.32.refs_0_.refs_1_, f32[8,256,128]{2,1,0:T(8,128)S(1)} %all-to-all-done.1.refs_2_, f32[8,128,128]{2,1,0:T(8,128)S(1)} %copy-done, f32[32,16,128]{2,1,0:T(8,128)} %refs_4_.5, ...), custom_call_target="tpu_custom_call" | custom-call | flops 402653184 | bytes 4194304 | tf_op jit(solution)/shard_map/pallas_call | solution.py:49
  40.2 2.7 %collective-permute-start.4 = (f32[32,16,128]{2,1,0:T(8,128)S(1)}, f32[32,16,128]{2,1,0:T(8,128)S(1)}, u32[]{:S(2)}, u32[]{:S(2)}) collective-permute-start(f32[32,16,128]{2,1,0:T(8,128)S(1)} %shard_map.104.refs_2_), channel_id=1, source_target_pairs={{0,8},{1,9},{2,10},{3,11},{4,12},{5,13},{6,14},{7,15},{8,0},{9,1},... | collective-permute-start | bytes 786440 | tf_op jit(solution)/shard_map/ppermute | solution.py:848
  43.0 4.8 %shard_map.106 = (f32[8,144,128]{2,1,0:T(8,128)}, f32[32,16,128]{2,1,0:T(8,128)}) custom-call(s32[16,1,384]{2,1,0:T(1,128)S(1)} %all-to-all-done.refs_3_.list_in.refs_0_, s32[1,1,256]{2,1,0:T(1,128)S(1)} %collective-permute-done.1.refs_4_.refs_1_, f32[32,16,128]{2,1,0:T(8,128)S(1)} %shard_map.104.refs_2_, f32[8,128,128]{2,1,0:T(8,128)S(1)} %copy-done.1, ...), custom_call_target="tpu_custom_call" | custom-call | flops 805306368 | bytes 4194304 | tf_op jit(solution)/shard_map/pallas_call | solution.py:49
  47.7 3.7 %all-to-all-start.3 = ((f32[8,144,128]{2,1,0:T(8,128)}), f32[8,144,128]{2,1,0:T(8,128)S(1)}, u32[]{:S(2)}, u32[]{:S(2)}) async-start(f32[8,144,128]{2,1,0:T(8,128)} %get-tuple-element.52), calls=%async_computation.3 | async-start | bytes 1179648 | tf_op jit(solution)/shard_map/all_to_all | solution.py:767
  53.1 1.7 %collective-permute-done.4.mirror_ref = f32[32,16,128]{2,1,0:T(8,128)S(1)} collective-permute-done((f32[32,16,128]{2,1,0:T(8,128)S(1)}, f32[32,16,128]{2,1,0:T(8,128)S(1)}, u32[]{:S(2)}, u32[]{:S(2)}) %collective-permute-start.4) | collective-permute-done | bytes 262176 | tf_op jit(solution)/shard_map/ppermute | solution.py:848
  54.7 1.9 %shard_map.105 = f32[8,128,128]{2,1,0:T(8,128)} custom-call(s32[16,1,384]{2,1,0:T(1,128)S(1)} %all-to-all-done.refs_3_.list_in.refs_0_, f32[32,16,128]{2,1,0:T(8,128)S(1)} %collective-permute-done.4.mirror_ref, f32[8,128,128]{2,1,0:T(8,128)S(1)} %copy-done.1), custom_call_target="tpu_custom_call" | custom-call | flops 40265318400 | bytes 4194304 | tf_op jit(solution)/shard_map/pallas_call | solution.py:49
  56.6 3.5 %collective-permute-done.5.refs_5_ = f32[32,16,128]{2,1,0:T(8,128)S(1)} collective-permute-done((f32[32,16,128]{2,1,0:T(8,128)}, f32[32,16,128]{2,1,0:T(8,128)S(1)}, u32[]{:S(2)}, u32[]{:S(2)}) %collective-permute-start.5) | collective-permute-done | bytes 262176 | tf_op jit(solution)/shard_map/ppermute | solution.py:647
  61.1 3.5 %all-to-all-start.2 = ((f32[8,128,128]{2,1,0:T(8,128)}), f32[8,128,128]{2,1,0:T(8,128)S(1)}, u32[]{:S(2)}, u32[]{:S(2)}) async-start(f32[8,128,128]{2,1,0:T(8,128)} %shard_map.105), calls=%async_computation.2 | async-start | bytes 1048576 | tf_op jit(solution)/shard_map/all_to_all | solution.py:887
  64.6 1.6 %collective-permute-start.6 = (f32[8,128]{1,0:T(8,128)S(1)}, f32[8,128]{1,0:T(8,128)S(1)}, u32[]{:S(2)}, u32[]{:S(2)}) collective-permute-start(f32[8,128]{1,0:T(8,128)S(1)} %get-tuple-element.55), channel_id=1, source_target_pairs={{0,16},{16,0},{1,17},{17,1},{2,18},{18,2},{3,19},{19,3},{4,20},{20... | collective-permute-start | bytes 12296 | tf_op jit(solution)/shard_map/ppermute | solution.py:892
  66.2 2.1 %collective-permute-done.6 = f32[8,128]{1,0:T(8,128)S(1)} collective-permute-done((f32[8,128]{1,0:T(8,128)S(1)}, f32[8,128]{1,0:T(8,128)S(1)}, u32[]{:S(2)}, u32[]{:S(2)}) %collective-permute-start.6) | collective-permute-done | bytes 4128 | tf_op jit(solution)/shard_map/ppermute | solution.py:892
  68.3 1.8 %collective-permute-start.7 = (f32[4,128]{1,0:T(4,128)S(1)}, f32[4,128]{1,0:T(4,128)S(1)}, u32[]{:S(2)}, u32[]{:S(2)}) collective-permute-start(f32[4,128]{1,0:T(4,128)S(1)} %get-tuple-element.57), channel_id=1, source_target_pairs={{0,8},{1,9},{2,10},{3,11},{4,12},{5,13},{6,14},{7,15},{8,0},{9,1},... | collective-permute-start | bytes 6152 | tf_op jit(solution)/shard_map/ppermute | solution.py:893
  70.1 1.8 %shard_map.107.refs_4_ = f32[32,16,128]{2,1,0:T(8,128)S(1)} custom-call(s32[1,1,128]{2,1,0:T(1,128)S(1)} %get-tuple-element.31.refs_0_, s32[1,1,256]{2,1,0:T(1,128)S(1)} %get-tuple-element.32.refs_0_.refs_1_, f32[8,144,128]{2,1,0:T(8,128)S(1)} %all-to-all-done.3.refs_2_.arrived_ref, f32[8,128,128]{2,1,0:T(8,128)S(1)} %copy-done, f32[32,16,128]{2,1,0:T(8,128)} %refs_4_.5, ...), custom_call_target="tpu_custom_call" | custom-call | flops 402653184 | bytes 4194304 | tf_op jit(solution)/shard_map/pallas_call | solution.py:49
  73.4 2.1 %shard_map.109 = f32[32,16,128]{2,1,0:T(8,128)} custom-call(s32[1,1,128]{2,1,0:T(1,128)S(1)} %get-tuple-element.31.refs_0_, s32[1,1,256]{2,1,0:T(1,128)S(1)} %get-tuple-element.32.refs_0_.refs_1_, f32[8,128,128]{2,1,0:T(8,128)S(1)} %all-to-all-done.2.refs_2_, f32[8,128,128]{2,1,0:T(8,128)S(1)} %copy-done, f32[32,16,128]{2,1,0:T(8,128)S(1)} %shard_map.107.refs_4_, ...), custom_call_target="tpu_custom_call" | custom-call | flops 402653184 | bytes 4194304 | tf_op jit(solution)/shard_map/pallas_call | solution.py:49
  (25 shorter events, 7.5 us)
Async XLA Ops:
  0.0 17.6 %copy-start.1 = (f32[8,128,128]{2,1,0:T(8,128)S(1)}, f32[8,128,128]{2,1,0:T(8,128)}, u32[]{:S(2)}) copy-start(f32[8,128,128]{2,1,0:T(8,128)} %refs_3_.5) | copy-start | bytes 1572868
  0.0 17.6 %collective-permute-start = (f32[32,16,128]{2,1,0:T(8,128)}, f32[32,16,128]{2,1,0:T(8,128)S(1)}, u32[]{:S(2)}, u32[]{:S(2)}) collective-permute-start(f32[32,16,128]{2,1,0:T(8,128)} %start_in.1), channel_id=1, source_target_pairs={{0,8},{1,9},{2,10},{3,11},{4,12},{5,13},{6,14},{7,15},{8,0},{9,1},... | collective-permute-start | bytes 786440 | tf_op jit(solution)/shard_map/ppermute | solution.py:692
  5.8 11.8 %all-to-all-start = ((s32[16,1,384]{2,1,0:T(1,128)}), s32[16,1,384]{2,1,0:T(1,128)S(1)}, u32[]{:S(2)}, u32[]{:S(2)}) async-start(s32[16,1,384]{2,1,0:T(1,128)} %get-tuple-element.33), calls=%async_computation | async-start | bytes 49152 | tf_op jit(solution)/shard_map/all_to_all | solution.py:704
  9.7 5.5 %collective-permute-start.1 = (s32[1,1,256]{2,1,0:T(1,128)S(1)}, s32[1,1,256]{2,1,0:T(1,128)S(1)}, u32[]{:S(2)}, u32[]{:S(2)}) collective-permute-start(s32[1,1,256]{2,1,0:T(1,128)S(1)} %get-tuple-element.32.refs_0_.refs_1_), channel_id=1, source_target_pairs={{0,16},{16,0},{1,17},{17,1},{2,18},{18,2},{3,19},{19,3},{4,20},{20... | collective-permute-start | bytes 3080 | tf_op jit(solution)/shard_map/ppermute | solution.py:706
  20.3 7.6 %copy-start.3 = (f32[32,16,128]{2,1,0:T(8,128)S(1)}, f32[32,16,128]{2,1,0:T(8,128)}, u32[]{:S(2)}) copy-start(f32[32,16,128]{2,1,0:T(8,128)} %get-tuple-element.45) | copy-start | bytes 786436
  20.4 9.5 %copy-start = (f32[8,128,128]{2,1,0:T(8,128)S(1)}, f32[8,128,128]{2,1,0:T(8,128)}, u32[]{:S(2)}) copy-start(f32[8,128,128]{2,1,0:T(8,128)} %refs_3_.7) | copy-start | bytes 1572868
  20.4 9.5 %copy-start.2 = (f32[8,128,128]{2,1,0:T(8,128)S(1)}, f32[8,128,128]{2,1,0:T(8,128)}, u32[]{:S(2)}) copy-start(f32[8,128,128]{2,1,0:T(8,128)} %refs_5_.1) | copy-start | bytes 1572868
  20.4 18.1 %all-to-all-start.1 = ((f32[8,256,128]{2,1,0:T(8,128)}), f32[8,256,128]{2,1,0:T(8,128)S(1)}, u32[]{:S(2)}, u32[]{:S(2)}) async-start(f32[8,256,128]{2,1,0:T(8,128)} %bitcast.14), calls=%async_computation.1 | async-start | bytes 2097152 | tf_op jit(solution)/shard_map/all_to_all | solution.py:767
  24.1 3.9 %collective-permute-start.2 = (s32[16,1,384]{2,1,0:T(1,128)S(1)}, s32[16,1,384]{2,1,0:T(1,128)S(1)}, u32[]{:S(2)}, u32[]{:S(2)}) collective-permute-start(s32[16,1,384]{2,1,0:T(1,128)S(1)} %all-to-all-done.refs_3_.list_in.refs_0_), channel_id=1, source_target_pairs={{0,16},{16,0},{1,17},{17,1},{2,18},{18,2},{3,19},{19,3},{4,20},{20... | collective-permute-start | bytes 73736 | tf_op jit(solution)/shard_map/ppermute | solution.py:762
  28.0 10.5 %collective-permute-start.3 = (f32[32,16,128]{2,1,0:T(8,128)S(1)}, f32[32,16,128]{2,1,0:T(8,128)S(1)}, u32[]{:S(2)}, u32[]{:S(2)}) collective-permute-start(f32[32,16,128]{2,1,0:T(8,128)S(1)} %copy-done.3), channel_id=1, source_target_pairs={{0,16},{16,0},{1,17},{17,1},{2,18},{18,2},{3,19},{19,3},{4,20},{20... | collective-permute-start | bytes 786440 | tf_op jit(solution)/shard_map/ppermute | solution.py:647
  40.2 14.5 %collective-permute-start.4 = (f32[32,16,128]{2,1,0:T(8,128)S(1)}, f32[32,16,128]{2,1,0:T(8,128)S(1)}, u32[]{:S(2)}, u32[]{:S(2)}) collective-permute-start(f32[32,16,128]{2,1,0:T(8,128)S(1)} %shard_map.104.refs_2_), channel_id=1, source_target_pairs={{0,8},{1,9},{2,10},{3,11},{4,12},{5,13},{6,14},{7,15},{8,0},{9,1},... | collective-permute-start | bytes 786440 | tf_op jit(solution)/shard_map/ppermute | solution.py:848
  47.7 13.3 %all-to-all-start.3 = ((f32[8,144,128]{2,1,0:T(8,128)}), f32[8,144,128]{2,1,0:T(8,128)S(1)}, u32[]{:S(2)}, u32[]{:S(2)}) async-start(f32[8,144,128]{2,1,0:T(8,128)} %get-tuple-element.52), calls=%async_computation.3 | async-start | bytes 1179648 | tf_op jit(solution)/shard_map/all_to_all | solution.py:767
  51.5 8.6 %collective-permute-start.5 = (f32[32,16,128]{2,1,0:T(8,128)}, f32[32,16,128]{2,1,0:T(8,128)S(1)}, u32[]{:S(2)}, u32[]{:S(2)}) collective-permute-start(f32[32,16,128]{2,1,0:T(8,128)} %get-tuple-element.50), channel_id=1, source_target_pairs={{0,16},{16,0},{1,17},{17,1},{2,18},{18,2},{3,19},{19,3},{4,20},{20... | collective-permute-start | bytes 786440 | tf_op jit(solution)/shard_map/ppermute | solution.py:647
  61.1 12.3 %all-to-all-start.2 = ((f32[8,128,128]{2,1,0:T(8,128)}), f32[8,128,128]{2,1,0:T(8,128)S(1)}, u32[]{:S(2)}, u32[]{:S(2)}) async-start(f32[8,128,128]{2,1,0:T(8,128)} %shard_map.105), calls=%async_computation.2 | async-start | bytes 1048576 | tf_op jit(solution)/shard_map/all_to_all | solution.py:887
  64.6 3.7 %collective-permute-start.6 = (f32[8,128]{1,0:T(8,128)S(1)}, f32[8,128]{1,0:T(8,128)S(1)}, u32[]{:S(2)}, u32[]{:S(2)}) collective-permute-start(f32[8,128]{1,0:T(8,128)S(1)} %get-tuple-element.55), channel_id=1, source_target_pairs={{0,16},{16,0},{1,17},{17,1},{2,18},{18,2},{3,19},{19,3},{4,20},{20... | collective-permute-start | bytes 12296 | tf_op jit(solution)/shard_map/ppermute | solution.py:892
  68.3 4.6 %collective-permute-start.7 = (f32[4,128]{1,0:T(4,128)S(1)}, f32[4,128]{1,0:T(4,128)S(1)}, u32[]{:S(2)}, u32[]{:S(2)}) collective-permute-start(f32[4,128]{1,0:T(4,128)S(1)} %get-tuple-element.57), channel_id=1, source_target_pairs={{0,8},{1,9},{2,10},{3,11},{4,12},{5,13},{6,14},{7,15},{8,0},{9,1},... | collective-permute-start | bytes 6152 | tf_op jit(solution)/shard_map/ppermute | solution.py:893

commit v13 on v12

--- a/solution.py
+++ b/solution.py
@@ -496,7 +496,7 @@
     body, half = cap * n_rhs, n_rows // 2
     upper = lax.axis_index("rows") >= half
     mine, others = jnp.where(upper, half, 0), jnp.where(upper, 0, half)
-    finish(fetched)
+    finish(fetched[:1])
     functional_ref, count_ref, place_ref, partial_ref = held
     n_blocks = n_rows * cap + rows
     n_func = spread_ref.shape[0] // n_blocks
@@ -521,6 +521,7 @@
             blocks = jnp.concatenate([send_ref[order - 1], send_ref[order]], axis=0)
             spread((order - 1) * cap, blocks, kinds)
             kinds = []
+    finish(fetched[1:])
     result = coarse_parts(n_rhs, n_blocks, count_ref, place_ref, partial_ref, spread_ref)
     result_ref[...] = result.reshape(result_ref.shape)
     depth = result_ref.shape[1]

time: 76.2 us -> 76.2 us (level)
  transfers between devices with their start and end apart: 12 -> 12, of which waited for: 9 -> 9; matrix products, arithmetic and copies ran while one was open for 0% -> 0% of each run, Pallas kernels for 28% -> 27%
where the time goes in v13:
time: 76.2 us; the launch traced here: 75.6 us
  starting transfers between devices  31.2 us (41%)
  Pallas kernels  26.8 us (35%)
  waiting for transfers between devices  16.8 us (22%)
    pallas_call x10, Pallas kernels, apply(): return run(*pinned)  26.8 us
    all_to_all x2, starting transfers between devices, exchange(): lax.all_to_all(sends[0], 'rows', split_axis=0, concat_axis=0, tiled=True,...  7.43 us
    ppermute x1, starting transfers between devices, on_device(): mirror = lax.ppermute(start_iterate, 'rows', to_mirror)  4.04 us
    all_to_all x1, starting transfers between devices, on_device(): lax.all_to_all(lists, 'rows', split_axis=0, concat_axis=0, tiled=True)  3.9 us
    all_to_all x1, starting transfers between devices, on_device(): lax.all_to_all(packed, 'rows', split_axis=0, concat_axis=0, tiled=True, a...  3.49 us
    all_to_all x2, waiting for transfers between devices, exchange(): lax.all_to_all(sends[0], 'rows', split_axis=0, concat_axis=0, tiled=True,...  3.41 us
    ppermute x2, starting transfers between devices, to_bands(): return (lax.ppermute(sends[0], 'band', [(0, 1), (1, 0)]),)  3.1 us
    ppermute x2, waiting for transfers between devices, to_bands(): return (lax.ppermute(sends[0], 'band', [(0, 1), (1, 0)]),)  2.88 us
  transfers between devices with their start and end apart: 12, of which 9 were waited for; matrix products, arithmetic and copies ran while one was open for 0% of the time, Pallas kernels for 27%

profile of v13, /device:TPU:0, one launch (start us, length us, event | category | flops | bytes accessed | tf_op | source)
XLA Modules:
  0.0 75.6 jit_solution(981459125064249134)
XLA Ops:
  0.0 4.0 %collective-permute-start = (f32[32,16,128]{2,1,0:T(8,128)}, f32[32,16,128]{2,1,0:T(8,128)S(1)}, u32[]{:S(2)}, u32[]{:S(2)}) collective-permute-start(f32[32,16,128]{2,1,0:T(8,128)} %start_in.1), channel_id=1, source_target_pairs={{0,8},{1,9},{2,10},{3,11},{4,12},{5,13},{6,14},{7,15},{8,0},{9,1},... | collective-permute-start | bytes 786440 | tf_op jit(solution)/shard_map/ppermute | solution.py:693
  4.0 1.8 %shard_map.100 = (s32[16,1,384]{2,1,0:T(1,128)}, s32[1,1,256]{2,1,0:T(1,128)S(1)}, s32[1,1,128]{2,1,0:T(1,128)S(1)}) custom-call(s32[2,32]{1,0:T(2,128)} %bitcast.18, s32[2,32]{1,0:T(2,128)} %bitcast.19, s32[4,32]{1,0:T(4,128)} %bitcast.17, s32[1,32]{1,0:T(1,128)} %bitcast.20, s32[1,32]{1,0:T(1,128)} %bitcast.21), custom_call_target="tpu_custom_call" | custom-call | tf_op jit(solution)/shard_map/pallas_call | solution.py:49
  5.8 3.9 %all-to-all-start = ((s32[16,1,384]{2,1,0:T(1,128)}), s32[16,1,384]{2,1,0:T(1,128)S(1)}, u32[]{:S(2)}, u32[]{:S(2)}) async-start(s32[16,1,384]{2,1,0:T(1,128)} %get-tuple-element.33), calls=%async_computation | async-start | bytes 49152 | tf_op jit(solution)/shard_map/all_to_all | solution.py:705
  9.7 1.6 %collective-permute-start.1 = (s32[1,1,256]{2,1,0:T(1,128)S(1)}, s32[1,1,256]{2,1,0:T(1,128)S(1)}, u32[]{:S(2)}, u32[]{:S(2)}) collective-permute-start(s32[1,1,256]{2,1,0:T(1,128)S(1)} %get-tuple-element.32.refs_0_.refs_1_), channel_id=1, source_target_pairs={{0,16},{16,0},{1,17},{17,1},{2,18},{18,2},{3,19},{19,3},{4,20},{20... | collective-permute-start | bytes 3080 | tf_op jit(solution)/shard_map/ppermute | solution.py:707
  11.3 3.9 %shard_map.101.refs_0_ = f32[256,16,128]{2,1,0:T(8,128)} custom-call(f32[32,16,128]{2,1,0:T(8,128)} %start_in.1, f32[8,128,128]{2,1,0:T(8,128)} %refs_3_.5), custom_call_target="tpu_custom_call" | custom-call | flops 402653184 | bytes 4194304 | tf_op jit(solution)/shard_map/pallas_call | solution.py:49
  15.2 2.4 %all-to-all-done.refs_3_.list_in.refs_0_ = s32[16,1,384]{2,1,0:T(1,128)S(1)} async-done(((s32[16,1,384]{2,1,0:T(1,128)}), s32[16,1,384]{2,1,0:T(1,128)S(1)}, u32[]{:S(2)}, u32[]{:S(2)}) %all-to-all-start) | async-done | bytes 24608 | tf_op jit(solution)/shard_map/all_to_all | solution.py:705
  17.6 2.7 %shard_map.102 = (f32[8,16,16,128]{3,2,1,0:T(8,128)}, f32[32,16,128]{2,1,0:T(8,128)}) custom-call(f32[256,16,128]{2,1,0:T(8,128)} %shard_map.101.refs_0_, f32[32,16,128]{2,1,0:T(8,128)S(1)} %collective-permute-done.refs_1_, f32[8,128,128]{2,1,0:T(8,128)S(1)} %copy-done.1, s32[16,1,384]{2,1,0:T(1,128)S(1)} %all-to-all-done.refs_3_.list_in.refs_0_, ...), custom_call_target="tpu_custom_call" | custom-call | flops 402653184 | bytes 4194304 | tf_op jit(solution)/shard_map/pallas_call | solution.py:49
  20.4 3.7 %all-to-all-start.1 = ((f32[8,256,128]{2,1,0:T(8,128)}), f32[8,256,128]{2,1,0:T(8,128)S(1)}, u32[]{:S(2)}, u32[]{:S(2)}) async-start(f32[8,256,128]{2,1,0:T(8,128)} %bitcast.14), calls=%async_computation.1 | async-start | bytes 2097152 | tf_op jit(solution)/shard_map/all_to_all | solution.py:768
  24.1 1.6 %collective-permute-start.2 = (s32[16,1,384]{2,1,0:T(1,128)S(1)}, s32[16,1,384]{2,1,0:T(1,128)S(1)}, u32[]{:S(2)}, u32[]{:S(2)}) collective-permute-start(s32[16,1,384]{2,1,0:T(1,128)S(1)} %all-to-all-done.refs_3_.list_in.refs_0_), channel_id=1, source_target_pairs={{0,16},{16,0},{1,17},{17,1},{2,18},{18,2},{3,19},{19,3},{4,20},{20... | collective-permute-start | bytes 73736 | tf_op jit(solution)/shard_map/ppermute | solution.py:763
  25.7 2.3 %collective-permute-done.2 = s32[16,1,384]{2,1,0:T(1,128)S(1)} collective-permute-done((s32[16,1,384]{2,1,0:T(1,128)S(1)}, s32[16,1,384]{2,1,0:T(1,128)S(1)}, u32[]{:S(2)}, u32[]{:S(2)}) %collective-permute-start.2) | collective-permute-done | bytes 24608 | tf_op jit(solution)/shard_map/ppermute | solution.py:763
  29.8 6.7 %shard_map.103 = (bf16[256,1440]{1,0:T(8,128)(2,1)}, bf16[128,384]{1,0:T(8,128)(2,1)}, bf16[1024,256]{1,0:T(8,128)(2,1)}, f32[256,128]{1,0:T(8,128)}, f32[4,128]{1,0:T(4,128)S(1)}) custom-call(s32[1,1,256]{2,1,0:T(1,128)S(1)} %get-tuple-element.32.refs_0_.refs_1_, f32[32,16,128]{2,1,0:T(8,128)} %refs_4_.5, s32[8,2,512]{2,1,0:T(2,128)S(1)} %reshape.7.refs_2_, ...), custom_call_target="tpu_custom_call" | custom-call | flops 1342177280 | bytes 4194304 | tf_op jit(solution)/shard_map/pallas_call | solution.py:49
  36.5 1.9 %all-to-all-done.1.refs_2_ = f32[8,256,128]{2,1,0:T(8,128)S(1)} async-done(((f32[8,256,128]{2,1,0:T(8,128)}), f32[8,256,128]{2,1,0:T(8,128)S(1)}, u32[]{:S(2)}, u32[]{:S(2)}) %all-to-all-start.1) | async-done | bytes 1048608 | tf_op jit(solution)/shard_map/all_to_all | solution.py:768
  38.5 1.8 %shard_map.104.refs_2_ = f32[32,16,128]{2,1,0:T(8,128)S(1)} custom-call(s32[1,1,128]{2,1,0:T(1,128)S(1)} %get-tuple-element.31.refs_0_, s32[1,1,256]{2,1,0:T(1,128)S(1)} %get-tuple-element.32.refs_0_.refs_1_, f32[8,256,128]{2,1,0:T(8,128)S(1)} %all-to-all-done.1.refs_2_, f32[8,128,128]{2,1,0:T(8,128)S(1)} %copy-done, f32[32,16,128]{2,1,0:T(8,128)} %refs_4_.5, ...), custom_call_target="tpu_custom_call" | custom-call | flops 402653184 | bytes 4194304 | tf_op jit(solution)/shard_map/pallas_call | solution.py:49
  40.2 2.7 %collective-permute-start.4 = (f32[32,16,128]{2,1,0:T(8,128)S(1)}, f32[32,16,128]{2,1,0:T(8,128)S(1)}, u32[]{:S(2)}, u32[]{:S(2)}) collective-permute-start(f32[32,16,128]{2,1,0:T(8,128)S(1)} %shard_map.104.refs_2_), channel_id=1, source_target_pairs={{0,8},{1,9},{2,10},{3,11},{4,12},{5,13},{6,14},{7,15},{8,0},{9,1},... | collective-permute-start | bytes 786440 | tf_op jit(solution)/shard_map/ppermute | solution.py:849
  43.0 4.2 %shard_map.106 = (f32[8,144,128]{2,1,0:T(8,128)}, f32[32,16,128]{2,1,0:T(8,128)}) custom-call(s32[16,1,384]{2,1,0:T(1,128)S(1)} %all-to-all-done.refs_3_.list_in.refs_0_, s32[1,1,256]{2,1,0:T(1,128)S(1)} %collective-permute-done.1.refs_4_.refs_1_, f32[32,16,128]{2,1,0:T(8,128)S(1)} %shard_map.104.refs_2_, f32[8,128,128]{2,1,0:T(8,128)S(1)} %copy-done.1, ...), custom_call_target="tpu_custom_call" | custom-call | flops 805306368 | bytes 4194304 | tf_op jit(solution)/shard_map/pallas_call | solution.py:49
  47.2 3.7 %all-to-all-start.3 = ((f32[8,144,128]{2,1,0:T(8,128)}), f32[8,144,128]{2,1,0:T(8,128)S(1)}, u32[]{:S(2)}, u32[]{:S(2)}) async-start(f32[8,144,128]{2,1,0:T(8,128)} %get-tuple-element.52), calls=%async_computation.3 | async-start | bytes 1179648 | tf_op jit(solution)/shard_map/all_to_all | solution.py:768
  52.5 2.3 %collective-permute-done.4.mirror_ref = f32[32,16,128]{2,1,0:T(8,128)S(1)} collective-permute-done((f32[32,16,128]{2,1,0:T(8,128)S(1)}, f32[32,16,128]{2,1,0:T(8,128)S(1)}, u32[]{:S(2)}, u32[]{:S(2)}) %collective-permute-start.4) | collective-permute-done | bytes 262176 | tf_op jit(solution)/shard_map/ppermute | solution.py:849
  54.8 1.9 %shard_map.105 = f32[8,128,128]{2,1,0:T(8,128)} custom-call(s32[16,1,384]{2,1,0:T(1,128)S(1)} %all-to-all-done.refs_3_.list_in.refs_0_, f32[32,16,128]{2,1,0:T(8,128)S(1)} %collective-permute-done.4.mirror_ref, f32[8,128,128]{2,1,0:T(8,128)S(1)} %copy-done.1), custom_call_target="tpu_custom_call" | custom-call | flops 40265318400 | bytes 4194304 | tf_op jit(solution)/shard_map/pallas_call | solution.py:49
  56.7 2.9 %collective-permute-done.5.refs_5_ = f32[32,16,128]{2,1,0:T(8,128)S(1)} collective-permute-done((f32[32,16,128]{2,1,0:T(8,128)}, f32[32,16,128]{2,1,0:T(8,128)S(1)}, u32[]{:S(2)}, u32[]{:S(2)}) %collective-permute-start.5) | collective-permute-done | bytes 262176 | tf_op jit(solution)/shard_map/ppermute | solution.py:648
  61.1 3.5 %all-to-all-start.2 = ((f32[8,128,128]{2,1,0:T(8,128)}), f32[8,128,128]{2,1,0:T(8,128)S(1)}, u32[]{:S(2)}, u32[]{:S(2)}) async-start(f32[8,128,128]{2,1,0:T(8,128)} %shard_map.105), calls=%async_computation.2 | async-start | bytes 1048576 | tf_op jit(solution)/shard_map/all_to_all | solution.py:888
  66.2 2.1 %collective-permute-done.6 = f32[8,128]{1,0:T(8,128)S(1)} collective-permute-done((f32[8,128]{1,0:T(8,128)S(1)}, f32[8,128]{1,0:T(8,128)S(1)}, u32[]{:S(2)}, u32[]{:S(2)}) %collective-permute-start.6) | collective-permute-done | bytes 4128 | tf_op jit(solution)/shard_map/ppermute | solution.py:893
  68.3 1.8 %collective-permute-start.7 = (f32[4,128]{1,0:T(4,128)S(1)}, f32[4,128]{1,0:T(4,128)S(1)}, u32[]{:S(2)}, u32[]{:S(2)}) collective-permute-start(f32[4,128]{1,0:T(4,128)S(1)} %get-tuple-element.57), channel_id=1, source_target_pairs={{0,8},{1,9},{2,10},{3,11},{4,12},{5,13},{6,14},{7,15},{8,0},{9,1},... | collective-permute-start | bytes 6152 | tf_op jit(solution)/shard_map/ppermute | solution.py:894
  70.1 1.8 %shard_map.107.refs_4_ = f32[32,16,128]{2,1,0:T(8,128)S(1)} custom-call(s32[1,1,128]{2,1,0:T(1,128)S(1)} %get-tuple-element.31.refs_0_, s32[1,1,256]{2,1,0:T(1,128)S(1)} %get-tuple-element.32.refs_0_.refs_1_, f32[8,144,128]{2,1,0:T(8,128)S(1)} %all-to-all-done.3.refs_2_.arrived_ref, f32[8,128,128]{2,1,0:T(8,128)S(1)} %copy-done, f32[32,16,128]{2,1,0:T(8,128)} %refs_4_.5, ...), custom_call_target="tpu_custom_call" | custom-call | flops 402653184 | bytes 4194304 | tf_op jit(solution)/shard_map/pallas_call | solution.py:49
  73.4 2.1 %shard_map.109 = f32[32,16,128]{2,1,0:T(8,128)} custom-call(s32[1,1,128]{2,1,0:T(1,128)S(1)} %get-tuple-element.31.refs_0_, s32[1,1,256]{2,1,0:T(1,128)S(1)} %get-tuple-element.32.refs_0_.refs_1_, f32[8,128,128]{2,1,0:T(8,128)S(1)} %all-to-all-done.2.refs_2_, f32[8,128,128]{2,1,0:T(8,128)S(1)} %copy-done, f32[32,16,128]{2,1,0:T(8,128)S(1)} %shard_map.107.refs_4_, ...), custom_call_target="tpu_custom_call" | custom-call | flops 402653184 | bytes 4194304 | tf_op jit(solution)/shard_map/pallas_call | solution.py:49
  (25 shorter events, 8.0 us)
Async XLA Ops:
  0.0 17.6 %copy-start.1 = (f32[8,128,128]{2,1,0:T(8,128)S(1)}, f32[8,128,128]{2,1,0:T(8,128)}, u32[]{:S(2)}) copy-start(f32[8,128,128]{2,1,0:T(8,128)} %refs_3_.5) | copy-start | bytes 1572868
  0.0 17.6 %collective-permute-start = (f32[32,16,128]{2,1,0:T(8,128)}, f32[32,16,128]{2,1,0:T(8,128)S(1)}, u32[]{:S(2)}, u32[]{:S(2)}) collective-permute-start(f32[32,16,128]{2,1,0:T(8,128)} %start_in.1), channel_id=1, source_target_pairs={{0,8},{1,9},{2,10},{3,11},{4,12},{5,13},{6,14},{7,15},{8,0},{9,1},... | collective-permute-start | bytes 786440 | tf_op jit(solution)/shard_map/ppermute | solution.py:693
  5.8 11.8 %all-to-all-start = ((s32[16,1,384]{2,1,0:T(1,128)}), s32[16,1,384]{2,1,0:T(1,128)S(1)}, u32[]{:S(2)}, u32[]{:S(2)}) async-start(s32[16,1,384]{2,1,0:T(1,128)} %get-tuple-element.33), calls=%async_computation | async-start | bytes 49152 | tf_op jit(solution)/shard_map/all_to_all | solution.py:705
  9.7 5.5 %collective-permute-start.1 = (s32[1,1,256]{2,1,0:T(1,128)S(1)}, s32[1,1,256]{2,1,0:T(1,128)S(1)}, u32[]{:S(2)}, u32[]{:S(2)}) collective-permute-start(s32[1,1,256]{2,1,0:T(1,128)S(1)} %get-tuple-element.32.refs_0_.refs_1_), channel_id=1, source_target_pairs={{0,16},{16,0},{1,17},{17,1},{2,18},{18,2},{3,19},{19,3},{4,20},{20... | collective-permute-start | bytes 3080 | tf_op jit(solution)/shard_map/ppermute | solution.py:707
  20.3 7.6 %copy-start.3 = (f32[32,16,128]{2,1,0:T(8,128)S(1)}, f32[32,16,128]{2,1,0:T(8,128)}, u32[]{:S(2)}) copy-start(f32[32,16,128]{2,1,0:T(8,128)} %get-tuple-element.45) | copy-start | bytes 786436
  20.4 9.5 %copy-start = (f32[8,128,128]{2,1,0:T(8,128)S(1)}, f32[8,128,128]{2,1,0:T(8,128)}, u32[]{:S(2)}) copy-start(f32[8,128,128]{2,1,0:T(8,128)} %refs_3_.7) | copy-start | bytes 1572868
  20.4 9.5 %copy-start.2 = (f32[8,128,128]{2,1,0:T(8,128)S(1)}, f32[8,128,128]{2,1,0:T(8,128)}, u32[]{:S(2)}) copy-start(f32[8,128,128]{2,1,0:T(8,128)} %refs_5_.1) | copy-start | bytes 1572868
  20.4 18.1 %all-to-all-start.1 = ((f32[8,256,128]{2,1,0:T(8,128)}), f32[8,256,128]{2,1,0:T(8,128)S(1)}, u32[]{:S(2)}, u32[]{:S(2)}) async-start(f32[8,256,128]{2,1,0:T(8,128)} %bitcast.14), calls=%async_computation.1 | async-start | bytes 2097152 | tf_op jit(solution)/shard_map/all_to_all | solution.py:768
  24.1 3.9 %collective-permute-start.2 = (s32[16,1,384]{2,1,0:T(1,128)S(1)}, s32[16,1,384]{2,1,0:T(1,128)S(1)}, u32[]{:S(2)}, u32[]{:S(2)}) collective-permute-start(s32[16,1,384]{2,1,0:T(1,128)S(1)} %all-to-all-done.refs_3_.list_in.refs_0_), channel_id=1, source_target_pairs={{0,16},{16,0},{1,17},{17,1},{2,18},{18,2},{3,19},{19,3},{4,20},{20... | collective-permute-start | bytes 73736 | tf_op jit(solution)/shard_map/ppermute | solution.py:763
  28.0 10.5 %collective-permute-start.3 = (f32[32,16,128]{2,1,0:T(8,128)S(1)}, f32[32,16,128]{2,1,0:T(8,128)S(1)}, u32[]{:S(2)}, u32[]{:S(2)}) collective-permute-start(f32[32,16,128]{2,1,0:T(8,128)S(1)} %copy-done.3), channel_id=1, source_target_pairs={{0,16},{16,0},{1,17},{17,1},{2,18},{18,2},{3,19},{19,3},{4,20},{20... | collective-permute-start | bytes 786440 | tf_op jit(solution)/shard_map/ppermute | solution.py:648
  40.2 14.5 %collective-permute-start.4 = (f32[32,16,128]{2,1,0:T(8,128)S(1)}, f32[32,16,128]{2,1,0:T(8,128)S(1)}, u32[]{:S(2)}, u32[]{:S(2)}) collective-permute-start(f32[32,16,128]{2,1,0:T(8,128)S(1)} %shard_map.104.refs_2_), channel_id=1, source_target_pairs={{0,8},{1,9},{2,10},{3,11},{4,12},{5,13},{6,14},{7,15},{8,0},{9,1},... | collective-permute-start | bytes 786440 | tf_op jit(solution)/shard_map/ppermute | solution.py:849
  47.2 13.9 %all-to-all-start.3 = ((f32[8,144,128]{2,1,0:T(8,128)}), f32[8,144,128]{2,1,0:T(8,128)S(1)}, u32[]{:S(2)}, u32[]{:S(2)}) async-start(f32[8,144,128]{2,1,0:T(8,128)} %get-tuple-element.52), calls=%async_computation.3 | async-start | bytes 1179648 | tf_op jit(solution)/shard_map/all_to_all | solution.py:768
  50.9 8.6 %collective-permute-start.5 = (f32[32,16,128]{2,1,0:T(8,128)}, f32[32,16,128]{2,1,0:T(8,128)S(1)}, u32[]{:S(2)}, u32[]{:S(2)}) collective-permute-start(f32[32,16,128]{2,1,0:T(8,128)} %get-tuple-element.50), channel_id=1, source_target_pairs={{0,16},{16,0},{1,17},{17,1},{2,18},{18,2},{3,19},{19,3},{4,20},{20... | collective-permute-start | bytes 786440 | tf_op jit(solution)/shard_map/ppermute | solution.py:648
  61.1 12.3 %all-to-all-start.2 = ((f32[8,128,128]{2,1,0:T(8,128)}), f32[8,128,128]{2,1,0:T(8,128)S(1)}, u32[]{:S(2)}, u32[]{:S(2)}) async-start(f32[8,128,128]{2,1,0:T(8,128)} %shard_map.105), calls=%async_computation.2 | async-start | bytes 1048576 | tf_op jit(solution)/shard_map/all_to_all | solution.py:888
  64.6 3.7 %collective-permute-start.6 = (f32[8,128]{1,0:T(8,128)S(1)}, f32[8,128]{1,0:T(8,128)S(1)}, u32[]{:S(2)}, u32[]{:S(2)}) collective-permute-start(f32[8,128]{1,0:T(8,128)S(1)} %get-tuple-element.55), channel_id=1, source_target_pairs={{0,16},{16,0},{1,17},{17,1},{2,18},{18,2},{3,19},{19,3},{4,20},{20... | collective-permute-start | bytes 12296 | tf_op jit(solution)/shard_map/ppermute | solution.py:893
  68.3 4.6 %collective-permute-start.7 = (f32[4,128]{1,0:T(4,128)S(1)}, f32[4,128]{1,0:T(4,128)S(1)}, u32[]{:S(2)}, u32[]{:S(2)}) collective-permute-start(f32[4,128]{1,0:T(4,128)S(1)} %get-tuple-element.57), channel_id=1, source_target_pairs={{0,8},{1,9},{2,10},{3,11},{4,12},{5,13},{6,14},{7,15},{8,0},{9,1},... | collective-permute-start | bytes 6152 | tf_op jit(solution)/shard_map/ppermute | solution.py:894

commit v14 on v13

--- a/solution.py
+++ b/solution.py
@@ -237,18 +237,22 @@
     values = mirror_ref[...].reshape(rows * n_rhs, -1)
     table_products(values, tile_ref, product_ref.at[1])
     finish(metadata)
-    finish(loads)
     copies = []
+    for side in (1, 0):
+        if side == 0:
+            finish(loads)
+        for device in range(half):
+            for rank in range(cap):
+                code = list_ref[device, 0, side * (LANES // 2) + rank]
+                block = product_ref[side, below(code, rows * n_tiles)]
+                send_ref[device, side * cap + rank] = block
+            place = (device, pl.ds(side * cap, cap))
+            copies += started(
+                [pltpu.make_async_copy(send_ref.at[place], send_out.at[place], send_sems.at[len(copies)])]
+            )
     pack_bands(sizes, width_k, product_ref.at[0], near_ref, band_refs)
-    for n, (ref, out) in enumerate(zip(band_refs, band_out)):
-        copies += started([pltpu.make_async_copy(ref, out, send_sems.at[half + n])])
-    for device in range(half):
-        for slot in range(2 * cap):
-            side, rank = slot // cap, slot % cap
-            code = list_ref[device, 0, side * (LANES // 2) + rank]
-            send_ref[device, slot] = product_ref[side, below(code, rows * n_tiles)]
-        copy = pltpu.make_async_copy(send_ref.at[device], send_out.at[device], send_sems.at[device])
-        copies += started([copy])
+    for ref, out in zip(band_refs, band_out):
+        copies += started([pltpu.make_async_copy(ref, out, send_sems.at[len(copies)])])
     finish(copies)
 
 
@@ -531,22 +535,29 @@
     finish(copies)
 
 
-def mirror_kernel(sizes, list_in, mirror_ref, tile_ref, send_out, list_ref, product_ref, send_ref, sems):
+def mirror_kernel(
+    sizes, list_in, mirror_ref, tile_ref, inverse_ref, send_out, list_ref, product_ref, block_ref, solved_ref, send_ref, sems
+):
     rows, n_rows, cap, n_tiles, n_rhs = sizes
-    half = n_rows // 2
+    half, n_diag = n_rows // 2, inverse_ref.shape[0]
     base = jnp.where(lax.axis_index("rows") >= half, half, 0)
     list_in = list_in.at[pl.ds(base, half), :, pl.ds(0, LANES)]
     metadata = started([pltpu.make_async_copy(list_in, list_ref, sems.at[half])])
     table_products(mirror_ref[...].reshape(rows * n_rhs, -1), tile_ref, product_ref)
     finish(metadata)
+    codes = [list_ref[n // cap, 0, LANES // 2 + n % cap] for n in range(half * cap)]
+    for n, code in enumerate(codes):
+        block_ref[n] = product_ref[below(code, rows * n_tiles)]
+    values = block_ref[...].reshape(half * cap * n_rhs, -1)
+    table_products(values, inverse_ref, solved_ref)
     copies = []
-    for device in range(half):
-        for rank in range(cap):
-            code = list_ref[device, 0, LANES // 2 + rank]
-            block = product_ref[below(code, rows * n_tiles)]
-            send_ref[device, rank * n_rhs : (rank + 1) * n_rhs, :] = block
-        copy = pltpu.make_async_copy(send_ref.at[device], send_out.at[device], sems.at[device])
-        copies += started([copy])
+    for n, code in enumerate(codes):
+        device, rank = n // cap, n % cap
+        kind = below(over(code, rows * n_tiles * rows), n_diag)
+        send_ref[device, rank * n_rhs : (rank + 1) * n_rhs, :] = solved_ref[kind * len(codes) + n]
+        if rank == cap - 1:
+            copy = pltpu.make_async_copy(send_ref.at[device], send_out.at[device], sems.at[device])
+            copies += started([copy])
     finish(copies)
 
 
@@ -615,26 +626,20 @@
 
 
 def final_kernel(sizes, width_k, *refs):
+    place_in, mirror_ref, base_ref, near_ref, far_ref, scale_ref, out_ref, place_ref, sem = refs
     rows, n_rows, cap, n_tiles, n_rhs = sizes
-    metadata_in, mirror_ref, inverse_ref, base_ref, near_ref, far_ref, scale_ref = refs[:2], *refs[2:8]
-    out_ref, metadata, sum_ref, product_ref, meta_sems = refs[8], refs[9:11], *refs[11:]
-    place_ref, index_ref = metadata
-    metadata = copies_of(zip(metadata_in, metadata), meta_sems)
+    metadata = pltpu.make_async_copy(place_in, place_ref, sem)
+    metadata.start()
     depth = scale_ref.shape[0]
     correction = (near_ref[...] + far_ref[...]) / scale_ref[...]
     padded = jnp.concatenate([correction, jnp.zeros((8 - depth, LANES), jnp.float32)], axis=0)
     turned = padded.T
-    finish(metadata)
+    metadata.wait()
     fetch = half_blocks_of(sizes, width_k, place_ref, mirror_ref, True)
-
-    def diags(row):
-        return index_ref[0, 0, rows + row]
-
-    gather_solve(sizes, fetch, diags, [], [], inverse_ref, sum_ref, product_ref)
     for row in range(rows):
         spot, place = row // depth, row % depth
         column = turned[spot * n_rhs : (spot + 1) * n_rhs, place : place + 1]
-        out_ref[row] = (base_ref[row] + column) + sum_ref[pl.ds(row * n_rhs, n_rhs), :]
+        out_ref[row] = (base_ref[row] + column) + fetch(row)
 
 
 def shifted(value, axis, steps):
@@ -753,7 +758,7 @@
             *band_scratch,
             pltpu.SemaphoreType.DMA((n_tiles,)),
             pltpu.SemaphoreType.DMA((2,)),
-            pltpu.SemaphoreType.DMA((half + n_ways,)),
+            pltpu.SemaphoreType.DMA((2 * half + n_ways,)),
         ],
         work * n_tiles,
         4 << 20,
@@ -873,17 +878,19 @@
         packed = call(
             functools.partial(mirror_kernel, sizes),
             jax.ShapeDtypeStruct((half, body, states), f32),
-            [ANY] + [VMEM] * 2,
+            [ANY] + [VMEM] * 3,
             HBM,
             [
                 list_scratch,
                 products,
+                pltpu.VMEM((half * cap, n_rhs, states), f32),
+                pltpu.VMEM((n_diag * half * cap, n_rhs, states), f32),
                 pltpu.VMEM((half, body, states), f32),
                 pltpu.SemaphoreType.DMA((half + 1,)),
             ],
             BEHIND_SWAP * work * n_tiles,
             4 << 20,
-        )(lists, mirror, coupling_tiles)
+        )(lists, mirror, coupling_tiles, inverse_table)
         packed, band = lax.optimization_barrier((packed, band))
         swapped = lax.all_to_all(
             packed, "rows", split_axis=0, concat_axis=0, tiled=True, axis_index_groups=halves_of_rows
@@ -911,12 +918,12 @@
         return call(
             functools.partial(final_kernel, sizes, width_k),
             jax.ShapeDtypeStruct(block, f32),
-            [ANY] * 2 + [VMEM] * 6,
+            [ANY] + [VMEM] * 5,
             VMEM,
-            [*row_scratch, sums, products, pltpu.SemaphoreType.DMA((2,))],
-            work * n_diag,
+            [row_scratch[0], pltpu.SemaphoreType.DMA],
+            0,
             4 << 20,
-        )(places, index, swapped, inverse_table, base, keep[:depth], far, scale)
+        )(places, swapped, base, keep[:depth], far, scale)
 
     sends = call(
         functools.partial(pack_kernel, sizes, width_k, n_ways),

time: 76.2 us -> 75.5 us (level)
  waiting for transfers between devices: 16.8 us -> 15.6 us
    ppermute x2, waiting for transfers between devices: 2.88 us -> 1.65 us  [to_bands(): return (lax.ppermute(sends[0], 'band', [(0, 1), (1, 0)]),)]
  transfers between devices with their start and end apart: 12 -> 12, of which waited for: 9 -> 9; matrix products, arithmetic and copies ran while one was open for 0% -> 0% of each run, Pallas kernels for 27% -> 29%
where the time goes in v14:
time: 75.5 us; the launch traced here: 74.9 us
  starting transfers between devices  31.3 us (41%)
  Pallas kernels  27.4 us (36%)
  waiting for transfers between devices  15.6 us (21%)
    pallas_call x10, Pallas kernels, apply(): return run(*pinned)  27.4 us
    all_to_all x2, starting transfers between devices, exchange(): lax.all_to_all(sends[0], 'rows', split_axis=0, concat_axis=0, tiled=True,...  7.43 us
    ppermute x1, starting transfers between devices, on_device(): mirror = lax.ppermute(start_iterate, 'rows', to_mirror)  4.04 us
    all_to_all x1, starting transfers between devices, on_device(): lax.all_to_all(lists, 'rows', split_axis=0, concat_axis=0, tiled=True)  3.9 us
    all_to_all x1, starting transfers between devices, on_device(): lax.all_to_all(packed, 'rows', split_axis=0, concat_axis=0, tiled=True, a...  3.49 us
    all_to_all x2, waiting for transfers between devices, exchange(): lax.all_to_all(sends[0], 'rows', split_axis=0, concat_axis=0, tiled=True,...  3.41 us
    ppermute x2, starting transfers between devices, to_bands(): return (lax.ppermute(sends[0], 'band', [(0, 1), (1, 0)]),)  3.1 us
    ppermute x1, starting transfers between devices, on_device(): mirror = lax.ppermute(first, 'rows', to_mirror)  2.73 us
  transfers between devices with their start and end apart: 12, of which 9 were waited for; matrix products, arithmetic and copies ran while one was open for 0% of the time, Pallas kernels for 29%

profile of v14, /device:TPU:0, one launch (start us, length us, event | category | flops | bytes accessed | tf_op | source)
XLA Modules:
  0.0 74.9 jit_solution(12578552393085024219)
XLA Ops:
  0.0 4.0 %collective-permute-start = (f32[32,16,128]{2,1,0:T(8,128)}, f32[32,16,128]{2,1,0:T(8,128)S(1)}, u32[]{:S(2)}, u32[]{:S(2)}) collective-permute-start(f32[32,16,128]{2,1,0:T(8,128)} %start_in.1), channel_id=1, source_target_pairs={{0,8},{1,9},{2,10},{3,11},{4,12},{5,13},{6,14},{7,15},{8,0},{9,1},... | collective-permute-start | bytes 786440 | tf_op jit(solution)/shard_map/ppermute | solution.py:698
  4.0 1.8 %shard_map.100 = (s32[16,1,384]{2,1,0:T(1,128)}, s32[1,1,256]{2,1,0:T(1,128)S(1)}, s32[1,1,128]{2,1,0:T(1,128)S(1)}) custom-call(s32[2,32]{1,0:T(2,128)} %bitcast.18, s32[2,32]{1,0:T(2,128)} %bitcast.19, s32[4,32]{1,0:T(4,128)} %bitcast.17, s32[1,32]{1,0:T(1,128)} %bitcast.20, s32[1,32]{1,0:T(1,128)} %bitcast.21), custom_call_target="tpu_custom_call" | custom-call | tf_op jit(solution)/shard_map/pallas_call | solution.py:49
  5.8 3.9 %all-to-all-start = ((s32[16,1,384]{2,1,0:T(1,128)}), s32[16,1,384]{2,1,0:T(1,128)S(1)}, u32[]{:S(2)}, u32[]{:S(2)}) async-start(s32[16,1,384]{2,1,0:T(1,128)} %get-tuple-element.32), calls=%async_computation | async-start | bytes 49152 | tf_op jit(solution)/shard_map/all_to_all | solution.py:710
  9.7 1.6 %collective-permute-start.1 = (s32[1,1,256]{2,1,0:T(1,128)S(1)}, s32[1,1,256]{2,1,0:T(1,128)S(1)}, u32[]{:S(2)}, u32[]{:S(2)}) collective-permute-start(s32[1,1,256]{2,1,0:T(1,128)S(1)} %get-tuple-element.33.refs_0_.refs_1_), channel_id=1, source_target_pairs={{0,16},{16,0},{1,17},{17,1},{2,18},{18,2},{3,19},{19,3},{4,20},{20... | collective-permute-start | bytes 3080 | tf_op jit(solution)/shard_map/ppermute | solution.py:712
  11.3 3.9 %shard_map.101.refs_0_ = f32[256,16,128]{2,1,0:T(8,128)} custom-call(f32[32,16,128]{2,1,0:T(8,128)} %start_in.1, f32[8,128,128]{2,1,0:T(8,128)} %refs_3_.4), custom_call_target="tpu_custom_call" | custom-call | flops 402653184 | bytes 4194304 | tf_op jit(solution)/shard_map/pallas_call | solution.py:49
  15.2 2.4 %all-to-all-done.refs_3_.list_in.refs_0_ = s32[16,1,384]{2,1,0:T(1,128)S(1)} async-done(((s32[16,1,384]{2,1,0:T(1,128)}), s32[16,1,384]{2,1,0:T(1,128)S(1)}, u32[]{:S(2)}, u32[]{:S(2)}) %all-to-all-start) | async-done | bytes 24608 | tf_op jit(solution)/shard_map/all_to_all | solution.py:710
  17.6 2.6 %shard_map.102 = (f32[8,16,16,128]{3,2,1,0:T(8,128)}, f32[32,16,128]{2,1,0:T(8,128)}) custom-call(f32[256,16,128]{2,1,0:T(8,128)} %shard_map.101.refs_0_, f32[32,16,128]{2,1,0:T(8,128)S(1)} %collective-permute-done.refs_1_, f32[8,128,128]{2,1,0:T(8,128)S(1)} %copy-done.1, s32[16,1,384]{2,1,0:T(1,128)S(1)} %all-to-all-done.refs_3_.list_in.refs_0_, ...), custom_call_target="tpu_custom_call" | custom-call | flops 402653184 | bytes 4194304 | tf_op jit(solution)/shard_map/pallas_call | solution.py:49
  20.3 3.7 %all-to-all-start.1 = ((f32[8,256,128]{2,1,0:T(8,128)}), f32[8,256,128]{2,1,0:T(8,128)S(1)}, u32[]{:S(2)}, u32[]{:S(2)}) async-start(f32[8,256,128]{2,1,0:T(8,128)} %bitcast.14), calls=%async_computation.1 | async-start | bytes 2097152 | tf_op jit(solution)/shard_map/all_to_all | solution.py:773
  24.0 1.6 %collective-permute-start.2 = (s32[16,1,384]{2,1,0:T(1,128)S(1)}, s32[16,1,384]{2,1,0:T(1,128)S(1)}, u32[]{:S(2)}, u32[]{:S(2)}) collective-permute-start(s32[16,1,384]{2,1,0:T(1,128)S(1)} %all-to-all-done.refs_3_.list_in.refs_0_), channel_id=1, source_target_pairs={{0,16},{16,0},{1,17},{17,1},{2,18},{18,2},{3,19},{19,3},{4,20},{20... | collective-permute-start | bytes 73736 | tf_op jit(solution)/shard_map/ppermute | solution.py:768
  25.6 2.3 %collective-permute-done.2 = s32[16,1,384]{2,1,0:T(1,128)S(1)} collective-permute-done((s32[16,1,384]{2,1,0:T(1,128)S(1)}, s32[16,1,384]{2,1,0:T(1,128)S(1)}, u32[]{:S(2)}, u32[]{:S(2)}) %collective-permute-start.2) | collective-permute-done | bytes 24608 | tf_op jit(solution)/shard_map/ppermute | solution.py:768
  29.7 6.7 %shard_map.103 = (bf16[256,1440]{1,0:T(8,128)(2,1)}, bf16[128,384]{1,0:T(8,128)(2,1)}, bf16[1024,256]{1,0:T(8,128)(2,1)}, f32[256,128]{1,0:T(8,128)}, f32[4,128]{1,0:T(4,128)S(1)}) custom-call(s32[1,1,256]{2,1,0:T(1,128)S(1)} %get-tuple-element.33.refs_0_.refs_1_, f32[32,16,128]{2,1,0:T(8,128)} %refs_4_.5, s32[8,2,512]{2,1,0:T(2,128)S(1)} %reshape.7.refs_2_, ...), custom_call_target="tpu_custom_call" | custom-call | flops 1342177280 | bytes 4194304 | tf_op jit(solution)/shard_map/pallas_call | solution.py:49
  36.4 1.9 %all-to-all-done.1.refs_2_ = f32[8,256,128]{2,1,0:T(8,128)S(1)} async-done(((f32[8,256,128]{2,1,0:T(8,128)}), f32[8,256,128]{2,1,0:T(8,128)S(1)}, u32[]{:S(2)}, u32[]{:S(2)}) %all-to-all-start.1) | async-done | bytes 1048608 | tf_op jit(solution)/shard_map/all_to_all | solution.py:773
  38.4 1.8 %shard_map.104.refs_2_ = f32[32,16,128]{2,1,0:T(8,128)S(1)} custom-call(s32[1,1,128]{2,1,0:T(1,128)S(1)} %get-tuple-element.31.refs_0_, s32[1,1,256]{2,1,0:T(1,128)S(1)} %get-tuple-element.33.refs_0_.refs_1_, f32[8,256,128]{2,1,0:T(8,128)S(1)} %all-to-all-done.1.refs_2_, f32[8,128,128]{2,1,0:T(8,128)S(1)} %copy-done, f32[32,16,128]{2,1,0:T(8,128)} %refs_4_.5, ...), custom_call_target="tpu_custom_call" | custom-call | flops 402653184 | bytes 4194304 | tf_op jit(solution)/shard_map/pallas_call | solution.py:49
  40.1 2.7 %collective-permute-start.4 = (f32[32,16,128]{2,1,0:T(8,128)S(1)}, f32[32,16,128]{2,1,0:T(8,128)S(1)}, u32[]{:S(2)}, u32[]{:S(2)}) collective-permute-start(f32[32,16,128]{2,1,0:T(8,128)S(1)} %shard_map.104.refs_2_), channel_id=1, source_target_pairs={{0,8},{1,9},{2,10},{3,11},{4,12},{5,13},{6,14},{7,15},{8,0},{9,1},... | collective-permute-start | bytes 786440 | tf_op jit(solution)/shard_map/ppermute | solution.py:854
  42.9 4.2 %shard_map.106 = (f32[8,144,128]{2,1,0:T(8,128)}, f32[32,16,128]{2,1,0:T(8,128)}) custom-call(s32[16,1,384]{2,1,0:T(1,128)S(1)} %all-to-all-done.refs_3_.list_in.refs_0_, s32[1,1,256]{2,1,0:T(1,128)S(1)} %collective-permute-done.1.refs_4_.refs_1_, f32[32,16,128]{2,1,0:T(8,128)S(1)} %shard_map.104.refs_2_, f32[8,128,128]{2,1,0:T(8,128)S(1)} %copy-done.1, ...), custom_call_target="tpu_custom_call" | custom-call | flops 805306368 | bytes 4194304 | tf_op jit(solution)/shard_map/pallas_call | solution.py:49
  47.1 3.7 %all-to-all-start.3 = ((f32[8,144,128]{2,1,0:T(8,128)}), f32[8,144,128]{2,1,0:T(8,128)S(1)}, u32[]{:S(2)}, u32[]{:S(2)}) async-start(f32[8,144,128]{2,1,0:T(8,128)} %get-tuple-element.52), calls=%async_computation.3 | async-start | bytes 1179648 | tf_op jit(solution)/shard_map/all_to_all | solution.py:773
  50.8 1.6 %collective-permute-start.5 = (f32[32,16,128]{2,1,0:T(8,128)}, f32[32,16,128]{2,1,0:T(8,128)S(1)}, u32[]{:S(2)}, u32[]{:S(2)}) collective-permute-start(f32[32,16,128]{2,1,0:T(8,128)} %get-tuple-element.50), channel_id=1, source_target_pairs={{0,16},{16,0},{1,17},{17,1},{2,18},{18,2},{3,19},{19,3},{4,20},{20... | collective-permute-start | bytes 786440 | tf_op jit(solution)/shard_map/ppermute | solution.py:653
  52.4 2.3 %collective-permute-done.4.mirror_ref = f32[32,16,128]{2,1,0:T(8,128)S(1)} collective-permute-done((f32[32,16,128]{2,1,0:T(8,128)S(1)}, f32[32,16,128]{2,1,0:T(8,128)S(1)}, u32[]{:S(2)}, u32[]{:S(2)}) %collective-permute-start.4) | collective-permute-done | bytes 262176 | tf_op jit(solution)/shard_map/ppermute | solution.py:854
  54.7 3.2 %shard_map.105 = f32[8,128,128]{2,1,0:T(8,128)} custom-call(s32[16,1,384]{2,1,0:T(1,128)S(1)} %all-to-all-done.refs_3_.list_in.refs_0_, f32[32,16,128]{2,1,0:T(8,128)S(1)} %collective-permute-done.4.mirror_ref, f32[8,128,128]{2,1,0:T(8,128)S(1)} %copy-done.1, f32[8,128,128]{2,1,0:T(8,128)S(1)} %copy-done), custom_call_target="tpu_custom_call" | custom-call | flops 40265318400 | bytes 4194304 | tf_op jit(solution)/shard_map/pallas_call | solution.py:49
  57.8 1.6 %collective-permute-done.5.refs_5_ = f32[32,16,128]{2,1,0:T(8,128)S(1)} collective-permute-done((f32[32,16,128]{2,1,0:T(8,128)}, f32[32,16,128]{2,1,0:T(8,128)S(1)}, u32[]{:S(2)}, u32[]{:S(2)}) %collective-permute-start.5) | collective-permute-done | bytes 262176 | tf_op jit(solution)/shard_map/ppermute | solution.py:653
  61.0 3.5 %all-to-all-start.2 = ((f32[8,128,128]{2,1,0:T(8,128)}), f32[8,128,128]{2,1,0:T(8,128)S(1)}, u32[]{:S(2)}, u32[]{:S(2)}) async-start(f32[8,128,128]{2,1,0:T(8,128)} %shard_map.105), calls=%async_computation.2 | async-start | bytes 1048576 | tf_op jit(solution)/shard_map/all_to_all | solution.py:895
  66.1 2.1 %collective-permute-done.6 = f32[8,128]{1,0:T(8,128)S(1)} collective-permute-done((f32[8,128]{1,0:T(8,128)S(1)}, f32[8,128]{1,0:T(8,128)S(1)}, u32[]{:S(2)}, u32[]{:S(2)}) %collective-permute-start.6) | collective-permute-done | bytes 4128 | tf_op jit(solution)/shard_map/ppermute | solution.py:900
  68.2 1.8 %collective-permute-start.7 = (f32[4,128]{1,0:T(4,128)S(1)}, f32[4,128]{1,0:T(4,128)S(1)}, u32[]{:S(2)}, u32[]{:S(2)}) collective-permute-start(f32[4,128]{1,0:T(4,128)S(1)} %get-tuple-element.57), channel_id=1, source_target_pairs={{0,8},{1,9},{2,10},{3,11},{4,12},{5,13},{6,14},{7,15},{8,0},{9,1},... | collective-permute-start | bytes 6152 | tf_op jit(solution)/shard_map/ppermute | solution.py:901
  70.0 1.8 %shard_map.107.refs_2_ = f32[32,16,128]{2,1,0:T(8,128)S(1)} custom-call(s32[1,1,128]{2,1,0:T(1,128)S(1)} %get-tuple-element.31.refs_0_, s32[1,1,256]{2,1,0:T(1,128)S(1)} %get-tuple-element.33.refs_0_.refs_1_, f32[8,144,128]{2,1,0:T(8,128)S(1)} %all-to-all-done.3.refs_2_.arrived_ref, f32[8,128,128]{2,1,0:T(8,128)S(1)} %copy-done, f32[32,16,128]{2,1,0:T(8,128)} %refs_4_.5, ...), custom_call_target="tpu_custom_call" | custom-call | flops 402653184 | bytes 4194304 | tf_op jit(solution)/shard_map/pallas_call | solution.py:49
  (25 shorter events, 7.9 us)
Async XLA Ops:
  0.0 17.6 %copy-start.1 = (f32[8,128,128]{2,1,0:T(8,128)S(1)}, f32[8,128,128]{2,1,0:T(8,128)}, u32[]{:S(2)}) copy-start(f32[8,128,128]{2,1,0:T(8,128)} %refs_3_.4) | copy-start | bytes 1572868
  0.0 17.6 %collective-permute-start = (f32[32,16,128]{2,1,0:T(8,128)}, f32[32,16,128]{2,1,0:T(8,128)S(1)}, u32[]{:S(2)}, u32[]{:S(2)}) collective-permute-start(f32[32,16,128]{2,1,0:T(8,128)} %start_in.1), channel_id=1, source_target_pairs={{0,8},{1,9},{2,10},{3,11},{4,12},{5,13},{6,14},{7,15},{8,0},{9,1},... | collective-permute-start | bytes 786440 | tf_op jit(solution)/shard_map/ppermute | solution.py:698
  5.8 11.8 %all-to-all-start = ((s32[16,1,384]{2,1,0:T(1,128)}), s32[16,1,384]{2,1,0:T(1,128)S(1)}, u32[]{:S(2)}, u32[]{:S(2)}) async-start(s32[16,1,384]{2,1,0:T(1,128)} %get-tuple-element.32), calls=%async_computation | async-start | bytes 49152 | tf_op jit(solution)/shard_map/all_to_all | solution.py:710
  9.7 5.5 %collective-permute-start.1 = (s32[1,1,256]{2,1,0:T(1,128)S(1)}, s32[1,1,256]{2,1,0:T(1,128)S(1)}, u32[]{:S(2)}, u32[]{:S(2)}) collective-permute-start(s32[1,1,256]{2,1,0:T(1,128)S(1)} %get-tuple-element.33.refs_0_.refs_1_), channel_id=1, source_target_pairs={{0,16},{16,0},{1,17},{17,1},{2,18},{18,2},{3,19},{19,3},{4,20},{20... | collective-permute-start | bytes 3080 | tf_op jit(solution)/shard_map/ppermute | solution.py:712
  20.2 7.6 %copy-start.3 = (f32[32,16,128]{2,1,0:T(8,128)S(1)}, f32[32,16,128]{2,1,0:T(8,128)}, u32[]{:S(2)}) copy-start(f32[32,16,128]{2,1,0:T(8,128)} %get-tuple-element.45) | copy-start | bytes 786436
  20.2 9.5 %copy-start = (f32[8,128,128]{2,1,0:T(8,128)S(1)}, f32[8,128,128]{2,1,0:T(8,128)}, u32[]{:S(2)}) copy-start(f32[8,128,128]{2,1,0:T(8,128)} %refs_3_.5) | copy-start | bytes 1572868
  20.3 9.5 %copy-start.2 = (f32[8,128,128]{2,1,0:T(8,128)S(1)}, f32[8,128,128]{2,1,0:T(8,128)}, u32[]{:S(2)}) copy-start(f32[8,128,128]{2,1,0:T(8,128)} %refs_5_.1) | copy-start | bytes 1572868
  20.3 18.1 %all-to-all-start.1 = ((f32[8,256,128]{2,1,0:T(8,128)}), f32[8,256,128]{2,1,0:T(8,128)S(1)}, u32[]{:S(2)}, u32[]{:S(2)}) async-start(f32[8,256,128]{2,1,0:T(8,128)} %bitcast.14), calls=%async_computation.1 | async-start | bytes 2097152 | tf_op jit(solution)/shard_map/all_to_all | solution.py:773
  24.0 3.9 %collective-permute-start.2 = (s32[16,1,384]{2,1,0:T(1,128)S(1)}, s32[16,1,384]{2,1,0:T(1,128)S(1)}, u32[]{:S(2)}, u32[]{:S(2)}) collective-permute-start(s32[16,1,384]{2,1,0:T(1,128)S(1)} %all-to-all-done.refs_3_.list_in.refs_0_), channel_id=1, source_target_pairs={{0,16},{16,0},{1,17},{17,1},{2,18},{18,2},{3,19},{19,3},{4,20},{20... | collective-permute-start | bytes 73736 | tf_op jit(solution)/shard_map/ppermute | solution.py:768
  27.9 10.5 %collective-permute-start.3 = (f32[32,16,128]{2,1,0:T(8,128)S(1)}, f32[32,16,128]{2,1,0:T(8,128)S(1)}, u32[]{:S(2)}, u32[]{:S(2)}) collective-permute-start(f32[32,16,128]{2,1,0:T(8,128)S(1)} %copy-done.3), channel_id=1, source_target_pairs={{0,16},{16,0},{1,17},{17,1},{2,18},{18,2},{3,19},{19,3},{4,20},{20... | collective-permute-start | bytes 786440 | tf_op jit(solution)/shard_map/ppermute | solution.py:653
  40.1 14.5 %collective-permute-start.4 = (f32[32,16,128]{2,1,0:T(8,128)S(1)}, f32[32,16,128]{2,1,0:T(8,128)S(1)}, u32[]{:S(2)}, u32[]{:S(2)}) collective-permute-start(f32[32,16,128]{2,1,0:T(8,128)S(1)} %shard_map.104.refs_2_), channel_id=1, source_target_pairs={{0,8},{1,9},{2,10},{3,11},{4,12},{5,13},{6,14},{7,15},{8,0},{9,1},... | collective-permute-start | bytes 786440 | tf_op jit(solution)/shard_map/ppermute | solution.py:854
  47.1 13.9 %all-to-all-start.3 = ((f32[8,144,128]{2,1,0:T(8,128)}), f32[8,144,128]{2,1,0:T(8,128)S(1)}, u32[]{:S(2)}, u32[]{:S(2)}) async-start(f32[8,144,128]{2,1,0:T(8,128)} %get-tuple-element.52), calls=%async_computation.3 | async-start | bytes 1179648 | tf_op jit(solution)/shard_map/all_to_all | solution.py:773
  50.8 8.6 %collective-permute-start.5 = (f32[32,16,128]{2,1,0:T(8,128)}, f32[32,16,128]{2,1,0:T(8,128)S(1)}, u32[]{:S(2)}, u32[]{:S(2)}) collective-permute-start(f32[32,16,128]{2,1,0:T(8,128)} %get-tuple-element.50), channel_id=1, source_target_pairs={{0,16},{16,0},{1,17},{17,1},{2,18},{18,2},{3,19},{19,3},{4,20},{20... | collective-permute-start | bytes 786440 | tf_op jit(solution)/shard_map/ppermute | solution.py:653
  61.0 12.3 %all-to-all-start.2 = ((f32[8,128,128]{2,1,0:T(8,128)}), f32[8,128,128]{2,1,0:T(8,128)S(1)}, u32[]{:S(2)}, u32[]{:S(2)}) async-start(f32[8,128,128]{2,1,0:T(8,128)} %shard_map.105), calls=%async_computation.2 | async-start | bytes 1048576 | tf_op jit(solution)/shard_map/all_to_all | solution.py:895
  64.5 3.7 %collective-permute-start.6 = (f32[8,128]{1,0:T(8,128)S(1)}, f32[8,128]{1,0:T(8,128)S(1)}, u32[]{:S(2)}, u32[]{:S(2)}) collective-permute-start(f32[8,128]{1,0:T(8,128)S(1)} %get-tuple-element.55), channel_id=1, source_target_pairs={{0,16},{16,0},{1,17},{17,1},{2,18},{18,2},{3,19},{19,3},{4,20},{20... | collective-permute-start | bytes 12296 | tf_op jit(solution)/shard_map/ppermute | solution.py:900
  68.2 4.6 %collective-permute-start.7 = (f32[4,128]{1,0:T(4,128)S(1)}, f32[4,128]{1,0:T(4,128)S(1)}, u32[]{:S(2)}, u32[]{:S(2)}) collective-permute-start(f32[4,128]{1,0:T(4,128)S(1)} %get-tuple-element.57), channel_id=1, source_target_pairs={{0,8},{1,9},{2,10},{3,11},{4,12},{5,13},{6,14},{7,15},{8,0},{9,1},... | collective-permute-start | bytes 6152 | tf_op jit(solution)/shard_map/ppermute | solution.py:901

commit v15 on v14

--- a/solution.py
+++ b/solution.py
@@ -203,54 +203,41 @@
     return started(copies)
 
 
-def product_kernel(start_in, tile_in, product_out, start_ref, tile_ref, product_ref, sems, tile_sems):
-    start = pltpu.make_async_copy(start_in, start_ref, sems.at[0])
+def product_kernel(start_in, tile_in, product_ref, start_ref, tile_ref, start_sem, tile_sems):
+    start = pltpu.make_async_copy(start_in, start_ref, start_sem)
     start.start()
     loads = table_loads(tile_in, tile_ref, tile_sems)
     start.wait()
-    copies = []
-
-    def done(first, count):
-        place = pl.ds(first, count)
-        source, target = product_ref.at[place], product_out.at[place]
-        copies.extend(started([pltpu.make_async_copy(source, target, sems.at[1 + len(copies)])]))
-
     rows, n_rhs, states = start_ref.shape
     values = start_ref[...].reshape(rows * n_rhs, states)
-    table_products(values, tile_ref, product_ref, done, loads)
-    finish(copies)
+    table_products(values, tile_ref, product_ref, None, loads)
 
 
 def first_kernel(sizes, width_k, n_band, *refs):
     rows, n_rows, cap, n_tiles, n_rhs = sizes
-    product_in, mirror_ref, tile_ref, list_in, near_in, send_out = refs[:6]
+    own_ref, mirror_ref, tile_ref, list_in, near_in, send_out = refs[:6]
     band_out, refs = refs[6 : 6 + n_band], refs[6 + n_band :]
     product_ref, list_ref, near_ref, send_ref = refs[:4]
-    band_refs, (load_sems, meta_sems, send_sems) = refs[4 : 4 + n_band], refs[4 + n_band :]
+    band_refs, (meta_sems, send_sems) = refs[4 : 4 + n_band], refs[4 + n_band :]
     half = n_rows // 2
     base = jnp.where(lax.axis_index("rows") >= half, half, 0)
     list_in = list_in.at[pl.ds(base, half), :, pl.ds(0, LANES)]
     metadata = copies_of(((list_in, list_ref), (near_in, near_ref)), meta_sems)
-    places = [pl.ds(tile * rows, rows) for tile in range(n_tiles)]
-    loads = [(product_in.at[place], product_ref.at[0, place]) for place in places]
-    loads = copies_of(loads, load_sems)
     values = mirror_ref[...].reshape(rows * n_rhs, -1)
-    table_products(values, tile_ref, product_ref.at[1])
+    table_products(values, tile_ref, product_ref)
     finish(metadata)
     copies = []
-    for side in (1, 0):
-        if side == 0:
-            finish(loads)
+    for side, blocks_ref in ((0, own_ref), (1, product_ref)):
         for device in range(half):
             for rank in range(cap):
                 code = list_ref[device, 0, side * (LANES // 2) + rank]
-                block = product_ref[side, below(code, rows * n_tiles)]
+                block = blocks_ref[below(code, rows * n_tiles)]
                 send_ref[device, side * cap + rank] = block
             place = (device, pl.ds(side * cap, cap))
             copies += started(
                 [pltpu.make_async_copy(send_ref.at[place], send_out.at[place], send_sems.at[len(copies)])]
             )
-    pack_bands(sizes, width_k, product_ref.at[0], near_ref, band_refs)
+    pack_bands(sizes, width_k, own_ref, near_ref, band_refs)
     for ref, out in zip(band_refs, band_out):
         copies += started([pltpu.make_async_copy(ref, out, send_sems.at[len(copies)])])
     finish(copies)
@@ -444,20 +431,17 @@
 
 def solve_kernel(sizes, width_k, n_band, field, *refs):
     metadata_in, arrived_ref, inverse_ref = refs[:2], *refs[2:4]
-    terms_in, refs = refs[4 : 5 + n_band], refs[5 + n_band :]
-    out_ref, metadata, sum_ref, product_ref = refs[0], refs[1:3], *refs[3:5]
+    terms, refs = refs[4 : 5 + n_band], refs[5 + n_band :]
+    out_ref, metadata, sum_ref, product_ref, meta_sems = refs[0], refs[1:3], *refs[3:]
     place_ref, index_ref = metadata
-    terms, (term_sems, meta_sems) = refs[5 : 6 + n_band], refs[6 + n_band :]
     rows = sizes[0]
-    metadata = copies_of(zip(metadata_in, metadata), meta_sems)
-    later = copies_of(zip(terms_in, terms), term_sems)
-    finish(metadata)
+    finish(copies_of(zip(metadata_in, metadata), meta_sems))
     fetch = arrived_blocks_of(sizes, width_k, place_ref, field, arrived_ref)
 
     def diags(row):
         return index_ref[0, 0, rows + row]
 
-    gather_solve(sizes, fetch, diags, later, terms, inverse_ref, sum_ref, product_ref)
+    gather_solve(sizes, fetch, diags, [], terms, inverse_ref, sum_ref, product_ref)
     out_ref[...] = sum_ref[...].reshape(out_ref.shape)
 
 
@@ -734,12 +718,11 @@
         product_kernel,
         jax.ShapeDtypeStruct(made_shape, f32),
         [HBM, HBM],
-        HBM,
+        VMEM,
         [
             pltpu.VMEM(block, f32),
             *table_scratch,
-            pltpu.VMEM(made_shape, f32),
-            pltpu.SemaphoreType.DMA((1 + n_tiles,)),
+            pltpu.SemaphoreType.DMA,
             table_sems,
         ],
         work * n_tiles,
@@ -748,15 +731,14 @@
     packed, *bands = call(
         functools.partial(first_kernel, sizes, width_k, n_ways),
         (jax.ShapeDtypeStruct((half, 2 * cap, n_rhs, states), f32), *band_shapes),
-        [HBM, VMEM, VMEM, ANY, ANY],
+        [VMEM, VMEM, VMEM, ANY, ANY],
         [HBM] * (1 + n_ways),
         [
-            pltpu.VMEM((2, *made_shape), f32),
+            pltpu.VMEM(made_shape, f32),
             list_scratch,
             near_scratch,
             pltpu.VMEM((half, 2 * cap, n_rhs, states), f32),
             *band_scratch,
-            pltpu.SemaphoreType.DMA((n_tiles,)),
             pltpu.SemaphoreType.DMA((2,)),
             pltpu.SemaphoreType.DMA((2 * half + n_ways,)),
         ],
@@ -833,16 +815,9 @@
         return call(
             functools.partial(solve_kernel, sizes, width_k, n_ways, field),
             jax.ShapeDtypeStruct(block, f32),
-            [ANY] * 2 + [VMEM] * 2 + [HBM] + [ANY] * n_ways,
+            [ANY] * 2 + [VMEM] * (3 + n_ways),
             VMEM,
-            [
-                *row_scratch,
-                sums,
-                products,
-                *term_scratch,
-                term_sems,
-                pltpu.SemaphoreType.DMA((2,)),
-            ],
+            [*row_scratch, sums, products, pltpu.SemaphoreType.DMA((2,))],
             work * n_diag,
             4 << 20,
         )(places, index, arrived, inverse_table, right_side, *bands)

time: 75.5 us -> 74.6 us (0.988)
  Pallas kernels: 27.4 us -> 25.7 us
  waiting for transfers between devices: 15.6 us -> 16.5 us
    pallas_call x10, Pallas kernels: 27.4 us -> 25.7 us  [apply(): return run(*pinned)]
    all_to_all x1, waiting for transfers between devices: 2.37 us -> 3.23 us  [on_device(): lax.all_to_all(lists, 'rows', split_axis=0, concat_axis=0, tiled=True)]
  transfers between devices with their start and end apart: 12 -> 12, of which waited for: 9 -> 9; matrix products, arithmetic and copies ran while one was open for 0% -> 0% of each run, Pallas kernels for 29% -> 28%
where the time goes in v15:
time: 74.6 us; the launch traced here: 74.1 us
  starting transfers between devices  31.2 us (42%)
  Pallas kernels  25.7 us (34%)
  waiting for transfers between devices  16.5 us (22%)
    pallas_call x10, Pallas kernels, apply(): return run(*pinned)  25.7 us
    all_to_all x2, starting transfers between devices, exchange(): lax.all_to_all(sends[0], 'rows', split_axis=0, concat_axis=0, tiled=True,...  7.43 us
    ppermute x1, starting transfers between devices, on_device(): mirror = lax.ppermute(start_iterate, 'rows', to_mirror)  4.04 us
    all_to_all x1, starting transfers between devices, on_device(): lax.all_to_all(lists, 'rows', split_axis=0, concat_axis=0, tiled=True)  3.9 us
    all_to_all x1, starting transfers between devices, on_device(): lax.all_to_all(packed, 'rows', split_axis=0, concat_axis=0, tiled=True, a...  3.49 us
    all_to_all x2, waiting for transfers between devices, exchange(): lax.all_to_all(sends[0], 'rows', split_axis=0, concat_axis=0, tiled=True,...  3.4 us
    all_to_all x1, waiting for transfers between devices, on_device(): lax.all_to_all(lists, 'rows', split_axis=0, concat_axis=0, tiled=True)  3.23 us
    ppermute x2, starting transfers between devices, to_bands(): return (lax.ppermute(sends[0], 'band', [(0, 1), (1, 0)]),)  3.09 us
  transfers between devices with their start and end apart: 12, of which 9 were waited for; matrix products, arithmetic and copies ran while one was open for 0% of the time, Pallas kernels for 28%

profile of v15, /device:TPU:0, one launch (start us, length us, event | category | flops | bytes accessed | tf_op | source)
XLA Modules:
  0.0 74.1 jit_solution(9289270793231307260)
XLA Ops:
  0.0 4.0 %collective-permute-start = (f32[32,16,128]{2,1,0:T(8,128)}, f32[32,16,128]{2,1,0:T(8,128)S(1)}, u32[]{:S(2)}, u32[]{:S(2)}) collective-permute-start(f32[32,16,128]{2,1,0:T(8,128)} %start_in.1), channel_id=1, source_target_pairs={{0,8},{1,9},{2,10},{3,11},{4,12},{5,13},{6,14},{7,15},{8,0},{9,1},... | collective-permute-start | bytes 786440 | tf_op jit(solution)/shard_map/ppermute | solution.py:682
  4.0 1.8 %shard_map.100 = (s32[16,1,384]{2,1,0:T(1,128)}, s32[1,1,256]{2,1,0:T(1,128)S(1)}, s32[1,1,128]{2,1,0:T(1,128)S(1)}) custom-call(s32[2,32]{1,0:T(2,128)} %bitcast.18, s32[2,32]{1,0:T(2,128)} %bitcast.19, s32[4,32]{1,0:T(4,128)} %bitcast.17, s32[1,32]{1,0:T(1,128)} %bitcast.20, s32[1,32]{1,0:T(1,128)} %bitcast.21), custom_call_target="tpu_custom_call" | custom-call | tf_op jit(solution)/shard_map/pallas_call | solution.py:49
  5.8 3.9 %all-to-all-start = ((s32[16,1,384]{2,1,0:T(1,128)}), s32[16,1,384]{2,1,0:T(1,128)S(1)}, u32[]{:S(2)}, u32[]{:S(2)}) async-start(s32[16,1,384]{2,1,0:T(1,128)} %get-tuple-element.32), calls=%async_computation | async-start | bytes 49152 | tf_op jit(solution)/shard_map/all_to_all | solution.py:694
  9.7 1.6 %collective-permute-start.1 = (s32[1,1,256]{2,1,0:T(1,128)S(1)}, s32[1,1,256]{2,1,0:T(1,128)S(1)}, u32[]{:S(2)}, u32[]{:S(2)}) collective-permute-start(s32[1,1,256]{2,1,0:T(1,128)S(1)} %get-tuple-element.33.refs_0_.refs_1_), channel_id=1, source_target_pairs={{0,16},{16,0},{1,17},{17,1},{2,18},{18,2},{3,19},{19,3},{4,20},{20... | collective-permute-start | bytes 3080 | tf_op jit(solution)/shard_map/ppermute | solution.py:696
  11.3 3.0 %shard_map.101.refs_0_ = f32[256,16,128]{2,1,0:T(8,128)S(1)} custom-call(f32[32,16,128]{2,1,0:T(8,128)} %start_in.1, f32[8,128,128]{2,1,0:T(8,128)} %refs_3_.4), custom_call_target="tpu_custom_call" | custom-call | flops 402653184 | bytes 4194304 | tf_op jit(solution)/shard_map/pallas_call | solution.py:49
  14.4 3.2 %all-to-all-done.refs_3_.list_in.refs_0_ = s32[16,1,384]{2,1,0:T(1,128)S(1)} async-done(((s32[16,1,384]{2,1,0:T(1,128)}), s32[16,1,384]{2,1,0:T(1,128)S(1)}, u32[]{:S(2)}, u32[]{:S(2)}) %all-to-all-start) | async-done | bytes 24608 | tf_op jit(solution)/shard_map/all_to_all | solution.py:694
  17.6 2.3 %shard_map.102 = (f32[8,16,16,128]{3,2,1,0:T(8,128)}, f32[32,16,128]{2,1,0:T(8,128)}) custom-call(f32[256,16,128]{2,1,0:T(8,128)S(1)} %shard_map.101.refs_0_, f32[32,16,128]{2,1,0:T(8,128)S(1)} %collective-permute-done.refs_1_, f32[8,128,128]{2,1,0:T(8,128)S(1)} %copy-done.1, s32[16,1,384]{2,1,0:T(1,128)S(1)} %all-to-all-done.refs_3_.list_in.refs_0_, ...), custom_call_target="tpu_custom_call" | custom-call | flops 402653184 | bytes 4194304 | tf_op jit(solution)/shard_map/pallas_call | solution.py:49
  19.9 3.7 %all-to-all-start.1 = ((f32[8,256,128]{2,1,0:T(8,128)}), f32[8,256,128]{2,1,0:T(8,128)S(1)}, u32[]{:S(2)}, u32[]{:S(2)}) async-start(f32[8,256,128]{2,1,0:T(8,128)} %bitcast.14), calls=%async_computation.1 | async-start | bytes 2097152 | tf_op jit(solution)/shard_map/all_to_all | solution.py:755
  23.6 1.6 %collective-permute-start.2 = (s32[16,1,384]{2,1,0:T(1,128)S(1)}, s32[16,1,384]{2,1,0:T(1,128)S(1)}, u32[]{:S(2)}, u32[]{:S(2)}) collective-permute-start(s32[16,1,384]{2,1,0:T(1,128)S(1)} %all-to-all-done.refs_3_.list_in.refs_0_), channel_id=1, source_target_pairs={{0,16},{16,0},{1,17},{17,1},{2,18},{18,2},{3,19},{19,3},{4,20},{20... | collective-permute-start | bytes 73736 | tf_op jit(solution)/shard_map/ppermute | solution.py:750
  25.2 2.3 %collective-permute-done.2 = s32[16,1,384]{2,1,0:T(1,128)S(1)} collective-permute-done((s32[16,1,384]{2,1,0:T(1,128)S(1)}, s32[16,1,384]{2,1,0:T(1,128)S(1)}, u32[]{:S(2)}, u32[]{:S(2)}) %collective-permute-start.2) | collective-permute-done | bytes 24608 | tf_op jit(solution)/shard_map/ppermute | solution.py:750
  29.4 6.7 %shard_map.103 = (bf16[256,1440]{1,0:T(8,128)(2,1)}, bf16[128,384]{1,0:T(8,128)(2,1)}, bf16[1024,256]{1,0:T(8,128)(2,1)}, f32[256,128]{1,0:T(8,128)}, f32[4,128]{1,0:T(4,128)S(1)}) custom-call(s32[1,1,256]{2,1,0:T(1,128)S(1)} %get-tuple-element.33.refs_0_.refs_1_, f32[32,16,128]{2,1,0:T(8,128)} %refs_4_.5, s32[8,2,512]{2,1,0:T(2,128)S(1)} %reshape.7.refs_2_, ...), custom_call_target="tpu_custom_call" | custom-call | flops 1342177280 | bytes 4194304 | tf_op jit(solution)/shard_map/pallas_call | solution.py:49
  36.1 1.9 %all-to-all-done.1.refs_2_ = f32[8,256,128]{2,1,0:T(8,128)S(1)} async-done(((f32[8,256,128]{2,1,0:T(8,128)}), f32[8,256,128]{2,1,0:T(8,128)S(1)}, u32[]{:S(2)}, u32[]{:S(2)}) %all-to-all-start.1) | async-done | bytes 1048608 | tf_op jit(solution)/shard_map/all_to_all | solution.py:755
  39.3 2.7 %collective-permute-start.4 = (f32[32,16,128]{2,1,0:T(8,128)S(1)}, f32[32,16,128]{2,1,0:T(8,128)S(1)}, u32[]{:S(2)}, u32[]{:S(2)}) collective-permute-start(f32[32,16,128]{2,1,0:T(8,128)S(1)} %shard_map.104.refs_2_), channel_id=1, source_target_pairs={{0,8},{1,9},{2,10},{3,11},{4,12},{5,13},{6,14},{7,15},{8,0},{9,1},... | collective-permute-start | bytes 786440 | tf_op jit(solution)/shard_map/ppermute | solution.py:829
  42.1 4.2 %shard_map.106 = (f32[8,144,128]{2,1,0:T(8,128)}, f32[32,16,128]{2,1,0:T(8,128)}) custom-call(s32[16,1,384]{2,1,0:T(1,128)S(1)} %all-to-all-done.refs_3_.list_in.refs_0_, s32[1,1,256]{2,1,0:T(1,128)S(1)} %collective-permute-done.1.refs_4_.refs_1_, f32[32,16,128]{2,1,0:T(8,128)S(1)} %shard_map.104.refs_2_, f32[8,128,128]{2,1,0:T(8,128)S(1)} %copy-done.1, ...), custom_call_target="tpu_custom_call" | custom-call | flops 805306368 | bytes 4194304 | tf_op jit(solution)/shard_map/pallas_call | solution.py:49
  46.3 3.7 %all-to-all-start.3 = ((f32[8,144,128]{2,1,0:T(8,128)}), f32[8,144,128]{2,1,0:T(8,128)S(1)}, u32[]{:S(2)}, u32[]{:S(2)}) async-start(f32[8,144,128]{2,1,0:T(8,128)} %get-tuple-element.52), calls=%async_computation.3 | async-start | bytes 1179648 | tf_op jit(solution)/shard_map/all_to_all | solution.py:755
  50.0 1.6 %collective-permute-start.5 = (f32[32,16,128]{2,1,0:T(8,128)}, f32[32,16,128]{2,1,0:T(8,128)S(1)}, u32[]{:S(2)}, u32[]{:S(2)}) collective-permute-start(f32[32,16,128]{2,1,0:T(8,128)} %get-tuple-element.50), channel_id=1, source_target_pairs={{0,16},{16,0},{1,17},{17,1},{2,18},{18,2},{3,19},{19,3},{4,20},{20... | collective-permute-start | bytes 786440 | tf_op jit(solution)/shard_map/ppermute | solution.py:637
  51.6 2.3 %collective-permute-done.4.mirror_ref = f32[32,16,128]{2,1,0:T(8,128)S(1)} collective-permute-done((f32[32,16,128]{2,1,0:T(8,128)S(1)}, f32[32,16,128]{2,1,0:T(8,128)S(1)}, u32[]{:S(2)}, u32[]{:S(2)}) %collective-permute-start.4) | collective-permute-done | bytes 262176 | tf_op jit(solution)/shard_map/ppermute | solution.py:829
  53.9 3.1 %shard_map.105 = f32[8,128,128]{2,1,0:T(8,128)} custom-call(s32[16,1,384]{2,1,0:T(1,128)S(1)} %all-to-all-done.refs_3_.list_in.refs_0_, f32[32,16,128]{2,1,0:T(8,128)S(1)} %collective-permute-done.4.mirror_ref, f32[8,128,128]{2,1,0:T(8,128)S(1)} %copy-done.1, f32[8,128,128]{2,1,0:T(8,128)S(1)} %copy-done), custom_call_target="tpu_custom_call" | custom-call | flops 40265318400 | bytes 4194304 | tf_op jit(solution)/shard_map/pallas_call | solution.py:49
  57.0 1.6 %collective-permute-done.5.refs_5_ = f32[32,16,128]{2,1,0:T(8,128)S(1)} collective-permute-done((f32[32,16,128]{2,1,0:T(8,128)}, f32[32,16,128]{2,1,0:T(8,128)S(1)}, u32[]{:S(2)}, u32[]{:S(2)}) %collective-permute-start.5) | collective-permute-done | bytes 262176 | tf_op jit(solution)/shard_map/ppermute | solution.py:637
  60.2 3.5 %all-to-all-start.2 = ((f32[8,128,128]{2,1,0:T(8,128)}), f32[8,128,128]{2,1,0:T(8,128)S(1)}, u32[]{:S(2)}, u32[]{:S(2)}) async-start(f32[8,128,128]{2,1,0:T(8,128)} %shard_map.105), calls=%async_computation.2 | async-start | bytes 1048576 | tf_op jit(solution)/shard_map/all_to_all | solution.py:870
  63.7 1.6 %collective-permute-start.6 = (f32[8,128]{1,0:T(8,128)S(1)}, f32[8,128]{1,0:T(8,128)S(1)}, u32[]{:S(2)}, u32[]{:S(2)}) collective-permute-start(f32[8,128]{1,0:T(8,128)S(1)} %get-tuple-element.55), channel_id=1, source_target_pairs={{0,16},{16,0},{1,17},{17,1},{2,18},{18,2},{3,19},{19,3},{4,20},{20... | collective-permute-start | bytes 12296 | tf_op jit(solution)/shard_map/ppermute | solution.py:875
  65.3 2.1 %collective-permute-done.6 = f32[8,128]{1,0:T(8,128)S(1)} collective-permute-done((f32[8,128]{1,0:T(8,128)S(1)}, f32[8,128]{1,0:T(8,128)S(1)}, u32[]{:S(2)}, u32[]{:S(2)}) %collective-permute-start.6) | collective-permute-done | bytes 4128 | tf_op jit(solution)/shard_map/ppermute | solution.py:875
  67.4 1.8 %collective-permute-start.7 = (f32[4,128]{1,0:T(4,128)S(1)}, f32[4,128]{1,0:T(4,128)S(1)}, u32[]{:S(2)}, u32[]{:S(2)}) collective-permute-start(f32[4,128]{1,0:T(4,128)S(1)} %get-tuple-element.57), channel_id=1, source_target_pairs={{0,8},{1,9},{2,10},{3,11},{4,12},{5,13},{6,14},{7,15},{8,0},{9,1},... | collective-permute-start | bytes 6152 | tf_op jit(solution)/shard_map/ppermute | solution.py:876
  69.2 1.8 %shard_map.107.refs_2_ = f32[32,16,128]{2,1,0:T(8,128)S(1)} custom-call(s32[1,1,128]{2,1,0:T(1,128)S(1)} %get-tuple-element.31.refs_0_, s32[1,1,256]{2,1,0:T(1,128)S(1)} %get-tuple-element.33.refs_0_.refs_1_, f32[8,144,128]{2,1,0:T(8,128)S(1)} %all-to-all-done.3.refs_2_.arrived_ref, f32[8,128,128]{2,1,0:T(8,128)S(1)} %copy-done, f32[32,16,128]{2,1,0:T(8,128)} %refs_4_.5, ...), custom_call_target="tpu_custom_call" | custom-call | flops 402653184 | bytes 4194304 | tf_op jit(solution)/shard_map/pallas_call | solution.py:49
  (25 shorter events, 7.7 us)
Async XLA Ops:
  0.0 17.6 %copy-start.1 = (f32[8,128,128]{2,1,0:T(8,128)S(1)}, f32[8,128,128]{2,1,0:T(8,128)}, u32[]{:S(2)}) copy-start(f32[8,128,128]{2,1,0:T(8,128)} %refs_3_.4) | copy-start | bytes 1572868
  0.0 17.6 %collective-permute-start = (f32[32,16,128]{2,1,0:T(8,128)}, f32[32,16,128]{2,1,0:T(8,128)S(1)}, u32[]{:S(2)}, u32[]{:S(2)}) collective-permute-start(f32[32,16,128]{2,1,0:T(8,128)} %start_in.1), channel_id=1, source_target_pairs={{0,8},{1,9},{2,10},{3,11},{4,12},{5,13},{6,14},{7,15},{8,0},{9,1},... | collective-permute-start | bytes 786440 | tf_op jit(solution)/shard_map/ppermute | solution.py:682
  5.8 11.8 %all-to-all-start = ((s32[16,1,384]{2,1,0:T(1,128)}), s32[16,1,384]{2,1,0:T(1,128)S(1)}, u32[]{:S(2)}, u32[]{:S(2)}) async-start(s32[16,1,384]{2,1,0:T(1,128)} %get-tuple-element.32), calls=%async_computation | async-start | bytes 49152 | tf_op jit(solution)/shard_map/all_to_all | solution.py:694
  9.7 4.6 %collective-permute-start.1 = (s32[1,1,256]{2,1,0:T(1,128)S(1)}, s32[1,1,256]{2,1,0:T(1,128)S(1)}, u32[]{:S(2)}, u32[]{:S(2)}) collective-permute-start(s32[1,1,256]{2,1,0:T(1,128)S(1)} %get-tuple-element.33.refs_0_.refs_1_), channel_id=1, source_target_pairs={{0,16},{16,0},{1,17},{17,1},{2,18},{18,2},{3,19},{19,3},{4,20},{20... | collective-permute-start | bytes 3080 | tf_op jit(solution)/shard_map/ppermute | solution.py:696
  19.9 9.5 %copy-start = (f32[8,128,128]{2,1,0:T(8,128)S(1)}, f32[8,128,128]{2,1,0:T(8,128)}, u32[]{:S(2)}) copy-start(f32[8,128,128]{2,1,0:T(8,128)} %refs_3_.5) | copy-start | bytes 1572868
  19.9 9.5 %copy-start.3 = (f32[8,128,128]{2,1,0:T(8,128)S(1)}, f32[8,128,128]{2,1,0:T(8,128)}, u32[]{:S(2)}) copy-start(f32[8,128,128]{2,1,0:T(8,128)} %refs_5_.1) | copy-start | bytes 1572868
  19.9 18.1 %all-to-all-start.1 = ((f32[8,256,128]{2,1,0:T(8,128)}), f32[8,256,128]{2,1,0:T(8,128)S(1)}, u32[]{:S(2)}, u32[]{:S(2)}) async-start(f32[8,256,128]{2,1,0:T(8,128)} %bitcast.14), calls=%async_computation.1 | async-start | bytes 2097152 | tf_op jit(solution)/shard_map/all_to_all | solution.py:755
  23.6 3.9 %collective-permute-start.2 = (s32[16,1,384]{2,1,0:T(1,128)S(1)}, s32[16,1,384]{2,1,0:T(1,128)S(1)}, u32[]{:S(2)}, u32[]{:S(2)}) collective-permute-start(s32[16,1,384]{2,1,0:T(1,128)S(1)} %all-to-all-done.refs_3_.list_in.refs_0_), channel_id=1, source_target_pairs={{0,16},{16,0},{1,17},{17,1},{2,18},{18,2},{3,19},{19,3},{4,20},{20... | collective-permute-start | bytes 73736 | tf_op jit(solution)/shard_map/ppermute | solution.py:750
  27.5 10.5 %collective-permute-start.3 = (f32[32,16,128]{2,1,0:T(8,128)}, f32[32,16,128]{2,1,0:T(8,128)S(1)}, u32[]{:S(2)}, u32[]{:S(2)}) collective-permute-start(f32[32,16,128]{2,1,0:T(8,128)} %get-tuple-element.45), channel_id=1, source_target_pairs={{0,16},{16,0},{1,17},{17,1},{2,18},{18,2},{3,19},{19,3},{4,20},{20... | collective-permute-start | bytes 786440 | tf_op jit(solution)/shard_map/ppermute | solution.py:637
  29.4 8.6 %copy-start.2 = (f32[32,16,128]{2,1,0:T(8,128)S(1)}, f32[32,16,128]{2,1,0:T(8,128)}, u32[]{:S(2)}) copy-start(f32[32,16,128]{2,1,0:T(8,128)} %refs_4_.5) | copy-start | bytes 786436
  39.3 14.5 %collective-permute-start.4 = (f32[32,16,128]{2,1,0:T(8,128)S(1)}, f32[32,16,128]{2,1,0:T(8,128)S(1)}, u32[]{:S(2)}, u32[]{:S(2)}) collective-permute-start(f32[32,16,128]{2,1,0:T(8,128)S(1)} %shard_map.104.refs_2_), channel_id=1, source_target_pairs={{0,8},{1,9},{2,10},{3,11},{4,12},{5,13},{6,14},{7,15},{8,0},{9,1},... | collective-permute-start | bytes 786440 | tf_op jit(solution)/shard_map/ppermute | solution.py:829
  46.3 13.9 %all-to-all-start.3 = ((f32[8,144,128]{2,1,0:T(8,128)}), f32[8,144,128]{2,1,0:T(8,128)S(1)}, u32[]{:S(2)}, u32[]{:S(2)}) async-start(f32[8,144,128]{2,1,0:T(8,128)} %get-tuple-element.52), calls=%async_computation.3 | async-start | bytes 1179648 | tf_op jit(solution)/shard_map/all_to_all | solution.py:755
  50.0 8.6 %collective-permute-start.5 = (f32[32,16,128]{2,1,0:T(8,128)}, f32[32,16,128]{2,1,0:T(8,128)S(1)}, u32[]{:S(2)}, u32[]{:S(2)}) collective-permute-start(f32[32,16,128]{2,1,0:T(8,128)} %get-tuple-element.50), channel_id=1, source_target_pairs={{0,16},{16,0},{1,17},{17,1},{2,18},{18,2},{3,19},{19,3},{4,20},{20... | collective-permute-start | bytes 786440 | tf_op jit(solution)/shard_map/ppermute | solution.py:637
  60.2 12.3 %all-to-all-start.2 = ((f32[8,128,128]{2,1,0:T(8,128)}), f32[8,128,128]{2,1,0:T(8,128)S(1)}, u32[]{:S(2)}, u32[]{:S(2)}) async-start(f32[8,128,128]{2,1,0:T(8,128)} %shard_map.105), calls=%async_computation.2 | async-start | bytes 1048576 | tf_op jit(solution)/shard_map/all_to_all | solution.py:870
  63.7 3.7 %collective-permute-start.6 = (f32[8,128]{1,0:T(8,128)S(1)}, f32[8,128]{1,0:T(8,128)S(1)}, u32[]{:S(2)}, u32[]{:S(2)}) collective-permute-start(f32[8,128]{1,0:T(8,128)S(1)} %get-tuple-element.55), channel_id=1, source_target_pairs={{0,16},{16,0},{1,17},{17,1},{2,18},{18,2},{3,19},{19,3},{4,20},{20... | collective-permute-start | bytes 12296 | tf_op jit(solution)/shard_map/ppermute | solution.py:875
  67.4 4.6 %collective-permute-start.7 = (f32[4,128]{1,0:T(4,128)S(1)}, f32[4,128]{1,0:T(4,128)S(1)}, u32[]{:S(2)}, u32[]{:S(2)}) collective-permute-start(f32[4,128]{1,0:T(4,128)S(1)} %get-tuple-element.57), channel_id=1, source_target_pairs={{0,8},{1,9},{2,10},{3,11},{4,12},{5,13},{6,14},{7,15},{8,0},{9,1},... | collective-permute-start | bytes 6152 | tf_op jit(solution)/shard_map/ppermute | solution.py:876

commit v16 on v15

--- a/solution.py
+++ b/solution.py
@@ -520,14 +520,28 @@
 
 
 def mirror_kernel(
-    sizes, list_in, mirror_ref, tile_ref, inverse_ref, send_out, list_ref, product_ref, block_ref, solved_ref, send_ref, sems
+    sizes,
+    list_in,
+    inner_ref,
+    outer_ref,
+    tile_ref,
+    inverse_ref,
+    send_out,
+    list_ref,
+    product_ref,
+    block_ref,
+    solved_ref,
+    send_ref,
+    sems,
 ):
     rows, n_rows, cap, n_tiles, n_rhs = sizes
     half, n_diag = n_rows // 2, inverse_ref.shape[0]
     base = jnp.where(lax.axis_index("rows") >= half, half, 0)
     list_in = list_in.at[pl.ds(base, half), :, pl.ds(0, LANES)]
     metadata = started([pltpu.make_async_copy(list_in, list_ref, sems.at[half])])
-    table_products(mirror_ref[...].reshape(rows * n_rhs, -1), tile_ref, product_ref)
+    quarter = lax.div(lax.axis_index("rows") * 4, n_rows)
+    mirror = jnp.where((quarter == 1) | (quarter == 2), outer_ref[...], inner_ref[...])
+    table_products(mirror.reshape(rows * n_rhs, -1), tile_ref, product_ref)
     finish(metadata)
     codes = [list_ref[n // cap, 0, LANES // 2 + n % cap] for n in range(half * cap)]
     for n, code in enumerate(codes):
@@ -665,6 +679,7 @@
         n_bands == 2
         and n_dev * rows * total_groups <= DENSE_LIMIT
         and depth == 4
+        and n_rows % 4 == 0
         and n_diag * n_func == LANES
         and n_tiles + 2 <= n_func
     )
@@ -826,7 +841,10 @@
     body = cap * n_rhs
     full_list = pltpu.SMEM((n_rows, 1, LANES), i32)
     if dense:
-        mirror = lax.ppermute(first, "rows", to_mirror)
+        outer = [(i, j) for i, j in to_mirror if i * 4 // n_rows in (0, 3)]
+        inner = [(i, j) for i, j in to_mirror if i * 4 // n_rows in (1, 2)]
+        inner = lax.ppermute(first, "rows", inner)
+        outer = lax.ppermute(first, "rows", outer)
         own, band = call(
             functools.partial(own_kernel, sizes, width_k),
             (
@@ -853,7 +871,7 @@
         packed = call(
             functools.partial(mirror_kernel, sizes),
             jax.ShapeDtypeStruct((half, body, states), f32),
-            [ANY] + [VMEM] * 3,
+            [ANY] + [VMEM] * 4,
             HBM,
             [
                 list_scratch,
@@ -865,7 +883,7 @@
             ],
             BEHIND_SWAP * work * n_tiles,
             4 << 20,
-        )(lists, mirror, coupling_tiles, inverse_table)
+        )(lists, inner, outer, coupling_tiles, inverse_table)
         packed, band = lax.optimization_barrier((packed, band))
         swapped = lax.all_to_all(
             packed, "rows", split_axis=0, concat_axis=0, tiled=True, axis_index_groups=halves_of_rows

time: 74.6 us -> 77.5 us (1.039)
  starting transfers between devices: 31.2 us -> 35.9 us
  waiting for transfers between devices: 16.5 us -> 14.3 us
    ppermute x1 -> x2, starting transfers between devices: 2.73 us -> 5.88 us  [the longest x1 4.59 us: on_device(): outer = lax.ppermute(first, 'rows', outer)]
    ppermute x2, waiting for transfers between devices: 1.64 us -> 3.2 us  [to_bands(): return (lax.ppermute(sends[0], 'band', [(0, 1), (1, 0)]),)]
    ppermute x1, starting transfers between devices: 1.8 us -> 3.32 us  [on_device(): far = lax.ppermute(keep[depth:], 'rows', to_mirror)]
    ppermute x1 -> x2, waiting for transfers between devices: 2.28 us -> 0.89 us  [the longest x1 0.89 us: on_device(): inner = lax.ppermute(first, 'rows', inner)]
    ppermute x1, waiting for transfers between devices: 1.03 us -> 0.01 us  [on_device(): far = lax.ppermute(keep[depth:], 'rows', to_mirror)]
    all_to_all x2, waiting for transfers between devices: 3.4 us -> 2.58 us  [exchange(): lax.all_to_all(sends[0], 'rows', split_axis=0, concat_axis=0, tiled=True,...]
  transfers between devices with their start and end apart: 12 -> 13, of which waited for: 9 -> 7; matrix products, arithmetic and copies ran while one was open for 0% -> 0% of each run, Pallas kernels for 28% -> 27%
where the time goes in v16:
time: 77.5 us; the launch traced here: 76.7 us
  starting transfers between devices  35.9 us (46%)
  Pallas kernels  25.7 us (33%)
  waiting for transfers between devices  14.3 us (18%)
    pallas_call x10, Pallas kernels, apply(): return run(*pinned)  25.7 us
    all_to_all x2, starting transfers between devices, exchange(): lax.all_to_all(sends[0], 'rows', split_axis=0, concat_axis=0, tiled=True,...  7.43 us
    ppermute x1, starting transfers between devices, on_device(): outer = lax.ppermute(first, 'rows', outer)  4.59 us
    ppermute x1, starting transfers between devices, on_device(): mirror = lax.ppermute(start_iterate, 'rows', to_mirror)  4.04 us
    all_to_all x1, starting transfers between devices, on_device(): lax.all_to_all(lists, 'rows', split_axis=0, concat_axis=0, tiled=True)  3.9 us
    all_to_all x1, starting transfers between devices, on_device(): lax.all_to_all(packed, 'rows', split_axis=0, concat_axis=0, tiled=True, a...  3.49 us
    ppermute x1, starting transfers between devices, on_device(): far = lax.ppermute(keep[depth:], 'rows', to_mirror)  3.32 us
    all_to_all x1, waiting for transfers between devices, on_device(): lax.all_to_all(lists, 'rows', split_axis=0, concat_axis=0, tiled=True)  3.23 us
  transfers between devices with their start and end apart: 13, of which 7 were waited for; matrix products, arithmetic and copies ran while one was open for 0% of the time, Pallas kernels for 27%

profile of v16, /device:TPU:0, one launch (start us, length us, event | category | flops | bytes accessed | tf_op | source)
XLA Modules:
  0.0 76.7 jit_solution(6799574212064195882)
XLA Ops:
  0.0 4.0 %collective-permute-start = (f32[32,16,128]{2,1,0:T(8,128)}, f32[32,16,128]{2,1,0:T(8,128)S(1)}, u32[]{:S(2)}, u32[]{:S(2)}) collective-permute-start(f32[32,16,128]{2,1,0:T(8,128)} %start_in.1), channel_id=1, source_target_pairs={{0,8},{1,9},{2,10},{3,11},{4,12},{5,13},{6,14},{7,15},{8,0},{9,1},... | collective-permute-start | bytes 786440 | tf_op jit(solution)/shard_map/ppermute | solution.py:697
  4.0 1.8 %shard_map.100 = (s32[16,1,384]{2,1,0:T(1,128)}, s32[1,1,256]{2,1,0:T(1,128)S(1)}, s32[1,1,128]{2,1,0:T(1,128)S(1)}) custom-call(s32[2,32]{1,0:T(2,128)} %bitcast.18, s32[2,32]{1,0:T(2,128)} %bitcast.19, s32[4,32]{1,0:T(4,128)} %bitcast.17, s32[1,32]{1,0:T(1,128)} %bitcast.20, s32[1,32]{1,0:T(1,128)} %bitcast.21), custom_call_target="tpu_custom_call" | custom-call | tf_op jit(solution)/shard_map/pallas_call | solution.py:49
  5.8 3.9 %all-to-all-start = ((s32[16,1,384]{2,1,0:T(1,128)}), s32[16,1,384]{2,1,0:T(1,128)S(1)}, u32[]{:S(2)}, u32[]{:S(2)}) async-start(s32[16,1,384]{2,1,0:T(1,128)} %get-tuple-element.32), calls=%async_computation | async-start | bytes 49152 | tf_op jit(solution)/shard_map/all_to_all | solution.py:709
  9.7 1.6 %collective-permute-start.1 = (s32[1,1,256]{2,1,0:T(1,128)S(1)}, s32[1,1,256]{2,1,0:T(1,128)S(1)}, u32[]{:S(2)}, u32[]{:S(2)}) collective-permute-start(s32[1,1,256]{2,1,0:T(1,128)S(1)} %get-tuple-element.33.refs_0_.refs_1_), channel_id=1, source_target_pairs={{0,16},{16,0},{1,17},{17,1},{2,18},{18,2},{3,19},{19,3},{4,20},{20... | collective-permute-start | bytes 3080 | tf_op jit(solution)/shard_map/ppermute | solution.py:711
  11.3 3.0 %shard_map.101.refs_0_ = f32[256,16,128]{2,1,0:T(8,128)S(1)} custom-call(f32[32,16,128]{2,1,0:T(8,128)} %start_in.1, f32[8,128,128]{2,1,0:T(8,128)} %refs_3_.4), custom_call_target="tpu_custom_call" | custom-call | flops 402653184 | bytes 4194304 | tf_op jit(solution)/shard_map/pallas_call | solution.py:49
  14.4 3.2 %all-to-all-done.refs_3_.list_in.refs_0_ = s32[16,1,384]{2,1,0:T(1,128)S(1)} async-done(((s32[16,1,384]{2,1,0:T(1,128)}), s32[16,1,384]{2,1,0:T(1,128)S(1)}, u32[]{:S(2)}, u32[]{:S(2)}) %all-to-all-start) | async-done | bytes 24608 | tf_op jit(solution)/shard_map/all_to_all | solution.py:709
  17.6 2.3 %shard_map.102 = (f32[8,16,16,128]{3,2,1,0:T(8,128)}, f32[32,16,128]{2,1,0:T(8,128)}) custom-call(f32[256,16,128]{2,1,0:T(8,128)S(1)} %shard_map.101.refs_0_, f32[32,16,128]{2,1,0:T(8,128)S(1)} %collective-permute-done.refs_1_, f32[8,128,128]{2,1,0:T(8,128)S(1)} %copy-done.1, s32[16,1,384]{2,1,0:T(1,128)S(1)} %all-to-all-done.refs_3_.list_in.refs_0_, ...), custom_call_target="tpu_custom_call" | custom-call | flops 402653184 | bytes 4194304 | tf_op jit(solution)/shard_map/pallas_call | solution.py:49
  19.9 3.7 %all-to-all-start.1 = ((f32[8,256,128]{2,1,0:T(8,128)}), f32[8,256,128]{2,1,0:T(8,128)S(1)}, u32[]{:S(2)}, u32[]{:S(2)}) async-start(f32[8,256,128]{2,1,0:T(8,128)} %bitcast.14), calls=%async_computation.1 | async-start | bytes 2097152 | tf_op jit(solution)/shard_map/all_to_all | solution.py:770
  23.6 1.6 %collective-permute-start.2 = (s32[16,1,384]{2,1,0:T(1,128)S(1)}, s32[16,1,384]{2,1,0:T(1,128)S(1)}, u32[]{:S(2)}, u32[]{:S(2)}) collective-permute-start(s32[16,1,384]{2,1,0:T(1,128)S(1)} %all-to-all-done.refs_3_.list_in.refs_0_), channel_id=1, source_target_pairs={{0,16},{16,0},{1,17},{17,1},{2,18},{18,2},{3,19},{19,3},{4,20},{20... | collective-permute-start | bytes 73736 | tf_op jit(solution)/shard_map/ppermute | solution.py:765
  25.2 2.3 %collective-permute-done.2 = s32[16,1,384]{2,1,0:T(1,128)S(1)} collective-permute-done((s32[16,1,384]{2,1,0:T(1,128)S(1)}, s32[16,1,384]{2,1,0:T(1,128)S(1)}, u32[]{:S(2)}, u32[]{:S(2)}) %collective-permute-start.2) | collective-permute-done | bytes 24608 | tf_op jit(solution)/shard_map/ppermute | solution.py:765
  27.5 1.5 %collective-permute-start.3 = (f32[32,16,128]{2,1,0:T(8,128)S(1)}, f32[32,16,128]{2,1,0:T(8,128)S(1)}, u32[]{:S(2)}, u32[]{:S(2)}) collective-permute-start(f32[32,16,128]{2,1,0:T(8,128)S(1)} %copy-done.4), channel_id=1, source_target_pairs={{0,16},{16,0},{1,17},{17,1},{2,18},{18,2},{3,19},{19,3},{4,20},{20... | collective-permute-start | bytes 786440 | tf_op jit(solution)/shard_map/ppermute | solution.py:651
  29.4 6.7 %shard_map.103 = (bf16[256,1440]{1,0:T(8,128)(2,1)}, bf16[128,384]{1,0:T(8,128)(2,1)}, bf16[1024,256]{1,0:T(8,128)(2,1)}, f32[256,128]{1,0:T(8,128)}, f32[4,128]{1,0:T(4,128)S(1)}) custom-call(s32[1,1,256]{2,1,0:T(1,128)S(1)} %get-tuple-element.33.refs_0_.refs_1_, f32[32,16,128]{2,1,0:T(8,128)} %refs_4_.5, s32[8,2,512]{2,1,0:T(2,128)S(1)} %reshape.7.refs_2_, ...), custom_call_target="tpu_custom_call" | custom-call | flops 1342177280 | bytes 4194304 | tf_op jit(solution)/shard_map/pallas_call | solution.py:49
  36.1 1.9 %all-to-all-done.1.refs_2_ = f32[8,256,128]{2,1,0:T(8,128)S(1)} async-done(((f32[8,256,128]{2,1,0:T(8,128)}), f32[8,256,128]{2,1,0:T(8,128)S(1)}, u32[]{:S(2)}, u32[]{:S(2)}) %all-to-all-start.1) | async-done | bytes 1048608 | tf_op jit(solution)/shard_map/all_to_all | solution.py:770
  39.4 4.6 %collective-permute-start.5 = (f32[32,16,128]{2,1,0:T(8,128)S(1)}, f32[32,16,128]{2,1,0:T(8,128)S(1)}, u32[]{:S(2)}, u32[]{:S(2)}) collective-permute-start(f32[32,16,128]{2,1,0:T(8,128)S(1)} %shard_map.104.refs_2_), channel_id=1, source_target_pairs={{0,8},{1,9},{2,10},{3,11},{12,4},{13,5},{14,6},{15,7},{16,24},{17,... | collective-permute-start | bytes 786440 | tf_op jit(solution)/shard_map/ppermute | solution.py:847
  45.2 4.2 %shard_map.106 = (f32[8,144,128]{2,1,0:T(8,128)}, f32[32,16,128]{2,1,0:T(8,128)}) custom-call(s32[16,1,384]{2,1,0:T(1,128)S(1)} %all-to-all-done.refs_3_.list_in.refs_0_, s32[1,1,256]{2,1,0:T(1,128)S(1)} %collective-permute-done.1.refs_4_.refs_1_, f32[32,16,128]{2,1,0:T(8,128)S(1)} %shard_map.104.refs_2_, f32[8,128,128]{2,1,0:T(8,128)S(1)} %copy-done.1, ...), custom_call_target="tpu_custom_call" | custom-call | flops 805306368 | bytes 4194304 | tf_op jit(solution)/shard_map/pallas_call | solution.py:49
  49.5 3.7 %all-to-all-start.3 = ((f32[8,144,128]{2,1,0:T(8,128)}), f32[8,144,128]{2,1,0:T(8,128)S(1)}, u32[]{:S(2)}, u32[]{:S(2)}) async-start(f32[8,144,128]{2,1,0:T(8,128)} %get-tuple-element.52), calls=%async_computation.3 | async-start | bytes 1179648 | tf_op jit(solution)/shard_map/all_to_all | solution.py:770
  53.2 1.6 %collective-permute-start.6 = (f32[32,16,128]{2,1,0:T(8,128)}, f32[32,16,128]{2,1,0:T(8,128)S(1)}, u32[]{:S(2)}, u32[]{:S(2)}) collective-permute-start(f32[32,16,128]{2,1,0:T(8,128)} %get-tuple-element.50), channel_id=1, source_target_pairs={{0,16},{16,0},{1,17},{17,1},{2,18},{18,2},{3,19},{19,3},{4,20},{20... | collective-permute-start | bytes 786440 | tf_op jit(solution)/shard_map/ppermute | solution.py:651
  55.7 3.2 %shard_map.105 = f32[8,128,128]{2,1,0:T(8,128)} custom-call(s32[16,1,384]{2,1,0:T(1,128)S(1)} %all-to-all-done.refs_3_.list_in.refs_0_, f32[32,16,128]{2,1,0:T(8,128)S(1)} %collective-permute-done.4.inner_ref, f32[32,16,128]{2,1,0:T(8,128)S(1)} %collective-permute-done.5.outer_ref, f32[8,128,128]{2,1,0:T(8,128)S(1)} %copy-done.1, f32[8,128,128]{2,1,0:T(8,128)S(1)} %copy-done), custom_call_target="tpu_custom_call" | custom-call | flops 40265318400 | bytes 4194304 | tf_op jit(solution)/shard_map/pallas_call | solution.py:49
  58.9 3.2 %collective-permute-done.6.refs_5_ = f32[32,16,128]{2,1,0:T(8,128)S(1)} collective-permute-done((f32[32,16,128]{2,1,0:T(8,128)}, f32[32,16,128]{2,1,0:T(8,128)S(1)}, u32[]{:S(2)}, u32[]{:S(2)}) %collective-permute-start.6) | collective-permute-done | bytes 262176 | tf_op jit(solution)/shard_map/ppermute | solution.py:651
  62.7 3.5 %all-to-all-start.2 = ((f32[8,128,128]{2,1,0:T(8,128)}), f32[8,128,128]{2,1,0:T(8,128)S(1)}, u32[]{:S(2)}, u32[]{:S(2)}) async-start(f32[8,128,128]{2,1,0:T(8,128)} %shard_map.105), calls=%async_computation.2 | async-start | bytes 1048576 | tf_op jit(solution)/shard_map/all_to_all | solution.py:888
  66.2 1.6 %collective-permute-start.7 = (f32[8,128]{1,0:T(8,128)S(1)}, f32[8,128]{1,0:T(8,128)S(1)}, u32[]{:S(2)}, u32[]{:S(2)}) collective-permute-start(f32[8,128]{1,0:T(8,128)S(1)} %get-tuple-element.55), channel_id=1, source_target_pairs={{0,16},{16,0},{1,17},{17,1},{2,18},{18,2},{3,19},{19,3},{4,20},{20... | collective-permute-start | bytes 12296 | tf_op jit(solution)/shard_map/ppermute | solution.py:893
  67.8 2.1 %collective-permute-done.7 = f32[8,128]{1,0:T(8,128)S(1)} collective-permute-done((f32[8,128]{1,0:T(8,128)S(1)}, f32[8,128]{1,0:T(8,128)S(1)}, u32[]{:S(2)}, u32[]{:S(2)}) %collective-permute-start.7) | collective-permute-done | bytes 4128 | tf_op jit(solution)/shard_map/ppermute | solution.py:893
  69.9 3.3 %collective-permute-start.8 = (f32[4,128]{1,0:T(4,128)S(1)}, f32[4,128]{1,0:T(4,128)S(1)}, u32[]{:S(2)}, u32[]{:S(2)}) collective-permute-start(f32[4,128]{1,0:T(4,128)S(1)} %get-tuple-element.57), channel_id=1, source_target_pairs={{0,8},{1,9},{2,10},{3,11},{4,12},{5,13},{6,14},{7,15},{8,0},{9,1},... | collective-permute-start | bytes 6152 | tf_op jit(solution)/shard_map/ppermute | solution.py:894
  73.2 1.8 %shard_map.107.refs_2_ = f32[32,16,128]{2,1,0:T(8,128)S(1)} custom-call(s32[1,1,128]{2,1,0:T(1,128)S(1)} %get-tuple-element.31.refs_0_, s32[1,1,256]{2,1,0:T(1,128)S(1)} %get-tuple-element.33.refs_0_.refs_1_, f32[8,144,128]{2,1,0:T(8,128)S(1)} %all-to-all-done.3.refs_2_.arrived_ref, f32[8,128,128]{2,1,0:T(8,128)S(1)} %copy-done, f32[32,16,128]{2,1,0:T(8,128)} %refs_4_.5, ...), custom_call_target="tpu_custom_call" | custom-call | flops 402653184 | bytes 4194304 | tf_op jit(solution)/shard_map/pallas_call | solution.py:49
  (29 shorter events, 6.0 us)
Async XLA Ops:
  0.0 17.6 %copy-start.1 = (f32[8,128,128]{2,1,0:T(8,128)S(1)}, f32[8,128,128]{2,1,0:T(8,128)}, u32[]{:S(2)}) copy-start(f32[8,128,128]{2,1,0:T(8,128)} %refs_3_.4) | copy-start | bytes 1572868
  0.0 17.6 %collective-permute-start = (f32[32,16,128]{2,1,0:T(8,128)}, f32[32,16,128]{2,1,0:T(8,128)S(1)}, u32[]{:S(2)}, u32[]{:S(2)}) collective-permute-start(f32[32,16,128]{2,1,0:T(8,128)} %start_in.1), channel_id=1, source_target_pairs={{0,8},{1,9},{2,10},{3,11},{4,12},{5,13},{6,14},{7,15},{8,0},{9,1},... | collective-permute-start | bytes 786440 | tf_op jit(solution)/shard_map/ppermute | solution.py:697
  5.8 11.8 %all-to-all-start = ((s32[16,1,384]{2,1,0:T(1,128)}), s32[16,1,384]{2,1,0:T(1,128)S(1)}, u32[]{:S(2)}, u32[]{:S(2)}) async-start(s32[16,1,384]{2,1,0:T(1,128)} %get-tuple-element.32), calls=%async_computation | async-start | bytes 49152 | tf_op jit(solution)/shard_map/all_to_all | solution.py:709
  9.7 4.6 %collective-permute-start.1 = (s32[1,1,256]{2,1,0:T(1,128)S(1)}, s32[1,1,256]{2,1,0:T(1,128)S(1)}, u32[]{:S(2)}, u32[]{:S(2)}) collective-permute-start(s32[1,1,256]{2,1,0:T(1,128)S(1)} %get-tuple-element.33.refs_0_.refs_1_), channel_id=1, source_target_pairs={{0,16},{16,0},{1,17},{17,1},{2,18},{18,2},{3,19},{19,3},{4,20},{20... | collective-permute-start | bytes 3080 | tf_op jit(solution)/shard_map/ppermute | solution.py:711
  19.9 7.6 %copy-start.4 = (f32[32,16,128]{2,1,0:T(8,128)S(1)}, f32[32,16,128]{2,1,0:T(8,128)}, u32[]{:S(2)}) copy-start(f32[32,16,128]{2,1,0:T(8,128)} %get-tuple-element.45) | copy-start | bytes 786436
  19.9 9.5 %copy-start = (f32[8,128,128]{2,1,0:T(8,128)S(1)}, f32[8,128,128]{2,1,0:T(8,128)}, u32[]{:S(2)}) copy-start(f32[8,128,128]{2,1,0:T(8,128)} %refs_3_.5) | copy-start | bytes 1572868
  19.9 9.5 %copy-start.3 = (f32[8,128,128]{2,1,0:T(8,128)S(1)}, f32[8,128,128]{2,1,0:T(8,128)}, u32[]{:S(2)}) copy-start(f32[8,128,128]{2,1,0:T(8,128)} %refs_5_.1) | copy-start | bytes 1572868
  19.9 18.1 %all-to-all-start.1 = ((f32[8,256,128]{2,1,0:T(8,128)}), f32[8,256,128]{2,1,0:T(8,128)S(1)}, u32[]{:S(2)}, u32[]{:S(2)}) async-start(f32[8,256,128]{2,1,0:T(8,128)} %bitcast.14), calls=%async_computation.1 | async-start | bytes 2097152 | tf_op jit(solution)/shard_map/all_to_all | solution.py:770
  23.6 3.9 %collective-permute-start.2 = (s32[16,1,384]{2,1,0:T(1,128)S(1)}, s32[16,1,384]{2,1,0:T(1,128)S(1)}, u32[]{:S(2)}, u32[]{:S(2)}) collective-permute-start(s32[16,1,384]{2,1,0:T(1,128)S(1)} %all-to-all-done.refs_3_.list_in.refs_0_), channel_id=1, source_target_pairs={{0,16},{16,0},{1,17},{17,1},{2,18},{18,2},{3,19},{19,3},{4,20},{20... | collective-permute-start | bytes 73736 | tf_op jit(solution)/shard_map/ppermute | solution.py:765
  27.5 10.5 %collective-permute-start.3 = (f32[32,16,128]{2,1,0:T(8,128)S(1)}, f32[32,16,128]{2,1,0:T(8,128)S(1)}, u32[]{:S(2)}, u32[]{:S(2)}) collective-permute-start(f32[32,16,128]{2,1,0:T(8,128)S(1)} %copy-done.4), channel_id=1, source_target_pairs={{0,16},{16,0},{1,17},{17,1},{2,18},{18,2},{3,19},{19,3},{4,20},{20... | collective-permute-start | bytes 786440 | tf_op jit(solution)/shard_map/ppermute | solution.py:651
  29.4 8.6 %copy-start.2 = (f32[32,16,128]{2,1,0:T(8,128)S(1)}, f32[32,16,128]{2,1,0:T(8,128)}, u32[]{:S(2)}) copy-start(f32[32,16,128]{2,1,0:T(8,128)} %refs_4_.5) | copy-start | bytes 786436
  39.4 15.4 %collective-permute-start.5 = (f32[32,16,128]{2,1,0:T(8,128)S(1)}, f32[32,16,128]{2,1,0:T(8,128)S(1)}, u32[]{:S(2)}, u32[]{:S(2)}) collective-permute-start(f32[32,16,128]{2,1,0:T(8,128)S(1)} %shard_map.104.refs_2_), channel_id=1, source_target_pairs={{0,8},{1,9},{2,10},{3,11},{12,4},{13,5},{14,6},{15,7},{16,24},{17,... | collective-permute-start | bytes 786440 | tf_op jit(solution)/shard_map/ppermute | solution.py:847
  43.9 11.7 %collective-permute-start.4 = (f32[32,16,128]{2,1,0:T(8,128)S(1)}, f32[32,16,128]{2,1,0:T(8,128)S(1)}, u32[]{:S(2)}, u32[]{:S(2)}) collective-permute-start(f32[32,16,128]{2,1,0:T(8,128)S(1)} %shard_map.104.refs_2_), channel_id=1, source_target_pairs={{4,12},{5,13},{6,14},{7,15},{8,0},{9,1},{10,2},{11,3},{20,28},{21,... | collective-permute-start | bytes 786440 | tf_op jit(solution)/shard_map/ppermute | solution.py:846
  49.5 13.3 %all-to-all-start.3 = ((f32[8,144,128]{2,1,0:T(8,128)}), f32[8,144,128]{2,1,0:T(8,128)S(1)}, u32[]{:S(2)}, u32[]{:S(2)}) async-start(f32[8,144,128]{2,1,0:T(8,128)} %get-tuple-element.52), calls=%async_computation.3 | async-start | bytes 1179648 | tf_op jit(solution)/shard_map/all_to_all | solution.py:770
  53.2 8.9 %collective-permute-start.6 = (f32[32,16,128]{2,1,0:T(8,128)}, f32[32,16,128]{2,1,0:T(8,128)S(1)}, u32[]{:S(2)}, u32[]{:S(2)}) collective-permute-start(f32[32,16,128]{2,1,0:T(8,128)} %get-tuple-element.50), channel_id=1, source_target_pairs={{0,16},{16,0},{1,17},{17,1},{2,18},{18,2},{3,19},{19,3},{4,20},{20... | collective-permute-start | bytes 786440 | tf_op jit(solution)/shard_map/ppermute | solution.py:651
  62.7 12.3 %all-to-all-start.2 = ((f32[8,128,128]{2,1,0:T(8,128)}), f32[8,128,128]{2,1,0:T(8,128)S(1)}, u32[]{:S(2)}, u32[]{:S(2)}) async-start(f32[8,128,128]{2,1,0:T(8,128)} %shard_map.105), calls=%async_computation.2 | async-start | bytes 1048576 | tf_op jit(solution)/shard_map/all_to_all | solution.py:888
  66.2 3.7 %collective-permute-start.7 = (f32[8,128]{1,0:T(8,128)S(1)}, f32[8,128]{1,0:T(8,128)S(1)}, u32[]{:S(2)}, u32[]{:S(2)}) collective-permute-start(f32[8,128]{1,0:T(8,128)S(1)} %get-tuple-element.55), channel_id=1, source_target_pairs={{0,16},{16,0},{1,17},{17,1},{2,18},{18,2},{3,19},{19,3},{4,20},{20... | collective-permute-start | bytes 12296 | tf_op jit(solution)/shard_map/ppermute | solution.py:893
  69.9 5.1 %collective-permute-start.8 = (f32[4,128]{1,0:T(4,128)S(1)}, f32[4,128]{1,0:T(4,128)S(1)}, u32[]{:S(2)}, u32[]{:S(2)}) collective-permute-start(f32[4,128]{1,0:T(4,128)S(1)} %get-tuple-element.57), channel_id=1, source_target_pairs={{0,8},{1,9},{2,10},{3,11},{4,12},{5,13},{6,14},{7,15},{8,0},{9,1},... | collective-permute-start | bytes 6152 | tf_op jit(solution)/shard_map/ppermute | solution.py:894

commit v17 on v15

--- a/solution.py
+++ b/solution.py
@@ -435,13 +435,22 @@
     out_ref, metadata, sum_ref, product_ref, meta_sems = refs[0], refs[1:3], *refs[3:]
     place_ref, index_ref = metadata
     rows = sizes[0]
-    finish(copies_of(zip(metadata_in, metadata), meta_sems))
-    fetch = arrived_blocks_of(sizes, width_k, place_ref, field, arrived_ref)
+    metadata = copies_of(zip(metadata_in, metadata), meta_sems)
+    total = terms[0][...].reshape(sum_ref.shape)
+    for term in terms[1:]:
+        total = total + term[...].reshape(sum_ref.shape)
+    sum_ref[...] = total
+    finish(metadata)
+    arrived = arrived_blocks_of(sizes, width_k, place_ref, field, arrived_ref)
+    n_rhs = sizes[4]
+
+    def fetch(row):
+        return sum_ref[pl.ds(row * n_rhs, n_rhs), :] + arrived(row)
 
     def diags(row):
         return index_ref[0, 0, rows + row]
 
-    gather_solve(sizes, fetch, diags, [], terms, inverse_ref, sum_ref, product_ref)
+    gather_solve(sizes, fetch, diags, [], [], inverse_ref, sum_ref, product_ref)
     out_ref[...] = sum_ref[...].reshape(out_ref.shape)
 
 
@@ -610,7 +619,7 @@
 
 
 def final_kernel(sizes, width_k, *refs):
-    place_in, mirror_ref, base_ref, near_ref, far_ref, scale_ref, out_ref, place_ref, sem = refs
+    place_in, mirror_ref, base_ref, near_ref, far_ref, scale_ref, out, place_ref, out_ref, sem, out_sems = refs
     rows, n_rows, cap, n_tiles, n_rhs = sizes
     metadata = pltpu.make_async_copy(place_in, place_ref, sem)
     metadata.start()
@@ -618,12 +627,22 @@
     correction = (near_ref[...] + far_ref[...]) / scale_ref[...]
     padded = jnp.concatenate([correction, jnp.zeros((8 - depth, LANES), jnp.float32)], axis=0)
     turned = padded.T
-    metadata.wait()
-    fetch = half_blocks_of(sizes, width_k, place_ref, mirror_ref, True)
     for row in range(rows):
         spot, place = row // depth, row % depth
         column = turned[spot * n_rhs : (spot + 1) * n_rhs, place : place + 1]
-        out_ref[row] = (base_ref[row] + column) + fetch(row)
+        out_ref[row] = base_ref[row] + column
+    metadata.wait()
+    fetch = half_blocks_of(sizes, width_k, place_ref, mirror_ref, True)
+    step = -(-rows // out_sems.shape[0])
+    copies = []
+    for first in range(0, rows, step):
+        count = min(step, rows - first)
+        for row in range(first, first + count):
+            out_ref[row] = out_ref[row] + fetch(row)
+        place = pl.ds(first, count)
+        copy = pltpu.make_async_copy(out_ref.at[place], out.at[place], out_sems.at[len(copies)])
+        copies += started([copy])
+    finish(copies)
 
 
 def shifted(value, axis, steps):
@@ -894,8 +913,13 @@
             functools.partial(final_kernel, sizes, width_k),
             jax.ShapeDtypeStruct(block, f32),
             [ANY] + [VMEM] * 5,
-            VMEM,
-            [row_scratch[0], pltpu.SemaphoreType.DMA],
+            HBM,
+            [
+                row_scratch[0],
+                pltpu.VMEM(block, f32),
+                pltpu.SemaphoreType.DMA,
+                pltpu.SemaphoreType.DMA((4,)),
+            ],
             0,
             4 << 20,
         )(places, swapped, base, keep[:depth], far, scale)

time: 74.6 us -> 74.6 us (level)
  no operation moved by 1% of the time
where the time goes in v17:
time: 74.6 us; the launch traced here: 74 us
  starting transfers between devices  31.2 us (42%)
  Pallas kernels  25.7 us (34%)
  waiting for transfers between devices  16.5 us (22%)
    pallas_call x10, Pallas kernels, apply(): return run(*pinned)  25.7 us
    all_to_all x2, starting transfers between devices, exchange(): lax.all_to_all(sends[0], 'rows', split_axis=0, concat_axis=0, tiled=True,...  7.43 us
    ppermute x1, starting transfers between devices, on_device(): mirror = lax.ppermute(start_iterate, 'rows', to_mirror)  4.04 us
    all_to_all x1, starting transfers between devices, on_device(): lax.all_to_all(lists, 'rows', split_axis=0, concat_axis=0, tiled=True)  3.9 us
    all_to_all x1, starting transfers between devices, on_device(): lax.all_to_all(packed, 'rows', split_axis=0, concat_axis=0, tiled=True, a...  3.49 us
    all_to_all x2, waiting for transfers between devices, exchange(): lax.all_to_all(sends[0], 'rows', split_axis=0, concat_axis=0, tiled=True,...  3.39 us
    all_to_all x1, waiting for transfers between devices, on_device(): lax.all_to_all(lists, 'rows', split_axis=0, concat_axis=0, tiled=True)  3.23 us
    ppermute x2, starting transfers between devices, to_bands(): return (lax.ppermute(sends[0], 'band', [(0, 1), (1, 0)]),)  3.1 us
  transfers between devices with their start and end apart: 12, of which 9 were waited for; matrix products, arithmetic and copies ran while one was open for 0% of the time, Pallas kernels for 28%

profile of v17, /device:TPU:0, one launch (start us, length us, event | category | flops | bytes accessed | tf_op | source)
XLA Modules:
  0.0 74.0 jit_solution(10279755150407831463)
XLA Ops:
  0.0 4.0 %collective-permute-start = (f32[32,16,128]{2,1,0:T(8,128)}, f32[32,16,128]{2,1,0:T(8,128)S(1)}, u32[]{:S(2)}, u32[]{:S(2)}) collective-permute-start(f32[32,16,128]{2,1,0:T(8,128)} %start_in.1), channel_id=1, source_target_pairs={{0,8},{1,9},{2,10},{3,11},{4,12},{5,13},{6,14},{7,15},{8,0},{9,1},... | collective-permute-start | bytes 786440 | tf_op jit(solution)/shard_map/ppermute | solution.py:701
  4.0 1.8 %shard_map.100 = (s32[16,1,384]{2,1,0:T(1,128)}, s32[1,1,256]{2,1,0:T(1,128)S(1)}, s32[1,1,128]{2,1,0:T(1,128)S(1)}) custom-call(s32[2,32]{1,0:T(2,128)} %bitcast.18, s32[2,32]{1,0:T(2,128)} %bitcast.19, s32[4,32]{1,0:T(4,128)} %bitcast.17, s32[1,32]{1,0:T(1,128)} %bitcast.20, s32[1,32]{1,0:T(1,128)} %bitcast.21), custom_call_target="tpu_custom_call" | custom-call | tf_op jit(solution)/shard_map/pallas_call | solution.py:49
  5.8 3.9 %all-to-all-start = ((s32[16,1,384]{2,1,0:T(1,128)}), s32[16,1,384]{2,1,0:T(1,128)S(1)}, u32[]{:S(2)}, u32[]{:S(2)}) async-start(s32[16,1,384]{2,1,0:T(1,128)} %get-tuple-element.32), calls=%async_computation | async-start | bytes 49152 | tf_op jit(solution)/shard_map/all_to_all | solution.py:713
  9.7 1.6 %collective-permute-start.1 = (s32[1,1,256]{2,1,0:T(1,128)S(1)}, s32[1,1,256]{2,1,0:T(1,128)S(1)}, u32[]{:S(2)}, u32[]{:S(2)}) collective-permute-start(s32[1,1,256]{2,1,0:T(1,128)S(1)} %get-tuple-element.33.refs_0_.refs_1_), channel_id=1, source_target_pairs={{0,16},{16,0},{1,17},{17,1},{2,18},{18,2},{3,19},{19,3},{4,20},{20... | collective-permute-start | bytes 3080 | tf_op jit(solution)/shard_map/ppermute | solution.py:715
  11.3 3.0 %shard_map.101.refs_0_ = f32[256,16,128]{2,1,0:T(8,128)S(1)} custom-call(f32[32,16,128]{2,1,0:T(8,128)} %start_in.1, f32[8,128,128]{2,1,0:T(8,128)} %refs_3_.4), custom_call_target="tpu_custom_call" | custom-call | flops 402653184 | bytes 4194304 | tf_op jit(solution)/shard_map/pallas_call | solution.py:49
  14.4 3.2 %all-to-all-done.refs_3_.list_in.refs_0_ = s32[16,1,384]{2,1,0:T(1,128)S(1)} async-done(((s32[16,1,384]{2,1,0:T(1,128)}), s32[16,1,384]{2,1,0:T(1,128)S(1)}, u32[]{:S(2)}, u32[]{:S(2)}) %all-to-all-start) | async-done | bytes 24608 | tf_op jit(solution)/shard_map/all_to_all | solution.py:713
  17.6 2.3 %shard_map.102 = (f32[8,16,16,128]{3,2,1,0:T(8,128)}, f32[32,16,128]{2,1,0:T(8,128)}) custom-call(f32[256,16,128]{2,1,0:T(8,128)S(1)} %shard_map.101.refs_0_, f32[32,16,128]{2,1,0:T(8,128)S(1)} %collective-permute-done.refs_1_, f32[8,128,128]{2,1,0:T(8,128)S(1)} %copy-done.1, s32[16,1,384]{2,1,0:T(1,128)S(1)} %all-to-all-done.refs_3_.list_in.refs_0_, ...), custom_call_target="tpu_custom_call" | custom-call | flops 402653184 | bytes 4194304 | tf_op jit(solution)/shard_map/pallas_call | solution.py:49
  19.9 3.7 %all-to-all-start.1 = ((f32[8,256,128]{2,1,0:T(8,128)}), f32[8,256,128]{2,1,0:T(8,128)S(1)}, u32[]{:S(2)}, u32[]{:S(2)}) async-start(f32[8,256,128]{2,1,0:T(8,128)} %bitcast.14), calls=%async_computation.1 | async-start | bytes 2097152 | tf_op jit(solution)/shard_map/all_to_all | solution.py:774
  23.6 1.6 %collective-permute-start.2 = (s32[16,1,384]{2,1,0:T(1,128)S(1)}, s32[16,1,384]{2,1,0:T(1,128)S(1)}, u32[]{:S(2)}, u32[]{:S(2)}) collective-permute-start(s32[16,1,384]{2,1,0:T(1,128)S(1)} %all-to-all-done.refs_3_.list_in.refs_0_), channel_id=1, source_target_pairs={{0,16},{16,0},{1,17},{17,1},{2,18},{18,2},{3,19},{19,3},{4,20},{20... | collective-permute-start | bytes 73736 | tf_op jit(solution)/shard_map/ppermute | solution.py:769
  25.2 2.3 %collective-permute-done.2 = s32[16,1,384]{2,1,0:T(1,128)S(1)} collective-permute-done((s32[16,1,384]{2,1,0:T(1,128)S(1)}, s32[16,1,384]{2,1,0:T(1,128)S(1)}, u32[]{:S(2)}, u32[]{:S(2)}) %collective-permute-start.2) | collective-permute-done | bytes 24608 | tf_op jit(solution)/shard_map/ppermute | solution.py:769
  29.4 6.7 %shard_map.103 = (bf16[256,1440]{1,0:T(8,128)(2,1)}, bf16[128,384]{1,0:T(8,128)(2,1)}, bf16[1024,256]{1,0:T(8,128)(2,1)}, f32[256,128]{1,0:T(8,128)}, f32[4,128]{1,0:T(4,128)S(1)}) custom-call(s32[1,1,256]{2,1,0:T(1,128)S(1)} %get-tuple-element.33.refs_0_.refs_1_, f32[32,16,128]{2,1,0:T(8,128)} %refs_4_.5, s32[8,2,512]{2,1,0:T(2,128)S(1)} %reshape.7.refs_2_, ...), custom_call_target="tpu_custom_call" | custom-call | flops 1342177280 | bytes 4194304 | tf_op jit(solution)/shard_map/pallas_call | solution.py:49
  36.1 1.9 %all-to-all-done.1.refs_2_ = f32[8,256,128]{2,1,0:T(8,128)S(1)} async-done(((f32[8,256,128]{2,1,0:T(8,128)}), f32[8,256,128]{2,1,0:T(8,128)S(1)}, u32[]{:S(2)}, u32[]{:S(2)}) %all-to-all-start.1) | async-done | bytes 1048608 | tf_op jit(solution)/shard_map/all_to_all | solution.py:774
  39.3 2.7 %collective-permute-start.4 = (f32[32,16,128]{2,1,0:T(8,128)S(1)}, f32[32,16,128]{2,1,0:T(8,128)S(1)}, u32[]{:S(2)}, u32[]{:S(2)}) collective-permute-start(f32[32,16,128]{2,1,0:T(8,128)S(1)} %shard_map.104.refs_2_), channel_id=1, source_target_pairs={{0,8},{1,9},{2,10},{3,11},{4,12},{5,13},{6,14},{7,15},{8,0},{9,1},... | collective-permute-start | bytes 786440 | tf_op jit(solution)/shard_map/ppermute | solution.py:848
  42.1 4.2 %shard_map.106 = (f32[8,144,128]{2,1,0:T(8,128)}, f32[32,16,128]{2,1,0:T(8,128)}) custom-call(s32[16,1,384]{2,1,0:T(1,128)S(1)} %all-to-all-done.refs_3_.list_in.refs_0_, s32[1,1,256]{2,1,0:T(1,128)S(1)} %collective-permute-done.1.refs_4_.refs_1_, f32[32,16,128]{2,1,0:T(8,128)S(1)} %shard_map.104.refs_2_, f32[8,128,128]{2,1,0:T(8,128)S(1)} %copy-done.1, ...), custom_call_target="tpu_custom_call" | custom-call | flops 805306368 | bytes 4194304 | tf_op jit(solution)/shard_map/pallas_call | solution.py:49
  46.3 3.7 %all-to-all-start.3 = ((f32[8,144,128]{2,1,0:T(8,128)}), f32[8,144,128]{2,1,0:T(8,128)S(1)}, u32[]{:S(2)}, u32[]{:S(2)}) async-start(f32[8,144,128]{2,1,0:T(8,128)} %get-tuple-element.52), calls=%async_computation.3 | async-start | bytes 1179648 | tf_op jit(solution)/shard_map/all_to_all | solution.py:774
  50.0 1.6 %collective-permute-start.5 = (f32[32,16,128]{2,1,0:T(8,128)}, f32[32,16,128]{2,1,0:T(8,128)S(1)}, u32[]{:S(2)}, u32[]{:S(2)}) collective-permute-start(f32[32,16,128]{2,1,0:T(8,128)} %get-tuple-element.50), channel_id=1, source_target_pairs={{0,16},{16,0},{1,17},{17,1},{2,18},{18,2},{3,19},{19,3},{4,20},{20... | collective-permute-start | bytes 786440 | tf_op jit(solution)/shard_map/ppermute | solution.py:656
  51.6 2.3 %collective-permute-done.4.mirror_ref = f32[32,16,128]{2,1,0:T(8,128)S(1)} collective-permute-done((f32[32,16,128]{2,1,0:T(8,128)S(1)}, f32[32,16,128]{2,1,0:T(8,128)S(1)}, u32[]{:S(2)}, u32[]{:S(2)}) %collective-permute-start.4) | collective-permute-done | bytes 262176 | tf_op jit(solution)/shard_map/ppermute | solution.py:848
  53.9 3.1 %shard_map.105 = f32[8,128,128]{2,1,0:T(8,128)} custom-call(s32[16,1,384]{2,1,0:T(1,128)S(1)} %all-to-all-done.refs_3_.list_in.refs_0_, f32[32,16,128]{2,1,0:T(8,128)S(1)} %collective-permute-done.4.mirror_ref, f32[8,128,128]{2,1,0:T(8,128)S(1)} %copy-done.1, f32[8,128,128]{2,1,0:T(8,128)S(1)} %copy-done), custom_call_target="tpu_custom_call" | custom-call | flops 40265318400 | bytes 4194304 | tf_op jit(solution)/shard_map/pallas_call | solution.py:49
  57.0 1.7 %collective-permute-done.5.refs_5_ = f32[32,16,128]{2,1,0:T(8,128)S(1)} collective-permute-done((f32[32,16,128]{2,1,0:T(8,128)}, f32[32,16,128]{2,1,0:T(8,128)S(1)}, u32[]{:S(2)}, u32[]{:S(2)}) %collective-permute-start.5) | collective-permute-done | bytes 262176 | tf_op jit(solution)/shard_map/ppermute | solution.py:656
  60.2 3.5 %all-to-all-start.2 = ((f32[8,128,128]{2,1,0:T(8,128)}), f32[8,128,128]{2,1,0:T(8,128)S(1)}, u32[]{:S(2)}, u32[]{:S(2)}) async-start(f32[8,128,128]{2,1,0:T(8,128)} %shard_map.105), calls=%async_computation.2 | async-start | bytes 1048576 | tf_op jit(solution)/shard_map/all_to_all | solution.py:889
  63.7 1.6 %collective-permute-start.6 = (f32[8,128]{1,0:T(8,128)S(1)}, f32[8,128]{1,0:T(8,128)S(1)}, u32[]{:S(2)}, u32[]{:S(2)}) collective-permute-start(f32[8,128]{1,0:T(8,128)S(1)} %get-tuple-element.55), channel_id=1, source_target_pairs={{0,16},{16,0},{1,17},{17,1},{2,18},{18,2},{3,19},{19,3},{4,20},{20... | collective-permute-start | bytes 12296 | tf_op jit(solution)/shard_map/ppermute | solution.py:894
  65.3 2.1 %collective-permute-done.6 = f32[8,128]{1,0:T(8,128)S(1)} collective-permute-done((f32[8,128]{1,0:T(8,128)S(1)}, f32[8,128]{1,0:T(8,128)S(1)}, u32[]{:S(2)}, u32[]{:S(2)}) %collective-permute-start.6) | collective-permute-done | bytes 4128 | tf_op jit(solution)/shard_map/ppermute | solution.py:894
  67.4 1.8 %collective-permute-start.7 = (f32[4,128]{1,0:T(4,128)S(1)}, f32[4,128]{1,0:T(4,128)S(1)}, u32[]{:S(2)}, u32[]{:S(2)}) collective-permute-start(f32[4,128]{1,0:T(4,128)S(1)} %get-tuple-element.57), channel_id=1, source_target_pairs={{0,8},{1,9},{2,10},{3,11},{4,12},{5,13},{6,14},{7,15},{8,0},{9,1},... | collective-permute-start | bytes 6152 | tf_op jit(solution)/shard_map/ppermute | solution.py:895
  69.2 1.8 %shard_map.107.refs_2_ = f32[32,16,128]{2,1,0:T(8,128)S(1)} custom-call(s32[1,1,128]{2,1,0:T(1,128)S(1)} %get-tuple-element.31.refs_0_, s32[1,1,256]{2,1,0:T(1,128)S(1)} %get-tuple-element.33.refs_0_.refs_1_, f32[8,144,128]{2,1,0:T(8,128)S(1)} %all-to-all-done.3.refs_2_.arrived_ref, f32[8,128,128]{2,1,0:T(8,128)S(1)} %copy-done, f32[32,16,128]{2,1,0:T(8,128)} %refs_4_.5, ...), custom_call_target="tpu_custom_call" | custom-call | flops 402653184 | bytes 4194304 | tf_op jit(solution)/shard_map/pallas_call | solution.py:49
  (25 shorter events, 7.6 us)
Async XLA Ops:
  0.0 17.6 %copy-start.1 = (f32[8,128,128]{2,1,0:T(8,128)S(1)}, f32[8,128,128]{2,1,0:T(8,128)}, u32[]{:S(2)}) copy-start(f32[8,128,128]{2,1,0:T(8,128)} %refs_3_.4) | copy-start | bytes 1572868
  0.0 17.6 %collective-permute-start = (f32[32,16,128]{2,1,0:T(8,128)}, f32[32,16,128]{2,1,0:T(8,128)S(1)}, u32[]{:S(2)}, u32[]{:S(2)}) collective-permute-start(f32[32,16,128]{2,1,0:T(8,128)} %start_in.1), channel_id=1, source_target_pairs={{0,8},{1,9},{2,10},{3,11},{4,12},{5,13},{6,14},{7,15},{8,0},{9,1},... | collective-permute-start | bytes 786440 | tf_op jit(solution)/shard_map/ppermute | solution.py:701
  5.8 11.8 %all-to-all-start = ((s32[16,1,384]{2,1,0:T(1,128)}), s32[16,1,384]{2,1,0:T(1,128)S(1)}, u32[]{:S(2)}, u32[]{:S(2)}) async-start(s32[16,1,384]{2,1,0:T(1,128)} %get-tuple-element.32), calls=%async_computation | async-start | bytes 49152 | tf_op jit(solution)/shard_map/all_to_all | solution.py:713
  9.7 4.6 %collective-permute-start.1 = (s32[1,1,256]{2,1,0:T(1,128)S(1)}, s32[1,1,256]{2,1,0:T(1,128)S(1)}, u32[]{:S(2)}, u32[]{:S(2)}) collective-permute-start(s32[1,1,256]{2,1,0:T(1,128)S(1)} %get-tuple-element.33.refs_0_.refs_1_), channel_id=1, source_target_pairs={{0,16},{16,0},{1,17},{17,1},{2,18},{18,2},{3,19},{19,3},{4,20},{20... | collective-permute-start | bytes 3080 | tf_op jit(solution)/shard_map/ppermute | solution.py:715
  19.9 9.5 %copy-start = (f32[8,128,128]{2,1,0:T(8,128)S(1)}, f32[8,128,128]{2,1,0:T(8,128)}, u32[]{:S(2)}) copy-start(f32[8,128,128]{2,1,0:T(8,128)} %refs_3_.5) | copy-start | bytes 1572868
  19.9 9.5 %copy-start.3 = (f32[8,128,128]{2,1,0:T(8,128)S(1)}, f32[8,128,128]{2,1,0:T(8,128)}, u32[]{:S(2)}) copy-start(f32[8,128,128]{2,1,0:T(8,128)} %refs_5_.1) | copy-start | bytes 1572868
  19.9 18.1 %all-to-all-start.1 = ((f32[8,256,128]{2,1,0:T(8,128)}), f32[8,256,128]{2,1,0:T(8,128)S(1)}, u32[]{:S(2)}, u32[]{:S(2)}) async-start(f32[8,256,128]{2,1,0:T(8,128)} %bitcast.14), calls=%async_computation.1 | async-start | bytes 2097152 | tf_op jit(solution)/shard_map/all_to_all | solution.py:774
  23.6 3.9 %collective-permute-start.2 = (s32[16,1,384]{2,1,0:T(1,128)S(1)}, s32[16,1,384]{2,1,0:T(1,128)S(1)}, u32[]{:S(2)}, u32[]{:S(2)}) collective-permute-start(s32[16,1,384]{2,1,0:T(1,128)S(1)} %all-to-all-done.refs_3_.list_in.refs_0_), channel_id=1, source_target_pairs={{0,16},{16,0},{1,17},{17,1},{2,18},{18,2},{3,19},{19,3},{4,20},{20... | collective-permute-start | bytes 73736 | tf_op jit(solution)/shard_map/ppermute | solution.py:769
  27.5 10.5 %collective-permute-start.3 = (f32[32,16,128]{2,1,0:T(8,128)}, f32[32,16,128]{2,1,0:T(8,128)S(1)}, u32[]{:S(2)}, u32[]{:S(2)}) collective-permute-start(f32[32,16,128]{2,1,0:T(8,128)} %get-tuple-element.45), channel_id=1, source_target_pairs={{0,16},{16,0},{1,17},{17,1},{2,18},{18,2},{3,19},{19,3},{4,20},{20... | collective-permute-start | bytes 786440 | tf_op jit(solution)/shard_map/ppermute | solution.py:656
  29.4 8.6 %copy-start.2 = (f32[32,16,128]{2,1,0:T(8,128)S(1)}, f32[32,16,128]{2,1,0:T(8,128)}, u32[]{:S(2)}) copy-start(f32[32,16,128]{2,1,0:T(8,128)} %refs_4_.5) | copy-start | bytes 786436
  39.3 14.5 %collective-permute-start.4 = (f32[32,16,128]{2,1,0:T(8,128)S(1)}, f32[32,16,128]{2,1,0:T(8,128)S(1)}, u32[]{:S(2)}, u32[]{:S(2)}) collective-permute-start(f32[32,16,128]{2,1,0:T(8,128)S(1)} %shard_map.104.refs_2_), channel_id=1, source_target_pairs={{0,8},{1,9},{2,10},{3,11},{4,12},{5,13},{6,14},{7,15},{8,0},{9,1},... | collective-permute-start | bytes 786440 | tf_op jit(solution)/shard_map/ppermute | solution.py:848
  46.3 13.9 %all-to-all-start.3 = ((f32[8,144,128]{2,1,0:T(8,128)}), f32[8,144,128]{2,1,0:T(8,128)S(1)}, u32[]{:S(2)}, u32[]{:S(2)}) async-start(f32[8,144,128]{2,1,0:T(8,128)} %get-tuple-element.52), calls=%async_computation.3 | async-start | bytes 1179648 | tf_op jit(solution)/shard_map/all_to_all | solution.py:774
  50.0 8.6 %collective-permute-start.5 = (f32[32,16,128]{2,1,0:T(8,128)}, f32[32,16,128]{2,1,0:T(8,128)S(1)}, u32[]{:S(2)}, u32[]{:S(2)}) collective-permute-start(f32[32,16,128]{2,1,0:T(8,128)} %get-tuple-element.50), channel_id=1, source_target_pairs={{0,16},{16,0},{1,17},{17,1},{2,18},{18,2},{3,19},{19,3},{4,20},{20... | collective-permute-start | bytes 786440 | tf_op jit(solution)/shard_map/ppermute | solution.py:656
  60.2 12.3 %all-to-all-start.2 = ((f32[8,128,128]{2,1,0:T(8,128)}), f32[8,128,128]{2,1,0:T(8,128)S(1)}, u32[]{:S(2)}, u32[]{:S(2)}) async-start(f32[8,128,128]{2,1,0:T(8,128)} %shard_map.105), calls=%async_computation.2 | async-start | bytes 1048576 | tf_op jit(solution)/shard_map/all_to_all | solution.py:889
  63.7 3.7 %collective-permute-start.6 = (f32[8,128]{1,0:T(8,128)S(1)}, f32[8,128]{1,0:T(8,128)S(1)}, u32[]{:S(2)}, u32[]{:S(2)}) collective-permute-start(f32[8,128]{1,0:T(8,128)S(1)} %get-tuple-element.55), channel_id=1, source_target_pairs={{0,16},{16,0},{1,17},{17,1},{2,18},{18,2},{3,19},{19,3},{4,20},{20... | collective-permute-start | bytes 12296 | tf_op jit(solution)/shard_map/ppermute | solution.py:894
  67.4 4.6 %collective-permute-start.7 = (f32[4,128]{1,0:T(4,128)S(1)}, f32[4,128]{1,0:T(4,128)S(1)}, u32[]{:S(2)}, u32[]{:S(2)}) collective-permute-start(f32[4,128]{1,0:T(4,128)S(1)} %get-tuple-element.57), channel_id=1, source_target_pairs={{0,8},{1,9},{2,10},{3,11},{4,12},{5,13},{6,14},{7,15},{8,0},{9,1},... | collective-permute-start | bytes 6152 | tf_op jit(solution)/shard_map/ppermute | solution.py:895

commit v18 on v17

--- a/solution.py
+++ b/solution.py
@@ -227,19 +227,20 @@
     table_products(values, tile_ref, product_ref)
     finish(metadata)
     copies = []
+    def send(source, target):
+        copies.extend(started([pltpu.make_async_copy(source, target, send_sems.at[len(copies)])]))
+
     for side, blocks_ref in ((0, own_ref), (1, product_ref)):
         for device in range(half):
             for rank in range(cap):
                 code = list_ref[device, 0, side * (LANES // 2) + rank]
-                block = blocks_ref[below(code, rows * n_tiles)]
-                send_ref[device, side * cap + rank] = block
-            place = (device, pl.ds(side * cap, cap))
-            copies += started(
-                [pltpu.make_async_copy(send_ref.at[place], send_out.at[place], send_sems.at[len(copies)])]
-            )
-    pack_bands(sizes, width_k, own_ref, near_ref, band_refs)
-    for ref, out in zip(band_refs, band_out):
-        copies += started([pltpu.make_async_copy(ref, out, send_sems.at[len(copies)])])
+                send_ref[device, side * cap + rank] = blocks_ref[below(code, rows * n_tiles)]
+        place = (slice(None), pl.ds(side * cap, cap))
+        send(send_ref.at[place], send_out.at[place])
+        if side == 0:
+            pack_bands(sizes, width_k, own_ref, near_ref, band_refs)
+            for ref, out in zip(band_refs, band_out):
+                send(ref, out)
     finish(copies)
 
 

time: 74.6 us -> 74.7 us (level)
  no operation moved by 1% of the time
where the time goes in v18:
time: 74.7 us; the launch traced here: 74.1 us
  starting transfers between devices  31.3 us (42%)
  Pallas kernels  25.8 us (35%)
  waiting for transfers between devices  16.4 us (22%)
    pallas_call x10, Pallas kernels, apply(): return run(*pinned)  25.8 us
    all_to_all x2, starting transfers between devices, exchange(): lax.all_to_all(sends[0], 'rows', split_axis=0, concat_axis=0, tiled=True,...  7.43 us
    ppermute x1, starting transfers between devices, on_device(): mirror = lax.ppermute(start_iterate, 'rows', to_mirror)  4.04 us
    all_to_all x1, starting transfers between devices, on_device(): lax.all_to_all(lists, 'rows', split_axis=0, concat_axis=0, tiled=True)  3.9 us
    all_to_all x1, starting transfers between devices, on_device(): lax.all_to_all(packed, 'rows', split_axis=0, concat_axis=0, tiled=True, a...  3.49 us
    all_to_all x2, waiting for transfers between devices, exchange(): lax.all_to_all(sends[0], 'rows', split_axis=0, concat_axis=0, tiled=True,...  3.39 us
    all_to_all x1, waiting for transfers between devices, on_device(): lax.all_to_all(lists, 'rows', split_axis=0, concat_axis=0, tiled=True)  3.23 us
    ppermute x2, starting transfers between devices, to_bands(): return (lax.ppermute(sends[0], 'band', [(0, 1), (1, 0)]),)  3.1 us
  transfers between devices with their start and end apart: 12, of which 9 were waited for; matrix products, arithmetic and copies ran while one was open for 0% of the time, Pallas kernels for 28%

profile of v18, /device:TPU:0, one launch (start us, length us, event | category | flops | bytes accessed | tf_op | source)
XLA Modules:
  0.0 74.1 jit_solution(17688500853641375958)
XLA Ops:
  0.0 4.0 %collective-permute-start = (f32[32,16,128]{2,1,0:T(8,128)}, f32[32,16,128]{2,1,0:T(8,128)S(1)}, u32[]{:S(2)}, u32[]{:S(2)}) collective-permute-start(f32[32,16,128]{2,1,0:T(8,128)} %start_in.1), channel_id=1, source_target_pairs={{0,8},{1,9},{2,10},{3,11},{4,12},{5,13},{6,14},{7,15},{8,0},{9,1},... | collective-permute-start | bytes 786440 | tf_op jit(solution)/shard_map/ppermute | solution.py:702
  4.0 1.8 %shard_map.100 = (s32[16,1,384]{2,1,0:T(1,128)}, s32[1,1,256]{2,1,0:T(1,128)S(1)}, s32[1,1,128]{2,1,0:T(1,128)S(1)}) custom-call(s32[2,32]{1,0:T(2,128)} %bitcast.18, s32[2,32]{1,0:T(2,128)} %bitcast.19, s32[4,32]{1,0:T(4,128)} %bitcast.17, s32[1,32]{1,0:T(1,128)} %bitcast.20, s32[1,32]{1,0:T(1,128)} %bitcast.21), custom_call_target="tpu_custom_call" | custom-call | tf_op jit(solution)/shard_map/pallas_call | solution.py:49
  5.8 3.9 %all-to-all-start = ((s32[16,1,384]{2,1,0:T(1,128)}), s32[16,1,384]{2,1,0:T(1,128)S(1)}, u32[]{:S(2)}, u32[]{:S(2)}) async-start(s32[16,1,384]{2,1,0:T(1,128)} %get-tuple-element.32), calls=%async_computation | async-start | bytes 49152 | tf_op jit(solution)/shard_map/all_to_all | solution.py:714
  9.7 1.6 %collective-permute-start.1 = (s32[1,1,256]{2,1,0:T(1,128)S(1)}, s32[1,1,256]{2,1,0:T(1,128)S(1)}, u32[]{:S(2)}, u32[]{:S(2)}) collective-permute-start(s32[1,1,256]{2,1,0:T(1,128)S(1)} %get-tuple-element.33.refs_0_.refs_1_), channel_id=1, source_target_pairs={{0,16},{16,0},{1,17},{17,1},{2,18},{18,2},{3,19},{19,3},{4,20},{20... | collective-permute-start | bytes 3080 | tf_op jit(solution)/shard_map/ppermute | solution.py:716
  11.3 3.0 %shard_map.101.refs_0_ = f32[256,16,128]{2,1,0:T(8,128)S(1)} custom-call(f32[32,16,128]{2,1,0:T(8,128)} %start_in.1, f32[8,128,128]{2,1,0:T(8,128)} %refs_3_.4), custom_call_target="tpu_custom_call" | custom-call | flops 402653184 | bytes 4194304 | tf_op jit(solution)/shard_map/pallas_call | solution.py:49
  14.4 3.2 %all-to-all-done.refs_3_.list_in.refs_0_ = s32[16,1,384]{2,1,0:T(1,128)S(1)} async-done(((s32[16,1,384]{2,1,0:T(1,128)}), s32[16,1,384]{2,1,0:T(1,128)S(1)}, u32[]{:S(2)}, u32[]{:S(2)}) %all-to-all-start) | async-done | bytes 24608 | tf_op jit(solution)/shard_map/all_to_all | solution.py:714
  17.6 2.4 %shard_map.102 = (f32[8,16,16,128]{3,2,1,0:T(8,128)}, f32[32,16,128]{2,1,0:T(8,128)}) custom-call(f32[256,16,128]{2,1,0:T(8,128)S(1)} %shard_map.101.refs_0_, f32[32,16,128]{2,1,0:T(8,128)S(1)} %collective-permute-done.refs_1_, f32[8,128,128]{2,1,0:T(8,128)S(1)} %copy-done.1, s32[16,1,384]{2,1,0:T(1,128)S(1)} %all-to-all-done.refs_3_.list_in.refs_0_, ...), custom_call_target="tpu_custom_call" | custom-call | flops 402653184 | bytes 4194304 | tf_op jit(solution)/shard_map/pallas_call | solution.py:49
  20.0 3.7 %all-to-all-start.1 = ((f32[8,256,128]{2,1,0:T(8,128)}), f32[8,256,128]{2,1,0:T(8,128)S(1)}, u32[]{:S(2)}, u32[]{:S(2)}) async-start(f32[8,256,128]{2,1,0:T(8,128)} %bitcast.14), calls=%async_computation.1 | async-start | bytes 2097152 | tf_op jit(solution)/shard_map/all_to_all | solution.py:775
  23.7 1.6 %collective-permute-start.2 = (s32[16,1,384]{2,1,0:T(1,128)S(1)}, s32[16,1,384]{2,1,0:T(1,128)S(1)}, u32[]{:S(2)}, u32[]{:S(2)}) collective-permute-start(s32[16,1,384]{2,1,0:T(1,128)S(1)} %all-to-all-done.refs_3_.list_in.refs_0_), channel_id=1, source_target_pairs={{0,16},{16,0},{1,17},{17,1},{2,18},{18,2},{3,19},{19,3},{4,20},{20... | collective-permute-start | bytes 73736 | tf_op jit(solution)/shard_map/ppermute | solution.py:770
  25.3 2.3 %collective-permute-done.2 = s32[16,1,384]{2,1,0:T(1,128)S(1)} collective-permute-done((s32[16,1,384]{2,1,0:T(1,128)S(1)}, s32[16,1,384]{2,1,0:T(1,128)S(1)}, u32[]{:S(2)}, u32[]{:S(2)}) %collective-permute-start.2) | collective-permute-done | bytes 24608 | tf_op jit(solution)/shard_map/ppermute | solution.py:770
  29.5 6.7 %shard_map.103 = (bf16[256,1440]{1,0:T(8,128)(2,1)}, bf16[128,384]{1,0:T(8,128)(2,1)}, bf16[1024,256]{1,0:T(8,128)(2,1)}, f32[256,128]{1,0:T(8,128)}, f32[4,128]{1,0:T(4,128)S(1)}) custom-call(s32[1,1,256]{2,1,0:T(1,128)S(1)} %get-tuple-element.33.refs_0_.refs_1_, f32[32,16,128]{2,1,0:T(8,128)} %refs_4_.5, s32[8,2,512]{2,1,0:T(2,128)S(1)} %reshape.7.refs_2_, ...), custom_call_target="tpu_custom_call" | custom-call | flops 1342177280 | bytes 4194304 | tf_op jit(solution)/shard_map/pallas_call | solution.py:49
  36.2 1.9 %all-to-all-done.1.refs_2_ = f32[8,256,128]{2,1,0:T(8,128)S(1)} async-done(((f32[8,256,128]{2,1,0:T(8,128)}), f32[8,256,128]{2,1,0:T(8,128)S(1)}, u32[]{:S(2)}, u32[]{:S(2)}) %all-to-all-start.1) | async-done | bytes 1048608 | tf_op jit(solution)/shard_map/all_to_all | solution.py:775
  39.4 2.7 %collective-permute-start.4 = (f32[32,16,128]{2,1,0:T(8,128)S(1)}, f32[32,16,128]{2,1,0:T(8,128)S(1)}, u32[]{:S(2)}, u32[]{:S(2)}) collective-permute-start(f32[32,16,128]{2,1,0:T(8,128)S(1)} %shard_map.104.refs_2_), channel_id=1, source_target_pairs={{0,8},{1,9},{2,10},{3,11},{4,12},{5,13},{6,14},{7,15},{8,0},{9,1},... | collective-permute-start | bytes 786440 | tf_op jit(solution)/shard_map/ppermute | solution.py:849
  42.2 4.2 %shard_map.106 = (f32[8,144,128]{2,1,0:T(8,128)}, f32[32,16,128]{2,1,0:T(8,128)}) custom-call(s32[16,1,384]{2,1,0:T(1,128)S(1)} %all-to-all-done.refs_3_.list_in.refs_0_, s32[1,1,256]{2,1,0:T(1,128)S(1)} %collective-permute-done.1.refs_4_.refs_1_, f32[32,16,128]{2,1,0:T(8,128)S(1)} %shard_map.104.refs_2_, f32[8,128,128]{2,1,0:T(8,128)S(1)} %copy-done.1, ...), custom_call_target="tpu_custom_call" | custom-call | flops 805306368 | bytes 4194304 | tf_op jit(solution)/shard_map/pallas_call | solution.py:49
  46.4 3.7 %all-to-all-start.3 = ((f32[8,144,128]{2,1,0:T(8,128)}), f32[8,144,128]{2,1,0:T(8,128)S(1)}, u32[]{:S(2)}, u32[]{:S(2)}) async-start(f32[8,144,128]{2,1,0:T(8,128)} %get-tuple-element.52), calls=%async_computation.3 | async-start | bytes 1179648 | tf_op jit(solution)/shard_map/all_to_all | solution.py:775
  50.1 1.6 %collective-permute-start.5 = (f32[32,16,128]{2,1,0:T(8,128)}, f32[32,16,128]{2,1,0:T(8,128)S(1)}, u32[]{:S(2)}, u32[]{:S(2)}) collective-permute-start(f32[32,16,128]{2,1,0:T(8,128)} %get-tuple-element.50), channel_id=1, source_target_pairs={{0,16},{16,0},{1,17},{17,1},{2,18},{18,2},{3,19},{19,3},{4,20},{20... | collective-permute-start | bytes 786440 | tf_op jit(solution)/shard_map/ppermute | solution.py:657
  51.7 2.3 %collective-permute-done.4.mirror_ref = f32[32,16,128]{2,1,0:T(8,128)S(1)} collective-permute-done((f32[32,16,128]{2,1,0:T(8,128)S(1)}, f32[32,16,128]{2,1,0:T(8,128)S(1)}, u32[]{:S(2)}, u32[]{:S(2)}) %collective-permute-start.4) | collective-permute-done | bytes 262176 | tf_op jit(solution)/shard_map/ppermute | solution.py:849
  54.0 3.2 %shard_map.105 = f32[8,128,128]{2,1,0:T(8,128)} custom-call(s32[16,1,384]{2,1,0:T(1,128)S(1)} %all-to-all-done.refs_3_.list_in.refs_0_, f32[32,16,128]{2,1,0:T(8,128)S(1)} %collective-permute-done.4.mirror_ref, f32[8,128,128]{2,1,0:T(8,128)S(1)} %copy-done.1, f32[8,128,128]{2,1,0:T(8,128)S(1)} %copy-done), custom_call_target="tpu_custom_call" | custom-call | flops 40265318400 | bytes 4194304 | tf_op jit(solution)/shard_map/pallas_call | solution.py:49
  57.1 1.6 %collective-permute-done.5.refs_5_ = f32[32,16,128]{2,1,0:T(8,128)S(1)} collective-permute-done((f32[32,16,128]{2,1,0:T(8,128)}, f32[32,16,128]{2,1,0:T(8,128)S(1)}, u32[]{:S(2)}, u32[]{:S(2)}) %collective-permute-start.5) | collective-permute-done | bytes 262176 | tf_op jit(solution)/shard_map/ppermute | solution.py:657
  60.3 3.5 %all-to-all-start.2 = ((f32[8,128,128]{2,1,0:T(8,128)}), f32[8,128,128]{2,1,0:T(8,128)S(1)}, u32[]{:S(2)}, u32[]{:S(2)}) async-start(f32[8,128,128]{2,1,0:T(8,128)} %shard_map.105), calls=%async_computation.2 | async-start | bytes 1048576 | tf_op jit(solution)/shard_map/all_to_all | solution.py:890
  63.8 1.6 %collective-permute-start.6 = (f32[8,128]{1,0:T(8,128)S(1)}, f32[8,128]{1,0:T(8,128)S(1)}, u32[]{:S(2)}, u32[]{:S(2)}) collective-permute-start(f32[8,128]{1,0:T(8,128)S(1)} %get-tuple-element.55), channel_id=1, source_target_pairs={{0,16},{16,0},{1,17},{17,1},{2,18},{18,2},{3,19},{19,3},{4,20},{20... | collective-permute-start | bytes 12296 | tf_op jit(solution)/shard_map/ppermute | solution.py:895
  65.4 2.1 %collective-permute-done.6 = f32[8,128]{1,0:T(8,128)S(1)} collective-permute-done((f32[8,128]{1,0:T(8,128)S(1)}, f32[8,128]{1,0:T(8,128)S(1)}, u32[]{:S(2)}, u32[]{:S(2)}) %collective-permute-start.6) | collective-permute-done | bytes 4128 | tf_op jit(solution)/shard_map/ppermute | solution.py:895
  67.5 1.8 %collective-permute-start.7 = (f32[4,128]{1,0:T(4,128)S(1)}, f32[4,128]{1,0:T(4,128)S(1)}, u32[]{:S(2)}, u32[]{:S(2)}) collective-permute-start(f32[4,128]{1,0:T(4,128)S(1)} %get-tuple-element.57), channel_id=1, source_target_pairs={{0,8},{1,9},{2,10},{3,11},{4,12},{5,13},{6,14},{7,15},{8,0},{9,1},... | collective-permute-start | bytes 6152 | tf_op jit(solution)/shard_map/ppermute | solution.py:896
  69.3 1.8 %shard_map.107.refs_2_ = f32[32,16,128]{2,1,0:T(8,128)S(1)} custom-call(s32[1,1,128]{2,1,0:T(1,128)S(1)} %get-tuple-element.31.refs_0_, s32[1,1,256]{2,1,0:T(1,128)S(1)} %get-tuple-element.33.refs_0_.refs_1_, f32[8,144,128]{2,1,0:T(8,128)S(1)} %all-to-all-done.3.refs_2_.arrived_ref, f32[8,128,128]{2,1,0:T(8,128)S(1)} %copy-done, f32[32,16,128]{2,1,0:T(8,128)} %refs_4_.5, ...), custom_call_target="tpu_custom_call" | custom-call | flops 402653184 | bytes 4194304 | tf_op jit(solution)/shard_map/pallas_call | solution.py:49
  (25 shorter events, 7.6 us)
Async XLA Ops:
  0.0 17.6 %copy-start.1 = (f32[8,128,128]{2,1,0:T(8,128)S(1)}, f32[8,128,128]{2,1,0:T(8,128)}, u32[]{:S(2)}) copy-start(f32[8,128,128]{2,1,0:T(8,128)} %refs_3_.4) | copy-start | bytes 1572868
  0.0 17.6 %collective-permute-start = (f32[32,16,128]{2,1,0:T(8,128)}, f32[32,16,128]{2,1,0:T(8,128)S(1)}, u32[]{:S(2)}, u32[]{:S(2)}) collective-permute-start(f32[32,16,128]{2,1,0:T(8,128)} %start_in.1), channel_id=1, source_target_pairs={{0,8},{1,9},{2,10},{3,11},{4,12},{5,13},{6,14},{7,15},{8,0},{9,1},... | collective-permute-start | bytes 786440 | tf_op jit(solution)/shard_map/ppermute | solution.py:702
  5.8 11.8 %all-to-all-start = ((s32[16,1,384]{2,1,0:T(1,128)}), s32[16,1,384]{2,1,0:T(1,128)S(1)}, u32[]{:S(2)}, u32[]{:S(2)}) async-start(s32[16,1,384]{2,1,0:T(1,128)} %get-tuple-element.32), calls=%async_computation | async-start | bytes 49152 | tf_op jit(solution)/shard_map/all_to_all | solution.py:714
  9.7 4.6 %collective-permute-start.1 = (s32[1,1,256]{2,1,0:T(1,128)S(1)}, s32[1,1,256]{2,1,0:T(1,128)S(1)}, u32[]{:S(2)}, u32[]{:S(2)}) collective-permute-start(s32[1,1,256]{2,1,0:T(1,128)S(1)} %get-tuple-element.33.refs_0_.refs_1_), channel_id=1, source_target_pairs={{0,16},{16,0},{1,17},{17,1},{2,18},{18,2},{3,19},{19,3},{4,20},{20... | collective-permute-start | bytes 3080 | tf_op jit(solution)/shard_map/ppermute | solution.py:716
  20.0 9.5 %copy-start = (f32[8,128,128]{2,1,0:T(8,128)S(1)}, f32[8,128,128]{2,1,0:T(8,128)}, u32[]{:S(2)}) copy-start(f32[8,128,128]{2,1,0:T(8,128)} %refs_3_.5) | copy-start | bytes 1572868
  20.0 9.5 %copy-start.3 = (f32[8,128,128]{2,1,0:T(8,128)S(1)}, f32[8,128,128]{2,1,0:T(8,128)}, u32[]{:S(2)}) copy-start(f32[8,128,128]{2,1,0:T(8,128)} %refs_5_.1) | copy-start | bytes 1572868
  20.0 18.1 %all-to-all-start.1 = ((f32[8,256,128]{2,1,0:T(8,128)}), f32[8,256,128]{2,1,0:T(8,128)S(1)}, u32[]{:S(2)}, u32[]{:S(2)}) async-start(f32[8,256,128]{2,1,0:T(8,128)} %bitcast.14), calls=%async_computation.1 | async-start | bytes 2097152 | tf_op jit(solution)/shard_map/all_to_all | solution.py:775
  23.7 3.9 %collective-permute-start.2 = (s32[16,1,384]{2,1,0:T(1,128)S(1)}, s32[16,1,384]{2,1,0:T(1,128)S(1)}, u32[]{:S(2)}, u32[]{:S(2)}) collective-permute-start(s32[16,1,384]{2,1,0:T(1,128)S(1)} %all-to-all-done.refs_3_.list_in.refs_0_), channel_id=1, source_target_pairs={{0,16},{16,0},{1,17},{17,1},{2,18},{18,2},{3,19},{19,3},{4,20},{20... | collective-permute-start | bytes 73736 | tf_op jit(solution)/shard_map/ppermute | solution.py:770
  27.6 10.5 %collective-permute-start.3 = (f32[32,16,128]{2,1,0:T(8,128)}, f32[32,16,128]{2,1,0:T(8,128)S(1)}, u32[]{:S(2)}, u32[]{:S(2)}) collective-permute-start(f32[32,16,128]{2,1,0:T(8,128)} %get-tuple-element.45), channel_id=1, source_target_pairs={{0,16},{16,0},{1,17},{17,1},{2,18},{18,2},{3,19},{19,3},{4,20},{20... | collective-permute-start | bytes 786440 | tf_op jit(solution)/shard_map/ppermute | solution.py:657
  29.5 8.6 %copy-start.2 = (f32[32,16,128]{2,1,0:T(8,128)S(1)}, f32[32,16,128]{2,1,0:T(8,128)}, u32[]{:S(2)}) copy-start(f32[32,16,128]{2,1,0:T(8,128)} %refs_4_.5) | copy-start | bytes 786436
  39.4 14.5 %collective-permute-start.4 = (f32[32,16,128]{2,1,0:T(8,128)S(1)}, f32[32,16,128]{2,1,0:T(8,128)S(1)}, u32[]{:S(2)}, u32[]{:S(2)}) collective-permute-start(f32[32,16,128]{2,1,0:T(8,128)S(1)} %shard_map.104.refs_2_), channel_id=1, source_target_pairs={{0,8},{1,9},{2,10},{3,11},{4,12},{5,13},{6,14},{7,15},{8,0},{9,1},... | collective-permute-start | bytes 786440 | tf_op jit(solution)/shard_map/ppermute | solution.py:849
  46.4 13.9 %all-to-all-start.3 = ((f32[8,144,128]{2,1,0:T(8,128)}), f32[8,144,128]{2,1,0:T(8,128)S(1)}, u32[]{:S(2)}, u32[]{:S(2)}) async-start(f32[8,144,128]{2,1,0:T(8,128)} %get-tuple-element.52), calls=%async_computation.3 | async-start | bytes 1179648 | tf_op jit(solution)/shard_map/all_to_all | solution.py:775
  50.1 8.6 %collective-permute-start.5 = (f32[32,16,128]{2,1,0:T(8,128)}, f32[32,16,128]{2,1,0:T(8,128)S(1)}, u32[]{:S(2)}, u32[]{:S(2)}) collective-permute-start(f32[32,16,128]{2,1,0:T(8,128)} %get-tuple-element.50), channel_id=1, source_target_pairs={{0,16},{16,0},{1,17},{17,1},{2,18},{18,2},{3,19},{19,3},{4,20},{20... | collective-permute-start | bytes 786440 | tf_op jit(solution)/shard_map/ppermute | solution.py:657
  60.3 12.3 %all-to-all-start.2 = ((f32[8,128,128]{2,1,0:T(8,128)}), f32[8,128,128]{2,1,0:T(8,128)S(1)}, u32[]{:S(2)}, u32[]{:S(2)}) async-start(f32[8,128,128]{2,1,0:T(8,128)} %shard_map.105), calls=%async_computation.2 | async-start | bytes 1048576 | tf_op jit(solution)/shard_map/all_to_all | solution.py:890
  63.8 3.7 %collective-permute-start.6 = (f32[8,128]{1,0:T(8,128)S(1)}, f32[8,128]{1,0:T(8,128)S(1)}, u32[]{:S(2)}, u32[]{:S(2)}) collective-permute-start(f32[8,128]{1,0:T(8,128)S(1)} %get-tuple-element.55), channel_id=1, source_target_pairs={{0,16},{16,0},{1,17},{17,1},{2,18},{18,2},{3,19},{19,3},{4,20},{20... | collective-permute-start | bytes 12296 | tf_op jit(solution)/shard_map/ppermute | solution.py:895
  67.5 4.6 %collective-permute-start.7 = (f32[4,128]{1,0:T(4,128)S(1)}, f32[4,128]{1,0:T(4,128)S(1)}, u32[]{:S(2)}, u32[]{:S(2)}) collective-permute-start(f32[4,128]{1,0:T(4,128)S(1)} %get-tuple-element.57), channel_id=1, source_target_pairs={{0,8},{1,9},{2,10},{3,11},{4,12},{5,13},{6,14},{7,15},{8,0},{9,1},... | collective-permute-start | bytes 6152 | tf_op jit(solution)/shard_map/ppermute | solution.py:896
